TPU v7x, 32 devices: a whole 2x2x4 slice. The times are simulated.
32 devices in a mesh: lvl: 8 (over y, x, core), col: 4 (over z).
Axes of the slice: x: 2, y: 2, z: 4, core: 2. Of those that a mesh axis runs over, the one named last changes fastest.
Arguments:
- up_blocks: float32 [16, 512, 512], P('lvl', None, 'col'), may hold values from -1.25 to 1.25
- level_blocks: float32 [16, 512, 512], P('lvl', None, 'col'), may hold values from -11 to 2, as said below
- down_blocks: float32 [16, 512, 512], P('lvl', None, 'col'), may hold values from -1.25 to 1.25
Outputs:
- reduced_level: float32 [8, 512, 512], P('lvl', None, 'col')
- reduced_up: float32 [8, 512, 512], P('lvl', None, 'col')
- reduced_down: float32 [8, 512, 512], P('lvl', None, 'col')
Inputs may be any that keep to these rules, and one draw needn't show every extreme that they name: `level_blocks`: every diagonal entry of every level's block is -1 or less.
All inputs are finite; a program needn't handle non-finite values.
Results may differ from a plain program's by a relative error of at most 0.00013.
Values sent between devices are 32-bit elements; how exact they have to be, the bound alone decides.
No kernel may reach another device: no remote copies, remote signals or barrier semaphores. Data moves between devices by JAX's collectives and lax.ppermute only.
A program may use at most 64 MiB of HBM per device.

v0:
```python
import jax
import jax.numpy as jnp
from jax import lax
from jax.sharding import PartitionSpec as P

SWEEPS = 2


def from_behind(block, axis, distance):
    devices = range(lax.axis_size(axis))
    route = [(i - distance, i) for i in devices if i - distance in devices]
    return lax.ppermute(block, axis, route)


def per_device(up_blocks, level_blocks, down_blocks):
    col_share = level_blocks.shape[2]
    odd_level = level_blocks[1::2]
    right_side = jnp.concatenate([up_blocks[1::2], down_blocks[1::2]], axis=2)
    full_level, full_up, full_down = (
        lax.all_gather(odd_level, "col", axis=2, tiled=True),
        lax.all_gather(up_blocks[0::2], "col", axis=2, tiled=True),
        lax.all_gather(down_blocks[0::2], "col", axis=2, tiled=True),
    )
    out_rates = -jnp.diagonal(full_level, axis1=1, axis2=2)
    inverse = (1.0 / out_rates)[:, :, None]
    solution = right_side * inverse
    for sweep_no in range(SWEEPS):
        product = jnp.einsum(
            "lpk,lkc->lpc",
            full_level,
            solution,
            precision=lax.Precision.HIGHEST,
            preferred_element_type=jnp.float32,
        )
        solution = (right_side + product + out_rates[:, :, None] * solution) * inverse
    from_below = from_behind(solution[-1], "lvl", 1)
    lower_side = jnp.concatenate([from_below[None], solution[:-1]], axis=0)
    upper_terms = jnp.einsum(
        "lpk,lkc->lpc",
        full_up,
        solution,
        precision=lax.Precision.HIGHEST,
        preferred_element_type=jnp.float32,
    )
    lower_terms = jnp.einsum(
        "lpk,lkc->lpc",
        full_down,
        lower_side,
        precision=lax.Precision.HIGHEST,
        preferred_element_type=jnp.float32,
    )
    row_start = lax.axis_index("col") * col_share
    own_square = lax.dynamic_slice_in_dim(level_blocks, row_start, col_share, 1)
    local_peak = jnp.max(-jnp.diagonal(own_square, axis1=1, axis2=2))
    top_rate = lax.pmax(local_peak, ("lvl", "col"))
    reduced_level = (
        level_blocks[0::2] + upper_terms[:, :, col_share:] + lower_terms[:, :, :col_share]
    ) / top_rate
    reduced_up = upper_terms[:, :, :col_share] / top_rate
    reduced_down = lower_terms[:, :, col_share:] / top_rate
    return (reduced_level, reduced_up, reduced_down)


def solution(mesh):
    placed = (P("lvl", None, "col"), P("lvl", None, "col"), P("lvl", None, "col"))
    return jax.shard_map(
        per_device,
        mesh=mesh,
        in_specs=placed,
        out_specs=(P("lvl", None, "col"), P("lvl", None, "col"), P("lvl", None, "col")),
        check_vma=False,
    )
```

profile of v0, /device:TPU:0, one launch (start us, length us, event | category | flops | bytes accessed | tf_op | source)
XLA Modules:
  0.0 123.4 jit_solution(12844497460994838590)
XLA Ops:
  7.2 0.0 all-gather.4.cloned.1.call-start
  7.2 1.8 %fusion.18 = (f32[1,512,128]{2,1,0:T(8,128)S(1)}, f32[1,512,128]{2,1,0:T(8,128)}) fusion(f32[2,512,128]{2,1,0:T(8,128)} %param.4), kind=kLoop, calls=%fused_computation.34 | loop fusion | bytes 1048576 | tf_op jit(solution)/shard_map/slice | solution.py:57
  9.0 0.0 all-gather.4.cloned.1.call-update
  9.0 0.0 all-gather.6.cloned.1.call-start
  9.1 1.8 %fusion.17 = (f32[1,512,128]{2,1,0:T(8,128)}, f32[1,512,128]{2,1,0:T(8,128)S(1)}) fusion(f32[2,512,128]{2,1,0:T(8,128)} %param.3), kind=kLoop, calls=%fused_computation.33 | loop fusion | bytes 1048576 | tf_op jit(solution)/shard_map/slice | solution.py:21
  10.8 0.0 all-gather.6.cloned.1.call-update
  10.8 0.0 all-gather.8.cloned.1.call-start
  10.9 1.8 %fusion.19 = (f32[1,512,128]{2,1,0:T(8,128)}, f32[1,512,128]{2,1,0:T(8,128)S(1)}) fusion(f32[2,512,128]{2,1,0:T(8,128)} %param.5), kind=kLoop, calls=%fused_computation.35 | loop fusion | bytes 1048576 | tf_op jit(solution)/shard_map/slice | solution.py:22
  12.7 0.0 all-gather.8.cloned.1.call-update
  12.7 0.1 copy.21
  12.8 0.1 copy.22
  13.0 30.1 %all-gather.4.cloned.1.call-done = f32[1,512,512]{2,1,0:T(8,128)} async-done(((f32[1,512,128]{2,1,0:T(8,128)}), f32[1,512,512]{2,1,0:T(8,128)}) %all-gather.4.cloned.1.call-update) | async-done | bytes 1048592 | tf_op jit(solution)/shard_map/all_gather | solution.py:20
  43.1 8.5 %gather_fusion = f32[512]{0:T(512)S(1)} fusion(f32[512,512]{1,0:T(8,128)} %bitcast.49, s32[512]{0:T(512)S(1)} %bitcast.48), kind=kCustom, calls=%fused_computation | custom fusion | bytes 8192 | tf_op jit(solution)/shard_map/jit(diagonal)/gather | solution.py:24
  51.6 2.3 %fusion.4 = f32[512,256]{0,1:T(8,128)S(1)} fusion(f32[1,512,1,1,1,1,128]{1,6,5,4,3,2,0:T(8,128)S(1)} %bitcast.53, f32[1,512,1,1,1,1,128]{1,6,5,4,3,2,0:T(8,128)S(1)} %bitcast.50, f32[512,128]{0,1:T(8,128)S(1)} %bitcast.54, f32[512,128]{0,1:T(8,128)S(1)} %bitcast.51, f32[512]{0:T(512)S(1)} %get-tuple-element.19, f32[512]{0:T(512)S(1)} %get-tuple-element.18, ...), kind=kOutput, calls=%fused_computation.10 | convolution fusion | flops 806354944 | bytes 2625536 | tf_op jit(solution)/shard_map/lpk,lkc->lpc/dot_general | solution.py:28
  54.0 2.3 %fusion.5 = f32[512,256]{0,1:T(8,128)S(1)} fusion(f32[512,256]{0,1:T(8,128)S(1)} %fusion.4, f32[512,128]{0,1:T(8,128)S(1)} %bitcast.55, f32[512,128]{0,1:T(8,128)S(1)} %bitcast.52, f32[512]{0:T(512)S(1)} %get-tuple-element.19, f32[512]{0:T(512)S(1)} %get-tuple-element.18, f32[1,512,512]{2,1,0:T(8,128)} %all-gather.4.cloned.1.call-done), kind=kOutput, calls=%fused_computation.11 | convolution fusion | flops 805961728 | bytes 2625536 | tf_op jit(solution)/shard_map/lpk,lkc->lpc/dot_general | solution.py:28
  56.3 1.3 %collective-permute-start = (f32[512,256]{0,1:T(8,128)S(1)}, f32[512,256]{0,1:T(8,128)S(1)}, u32[]{:S(2)}, u32[]{:S(2)}) collective-permute-start(f32[512,256]{0,1:T(8,128)S(1)} %fusion.5), channel_id=1, source_target_pairs={{0,4},{4,8},{8,12},{12,16},{16,20},{20,24},{24,28},{1,5},{5,9},{9,... | collective-permute-start | bytes 1572872 | tf_op jit(solution)/shard_map/ppermute | solution.py:12
  57.6 0.9 constant_dynamic-slice_fusion
  58.5 4.6 %copy.23 = f32[2,128,128]{0,2,1:T(8,128)} copy(f32[2,128,128]{2,1,0:T(8,128)S(1)} %constant_dynamic-slice_fusion) | data formatting | bytes 262144
  63.2 1.8 %gather_fusion.1 = f32[128,2]{1,0:T(8,128)S(1)} fusion(f32[2,128,128]{0,2,1:T(8,128)} %copy.23, s32[128]{0:T(128)S(1)} %or_bitcast_fusion), kind=kCustom, calls=%fused_computation.1 | custom fusion | bytes 3072 | tf_op jit(solution)/shard_map/jit(diagonal)/gather | solution.py:54
  64.9 0.6 negate_reduce_fusion
  65.6 43.2 %pmax.7 = f32[]{:T(128)} all-reduce(f32[]{:T(128)} %negate_reduce_fusion), channel_id=1, replica_groups=mesh['lvl'=8,'col'=4] {'lvl','col'}, use_global_device_ids=true, to_apply=%region_1.2 | all-reduce | flops 1 | bytes 8 | tf_op jit(solution)/shard_map/pmax | solution.py:55
  108.8 0.1 copy.20
  108.9 0.0 all-gather.6.cloned.1.call-done
  109.0 2.3 %convolution_bitcast_fusion.1 = f32[1,512,256]{1,2,0:T(8,128)S(1)} fusion(f32[512,256]{0,1:T(8,128)S(1)} %fusion.5, f32[1,512,512]{2,1,0:T(8,128)} %all-gather.6.cloned.1.call-done), kind=kOutput, calls=%fused_computation.3 | convolution fusion | flops 805306368 | bytes 2097152 | tf_op jit(solution)/shard_map/lpk,lkc->lpc/dot_general | solution.py:38
  111.2 0.0 all-gather.8.cloned.1.call-done
  111.3 0.0 collective-permute-done
  111.3 2.3 %convolution_bitcast_fusion = f32[1,512,256]{1,2,0:T(8,128)S(1)} fusion(f32[512,256]{0,1:T(8,128)S(1)} %collective-permute-done, f32[1,512,512]{2,1,0:T(8,128)} %all-gather.8.cloned.1.call-done), kind=kOutput, calls=%fused_computation.2 | convolution fusion | flops 805306368 | bytes 2097152 | tf_op jit(solution)/shard_map/lpk,lkc->lpc/dot_general | solution.py:45
  113.6 0.8 slice_divide_fusion
  114.4 0.8 copy.17
  115.2 0.8 copy.18
  116.0 0.8 copy.19
  (3 shorter events, 0.0 us)
Async XLA Ops:
  7.2 35.9 %all-gather.4.cloned.1.call-start = ((), (), s32[]{:S(2)}) async-start(), calls=%async_computation | async-start | bytes 1310720 | tf_op jit(solution)/shard_map/all_gather | solution.py:20
  9.0 99.9 %all-gather.6.cloned.1.call-start = ((), (), s32[]{:S(2)}) async-start(), calls=%async_computation.1 | async-start | bytes 1310720 | tf_op jit(solution)/shard_map/all_gather | solution.py:21
  10.8 100.4 %all-gather.8.cloned.1.call-start = ((), (), s32[]{:S(2)}) async-start(), calls=%async_computation.2 | async-start | bytes 1310720 | tf_op jit(solution)/shard_map/all_gather | solution.py:22
  56.3 55.0 %collective-permute-start = (f32[512,256]{0,1:T(8,128)S(1)}, f32[512,256]{0,1:T(8,128)S(1)}, u32[]{:S(2)}, u32[]{:S(2)}) collective-permute-start(f32[512,256]{0,1:T(8,128)S(1)} %fusion.5), channel_id=1, source_target_pairs={{0,4},{4,8},{8,12},{12,16},{16,20},{20,24},{24,28},{1,5},{5,9},{9,... | collective-permute-start | bytes 1572872 | tf_op jit(solution)/shard_map/ppermute | solution.py:12
Sparse Core Ops, SparseCore 0:
  10.1 32.8 all-gather.3
  45.2 28.4 all-gather.5
  75.9 28.9 all-gather.7
where the time goes:
time: 124 us; the launch traced here: 123 us
  blocking collectives  43.2 us (35%)
  waiting for transfers between devices  30.2 us (24%)
  local copies, waits for them, and re-layouts  24.1 us (19%)
  between operations  13.9 us (11%)
  matrix products  9.18 us (7%)
  starting transfers between devices  1.44 us (1%)
  other arithmetic  1.41 us (1%)
    pmax x1, blocking collectives, per_device(): top_rate = lax.pmax(local_peak, ('lvl', 'col'))  43.2 us
    all_gather x1, waiting for transfers between devices, per_device(): lax.all_gather(odd_level, 'col', axis=2, tiled=True)  30.1 us
    gather x1, local copies, waits for them, and re-layouts, per_device(): out_rates = -jnp.diagonal(full_level, axis1=1, axis2=2)  8.54 us
    unnamed x7, local copies, waits for them, and re-layouts  7.54 us
    dot_general x2, matrix products, per_device(): jnp.einsum('lpk,lkc->lpc', full_level, solution, precision=lax.Precision....  4.62 us
  transfers between devices with their start and end apart: 4, of which 1 were waited for; matrix products, arithmetic and copies ran while one was open for 22% of the time, Pallas kernels for 0%

commit v1 on v0

v1 whole, which is shorter than its diff:
```python
import jax
import jax.numpy as jnp
from jax import lax
from jax.experimental import pallas as pl
from jax.experimental.pallas import tpu as pltpu
from jax.sharding import PartitionSpec as P

SWEEPS = 2
PEAK_ROWS = 8
F32 = jnp.float32
BF16 = jnp.bfloat16
VMEM = pl.BlockSpec(memory_space=pltpu.VMEM)
SMEM = pl.BlockSpec(memory_space=pltpu.SMEM)


def ring_offsets(shards):
    return [0, *[-d for d in range(1, shards // 2 + 1)], *range(1, (shards - 1) // 2 + 1)]


def split(x):
    high = x.astype(BF16)
    return high, (x - high.astype(F32)).astype(BF16)


def exact_dot(left, right):
    (left_high, left_low), (right_high, right_low) = left, right
    dot = lambda a, b: jnp.dot(a, b, preferred_element_type=F32)
    return dot(left_high, right_high) + (dot(left_high, right_low) + dot(left_low, right_high))


def on_diagonal(rows, cols):
    row = lax.broadcasted_iota(jnp.int32, (rows, cols), 0)
    return row == lax.broadcasted_iota(jnp.int32, (rows, cols), 1)


def pack_kernel(own_row, level_ref, packed_ref):
    _, phases, cols = level_ref.shape
    start = pl.multiple_of(own_row[0], cols)
    own = level_ref[:, pl.ds(start, cols), :]
    lowest = jnp.min(jnp.where(on_diagonal(cols, cols)[None], own, 0.0))
    packed_ref[pl.ds(0, phases), :] = level_ref[1]
    packed_ref[pl.ds(phases, PEAK_ROWS), :] = jnp.full((PEAK_ROWS, cols), -lowest, F32)


def owner_row(own_row, offset, cols, shards):
    return pl.multiple_of(lax.rem(own_row[0] + (offset + shards) * cols, shards * cols), cols)


def solve_kernel(own_row, *refs):
    shards = len(refs) - 9
    blocks = refs[:shards]
    up_ref, down_ref, solved_ref, peak_ref, inverse, high, low, s_high, s_low = refs[shards:]
    phases, cols = inverse.shape
    diagonal = on_diagonal(cols, cols)
    peak = None
    for slot, (offset, block) in enumerate(zip(ring_offsets(shards), blocks)):
        start = owner_row(own_row, offset, cols, shards)
        slot_cols = pl.ds(slot * cols, cols)
        high[:, slot_cols], low[:, slot_cols] = split(block[pl.ds(0, phases), :])
        square = block[pl.ds(start, cols), :]
        rate = -jnp.sum(jnp.where(diagonal, square, 0.0), axis=1, keepdims=True)
        inverse[pl.ds(start, cols), :] = jnp.broadcast_to(1.0 / rate, (cols, cols))
        rows = pl.ds(start, cols)
        high[rows, slot_cols], low[rows, slot_cols] = split(jnp.where(diagonal, 0.0, square))
        block_peak = block[pl.ds(phases, PEAK_ROWS), :]
        peak = block_peak if peak is None else jnp.maximum(peak, block_peak)
    peak_ref[...] = peak
    for side, ref in enumerate((up_ref, down_ref)):
        solved_ref[:, pl.ds(side * cols, cols)] = ref[0] * inverse[...]
    for _ in range(SWEEPS):
        for slot, offset in enumerate(ring_offsets(shards)):
            rows = pl.ds(owner_row(own_row, offset, cols, shards), cols)
            slot_rows = pl.ds(slot * cols, cols)
            s_high[slot_rows, :], s_low[slot_rows, :] = split(solved_ref[rows, :])
        product = exact_dot((high[...], low[...]), (s_high[...], s_low[...]))
        for side, ref in enumerate((up_ref, down_ref)):
            columns = slice(side * cols, (side + 1) * cols)
            solved_ref[:, columns] = (ref[0] + product[:, columns]) * inverse[...]


def gathered_product(own_row, blocks, solved_ref):
    shards, cols = len(blocks), blocks[0].shape[-1]
    left = split(jnp.concatenate([block[...] for block in blocks], axis=1))
    rows = [pl.ds(owner_row(own_row, offset, cols, shards), cols) for offset in ring_offsets(shards)]
    right = split(jnp.concatenate([solved_ref[r, :] for r in rows], axis=0))
    return exact_dot(left, right)


def upper_kernel(own_row, *refs):
    *blocks, solved_ref, out_ref = refs
    out_ref[...] = gathered_product(own_row, blocks, solved_ref)


def lower_kernel(own_row, *refs):
    *blocks, solved_ref, upper_ref, level_ref, peak_ref, new_level, new_up, new_down = refs
    cols = new_up.shape[-1]
    lower = gathered_product(own_row, blocks, solved_ref)
    scale = 1.0 / peak_ref[0:1, :]
    new_up[0] = upper_ref[:, :cols] * scale
    new_down[0] = lower[:, cols:] * scale
    new_level[0] = (level_ref[0] + upper_ref[:, cols:] + lower[:, :cols]) * scale


def per_device(up_blocks, level_blocks, down_blocks):
    levels, phases, cols = level_blocks.shape
    assert levels == 2
    shards = lax.axis_size("col")
    ranges = lax.axis_size("lvl")
    own_row = (lax.axis_index("col") * cols).astype(jnp.int32).reshape(1)
    params = pltpu.CompilerParams(vmem_limit_bytes=32 * 2**20)
    shape = lambda *dims, kind=F32: jax.ShapeDtypeStruct(dims, kind)

    def shifted(block, distance):
        return lax.ppermute(block, "col", [(i, (i + distance) % shards) for i in range(shards)])

    def after(value, *earlier):
        return lax.optimization_barrier((value, *earlier))[0]

    def odd(ref_cols):
        return pl.BlockSpec((1, phases, ref_cols), lambda step: (1, 0, 0))

    packed = pl.pallas_call(
        pack_kernel,
        out_shape=shape(phases + PEAK_ROWS, cols),
        in_specs=[SMEM, VMEM],
        out_specs=VMEM,
        grid=(1,),
        compiler_params=params,
    )(own_row, level_blocks)

    def gather(block):
        found = {0: block}
        for d in range(1, shards // 2 + 1):
            found[-d] = shifted(found[-d + 1], 1)
        for d in range(1, (shards - 1) // 2 + 1):
            found[d] = shifted(found[d - 1], -1)
        return [found[offset] for offset in ring_offsets(shards)]

    level_parts = gather(packed)
    up_parts = gather(after(up_blocks[0], level_parts[1]))
    down_parts = gather(after(down_blocks[0], up_parts[1]))

    solved, peak = pl.pallas_call(
        solve_kernel,
        out_shape=(shape(phases, 2 * cols), shape(PEAK_ROWS, cols)),
        in_specs=[SMEM, *[VMEM] * shards, odd(cols), odd(cols)],
        out_specs=(VMEM, VMEM),
        scratch_shapes=[
            pltpu.VMEM((phases, cols), F32),
            pltpu.VMEM((phases, phases), BF16),
            pltpu.VMEM((phases, phases), BF16),
            pltpu.VMEM((phases, 2 * cols), BF16),
            pltpu.VMEM((phases, 2 * cols), BF16),
        ],
        grid=(1,),
        compiler_params=params,
    )(own_row, *level_parts, up_blocks, down_blocks)

    from_below = lax.ppermute(solved, "lvl", [(i, i + 1) for i in range(ranges - 1)])
    reach = 1
    while reach < ranges:
        other = lax.ppermute(peak, "lvl", [(i, (i + reach) % ranges) for i in range(ranges)])
        peak = jnp.maximum(peak, other)
        reach *= 2

    upper = pl.pallas_call(
        upper_kernel,
        out_shape=shape(phases, 2 * cols),
        in_specs=[SMEM, *[VMEM] * (shards + 1)],
        out_specs=VMEM,
        grid=(1,),
        compiler_params=params,
    )(own_row, *up_parts, solved)

    even = pl.BlockSpec((1, phases, cols), lambda step: (0, 0, 0))
    return pl.pallas_call(
        lower_kernel,
        out_shape=(shape(1, phases, cols),) * 3,
        in_specs=[SMEM, *[VMEM] * (shards + 2), even, VMEM],
        out_specs=(VMEM,) * 3,
        grid=(1,),
        compiler_params=params,
    )(own_row, *down_parts, from_below, upper, level_blocks, peak)


def solution(mesh):
    placed = (P("lvl", None, "col"),) * 3
    return jax.shard_map(per_device, mesh=mesh, in_specs=placed, out_specs=placed, check_vma=False)
```

time: 124 us -> 76.4 us (0.62)
  blocking collectives: 43.2 us -> 0 us
  starting transfers between devices: 1.44 us -> 31.1 us
  local copies, waits for them, and re-layouts: 24.1 us -> 2.04 us
  between operations: 13.9 us -> 0.73 us
  matrix products: 9.18 us -> 0 us
  waiting for transfers between devices: 30.2 us -> 37.8 us
  Pallas kernels: 0 us -> 4.58 us
  other arithmetic: 1.41 us -> 0.01 us
    pmax x1 -> x0, blocking collectives: 43.2 us -> none  [per_device(): top_rate = lax.pmax(local_peak, ('lvl', 'col'))]
    ppermute x1 -> x13, waiting for transfers between devices: 0.01 us -> 37.8 us  [the longest x9 33.5 us: shifted(): lax.ppermute(block, 'col', [(i, (i + distance) % shards) for i in range(s...]
    all_gather x3 -> x0, waiting for transfers between devices: 30.1 us -> none  [the longest x1 30.1 us: per_device(): lax.all_gather(odd_level, 'col', axis=2, tiled=True)]
    ppermute x1 -> x13, starting transfers between devices: 1.32 us -> 31.1 us  [the longest x9 17.9 us: shifted(): lax.ppermute(block, 'col', [(i, (i + distance) % shards) for i in range(s...]
    gather x2 -> x0, local copies, waits for them, and re-layouts: 10.3 us -> none  [the longest x1 8.54 us: per_device(): out_rates = -jnp.diagonal(full_level, axis1=1, axis2=2)]
    dot_general x4 -> x0, matrix products: 9.18 us -> none  [the longest x2 4.62 us: per_device(): jnp.einsum('lpk,lkc->lpc', full_level, solution, precision=lax.Precision....]
    unnamed x7 -> x8, local copies, waits for them, and re-layouts: 7.54 us -> 1.05 us
    slice x3 -> x0, local copies, waits for them, and re-layouts: 5.3 us -> none  [the longest x1 1.77 us: per_device(): level_blocks[0::2] + upper_terms[:, :, col_share:]]
  transfers between devices with their start and end apart: 4 -> 13, of which waited for: 1 -> 8; matrix products, arithmetic and copies ran while one was open for 22% -> 1% of each run, Pallas kernels for 0% -> 4%
where the time goes in v1:
time: 76.4 us; the launch traced here: 76.2 us
  waiting for transfers between devices  37.8 us (49%)
  starting transfers between devices  31.1 us (41%)
  Pallas kernels  4.58 us (6%)
  local copies, waits for them, and re-layouts  2.04 us (3%)
    ppermute x9, waiting for transfers between devices, shifted(): lax.ppermute(block, 'col', [(i, (i + distance) % shards) for i in range(s...  33.5 us
    ppermute x9, starting transfers between devices, shifted(): lax.ppermute(block, 'col', [(i, (i + distance) % shards) for i in range(s...  17.9 us
    ppermute x3, starting transfers between devices, per_device(): lax.ppermute(peak, 'lvl', [(i, (i + reach) % ranges) for i in range(range...  11.9 us
    ppermute x3, waiting for transfers between devices, per_device(): lax.ppermute(peak, 'lvl', [(i, (i + reach) % ranges) for i in range(range...  4.28 us
    pallas_call x1, Pallas kernels, per_device(): pl.pallas_call(solve_kernel, out_shape=(shape(phases, 2 * cols), shape(PE...  2.39 us
  transfers between devices with their start and end apart: 13, of which 8 were waited for; matrix products, arithmetic and copies ran while one was open for 1% of the time, Pallas kernels for 4%

profile of v1, /device:TPU:0, one launch (start us, length us, event | category | flops | bytes accessed | tf_op | source)
XLA Modules:
  0.0 76.2 jit_solution(14721692581992111914)
XLA Ops:
  0.6 0.0 copy-start
  0.6 1.0 %copy-done = f32[2,512,128]{2,1,0:T(8,128)S(1)} copy-done((f32[2,512,128]{2,1,0:T(8,128)S(1)}, f32[2,512,128]{2,1,0:T(8,128)}, u32[]{:S(2)}) %copy-start) | copy-done | bytes 524312
  1.7 0.0 copy-start.2
  1.7 0.1 shard_map.58.refs_0_
  1.8 0.0 copy-start.3
  1.8 3.1 %collective-permute-start = (f32[520,128]{1,0:T(8,128)S(1)}, f32[520,128]{1,0:T(8,128)S(1)}, u32[]{:S(2)}, u32[]{:S(2)}) collective-permute-start(f32[520,128]{1,0:T(8,128)S(1)} %shard_map.58.refs_0_), channel_id=1, source_target_pairs={{0,1},{1,2},{2,3},{3,0},{4,5},{5,6},{6,7},{7,4},{8,9},{9,10},{10,1... | collective-permute-start | bytes 798728 | tf_op jit(solution)/shard_map/ppermute | solution.py:114
  4.9 2.1 %collective-permute-start.6 = (f32[520,128]{1,0:T(8,128)S(1)}, f32[520,128]{1,0:T(8,128)S(1)}, u32[]{:S(2)}, u32[]{:S(2)}) collective-permute-start(f32[520,128]{1,0:T(8,128)S(1)} %shard_map.58.refs_0_), channel_id=1, source_target_pairs={{0,3},{1,0},{2,1},{3,2},{4,7},{5,4},{6,5},{7,6},{8,11},{9,8},{10,9... | collective-permute-start | bytes 798728 | tf_op jit(solution)/shard_map/ppermute | solution.py:114
  7.0 7.2 %collective-permute-done.refs_1_ = f32[520,128]{1,0:T(8,128)S(1)} collective-permute-done((f32[520,128]{1,0:T(8,128)S(1)}, f32[520,128]{1,0:T(8,128)S(1)}, u32[]{:S(2)}, u32[]{:S(2)}) %collective-permute-start) | collective-permute-done | bytes 266272 | tf_op jit(solution)/shard_map/ppermute | solution.py:114
  14.2 0.0 collective-permute-start.5
  14.2 1.0 %slice_bitcast_fusion.refs_0_ = f32[512,128]{1,0:T(8,128)S(1)} fusion(f32[2,512,128]{2,1,0:T(8,128)} %refs_4_.1), kind=kLoop, calls=%fused_computation | loop fusion | bytes 524288 | tf_op jit(solution)/shard_map/squeeze | solution.py:140
  15.2 5.1 %collective-permute-start.1 = (f32[512,128]{1,0:T(8,128)S(1)}, f32[512,128]{1,0:T(8,128)S(1)}, u32[]{:S(2)}, u32[]{:S(2)}) collective-permute-start(f32[512,128]{1,0:T(8,128)S(1)} %slice_bitcast_fusion.refs_0_), channel_id=1, source_target_pairs={{0,1},{1,2},{2,3},{3,0},{4,5},{5,6},{6,7},{7,4},{8,9},{9,10},{10,1... | collective-permute-start | bytes 786440 | tf_op jit(solution)/shard_map/ppermute | solution.py:114
  20.3 0.0 copy-done.2
  20.3 10.1 %collective-permute-done.1.refs_1_ = f32[512,128]{1,0:T(8,128)S(1)} collective-permute-done((f32[512,128]{1,0:T(8,128)S(1)}, f32[512,128]{1,0:T(8,128)S(1)}, u32[]{:S(2)}, u32[]{:S(2)}) %collective-permute-start.1) | collective-permute-done | bytes 262176 | tf_op jit(solution)/shard_map/ppermute | solution.py:114
  30.4 0.0 collective-permute-start.2
  30.4 0.0 collective-permute-done.6.refs_3_
  30.4 0.0 collective-permute-done.5.refs_2_
  30.4 0.0 copy-done.3
  30.4 2.4 %shard_map.59 = (f32[512,256]{1,0:T(8,128)S(1)}, f32[8,128]{1,0:T(8,128)S(1)}) custom-call(s32[1]{0:T(128)} %bitcast.own_row, f32[520,128]{1,0:T(8,128)S(1)} %shard_map.58.refs_0_, f32[520,128]{1,0:T(8,128)S(1)} %collective-permute-done.refs_1_, f32[520,128]{1,0:T(8,128)S(1)} %collective-permute-done.5.refs_2_, ...), custom_call_target="tpu_custom_call" | custom-call | tf_op jit(solution)/shard_map/pallas_call | solution.py:143
  32.8 1.3 %collective-permute-start.7 = (f32[512,256]{1,0:T(8,128)S(1)}, f32[512,256]{1,0:T(8,128)S(1)}, u32[]{:S(2)}, u32[]{:S(2)}) collective-permute-start(f32[512,256]{1,0:T(8,128)S(1)} %get-tuple-element.9.refs_4_), channel_id=1, source_target_pairs={{0,4},{4,8},{8,12},{12,16},{16,20},{20,24},{24,28},{1,5},{5,9},{9,... | collective-permute-start | bytes 1572872 | tf_op jit(solution)/shard_map/ppermute | solution.py:159
  34.2 2.2 %collective-permute-start.10 = (f32[8,128]{1,0:T(8,128)S(1)}, f32[8,128]{1,0:T(8,128)S(1)}, u32[]{:S(2)}, u32[]{:S(2)}) collective-permute-start(f32[8,128]{1,0:T(8,128)S(1)} %get-tuple-element.10), channel_id=1, source_target_pairs={{0,4},{4,8},{8,12},{12,16},{16,20},{20,24},{24,28},{28,0},{1,5},{5... | collective-permute-start | bytes 12296 | tf_op jit(solution)/shard_map/ppermute | solution.py:162
  36.4 1.7 %collective-permute-done.10 = f32[8,128]{1,0:T(8,128)S(1)} collective-permute-done((f32[8,128]{1,0:T(8,128)S(1)}, f32[8,128]{1,0:T(8,128)S(1)}, u32[]{:S(2)}, u32[]{:S(2)}) %collective-permute-start.10) | collective-permute-done | bytes 4128 | tf_op jit(solution)/shard_map/ppermute | solution.py:162
  38.1 6.7 %collective-permute-start.11 = (f32[8,128]{1,0:T(8,128)S(1)}, f32[8,128]{1,0:T(8,128)S(1)}, u32[]{:S(2)}, u32[]{:S(2)}) collective-permute-start(f32[8,128]{1,0:T(8,128)S(1)} %max.9), channel_id=1, source_target_pairs={{0,8},{4,12},{8,16},{12,20},{16,24},{20,28},{24,0},{28,4},{1,9},{5... | collective-permute-start | bytes 12296 | tf_op jit(solution)/shard_map/ppermute | solution.py:162
  44.9 2.5 %collective-permute-done.11 = f32[8,128]{1,0:T(8,128)S(1)} collective-permute-done((f32[8,128]{1,0:T(8,128)S(1)}, f32[8,128]{1,0:T(8,128)S(1)}, u32[]{:S(2)}, u32[]{:S(2)}) %collective-permute-start.11) | collective-permute-done | bytes 4128 | tf_op jit(solution)/shard_map/ppermute | solution.py:162
  47.4 2.9 %collective-permute-start.12 = (f32[8,128]{1,0:T(8,128)S(1)}, f32[8,128]{1,0:T(8,128)S(1)}, u32[]{:S(2)}, u32[]{:S(2)}) collective-permute-start(f32[8,128]{1,0:T(8,128)S(1)} %max.10), channel_id=1, source_target_pairs={{0,16},{4,20},{8,24},{12,28},{16,0},{20,4},{24,8},{28,12},{1,17},{... | collective-permute-start | bytes 12296 | tf_op jit(solution)/shard_map/ppermute | solution.py:162
  50.3 3.8 %collective-permute-start.9 = (f32[512,128]{1,0:T(8,128)S(1)}, f32[512,128]{1,0:T(8,128)S(1)}, u32[]{:S(2)}, u32[]{:S(2)}) collective-permute-start(f32[512,128]{1,0:T(8,128)S(1)} %slice_bitcast_fusion.refs_0_), channel_id=1, source_target_pairs={{0,3},{1,0},{2,1},{3,2},{4,7},{5,4},{6,5},{7,6},{8,11},{9,8},{10,9... | collective-permute-start | bytes 786440 | tf_op jit(solution)/shard_map/ppermute | solution.py:114
  54.1 0.0 collective-permute-start.8
  54.1 0.0 collective-permute-done.12
  54.1 3.8 %collective-permute-start.4 = (f32[512,128]{1,0:T(8,128)S(1)}, f32[512,128]{1,0:T(8,128)S(1)}, u32[]{:S(2)}, u32[]{:S(2)}) collective-permute-start(f32[512,128]{1,0:T(8,128)S(1)} %slice_bitcast_fusion.1.refs_0_), channel_id=1, source_target_pairs={{0,3},{1,0},{2,1},{3,2},{4,7},{5,4},{6,5},{7,6},{8,11},{9,8},{10,9... | collective-permute-start | bytes 786440 | tf_op jit(solution)/shard_map/ppermute | solution.py:114
  57.9 0.0 collective-permute-done.2.refs_1_
  58.0 0.0 collective-permute-start.3
  58.0 0.0 copy-start.1
  58.0 4.1 %collective-permute-done.9.refs_3_ = f32[512,128]{1,0:T(8,128)S(1)} collective-permute-done((f32[512,128]{1,0:T(8,128)S(1)}, f32[512,128]{1,0:T(8,128)S(1)}, u32[]{:S(2)}, u32[]{:S(2)}) %collective-permute-start.9) | collective-permute-done | bytes 262176 | tf_op jit(solution)/shard_map/ppermute | solution.py:114
  62.1 4.9 %collective-permute-done.8.refs_2_ = f32[512,128]{1,0:T(8,128)S(1)} collective-permute-done((f32[512,128]{1,0:T(8,128)S(1)}, f32[512,128]{1,0:T(8,128)S(1)}, u32[]{:S(2)}, u32[]{:S(2)}) %collective-permute-start.8) | collective-permute-done | bytes 262176 | tf_op jit(solution)/shard_map/ppermute | solution.py:114
  67.0 0.6 shard_map.60.refs_5_
  67.6 3.2 %collective-permute-done.4.refs_3_ = f32[512,128]{1,0:T(8,128)S(1)} collective-permute-done((f32[512,128]{1,0:T(8,128)S(1)}, f32[512,128]{1,0:T(8,128)S(1)}, u32[]{:S(2)}, u32[]{:S(2)}) %collective-permute-start.4) | collective-permute-done | bytes 262176 | tf_op jit(solution)/shard_map/ppermute | solution.py:114
  70.8 3.9 %collective-permute-done.3.refs_2_ = f32[512,128]{1,0:T(8,128)S(1)} collective-permute-done((f32[512,128]{1,0:T(8,128)S(1)}, f32[512,128]{1,0:T(8,128)S(1)}, u32[]{:S(2)}, u32[]{:S(2)}) %collective-permute-start.3) | collective-permute-done | bytes 262176 | tf_op jit(solution)/shard_map/ppermute | solution.py:114
  74.7 0.0 collective-permute-done.7.refs_4_
  74.7 0.0 copy-done.1
  74.7 1.4 %shard_map.61 = (f32[1,512,128]{2,1,0:T(8,128)}, f32[1,512,128]{2,1,0:T(8,128)}, f32[1,512,128]{2,1,0:T(8,128)}) custom-call(s32[1]{0:T(128)} %bitcast.own_row, f32[512,128]{1,0:T(8,128)S(1)} %slice_bitcast_fusion.1.refs_0_, f32[512,128]{1,0:T(8,128)S(1)} %collective-permute-done.2.refs_1_, f32[512,128]{1,0:T(8,128)S(1)} %collective-permute-done.3.refs_2_, ...), custom_call_target="tpu_custom_call" | custom-call | tf_op jit(solution)/shard_map/pallas_call | solution.py:176
  (4 shorter events, 0.0 us)
Async XLA Ops:
  0.6 1.0 %copy-start = (f32[2,512,128]{2,1,0:T(8,128)S(1)}, f32[2,512,128]{2,1,0:T(8,128)}, u32[]{:S(2)}) copy-start(f32[2,512,128]{2,1,0:T(8,128)} %refs_6_.1) | copy-start | bytes 1572868
  1.7 18.6 %copy-start.2 = (f32[2,512,128]{2,1,0:T(8,128)S(1)}, f32[2,512,128]{2,1,0:T(8,128)}, u32[]{:S(2)}) copy-start(f32[2,512,128]{2,1,0:T(8,128)} %refs_5_.1) | copy-start | bytes 1572868
  1.8 28.6 %copy-start.3 = (f32[2,512,128]{2,1,0:T(8,128)S(1)}, f32[2,512,128]{2,1,0:T(8,128)}, u32[]{:S(2)}) copy-start(f32[2,512,128]{2,1,0:T(8,128)} %refs_4_.1) | copy-start | bytes 1572868
  1.8 12.4 %collective-permute-start = (f32[520,128]{1,0:T(8,128)S(1)}, f32[520,128]{1,0:T(8,128)S(1)}, u32[]{:S(2)}, u32[]{:S(2)}) collective-permute-start(f32[520,128]{1,0:T(8,128)S(1)} %shard_map.58.refs_0_), channel_id=1, source_target_pairs={{0,1},{1,2},{2,3},{3,0},{4,5},{5,6},{6,7},{7,4},{8,9},{9,10},{10,1... | collective-permute-start | bytes 798728 | tf_op jit(solution)/shard_map/ppermute | solution.py:114
  4.9 25.5 %collective-permute-start.6 = (f32[520,128]{1,0:T(8,128)S(1)}, f32[520,128]{1,0:T(8,128)S(1)}, u32[]{:S(2)}, u32[]{:S(2)}) collective-permute-start(f32[520,128]{1,0:T(8,128)S(1)} %shard_map.58.refs_0_), channel_id=1, source_target_pairs={{0,3},{1,0},{2,1},{3,2},{4,7},{5,4},{6,5},{7,6},{8,11},{9,8},{10,9... | collective-permute-start | bytes 798728 | tf_op jit(solution)/shard_map/ppermute | solution.py:114
  14.2 16.2 %collective-permute-start.5 = (f32[520,128]{1,0:T(8,128)S(1)}, f32[520,128]{1,0:T(8,128)S(1)}, u32[]{:S(2)}, u32[]{:S(2)}) collective-permute-start(f32[520,128]{1,0:T(8,128)S(1)} %collective-permute-done.refs_1_), channel_id=1, source_target_pairs={{0,1},{1,2},{2,3},{3,0},{4,5},{5,6},{6,7},{7,4},{8,9},{9,10},{10,1... | collective-permute-start | bytes 798728 | tf_op jit(solution)/shard_map/ppermute | solution.py:114
  15.2 15.2 %collective-permute-start.1 = (f32[512,128]{1,0:T(8,128)S(1)}, f32[512,128]{1,0:T(8,128)S(1)}, u32[]{:S(2)}, u32[]{:S(2)}) collective-permute-start(f32[512,128]{1,0:T(8,128)S(1)} %slice_bitcast_fusion.refs_0_), channel_id=1, source_target_pairs={{0,1},{1,2},{2,3},{3,0},{4,5},{5,6},{6,7},{7,4},{8,9},{9,10},{10,1... | collective-permute-start | bytes 786440 | tf_op jit(solution)/shard_map/ppermute | solution.py:114
  30.4 27.5 %collective-permute-start.2 = (f32[512,128]{1,0:T(8,128)S(1)}, f32[512,128]{1,0:T(8,128)S(1)}, u32[]{:S(2)}, u32[]{:S(2)}) collective-permute-start(f32[512,128]{1,0:T(8,128)S(1)} %slice_bitcast_fusion.1.refs_0_), channel_id=1, source_target_pairs={{0,1},{1,2},{2,3},{3,0},{4,5},{5,6},{6,7},{7,4},{8,9},{9,10},{10,1... | collective-permute-start | bytes 786440 | tf_op jit(solution)/shard_map/ppermute | solution.py:114
  32.8 41.9 %collective-permute-start.7 = (f32[512,256]{1,0:T(8,128)S(1)}, f32[512,256]{1,0:T(8,128)S(1)}, u32[]{:S(2)}, u32[]{:S(2)}) collective-permute-start(f32[512,256]{1,0:T(8,128)S(1)} %get-tuple-element.9.refs_4_), channel_id=1, source_target_pairs={{0,4},{4,8},{8,12},{12,16},{16,20},{20,24},{24,28},{1,5},{5,9},{9,... | collective-permute-start | bytes 1572872 | tf_op jit(solution)/shard_map/ppermute | solution.py:159
  34.2 4.0 %collective-permute-start.10 = (f32[8,128]{1,0:T(8,128)S(1)}, f32[8,128]{1,0:T(8,128)S(1)}, u32[]{:S(2)}, u32[]{:S(2)}) collective-permute-start(f32[8,128]{1,0:T(8,128)S(1)} %get-tuple-element.10), channel_id=1, source_target_pairs={{0,4},{4,8},{8,12},{12,16},{16,20},{20,24},{24,28},{28,0},{1,5},{5... | collective-permute-start | bytes 12296 | tf_op jit(solution)/shard_map/ppermute | solution.py:162
  38.1 9.3 %collective-permute-start.11 = (f32[8,128]{1,0:T(8,128)S(1)}, f32[8,128]{1,0:T(8,128)S(1)}, u32[]{:S(2)}, u32[]{:S(2)}) collective-permute-start(f32[8,128]{1,0:T(8,128)S(1)} %max.9), channel_id=1, source_target_pairs={{0,8},{4,12},{8,16},{12,20},{16,24},{20,28},{24,0},{28,4},{1,9},{5... | collective-permute-start | bytes 12296 | tf_op jit(solution)/shard_map/ppermute | solution.py:162
  47.4 6.7 %collective-permute-start.12 = (f32[8,128]{1,0:T(8,128)S(1)}, f32[8,128]{1,0:T(8,128)S(1)}, u32[]{:S(2)}, u32[]{:S(2)}) collective-permute-start(f32[8,128]{1,0:T(8,128)S(1)} %max.10), channel_id=1, source_target_pairs={{0,16},{4,20},{8,24},{12,28},{16,0},{20,4},{24,8},{28,12},{1,17},{... | collective-permute-start | bytes 12296 | tf_op jit(solution)/shard_map/ppermute | solution.py:162
  50.3 11.8 %collective-permute-start.9 = (f32[512,128]{1,0:T(8,128)S(1)}, f32[512,128]{1,0:T(8,128)S(1)}, u32[]{:S(2)}, u32[]{:S(2)}) collective-permute-start(f32[512,128]{1,0:T(8,128)S(1)} %slice_bitcast_fusion.refs_0_), channel_id=1, source_target_pairs={{0,3},{1,0},{2,1},{3,2},{4,7},{5,4},{6,5},{7,6},{8,11},{9,8},{10,9... | collective-permute-start | bytes 786440 | tf_op jit(solution)/shard_map/ppermute | solution.py:114
  54.1 12.9 %collective-permute-start.8 = (f32[512,128]{1,0:T(8,128)S(1)}, f32[512,128]{1,0:T(8,128)S(1)}, u32[]{:S(2)}, u32[]{:S(2)}) collective-permute-start(f32[512,128]{1,0:T(8,128)S(1)} %collective-permute-done.1.refs_1_), channel_id=1, source_target_pairs={{0,1},{1,2},{2,3},{3,0},{4,5},{5,6},{6,7},{7,4},{8,9},{9,10},{10,1... | collective-permute-start | bytes 786440 | tf_op jit(solution)/shard_map/ppermute | solution.py:114
  54.1 16.7 %collective-permute-start.4 = (f32[512,128]{1,0:T(8,128)S(1)}, f32[512,128]{1,0:T(8,128)S(1)}, u32[]{:S(2)}, u32[]{:S(2)}) collective-permute-start(f32[512,128]{1,0:T(8,128)S(1)} %slice_bitcast_fusion.1.refs_0_), channel_id=1, source_target_pairs={{0,3},{1,0},{2,1},{3,2},{4,7},{5,4},{6,5},{7,6},{8,11},{9,8},{10,9... | collective-permute-start | bytes 786440 | tf_op jit(solution)/shard_map/ppermute | solution.py:114
  58.0 16.8 %collective-permute-start.3 = (f32[512,128]{1,0:T(8,128)S(1)}, f32[512,128]{1,0:T(8,128)S(1)}, u32[]{:S(2)}, u32[]{:S(2)}) collective-permute-start(f32[512,128]{1,0:T(8,128)S(1)} %collective-permute-done.2.refs_1_), channel_id=1, source_target_pairs={{0,1},{1,2},{2,3},{3,0},{4,5},{5,6},{6,7},{7,4},{8,9},{9,10},{10,1... | collective-permute-start | bytes 786440 | tf_op jit(solution)/shard_map/ppermute | solution.py:114
  58.0 16.8 %copy-start.1 = (f32[2,512,128]{2,1,0:T(8,128)S(1)}, f32[2,512,128]{2,1,0:T(8,128)}, u32[]{:S(2)}) copy-start(f32[2,512,128]{2,1,0:T(8,128)} %refs_6_.1) | copy-start | bytes 1572868

commit v2 on v1

v2 whole, which is shorter than its diff:
```python
import jax
import jax.numpy as jnp
from jax import lax
from jax.experimental import pallas as pl
from jax.experimental.pallas import tpu as pltpu
from jax.sharding import PartitionSpec as P

SWEEPS = 2
F32 = jnp.float32
BF16 = jnp.bfloat16
VMEM = pl.BlockSpec(memory_space=pltpu.VMEM)
SMEM = pl.BlockSpec(memory_space=pltpu.SMEM)


def ring_offsets(shards):
    return [0, *[-d for d in range(1, shards // 2 + 1)], *range(1, (shards - 1) // 2 + 1)]


def split(x):
    high = x.astype(BF16)
    return high, (x - high.astype(F32)).astype(BF16)


def exact_dot(left, right):
    (left_high, left_low), (right_high, right_low) = left, right
    dot = lambda a, b: jnp.dot(a, b, preferred_element_type=F32)
    return dot(left_high, right_high) + (dot(left_high, right_low) + dot(left_low, right_high))


def on_diagonal(rows, cols):
    row = lax.broadcasted_iota(jnp.int32, (rows, cols), 0)
    return row == lax.broadcasted_iota(jnp.int32, (rows, cols), 1)


def pack_kernel(own_row, level_ref, packed_ref, peak_ref):
    cols = level_ref.shape[-1]
    own = level_ref[:, pl.ds(pl.multiple_of(own_row[0], cols), cols), :]
    peak_ref[0, 0] = -jnp.min(jnp.where(on_diagonal(cols, cols)[None], own, 0.0))
    packed_ref[...] = level_ref[1]


def stack_kernel(up_ref, down_ref, stacked_ref):
    phases = up_ref.shape[1]
    stacked_ref[pl.ds(0, phases), :] = up_ref[0]
    stacked_ref[pl.ds(phases, phases), :] = down_ref[0]


def owner_row(own_row, offset, cols, shards):
    return pl.multiple_of(lax.rem(own_row[0] + (offset + shards) * cols, shards * cols), cols)


def solve_kernel(own_row, *refs):
    shards = len(refs) - 8
    blocks = refs[:shards]
    up_ref, down_ref, solved_ref, inverse, high, low, s_high, s_low = refs[shards:]
    phases, cols = inverse.shape
    diagonal = on_diagonal(cols, cols)
    for slot, (offset, block) in enumerate(zip(ring_offsets(shards), blocks)):
        rows = pl.ds(owner_row(own_row, offset, cols, shards), cols)
        slot_cols = pl.ds(slot * cols, cols)
        high[:, slot_cols], low[:, slot_cols] = split(block[...])
        square = block[rows, :]
        rate = -jnp.sum(jnp.where(diagonal, square, 0.0), axis=1, keepdims=True)
        inverse[rows, :] = jnp.broadcast_to(1.0 / rate, (cols, cols))
        high[rows, slot_cols], low[rows, slot_cols] = split(jnp.where(diagonal, 0.0, square))
    for side, ref in enumerate((up_ref, down_ref)):
        solved_ref[:, pl.ds(side * cols, cols)] = ref[0] * inverse[...]
    for _ in range(SWEEPS):
        for slot, offset in enumerate(ring_offsets(shards)):
            rows = pl.ds(owner_row(own_row, offset, cols, shards), cols)
            slot_rows = pl.ds(slot * cols, cols)
            s_high[slot_rows, :], s_low[slot_rows, :] = split(solved_ref[rows, :])
        product = exact_dot((high[...], low[...]), (s_high[...], s_low[...]))
        for side, ref in enumerate((up_ref, down_ref)):
            columns = slice(side * cols, (side + 1) * cols)
            solved_ref[:, columns] = (ref[0] + product[:, columns]) * inverse[...]


def gathered_product(own_row, blocks, first_row, solved_ref):
    shards, cols = len(blocks), blocks[0].shape[-1]
    phases = solved_ref.shape[0]
    left = split(jnp.concatenate([block[pl.ds(first_row, phases), :] for block in blocks], axis=1))
    rows = [pl.ds(owner_row(own_row, offset, cols, shards), cols) for offset in ring_offsets(shards)]
    right = split(jnp.concatenate([solved_ref[r, :] for r in rows], axis=0))
    return exact_dot(left, right)


def output_kernel(own_row, peak_ref, *refs):
    *blocks, solved_ref, below_ref, level_ref, new_level, new_up, new_down = refs
    _, phases, cols = new_up.shape
    scale = 1.0 / jnp.full((1, cols), peak_ref[0, 0], F32)
    upper = gathered_product(own_row, blocks, 0, solved_ref)
    new_up[0] = upper[:, :cols] * scale
    lower = gathered_product(own_row, blocks, phases, below_ref)
    new_down[0] = lower[:, cols:] * scale
    new_level[0] = (level_ref[0] + upper[:, cols:] + lower[:, :cols]) * scale


def per_device(up_blocks, level_blocks, down_blocks):
    levels, phases, cols = level_blocks.shape
    assert levels == 2
    shards = lax.axis_size("col")
    ranges = lax.axis_size("lvl")
    own_row = (lax.axis_index("col") * cols).astype(jnp.int32).reshape(1)
    params = pltpu.CompilerParams(vmem_limit_bytes=32 * 2**20)
    shape = lambda *dims, kind=F32: jax.ShapeDtypeStruct(dims, kind)

    def shifted(block, distance):
        return lax.ppermute(block, "col", [(i, (i + distance) % shards) for i in range(shards)])

    def after(value, *earlier):
        return lax.optimization_barrier((value, *earlier))[0]

    def one_level(parity):
        return pl.BlockSpec((1, phases, cols), lambda step: (parity, 0, 0))

    odd, even = one_level(1), one_level(0)
    packed, peak = pl.pallas_call(
        pack_kernel,
        out_shape=(shape(phases, cols), shape(1, 1)),
        in_specs=[SMEM, VMEM],
        out_specs=(VMEM, SMEM),
        grid=(1,),
        compiler_params=params,
    )(own_row, level_blocks)
    stacked = pl.pallas_call(
        stack_kernel,
        out_shape=shape(2 * phases, cols),
        in_specs=[even, even],
        out_specs=VMEM,
        grid=(1,),
        compiler_params=params,
    )(up_blocks, down_blocks)

    level_parts, even_parts = {0: packed}, {0: stacked}

    def step(parts, reached, distance, *earlier):
        block = after(parts[reached], *earlier) if earlier else parts[reached]
        parts[reached - distance] = shifted(block, distance)

    behind, ahead = range(shards // 2), range((shards - 1) // 2)
    step(level_parts, 0, 1)
    for reached in ahead:
        step(level_parts, reached, -1)
    top_rate = lax.pmax(peak, ("lvl", "col"))
    step(even_parts, 0, 1, *[part for at, part in level_parts.items() if at], top_rate)
    for reached in behind[1:]:
        step(level_parts, -reached, 1)
    for reached in ahead:
        step(even_parts, reached, -1, level_parts[-len(behind)])
    for reached in behind[1:]:
        step(even_parts, -reached, 1)
    level_parts = [level_parts[offset] for offset in ring_offsets(shards)]
    even_parts = [even_parts[offset] for offset in ring_offsets(shards)]

    solved = pl.pallas_call(
        solve_kernel,
        out_shape=shape(phases, 2 * cols),
        in_specs=[SMEM, *[VMEM] * shards, odd, odd],
        out_specs=VMEM,
        scratch_shapes=[
            pltpu.VMEM((phases, cols), F32),
            pltpu.VMEM((phases, phases), BF16),
            pltpu.VMEM((phases, phases), BF16),
            pltpu.VMEM((phases, 2 * cols), BF16),
            pltpu.VMEM((phases, 2 * cols), BF16),
        ],
        grid=(1,),
        compiler_params=params,
    )(own_row, *level_parts, up_blocks, down_blocks)
    from_below = lax.ppermute(solved, "lvl", [(i, i + 1) for i in range(ranges - 1)])

    return pl.pallas_call(
        output_kernel,
        out_shape=(shape(1, phases, cols),) * 3,
        in_specs=[SMEM, SMEM, *[VMEM] * (shards + 2), even],
        out_specs=(VMEM,) * 3,
        grid=(1,),
        compiler_params=params,
    )(own_row, top_rate, *even_parts, solved, from_below, level_blocks)


def solution(mesh):
    placed = (P("lvl", None, "col"),) * 3
    return jax.shard_map(per_device, mesh=mesh, in_specs=placed, out_specs=placed, check_vma=False)
```

time: 76.4 us -> 96.4 us (1.26)
  blocking collectives: 0 us -> 40.3 us
  starting transfers between devices: 31.1 us -> 12.1 us
  waiting for transfers between devices: 37.8 us -> 35.2 us
  Pallas kernels: 4.58 us -> 5.57 us
    pmax x0 -> x1, blocking collectives: none -> 40.3 us  [per_device(): top_rate = lax.pmax(peak, ('lvl', 'col'))]
    ppermute x3 -> x0, starting transfers between devices: 11.9 us -> none  [per_device(): lax.ppermute(peak, 'lvl', [(i, (i + reach) % ranges) for i in range(range...]
    ppermute x9 -> x6, starting transfers between devices: 17.9 us -> 10.7 us  [shifted(): lax.ppermute(block, 'col', [(i, (i + distance) % shards) for i in range(s...]
    ppermute x3 -> x0, waiting for transfers between devices: 4.28 us -> none  [per_device(): lax.ppermute(peak, 'lvl', [(i, (i + reach) % ranges) for i in range(range...]
    ppermute x9 -> x6, waiting for transfers between devices: 33.5 us -> 35.2 us  [shifted(): lax.ppermute(block, 'col', [(i, (i + distance) % shards) for i in range(s...]
    unnamed x8 -> x10, local copies, waits for them, and re-layouts: 1.05 us -> 2.15 us
    pallas_call x4, Pallas kernels: 4.58 us -> 5.57 us  [the longest x1 2.52 us: per_device(): pl.pallas_call(output_kernel, out_shape=(shape(1, phases, cols),) * 3, in...]
    squeeze x2 -> x0, local copies, waits for them, and re-layouts: 0.99 us -> none  [the longest x1 0.97 us: per_device(): up_parts = gather(after(up_blocks[0], level_parts[1]))]
  transfers between devices with their start and end apart: 13 -> 7, of which waited for: 8 -> 3; matrix products, arithmetic and copies ran while one was open for 1% -> 0% of each run, Pallas kernels for 4% -> 3%
where the time goes in v2:
time: 96.4 us; the launch traced here: 96 us
  blocking collectives  40.3 us (42%)
  waiting for transfers between devices  35.2 us (37%)
  starting transfers between devices  12.1 us (13%)
  Pallas kernels  5.57 us (6%)
  local copies, waits for them, and re-layouts  2.15 us (2%)
    pmax x1, blocking collectives, per_device(): top_rate = lax.pmax(peak, ('lvl', 'col'))  40.3 us
    ppermute x6, waiting for transfers between devices, shifted(): lax.ppermute(block, 'col', [(i, (i + distance) % shards) for i in range(s...  35.2 us
    ppermute x6, starting transfers between devices, shifted(): lax.ppermute(block, 'col', [(i, (i + distance) % shards) for i in range(s...  10.7 us
    pallas_call x1, Pallas kernels, per_device(): pl.pallas_call(output_kernel, out_shape=(shape(1, phases, cols),) * 3, in...  2.52 us
    pallas_call x1, Pallas kernels, per_device(): pl.pallas_call(solve_kernel, out_shape=shape(phases, 2 * cols), in_specs=...  2.37 us
    unnamed x10, local copies, waits for them, and re-layouts  2.15 us
  transfers between devices with their start and end apart: 7, of which 3 were waited for; matrix products, arithmetic and copies ran while one was open for 0% of the time, Pallas kernels for 3%

profile of v2, /device:TPU:0, one launch (start us, length us, event | category | flops | bytes accessed | tf_op | source)
XLA Modules:
  0.0 96.0 jit_solution(16472152079499471226)
XLA Ops:
  0.6 0.0 copy-start
  0.6 0.0 copy-start.3
  0.7 1.1 %copy-done.3 = f32[2,512,128]{2,1,0:T(8,128)S(1)} copy-done((f32[2,512,128]{2,1,0:T(8,128)S(1)}, f32[2,512,128]{2,1,0:T(8,128)}, u32[]{:S(2)}) %copy-start.3) | copy-done | bytes 524312
  1.7 0.6 shard_map.58
  2.4 5.1 %collective-permute-start.1 = (f32[512,128]{1,0:T(8,128)S(1)}, f32[512,128]{1,0:T(8,128)S(1)}, u32[]{:S(2)}, u32[]{:S(2)}) collective-permute-start(f32[512,128]{1,0:T(8,128)S(1)} %get-tuple-element.8.refs_0_), channel_id=1, source_target_pairs={{0,3},{1,0},{2,1},{3,2},{4,7},{5,4},{6,5},{7,6},{8,11},{9,8},{10,9... | collective-permute-start | bytes 786440 | tf_op jit(solution)/shard_map/ppermute | solution.py:109
  7.5 0.0 collective-permute-start
  7.5 40.3 %pmax.7.peak_ref = f32[1,1]{1,0:T(1,128)} all-reduce(f32[1,1]{1,0:T(1,128)} %get-tuple-element.7), channel_id=1, replica_groups=mesh['lvl'=8,'col'=4] {'lvl','col'}, use_global_device_ids=true, to_apply=%region_0.0 | all-reduce | flops 1 | bytes 8 | tf_op jit(solution)/shard_map/pmax | solution.py:145
  47.8 0.0 copy-done
  47.8 0.0 copy-start.1
  47.8 1.0 %copy-done.1 = f32[2,512,128]{2,1,0:T(8,128)S(1)} copy-done((f32[2,512,128]{2,1,0:T(8,128)S(1)}, f32[2,512,128]{2,1,0:T(8,128)}, u32[]{:S(2)}) %copy-start.1) | copy-done | bytes 524312
  48.9 0.0 copy-start.2
  48.9 0.0 copy-start.4
  48.9 0.0 collective-permute-done.1.refs_3_
  48.9 0.0 collective-permute-done.refs_1_
  49.0 2.2 %collective-permute-start.2 = (f32[1024,128]{1,0:T(8,128)S(1)}, f32[1024,128]{1,0:T(8,128)S(1)}, u32[]{:S(2)}, u32[]{:S(2)}) collective-permute-start(f32[1024,128]{1,0:T(8,128)S(1)} %shard_map.59.refs_0_), channel_id=1, source_target_pairs={{0,1},{1,2},{2,3},{3,0},{4,5},{5,6},{6,7},{7,4},{8,9},{9,10},{10,1... | collective-permute-start | bytes 1572872 | tf_op jit(solution)/shard_map/ppermute | solution.py:109
  51.2 1.4 %collective-permute-start.4 = (f32[512,128]{1,0:T(8,128)S(1)}, f32[512,128]{1,0:T(8,128)S(1)}, u32[]{:S(2)}, u32[]{:S(2)}) collective-permute-start(f32[512,128]{1,0:T(8,128)S(1)} %collective-permute-done.refs_1_), channel_id=1, source_target_pairs={{0,1},{1,2},{2,3},{3,0},{4,5},{5,6},{6,7},{7,4},{8,9},{9,10},{10,1... | collective-permute-start | bytes 786440 | tf_op jit(solution)/shard_map/ppermute | solution.py:109
  52.5 17.0 %collective-permute-done.4.refs_2_ = f32[512,128]{1,0:T(8,128)S(1)} collective-permute-done((f32[512,128]{1,0:T(8,128)S(1)}, f32[512,128]{1,0:T(8,128)S(1)}, u32[]{:S(2)}, u32[]{:S(2)}) %collective-permute-start.4) | collective-permute-done | bytes 262176 | tf_op jit(solution)/shard_map/ppermute | solution.py:109
  69.5 0.9 collective-permute-start.5
  70.4 0.0 copy-done.2
  70.4 2.4 %shard_map.60.refs_4_ = f32[512,256]{1,0:T(8,128)S(1)} custom-call(s32[1]{0:T(128)} %bitcast.own_row, f32[512,128]{1,0:T(8,128)S(1)} %get-tuple-element.8.refs_0_, f32[512,128]{1,0:T(8,128)S(1)} %collective-permute-done.refs_1_, f32[512,128]{1,0:T(8,128)S(1)} %collective-permute-done.4.refs_2_, f32[512,128]{1,0:T(8,128)S(1)} %collective-permute-done.1.refs_3_, ...), custom_call_target="tpu_custom_call" | custom-call | tf_op jit(solution)/shard_map/pallas_call | solution.py:156
  72.8 1.3 %collective-permute-start.6 = (f32[512,256]{1,0:T(8,128)S(1)}, f32[512,256]{1,0:T(8,128)S(1)}, u32[]{:S(2)}, u32[]{:S(2)}) collective-permute-start(f32[512,256]{1,0:T(8,128)S(1)} %shard_map.60.refs_4_), channel_id=1, source_target_pairs={{0,4},{4,8},{8,12},{12,16},{16,20},{20,24},{24,28},{1,5},{5,9},{9,... | collective-permute-start | bytes 1572872 | tf_op jit(solution)/shard_map/ppermute | solution.py:171
  74.1 0.0 collective-permute-done.2.refs_1_
  74.1 1.2 %collective-permute-start.3 = (f32[1024,128]{1,0:T(8,128)S(1)}, f32[1024,128]{1,0:T(8,128)S(1)}, u32[]{:S(2)}, u32[]{:S(2)}) collective-permute-start(f32[1024,128]{1,0:T(8,128)S(1)} %collective-permute-done.2.refs_1_), channel_id=1, source_target_pairs={{0,1},{1,2},{2,3},{3,0},{4,5},{5,6},{6,7},{7,4},{8,9},{9,10},{10,1... | collective-permute-start | bytes 1572872 | tf_op jit(solution)/shard_map/ppermute | solution.py:109
  75.3 7.5 %collective-permute-done.5.refs_3_ = f32[1024,128]{1,0:T(8,128)S(1)} collective-permute-done((f32[1024,128]{1,0:T(8,128)S(1)}, f32[1024,128]{1,0:T(8,128)S(1)}, u32[]{:S(2)}, u32[]{:S(2)}) %collective-permute-start.5) | collective-permute-done | bytes 524320 | tf_op jit(solution)/shard_map/ppermute | solution.py:109
  82.8 0.0 collective-permute-done.6.refs_5_
  82.8 10.7 %collective-permute-done.3.refs_2_ = f32[1024,128]{1,0:T(8,128)S(1)} collective-permute-done((f32[1024,128]{1,0:T(8,128)S(1)}, f32[1024,128]{1,0:T(8,128)S(1)}, u32[]{:S(2)}, u32[]{:S(2)}) %collective-permute-start.3) | collective-permute-done | bytes 524320 | tf_op jit(solution)/shard_map/ppermute | solution.py:109
  93.5 0.0 copy-done.4
  93.5 2.5 %shard_map.61 = (f32[1,512,128]{2,1,0:T(8,128)}, f32[1,512,128]{2,1,0:T(8,128)}, f32[1,512,128]{2,1,0:T(8,128)}) custom-call(s32[1]{0:T(128)} %bitcast.own_row, f32[1,1]{1,0:T(1,128)} %pmax.7.peak_ref, f32[1024,128]{1,0:T(8,128)S(1)} %shard_map.59.refs_0_, f32[1024,128]{1,0:T(8,128)S(1)} %collective-permute-done.2.refs_1_, ...), custom_call_target="tpu_custom_call" | custom-call | tf_op jit(solution)/shard_map/pallas_call | solution.py:173
  (1 shorter events, 0.0 us)
Async XLA Ops:
  0.6 47.2 %copy-start = (f32[2,512,128]{2,1,0:T(8,128)S(1)}, f32[2,512,128]{2,1,0:T(8,128)}, u32[]{:S(2)}) copy-start(f32[2,512,128]{2,1,0:T(8,128)} %refs_4_.1) | copy-start | bytes 1572868
  0.6 1.1 %copy-start.3 = (f32[2,512,128]{2,1,0:T(8,128)S(1)}, f32[2,512,128]{2,1,0:T(8,128)}, u32[]{:S(2)}) copy-start(f32[2,512,128]{2,1,0:T(8,128)} %refs_6_.1) | copy-start | bytes 1572868
  2.4 46.5 %collective-permute-start.1 = (f32[512,128]{1,0:T(8,128)S(1)}, f32[512,128]{1,0:T(8,128)S(1)}, u32[]{:S(2)}, u32[]{:S(2)}) collective-permute-start(f32[512,128]{1,0:T(8,128)S(1)} %get-tuple-element.8.refs_0_), channel_id=1, source_target_pairs={{0,3},{1,0},{2,1},{3,2},{4,7},{5,4},{6,5},{7,6},{8,11},{9,8},{10,9... | collective-permute-start | bytes 786440 | tf_op jit(solution)/shard_map/ppermute | solution.py:109
  7.5 41.4 %collective-permute-start = (f32[512,128]{1,0:T(8,128)S(1)}, f32[512,128]{1,0:T(8,128)S(1)}, u32[]{:S(2)}, u32[]{:S(2)}) collective-permute-start(f32[512,128]{1,0:T(8,128)S(1)} %get-tuple-element.8.refs_0_), channel_id=1, source_target_pairs={{0,1},{1,2},{2,3},{3,0},{4,5},{5,6},{6,7},{7,4},{8,9},{9,10},{10,1... | collective-permute-start | bytes 786440 | tf_op jit(solution)/shard_map/ppermute | solution.py:109
  47.8 1.0 %copy-start.1 = (f32[2,512,128]{2,1,0:T(8,128)S(1)}, f32[2,512,128]{2,1,0:T(8,128)}, u32[]{:S(2)}) copy-start(f32[2,512,128]{2,1,0:T(8,128)} %refs_5_.1) | copy-start | bytes 1572868
  48.9 21.5 %copy-start.2 = (f32[2,512,128]{2,1,0:T(8,128)S(1)}, f32[2,512,128]{2,1,0:T(8,128)}, u32[]{:S(2)}) copy-start(f32[2,512,128]{2,1,0:T(8,128)} %refs_5_.1) | copy-start | bytes 1572868
  48.9 44.6 %copy-start.4 = (f32[2,512,128]{2,1,0:T(8,128)S(1)}, f32[2,512,128]{2,1,0:T(8,128)}, u32[]{:S(2)}) copy-start(f32[2,512,128]{2,1,0:T(8,128)} %refs_6_.1) | copy-start | bytes 1572868
  49.0 25.2 %collective-permute-start.2 = (f32[1024,128]{1,0:T(8,128)S(1)}, f32[1024,128]{1,0:T(8,128)S(1)}, u32[]{:S(2)}, u32[]{:S(2)}) collective-permute-start(f32[1024,128]{1,0:T(8,128)S(1)} %shard_map.59.refs_0_), channel_id=1, source_target_pairs={{0,1},{1,2},{2,3},{3,0},{4,5},{5,6},{6,7},{7,4},{8,9},{9,10},{10,1... | collective-permute-start | bytes 1572872 | tf_op jit(solution)/shard_map/ppermute | solution.py:109
  51.2 18.4 %collective-permute-start.4 = (f32[512,128]{1,0:T(8,128)S(1)}, f32[512,128]{1,0:T(8,128)S(1)}, u32[]{:S(2)}, u32[]{:S(2)}) collective-permute-start(f32[512,128]{1,0:T(8,128)S(1)} %collective-permute-done.refs_1_), channel_id=1, source_target_pairs={{0,1},{1,2},{2,3},{3,0},{4,5},{5,6},{6,7},{7,4},{8,9},{9,10},{10,1... | collective-permute-start | bytes 786440 | tf_op jit(solution)/shard_map/ppermute | solution.py:109
  69.5 13.3 %collective-permute-start.5 = (f32[1024,128]{1,0:T(8,128)S(1)}, f32[1024,128]{1,0:T(8,128)S(1)}, u32[]{:S(2)}, u32[]{:S(2)}) collective-permute-start(f32[1024,128]{1,0:T(8,128)S(1)} %shard_map.59.refs_0_), channel_id=1, source_target_pairs={{0,3},{1,0},{2,1},{3,2},{4,7},{5,4},{6,5},{7,6},{8,11},{9,8},{10,9... | collective-permute-start | bytes 1572872 | tf_op jit(solution)/shard_map/ppermute | solution.py:109
  72.8 10.0 %collective-permute-start.6 = (f32[512,256]{1,0:T(8,128)S(1)}, f32[512,256]{1,0:T(8,128)S(1)}, u32[]{:S(2)}, u32[]{:S(2)}) collective-permute-start(f32[512,256]{1,0:T(8,128)S(1)} %shard_map.60.refs_4_), channel_id=1, source_target_pairs={{0,4},{4,8},{8,12},{12,16},{16,20},{20,24},{24,28},{1,5},{5,9},{9,... | collective-permute-start | bytes 1572872 | tf_op jit(solution)/shard_map/ppermute | solution.py:171
  74.1 19.4 %collective-permute-start.3 = (f32[1024,128]{1,0:T(8,128)S(1)}, f32[1024,128]{1,0:T(8,128)S(1)}, u32[]{:S(2)}, u32[]{:S(2)}) collective-permute-start(f32[1024,128]{1,0:T(8,128)S(1)} %collective-permute-done.2.refs_1_), channel_id=1, source_target_pairs={{0,1},{1,2},{2,3},{3,0},{4,5},{5,6},{6,7},{7,4},{8,9},{9,10},{10,1... | collective-permute-start | bytes 1572872 | tf_op jit(solution)/shard_map/ppermute | solution.py:109

commit v3 on v2

--- a/solution.py
+++ b/solution.py
@@ -1,3 +1,5 @@
+import functools
+
 import jax
 import jax.numpy as jnp
 from jax import lax
@@ -6,6 +8,7 @@
 from jax.sharding import PartitionSpec as P
 
 SWEEPS = 2
+PEAK_ROWS = 8
 F32 = jnp.float32
 BF16 = jnp.bfloat16
 VMEM = pl.BlockSpec(memory_space=pltpu.VMEM)
@@ -32,11 +35,12 @@
     return row == lax.broadcasted_iota(jnp.int32, (rows, cols), 1)
 
 
-def pack_kernel(own_row, level_ref, packed_ref, peak_ref):
-    cols = level_ref.shape[-1]
+def pack_kernel(own_row, level_ref, packed_ref):
+    _, phases, cols = level_ref.shape
     own = level_ref[:, pl.ds(pl.multiple_of(own_row[0], cols), cols), :]
-    peak_ref[0, 0] = -jnp.min(jnp.where(on_diagonal(cols, cols)[None], own, 0.0))
-    packed_ref[...] = level_ref[1]
+    lowest = jnp.min(jnp.where(on_diagonal(cols, cols)[None], own, 0.0))
+    packed_ref[pl.ds(0, phases), :] = level_ref[1]
+    packed_ref[pl.ds(phases, PEAK_ROWS), :] = jnp.full((PEAK_ROWS, cols), -lowest, F32)
 
 
 def stack_kernel(up_ref, down_ref, stacked_ref):
@@ -50,19 +54,23 @@
 
 
 def solve_kernel(own_row, *refs):
-    shards = len(refs) - 8
+    shards = len(refs) - 9
     blocks = refs[:shards]
-    up_ref, down_ref, solved_ref, inverse, high, low, s_high, s_low = refs[shards:]
+    up_ref, down_ref, solved_ref, peak_ref, inverse, high, low, s_high, s_low = refs[shards:]
     phases, cols = inverse.shape
     diagonal = on_diagonal(cols, cols)
+    peak = None
     for slot, (offset, block) in enumerate(zip(ring_offsets(shards), blocks)):
         rows = pl.ds(owner_row(own_row, offset, cols, shards), cols)
         slot_cols = pl.ds(slot * cols, cols)
-        high[:, slot_cols], low[:, slot_cols] = split(block[...])
+        high[:, slot_cols], low[:, slot_cols] = split(block[pl.ds(0, phases), :])
         square = block[rows, :]
         rate = -jnp.sum(jnp.where(diagonal, square, 0.0), axis=1, keepdims=True)
         inverse[rows, :] = jnp.broadcast_to(1.0 / rate, (cols, cols))
         high[rows, slot_cols], low[rows, slot_cols] = split(jnp.where(diagonal, 0.0, square))
+        block_peak = block[pl.ds(phases, PEAK_ROWS), :]
+        peak = block_peak if peak is None else jnp.maximum(peak, block_peak)
+    peak_ref[...] = peak
     for side, ref in enumerate((up_ref, down_ref)):
         solved_ref[:, pl.ds(side * cols, cols)] = ref[0] * inverse[...]
     for _ in range(SWEEPS):
@@ -76,24 +84,34 @@
             solved_ref[:, columns] = (ref[0] + product[:, columns]) * inverse[...]
 
 
-def gathered_product(own_row, blocks, first_row, solved_ref):
-    shards, cols = len(blocks), blocks[0].shape[-1]
+def gathered_product(own_row, blocks, offsets, shards, first_row, solved_ref):
+    cols = blocks[0].shape[-1]
     phases = solved_ref.shape[0]
     left = split(jnp.concatenate([block[pl.ds(first_row, phases), :] for block in blocks], axis=1))
-    rows = [pl.ds(owner_row(own_row, offset, cols, shards), cols) for offset in ring_offsets(shards)]
+    rows = [pl.ds(owner_row(own_row, offset, cols, shards), cols) for offset in offsets]
     right = split(jnp.concatenate([solved_ref[r, :] for r in rows], axis=0))
     return exact_dot(left, right)
 
 
-def output_kernel(own_row, peak_ref, *refs):
-    *blocks, solved_ref, below_ref, level_ref, new_level, new_up, new_down = refs
-    _, phases, cols = new_up.shape
-    scale = 1.0 / jnp.full((1, cols), peak_ref[0, 0], F32)
-    upper = gathered_product(own_row, blocks, 0, solved_ref)
-    new_up[0] = upper[:, :cols] * scale
-    lower = gathered_product(own_row, blocks, phases, below_ref)
-    new_down[0] = lower[:, cols:] * scale
-    new_level[0] = (level_ref[0] + upper[:, cols:] + lower[:, :cols]) * scale
+def partial_kernel(offsets, shards, own_row, *refs):
+    *blocks, solved_ref, below_ref, level_ref, part_level, part_up, part_down = refs
+    phases, cols = part_up.shape
+    upper = gathered_product(own_row, blocks, offsets, shards, 0, solved_ref)
+    part_up[...] = upper[:, :cols]
+    lower = gathered_product(own_row, blocks, offsets, shards, phases, below_ref)
+    part_down[...] = lower[:, cols:]
+    part_level[...] = level_ref[0] + upper[:, cols:] + lower[:, :cols]
+
+
+def output_kernel(offsets, shards, own_row, *refs):
+    *blocks, solved_ref, below_ref, part_level, part_up, part_down, peak_ref, new_level, new_up, new_down = refs
+    phases, cols = part_up.shape
+    scale = 1.0 / peak_ref[0:1, :]
+    upper = gathered_product(own_row, blocks, offsets, shards, 0, solved_ref)
+    new_up[0] = (part_up[...] + upper[:, :cols]) * scale
+    lower = gathered_product(own_row, blocks, offsets, shards, phases, below_ref)
+    new_down[0] = (part_down[...] + lower[:, cols:]) * scale
+    new_level[0] = (part_level[...] + upper[:, cols:] + lower[:, :cols]) * scale
 
 
 def per_device(up_blocks, level_blocks, down_blocks):
@@ -115,11 +133,11 @@
         return pl.BlockSpec((1, phases, cols), lambda step: (parity, 0, 0))
 
     odd, even = one_level(1), one_level(0)
-    packed, peak = pl.pallas_call(
+    packed = pl.pallas_call(
         pack_kernel,
-        out_shape=(shape(phases, cols), shape(1, 1)),
+        out_shape=shape(phases + PEAK_ROWS, cols),
         in_specs=[SMEM, VMEM],
-        out_specs=(VMEM, SMEM),
+        out_specs=VMEM,
         grid=(1,),
         compiler_params=params,
     )(own_row, level_blocks)
@@ -138,26 +156,24 @@
         block = after(parts[reached], *earlier) if earlier else parts[reached]
         parts[reached - distance] = shifted(block, distance)
 
+    offsets = ring_offsets(shards)
     behind, ahead = range(shards // 2), range((shards - 1) // 2)
     step(level_parts, 0, 1)
     for reached in ahead:
         step(level_parts, reached, -1)
-    top_rate = lax.pmax(peak, ("lvl", "col"))
-    step(even_parts, 0, 1, *[part for at, part in level_parts.items() if at], top_rate)
+    step(even_parts, 0, 1)
     for reached in behind[1:]:
         step(level_parts, -reached, 1)
     for reached in ahead:
-        step(even_parts, reached, -1, level_parts[-len(behind)])
+        step(even_parts, reached, -1, level_parts[-1])
     for reached in behind[1:]:
         step(even_parts, -reached, 1)
-    level_parts = [level_parts[offset] for offset in ring_offsets(shards)]
-    even_parts = [even_parts[offset] for offset in ring_offsets(shards)]
-
-    solved = pl.pallas_call(
+
+    solved, peak = pl.pallas_call(
         solve_kernel,
-        out_shape=shape(phases, 2 * cols),
+        out_shape=(shape(phases, 2 * cols), shape(PEAK_ROWS, cols)),
         in_specs=[SMEM, *[VMEM] * shards, odd, odd],
-        out_specs=VMEM,
+        out_specs=(VMEM, VMEM),
         scratch_shapes=[
             pltpu.VMEM((phases, cols), F32),
             pltpu.VMEM((phases, phases), BF16),
@@ -167,17 +183,34 @@
         ],
         grid=(1,),
         compiler_params=params,
-    )(own_row, *level_parts, up_blocks, down_blocks)
+    )(own_row, *[level_parts[offset] for offset in offsets], up_blocks, down_blocks)
     from_below = lax.ppermute(solved, "lvl", [(i, i + 1) for i in range(ranges - 1)])
 
+    peak = after(peak, even_parts[-1])
+    reach = 1
+    while reach < ranges:
+        other = lax.ppermute(peak, "lvl", [(i, (i + reach) % ranges) for i in range(ranges)])
+        peak = jnp.maximum(peak, other)
+        reach *= 2
+
+    last = -len(behind)
+    early = [offset for offset in offsets if offset != last]
+    parts = pl.pallas_call(
+        functools.partial(partial_kernel, early, shards),
+        out_shape=(shape(phases, cols),) * 3,
+        in_specs=[SMEM, *[VMEM] * (len(early) + 2), even],
+        out_specs=(VMEM,) * 3,
+        grid=(1,),
+        compiler_params=params,
+    )(own_row, *[even_parts[offset] for offset in early], solved, from_below, level_blocks)
     return pl.pallas_call(
-        output_kernel,
+        functools.partial(output_kernel, [last], shards),
         out_shape=(shape(1, phases, cols),) * 3,
-        in_specs=[SMEM, SMEM, *[VMEM] * (shards + 2), even],
+        in_specs=[SMEM, *[VMEM] * 7],
         out_specs=(VMEM,) * 3,
         grid=(1,),
         compiler_params=params,
-    )(own_row, top_rate, *even_parts, solved, from_below, level_blocks)
+    )(own_row, even_parts[last], solved, from_below, *parts, peak)
 
 
 def solution(mesh):

time: 96.4 us -> 67.8 us (0.70)
  the two profiles are of different devices: /device:TPU:0 before, /device:TPU:28 now
where the time goes in v3:
time: 67.8 us; the launch traced here: 67.6 us
  waiting for transfers between devices  51.4 us (76%)
  starting transfers between devices  8.28 us (12%)
  Pallas kernels  5.03 us (7%)
  local copies, waits for them, and re-layouts  2.14 us (3%)
  between operations  0.74 us (1%)
    ppermute x6, waiting for transfers between devices, shifted(): lax.ppermute(block, 'col', [(i, (i + distance) % shards) for i in range(s...  35.7 us
    ppermute x3, waiting for transfers between devices, per_device(): lax.ppermute(peak, 'lvl', [(i, (i + reach) % ranges) for i in range(range...  15.8 us
    ppermute x6, starting transfers between devices, shifted(): lax.ppermute(block, 'col', [(i, (i + distance) % shards) for i in range(s...  4.58 us
    pallas_call x1, Pallas kernels, per_device(): pl.pallas_call(solve_kernel, out_shape=(shape(phases, 2 * cols), shape(PE...  2.39 us
    unnamed x8, local copies, waits for them, and re-layouts  2.14 us
    ppermute x1, starting transfers between devices, per_device(): lax.ppermute(solved, 'lvl', [(i, i + 1) for i in range(ranges - 1)])  1.92 us
    ppermute x3, starting transfers between devices, per_device(): lax.ppermute(peak, 'lvl', [(i, (i + reach) % ranges) for i in range(range...  1.78 us
    pallas_call x1, Pallas kernels, per_device(): pl.pallas_call(functools.partial(output_kernel, [last], shards), out_shap...  1.46 us
  transfers between devices with their start and end apart: 10, of which 6 were waited for; matrix products, arithmetic and copies ran while one was open for 0% of the time, Pallas kernels for 5%

profile of v3, /device:TPU:28, one launch (start us, length us, event | category | flops | bytes accessed | tf_op | source)
XLA Modules:
  0.0 67.6 jit_solution(7960302150739750932)
XLA Ops:
  0.6 0.0 copy-start
  0.6 0.0 copy-start.2
  0.7 1.1 %copy-done.2 = f32[2,512,128]{2,1,0:T(8,128)S(1)} copy-done((f32[2,512,128]{2,1,0:T(8,128)S(1)}, f32[2,512,128]{2,1,0:T(8,128)}, u32[]{:S(2)}) %copy-start.2) | copy-done | bytes 524312
  1.7 0.1 shard_map.59.refs_0_
  1.9 0.3 collective-permute-start.2
  2.2 0.0 copy-done
  2.2 0.0 copy-start.1
  2.2 1.0 %copy-done.1 = f32[2,512,128]{2,1,0:T(8,128)S(1)} copy-done((f32[2,512,128]{2,1,0:T(8,128)S(1)}, f32[2,512,128]{2,1,0:T(8,128)}, u32[]{:S(2)}) %copy-start.1) | copy-done | bytes 524312
  3.2 0.0 copy-start.3
  3.3 1.6 %collective-permute-start = (f32[1024,128]{1,0:T(8,128)S(1)}, f32[1024,128]{1,0:T(8,128)S(1)}, u32[]{:S(2)}, u32[]{:S(2)}) collective-permute-start(f32[1024,128]{1,0:T(8,128)S(1)} %shard_map.58.refs_0_), channel_id=1, source_target_pairs={{0,1},{1,2},{2,3},{3,0},{4,5},{5,6},{6,7},{7,4},{8,9},{9,10},{10,1... | collective-permute-start | bytes 1572872 | tf_op jit(solution)/shard_map/ppermute | solution.py:127
  4.9 0.4 collective-permute-start.4
  5.3 5.9 %collective-permute-done.2.refs_1_ = f32[520,128]{1,0:T(8,128)S(1)} collective-permute-done((f32[520,128]{1,0:T(8,128)S(1)}, f32[520,128]{1,0:T(8,128)S(1)}, u32[]{:S(2)}, u32[]{:S(2)}) %collective-permute-start.2) | collective-permute-done | bytes 266272 | tf_op jit(solution)/shard_map/ppermute | solution.py:127
  11.2 2.2 %collective-permute-start.3 = (f32[520,128]{1,0:T(8,128)S(1)}, f32[520,128]{1,0:T(8,128)S(1)}, u32[]{:S(2)}, u32[]{:S(2)}) collective-permute-start(f32[520,128]{1,0:T(8,128)S(1)} %collective-permute-done.2.refs_1_), channel_id=1, source_target_pairs={{0,1},{1,2},{2,3},{3,0},{4,5},{5,6},{6,7},{7,4},{8,9},{9,10},{10,1... | collective-permute-start | bytes 798728 | tf_op jit(solution)/shard_map/ppermute | solution.py:127
  13.4 0.0 collective-permute-start.6
  13.4 14.6 %collective-permute-done.4.refs_3_ = f32[520,128]{1,0:T(8,128)S(1)} collective-permute-done((f32[520,128]{1,0:T(8,128)S(1)}, f32[520,128]{1,0:T(8,128)S(1)}, u32[]{:S(2)}, u32[]{:S(2)}) %collective-permute-start.4) | collective-permute-done | bytes 266272 | tf_op jit(solution)/shard_map/ppermute | solution.py:127
  28.0 15.2 %collective-permute-done.3.refs_2_ = f32[520,128]{1,0:T(8,128)S(1)} collective-permute-done((f32[520,128]{1,0:T(8,128)S(1)}, f32[520,128]{1,0:T(8,128)S(1)}, u32[]{:S(2)}, u32[]{:S(2)}) %collective-permute-start.3) | collective-permute-done | bytes 266272 | tf_op jit(solution)/shard_map/ppermute | solution.py:127
  43.2 2.4 %shard_map.60 = (f32[512,256]{1,0:T(8,128)S(1)}, f32[8,128]{1,0:T(8,128)S(1)}) custom-call(s32[1]{0:T(128)} %bitcast.own_row, f32[520,128]{1,0:T(8,128)S(1)} %shard_map.59.refs_0_, f32[520,128]{1,0:T(8,128)S(1)} %collective-permute-done.2.refs_1_, f32[520,128]{1,0:T(8,128)S(1)} %collective-permute-done.3.refs_2_, ...), custom_call_target="tpu_custom_call" | custom-call | tf_op jit(solution)/shard_map/pallas_call | solution.py:172
  45.6 1.9 %collective-permute-start.5 = (f32[512,256]{1,0:T(8,128)S(1)}, f32[512,256]{1,0:T(8,128)S(1)}, u32[]{:S(2)}, u32[]{:S(2)}) collective-permute-start(f32[512,256]{1,0:T(8,128)S(1)} %get-tuple-element.10.refs_3_.refs_1_), channel_id=1, source_target_pairs={{0,4},{4,8},{8,12},{12,16},{16,20},{20,24},{24,28},{1,5},{5,9},{9,... | collective-permute-start | bytes 1572872 | tf_op jit(solution)/shard_map/ppermute | solution.py:187
  47.5 0.0 collective-permute-done.refs_1_
  47.5 0.1 collective-permute-start.1
  47.6 1.4 %collective-permute-start.7 = (f32[8,128]{1,0:T(8,128)S(1)}, f32[8,128]{1,0:T(8,128)S(1)}, u32[]{:S(2)}, u32[]{:S(2)}) collective-permute-start(f32[8,128]{1,0:T(8,128)S(1)} %get-tuple-element.16), channel_id=1, source_target_pairs={{0,4},{4,8},{8,12},{12,16},{16,20},{20,24},{24,28},{28,0},{1,5},{5... | collective-permute-start | bytes 12296 | tf_op jit(solution)/shard_map/ppermute | solution.py:192
  49.0 8.0 %collective-permute-done.7 = f32[8,128]{1,0:T(8,128)S(1)} collective-permute-done((f32[8,128]{1,0:T(8,128)S(1)}, f32[8,128]{1,0:T(8,128)S(1)}, u32[]{:S(2)}, u32[]{:S(2)}) %collective-permute-start.7) | collective-permute-done | bytes 4128 | tf_op jit(solution)/shard_map/ppermute | solution.py:192
  57.0 0.4 collective-permute-start.8
  57.4 4.1 %collective-permute-done.8 = f32[8,128]{1,0:T(8,128)S(1)} collective-permute-done((f32[8,128]{1,0:T(8,128)S(1)}, f32[8,128]{1,0:T(8,128)S(1)}, u32[]{:S(2)}, u32[]{:S(2)}) %collective-permute-start.8) | collective-permute-done | bytes 4128 | tf_op jit(solution)/shard_map/ppermute | solution.py:192
  61.5 0.0 collective-permute-start.9
  61.5 3.6 %collective-permute-done.9 = f32[8,128]{1,0:T(8,128)S(1)} collective-permute-done((f32[8,128]{1,0:T(8,128)S(1)}, f32[8,128]{1,0:T(8,128)S(1)}, u32[]{:S(2)}, u32[]{:S(2)}) %collective-permute-start.9) | collective-permute-done | bytes 4128 | tf_op jit(solution)/shard_map/ppermute | solution.py:192
  65.1 0.0 collective-permute-done.6.refs_2_
  65.1 0.0 collective-permute-done.5.refs_4_.refs_2_
  65.1 0.0 copy-done.3
  65.2 1.0 %shard_map.61 = (f32[512,128]{1,0:T(8,128)S(1)}, f32[512,128]{1,0:T(8,128)S(1)}, f32[512,128]{1,0:T(8,128)S(1)}) custom-call(s32[1]{0:T(128)} %bitcast.own_row, f32[1024,128]{1,0:T(8,128)S(1)} %shard_map.58.refs_0_, f32[1024,128]{1,0:T(8,128)S(1)} %collective-permute-done.refs_1_, f32[1024,128]{1,0:T(8,128)S(1)} %collective-permute-done.6.refs_2_, ...), custom_call_target="tpu_custom_call" | custom-call | tf_op jit(solution)/shard_map/pallas_call | solution.py:198
  66.2 0.0 collective-permute-done.1.refs_0_
  66.2 1.5 %shard_map.62 = (f32[1,512,128]{2,1,0:T(8,128)}, f32[1,512,128]{2,1,0:T(8,128)}, f32[1,512,128]{2,1,0:T(8,128)}) custom-call(s32[1]{0:T(128)} %bitcast.own_row, f32[1024,128]{1,0:T(8,128)S(1)} %collective-permute-done.1.refs_0_, f32[512,256]{1,0:T(8,128)S(1)} %get-tuple-element.10.refs_3_.refs_1_, f32[512,256]{1,0:T(8,128)S(1)} %collective-permute-done.5.refs_4_.refs_2_, ...), custom_call_target="tpu_custom_call" | custom-call | tf_op jit(solution)/shard_map/pallas_call | solution.py:206
  (4 shorter events, 0.0 us)
Async XLA Ops:
  0.6 1.5 %copy-start = (f32[2,512,128]{2,1,0:T(8,128)S(1)}, f32[2,512,128]{2,1,0:T(8,128)}, u32[]{:S(2)}) copy-start(f32[2,512,128]{2,1,0:T(8,128)} %refs_4_.1) | copy-start | bytes 1572868
  0.6 1.1 %copy-start.2 = (f32[2,512,128]{2,1,0:T(8,128)S(1)}, f32[2,512,128]{2,1,0:T(8,128)}, u32[]{:S(2)}) copy-start(f32[2,512,128]{2,1,0:T(8,128)} %refs_5_.3) | copy-start | bytes 1572868
  1.9 9.3 %collective-permute-start.2 = (f32[520,128]{1,0:T(8,128)S(1)}, f32[520,128]{1,0:T(8,128)S(1)}, u32[]{:S(2)}, u32[]{:S(2)}) collective-permute-start(f32[520,128]{1,0:T(8,128)S(1)} %shard_map.59.refs_0_), channel_id=1, source_target_pairs={{0,1},{1,2},{2,3},{3,0},{4,5},{5,6},{6,7},{7,4},{8,9},{9,10},{10,1... | collective-permute-start | bytes 798728 | tf_op jit(solution)/shard_map/ppermute | solution.py:127
  2.2 1.0 %copy-start.1 = (f32[2,512,128]{2,1,0:T(8,128)S(1)}, f32[2,512,128]{2,1,0:T(8,128)}, u32[]{:S(2)}) copy-start(f32[2,512,128]{2,1,0:T(8,128)} %refs_5_.2) | copy-start | bytes 1572868
  3.2 61.9 %copy-start.3 = (f32[2,512,128]{2,1,0:T(8,128)S(1)}, f32[2,512,128]{2,1,0:T(8,128)}, u32[]{:S(2)}) copy-start(f32[2,512,128]{2,1,0:T(8,128)} %refs_5_.3) | copy-start | bytes 1572868
  3.3 44.2 %collective-permute-start = (f32[1024,128]{1,0:T(8,128)S(1)}, f32[1024,128]{1,0:T(8,128)S(1)}, u32[]{:S(2)}, u32[]{:S(2)}) collective-permute-start(f32[1024,128]{1,0:T(8,128)S(1)} %shard_map.58.refs_0_), channel_id=1, source_target_pairs={{0,1},{1,2},{2,3},{3,0},{4,5},{5,6},{6,7},{7,4},{8,9},{9,10},{10,1... | collective-permute-start | bytes 1572872 | tf_op jit(solution)/shard_map/ppermute | solution.py:127
  4.9 23.1 %collective-permute-start.4 = (f32[520,128]{1,0:T(8,128)S(1)}, f32[520,128]{1,0:T(8,128)S(1)}, u32[]{:S(2)}, u32[]{:S(2)}) collective-permute-start(f32[520,128]{1,0:T(8,128)S(1)} %shard_map.59.refs_0_), channel_id=1, source_target_pairs={{0,3},{1,0},{2,1},{3,2},{4,7},{5,4},{6,5},{7,6},{8,11},{9,8},{10,9... | collective-permute-start | bytes 798728 | tf_op jit(solution)/shard_map/ppermute | solution.py:127
  11.2 31.9 %collective-permute-start.3 = (f32[520,128]{1,0:T(8,128)S(1)}, f32[520,128]{1,0:T(8,128)S(1)}, u32[]{:S(2)}, u32[]{:S(2)}) collective-permute-start(f32[520,128]{1,0:T(8,128)S(1)} %collective-permute-done.2.refs_1_), channel_id=1, source_target_pairs={{0,1},{1,2},{2,3},{3,0},{4,5},{5,6},{6,7},{7,4},{8,9},{9,10},{10,1... | collective-permute-start | bytes 798728 | tf_op jit(solution)/shard_map/ppermute | solution.py:127
  13.4 51.7 %collective-permute-start.6 = (f32[1024,128]{1,0:T(8,128)S(1)}, f32[1024,128]{1,0:T(8,128)S(1)}, u32[]{:S(2)}, u32[]{:S(2)}) collective-permute-start(f32[1024,128]{1,0:T(8,128)S(1)} %shard_map.58.refs_0_), channel_id=1, source_target_pairs={{0,3},{1,0},{2,1},{3,2},{4,7},{5,4},{6,5},{7,6},{8,11},{9,8},{10,9... | collective-permute-start | bytes 1572872 | tf_op jit(solution)/shard_map/ppermute | solution.py:127
  45.6 19.6 %collective-permute-start.5 = (f32[512,256]{1,0:T(8,128)S(1)}, f32[512,256]{1,0:T(8,128)S(1)}, u32[]{:S(2)}, u32[]{:S(2)}) collective-permute-start(f32[512,256]{1,0:T(8,128)S(1)} %get-tuple-element.10.refs_3_.refs_1_), channel_id=1, source_target_pairs={{0,4},{4,8},{8,12},{12,16},{16,20},{20,24},{24,28},{1,5},{5,9},{9,... | collective-permute-start | bytes 1572872 | tf_op jit(solution)/shard_map/ppermute | solution.py:187
  47.5 18.7 %collective-permute-start.1 = (f32[1024,128]{1,0:T(8,128)S(1)}, f32[1024,128]{1,0:T(8,128)S(1)}, u32[]{:S(2)}, u32[]{:S(2)}) collective-permute-start(f32[1024,128]{1,0:T(8,128)S(1)} %collective-permute-done.refs_1_), channel_id=1, source_target_pairs={{0,1},{1,2},{2,3},{3,0},{4,5},{5,6},{6,7},{7,4},{8,9},{9,10},{10,1... | collective-permute-start | bytes 1572872 | tf_op jit(solution)/shard_map/ppermute | solution.py:127
  47.6 9.4 %collective-permute-start.7 = (f32[8,128]{1,0:T(8,128)S(1)}, f32[8,128]{1,0:T(8,128)S(1)}, u32[]{:S(2)}, u32[]{:S(2)}) collective-permute-start(f32[8,128]{1,0:T(8,128)S(1)} %get-tuple-element.16), channel_id=1, source_target_pairs={{0,4},{4,8},{8,12},{12,16},{16,20},{20,24},{24,28},{28,0},{1,5},{5... | collective-permute-start | bytes 12296 | tf_op jit(solution)/shard_map/ppermute | solution.py:192
  57.0 4.5 %collective-permute-start.8 = (f32[8,128]{1,0:T(8,128)S(1)}, f32[8,128]{1,0:T(8,128)S(1)}, u32[]{:S(2)}, u32[]{:S(2)}) collective-permute-start(f32[8,128]{1,0:T(8,128)S(1)} %max.9), channel_id=1, source_target_pairs={{0,8},{4,12},{8,16},{12,20},{16,24},{20,28},{24,0},{28,4},{1,9},{5... | collective-permute-start | bytes 12296 | tf_op jit(solution)/shard_map/ppermute | solution.py:192
  61.5 3.6 %collective-permute-start.9 = (f32[8,128]{1,0:T(8,128)S(1)}, f32[8,128]{1,0:T(8,128)S(1)}, u32[]{:S(2)}, u32[]{:S(2)}) collective-permute-start(f32[8,128]{1,0:T(8,128)S(1)} %max.10), channel_id=1, source_target_pairs={{0,16},{4,20},{8,24},{12,28},{16,0},{20,4},{24,8},{28,12},{1,17},{... | collective-permute-start | bytes 12296 | tf_op jit(solution)/shard_map/ppermute | solution.py:192

commit v4 on v3

--- a/solution.py
+++ b/solution.py
@@ -9,6 +9,7 @@
 
 SWEEPS = 2
 PEAK_ROWS = 8
+PAD_ROWS = 16
 F32 = jnp.float32
 BF16 = jnp.bfloat16
 VMEM = pl.BlockSpec(memory_space=pltpu.VMEM)
@@ -35,18 +36,24 @@
     return row == lax.broadcasted_iota(jnp.int32, (rows, cols), 1)
 
 
-def pack_kernel(own_row, level_ref, packed_ref):
-    _, phases, cols = level_ref.shape
+def peak_kernel(own_row, level_ref, peak_ref):
+    cols = level_ref.shape[-1]
     own = level_ref[:, pl.ds(pl.multiple_of(own_row[0], cols), cols), :]
     lowest = jnp.min(jnp.where(on_diagonal(cols, cols)[None], own, 0.0))
-    packed_ref[pl.ds(0, phases), :] = level_ref[1]
-    packed_ref[pl.ds(phases, PEAK_ROWS), :] = jnp.full((PEAK_ROWS, cols), -lowest, F32)
+    peak_ref[...] = jnp.full(peak_ref.shape, -lowest, F32)
+
+
+def pack_kernel(level_ref, peak_ref, packed_ref):
+    phases = level_ref.shape[1]
+    packed_ref[pl.ds(0, phases), :] = level_ref[0]
+    packed_ref[pl.ds(phases, PEAK_ROWS), :] = peak_ref[...]
 
 
 def stack_kernel(up_ref, down_ref, stacked_ref):
     phases = up_ref.shape[1]
     stacked_ref[pl.ds(0, phases), :] = up_ref[0]
     stacked_ref[pl.ds(phases, phases), :] = down_ref[0]
+    stacked_ref[pl.ds(2 * phases, PAD_ROWS), :] = jnp.zeros((PAD_ROWS, up_ref.shape[2]), F32)
 
 
 def owner_row(own_row, offset, cols, shards):
@@ -59,7 +66,10 @@
     up_ref, down_ref, solved_ref, peak_ref, inverse, high, low, s_high, s_low = refs[shards:]
     phases, cols = inverse.shape
     diagonal = on_diagonal(cols, cols)
-    peak = None
+    peak = blocks[0][pl.ds(phases, PEAK_ROWS), :]
+    for block in blocks[1:]:
+        peak = jnp.maximum(peak, block[pl.ds(phases, PEAK_ROWS), :])
+    peak_ref[...] = peak
     for slot, (offset, block) in enumerate(zip(ring_offsets(shards), blocks)):
         rows = pl.ds(owner_row(own_row, offset, cols, shards), cols)
         slot_cols = pl.ds(slot * cols, cols)
@@ -68,9 +78,6 @@
         rate = -jnp.sum(jnp.where(diagonal, square, 0.0), axis=1, keepdims=True)
         inverse[rows, :] = jnp.broadcast_to(1.0 / rate, (cols, cols))
         high[rows, slot_cols], low[rows, slot_cols] = split(jnp.where(diagonal, 0.0, square))
-        block_peak = block[pl.ds(phases, PEAK_ROWS), :]
-        peak = block_peak if peak is None else jnp.maximum(peak, block_peak)
-    peak_ref[...] = peak
     for side, ref in enumerate((up_ref, down_ref)):
         solved_ref[:, pl.ds(side * cols, cols)] = ref[0] * inverse[...]
     for _ in range(SWEEPS):
@@ -133,23 +140,36 @@
         return pl.BlockSpec((1, phases, cols), lambda step: (parity, 0, 0))
 
     odd, even = one_level(1), one_level(0)
+    stacked = pl.pallas_call(
+        stack_kernel,
+        out_shape=shape(2 * phases + PAD_ROWS, cols),
+        in_specs=[even, even],
+        out_specs=VMEM,
+        grid=(1,),
+        compiler_params=params,
+    )(up_blocks, down_blocks)
+
+    peak = pl.pallas_call(
+        peak_kernel,
+        out_shape=shape(PEAK_ROWS, cols),
+        in_specs=[SMEM, VMEM],
+        out_specs=VMEM,
+        grid=(1,),
+        compiler_params=params,
+    )(after(own_row, stacked), level_blocks)
+    reach = 1
+    while reach < ranges:
+        route = [(i, (i + reach) % ranges) for i in range(ranges)]
+        peak = jnp.maximum(peak, lax.ppermute(peak, "lvl", route))
+        reach *= 2
     packed = pl.pallas_call(
         pack_kernel,
         out_shape=shape(phases + PEAK_ROWS, cols),
-        in_specs=[SMEM, VMEM],
+        in_specs=[odd, VMEM],
         out_specs=VMEM,
         grid=(1,),
         compiler_params=params,
-    )(own_row, level_blocks)
-    stacked = pl.pallas_call(
-        stack_kernel,
-        out_shape=shape(2 * phases, cols),
-        in_specs=[even, even],
-        out_specs=VMEM,
-        grid=(1,),
-        compiler_params=params,
-    )(up_blocks, down_blocks)
-
+    )(level_blocks, peak)
     level_parts, even_parts = {0: packed}, {0: stacked}
 
     def step(parts, reached, distance, *earlier):
@@ -158,12 +178,11 @@
 
     offsets = ring_offsets(shards)
     behind, ahead = range(shards // 2), range((shards - 1) // 2)
-    step(level_parts, 0, 1)
+    step(even_parts, 0, 1)
+    for reached in behind:
+        step(level_parts, -reached, 1)
     for reached in ahead:
         step(level_parts, reached, -1)
-    step(even_parts, 0, 1)
-    for reached in behind[1:]:
-        step(level_parts, -reached, 1)
     for reached in ahead:
         step(even_parts, reached, -1, level_parts[-1])
     for reached in behind[1:]:
@@ -183,15 +202,8 @@
         ],
         grid=(1,),
         compiler_params=params,
-    )(own_row, *[level_parts[offset] for offset in offsets], up_blocks, down_blocks)
+    )(after(own_row, even_parts[-1]), *[level_parts[offset] for offset in offsets], up_blocks, down_blocks)
     from_below = lax.ppermute(solved, "lvl", [(i, i + 1) for i in range(ranges - 1)])
-
-    peak = after(peak, even_parts[-1])
-    reach = 1
-    while reach < ranges:
-        other = lax.ppermute(peak, "lvl", [(i, (i + reach) % ranges) for i in range(ranges)])
-        peak = jnp.maximum(peak, other)
-        reach *= 2
 
     last = -len(behind)
     early = [offset for offset in offsets if offset != last]
@@ -202,6 +214,7 @@
         out_specs=(VMEM,) * 3,
         grid=(1,),
         compiler_params=params,
+        cost_estimate=pl.CostEstimate(flops=0, bytes_accessed=0, transcendentals=0),
     )(own_row, *[even_parts[offset] for offset in early], solved, from_below, level_blocks)
     return pl.pallas_call(
         functools.partial(output_kernel, [last], shards),

time: 67.8 us -> 69 us (1.018)
  the two profiles are of different devices: /device:TPU:28 before, /device:TPU:26 now
where the time goes in v4:
time: 69 us; the launch traced here: 68.8 us
  waiting for transfers between devices  48 us (70%)
  starting transfers between devices  11.9 us (17%)
  Pallas kernels  5.07 us (7%)
  local copies, waits for them, and re-layouts  3.09 us (4%)
  between operations  0.73 us (1%)
    ppermute x6, waiting for transfers between devices, shifted(): lax.ppermute(block, 'col', [(i, (i + distance) % shards) for i in range(s...  33.1 us
    ppermute x1, waiting for transfers between devices, per_device(): lax.ppermute(solved, 'lvl', [(i, i + 1) for i in range(ranges - 1)])  8.56 us
    ppermute x3, waiting for transfers between devices, per_device(): peak = jnp.maximum(peak, lax.ppermute(peak, 'lvl', route))  6.32 us
    ppermute x6, starting transfers between devices, shifted(): lax.ppermute(block, 'col', [(i, (i + distance) % shards) for i in range(s...  6.13 us
    ppermute x3, starting transfers between devices, per_device(): peak = jnp.maximum(peak, lax.ppermute(peak, 'lvl', route))  3.86 us
    unnamed x10, local copies, waits for them, and re-layouts  3.09 us
    pallas_call x1, Pallas kernels, per_device(): pl.pallas_call(solve_kernel, out_shape=(shape(phases, 2 * cols), shape(PE...  2.4 us
    ppermute x1, starting transfers between devices, per_device(): lax.ppermute(solved, 'lvl', [(i, i + 1) for i in range(ranges - 1)])  1.92 us
  transfers between devices with their start and end apart: 10, of which 6 were waited for; matrix products, arithmetic and copies ran while one was open for 0% of the time, Pallas kernels for 5%

profile of v4, /device:TPU:26, one launch (start us, length us, event | category | flops | bytes accessed | tf_op | source)
XLA Modules:
  0.0 68.8 jit_solution(15912581218344570453)
XLA Ops:
  0.6 0.0 copy-start.1
  0.6 1.0 %copy-done.1 = f32[2,512,128]{2,1,0:T(8,128)S(1)} copy-done((f32[2,512,128]{2,1,0:T(8,128)S(1)}, f32[2,512,128]{2,1,0:T(8,128)}, u32[]{:S(2)}) %copy-start.1) | copy-done | bytes 524312
  1.7 0.0 copy-start.3
  1.7 1.0 %copy-done.3 = f32[2,512,128]{2,1,0:T(8,128)S(1)} copy-done((f32[2,512,128]{2,1,0:T(8,128)S(1)}, f32[2,512,128]{2,1,0:T(8,128)}, u32[]{:S(2)}) %copy-start.3) | copy-done | bytes 524312
  2.7 0.0 copy-start
  2.8 1.0 %copy-done = f32[2,512,128]{2,1,0:T(8,128)S(1)} copy-done((f32[2,512,128]{2,1,0:T(8,128)S(1)}, f32[2,512,128]{2,1,0:T(8,128)}, u32[]{:S(2)}) %copy-start) | copy-done | bytes 524312
  3.8 0.0 copy-start.4
  3.8 0.1 shard_map.59
  3.9 0.0 copy-start.2
  3.9 0.1 collective-permute-start.2
  4.0 3.0 %collective-permute-done.2 = f32[8,128]{1,0:T(8,128)S(1)} collective-permute-done((f32[8,128]{1,0:T(8,128)S(1)}, f32[8,128]{1,0:T(8,128)S(1)}, u32[]{:S(2)}, u32[]{:S(2)}) %collective-permute-start.2) | collective-permute-done | bytes 4128 | tf_op jit(solution)/shard_map/ppermute | solution.py:163
  7.0 2.4 %collective-permute-start.3 = (f32[8,128]{1,0:T(8,128)S(1)}, f32[8,128]{1,0:T(8,128)S(1)}, u32[]{:S(2)}, u32[]{:S(2)}) collective-permute-start(f32[8,128]{1,0:T(8,128)S(1)} %max.9), channel_id=1, source_target_pairs={{0,8},{4,12},{8,16},{12,20},{16,24},{20,28},{24,0},{28,4},{1,9},{5... | collective-permute-start | bytes 12296 | tf_op jit(solution)/shard_map/ppermute | solution.py:163
  9.4 0.2 collective-permute-start
  9.6 1.1 %collective-permute-done.3 = f32[8,128]{1,0:T(8,128)S(1)} collective-permute-done((f32[8,128]{1,0:T(8,128)S(1)}, f32[8,128]{1,0:T(8,128)S(1)}, u32[]{:S(2)}, u32[]{:S(2)}) %collective-permute-start.3) | collective-permute-done | bytes 4128 | tf_op jit(solution)/shard_map/ppermute | solution.py:163
  10.7 1.4 %collective-permute-start.4 = (f32[8,128]{1,0:T(8,128)S(1)}, f32[8,128]{1,0:T(8,128)S(1)}, u32[]{:S(2)}, u32[]{:S(2)}) collective-permute-start(f32[8,128]{1,0:T(8,128)S(1)} %max.10), channel_id=1, source_target_pairs={{0,16},{4,20},{8,24},{12,28},{16,0},{20,4},{24,8},{28,12},{1,17},{... | collective-permute-start | bytes 12296 | tf_op jit(solution)/shard_map/ppermute | solution.py:163
  12.1 2.2 %collective-permute-done.4 = f32[8,128]{1,0:T(8,128)S(1)} collective-permute-done((f32[8,128]{1,0:T(8,128)S(1)}, f32[8,128]{1,0:T(8,128)S(1)}, u32[]{:S(2)}, u32[]{:S(2)}) %collective-permute-start.4) | collective-permute-done | bytes 4128 | tf_op jit(solution)/shard_map/ppermute | solution.py:163
  14.4 0.5 collective-permute-start.5
  14.9 1.6 %collective-permute-start.7 = (f32[520,128]{1,0:T(8,128)S(1)}, f32[520,128]{1,0:T(8,128)S(1)}, u32[]{:S(2)}, u32[]{:S(2)}) collective-permute-start(f32[520,128]{1,0:T(8,128)S(1)} %shard_map.60.refs_0_), channel_id=1, source_target_pairs={{0,3},{1,0},{2,1},{3,2},{4,7},{5,4},{6,5},{7,6},{8,11},{9,8},{10,9... | collective-permute-start | bytes 798728 | tf_op jit(solution)/shard_map/ppermute | solution.py:134
  16.4 16.8 %collective-permute-done.5.refs_1_ = f32[520,128]{1,0:T(8,128)S(1)} collective-permute-done((f32[520,128]{1,0:T(8,128)S(1)}, f32[520,128]{1,0:T(8,128)S(1)}, u32[]{:S(2)}, u32[]{:S(2)}) %collective-permute-start.5) | collective-permute-done | bytes 266272 | tf_op jit(solution)/shard_map/ppermute | solution.py:134
  33.2 0.0 collective-permute-start.6
  33.2 2.0 %collective-permute-start.9 = (f32[1040,128]{1,0:T(8,128)S(1)}, f32[1040,128]{1,0:T(8,128)S(1)}, u32[]{:S(2)}, u32[]{:S(2)}) collective-permute-start(f32[1040,128]{1,0:T(8,128)S(1)} %shard_map.58.refs_0_), channel_id=1, source_target_pairs={{0,3},{1,0},{2,1},{3,2},{4,7},{5,4},{6,5},{7,6},{8,11},{9,8},{10,9... | collective-permute-start | bytes 1597448 | tf_op jit(solution)/shard_map/ppermute | solution.py:134
  35.3 0.0 collective-permute-done.refs_1_
  35.3 1.8 %collective-permute-start.1 = (f32[1040,128]{1,0:T(8,128)S(1)}, f32[1040,128]{1,0:T(8,128)S(1)}, u32[]{:S(2)}, u32[]{:S(2)}) collective-permute-start(f32[1040,128]{1,0:T(8,128)S(1)} %collective-permute-done.refs_1_), channel_id=1, source_target_pairs={{0,1},{1,2},{2,3},{3,0},{4,5},{5,6},{6,7},{7,4},{8,9},{9,10},{10,1... | collective-permute-start | bytes 1597448 | tf_op jit(solution)/shard_map/ppermute | solution.py:134
  37.1 0.0 collective-permute-done.7.refs_3_
  37.1 16.3 %collective-permute-done.6.refs_2_ = f32[520,128]{1,0:T(8,128)S(1)} collective-permute-done((f32[520,128]{1,0:T(8,128)S(1)}, f32[520,128]{1,0:T(8,128)S(1)}, u32[]{:S(2)}, u32[]{:S(2)}) %collective-permute-start.6) | collective-permute-done | bytes 266272 | tf_op jit(solution)/shard_map/ppermute | solution.py:134
  53.4 0.0 copy-done.4
  53.4 0.0 copy-done.2
  53.4 2.4 %shard_map.61 = (f32[512,256]{1,0:T(8,128)S(1)}, f32[8,128]{1,0:T(8,128)S(1)}) custom-call(s32[1]{0:T(128)} %bitcast.own_row, f32[520,128]{1,0:T(8,128)S(1)} %shard_map.60.refs_0_, f32[520,128]{1,0:T(8,128)S(1)} %collective-permute-done.5.refs_1_, f32[520,128]{1,0:T(8,128)S(1)} %collective-permute-done.6.refs_2_, ...), custom_call_target="tpu_custom_call" | custom-call | tf_op jit(solution)/shard_map/pallas_call | solution.py:191
  55.8 1.9 %collective-permute-start.8 = (f32[512,256]{1,0:T(8,128)S(1)}, f32[512,256]{1,0:T(8,128)S(1)}, u32[]{:S(2)}, u32[]{:S(2)}) collective-permute-start(f32[512,256]{1,0:T(8,128)S(1)} %get-tuple-element.13.refs_3_.refs_1_), channel_id=1, source_target_pairs={{0,4},{4,8},{8,12},{12,16},{16,20},{20,24},{24,28},{1,5},{5,9},{9,... | collective-permute-start | bytes 1572872 | tf_op jit(solution)/shard_map/ppermute | solution.py:206
  57.7 0.0 collective-permute-done.9.refs_2_
  57.7 8.6 %collective-permute-done.8.refs_4_.refs_2_ = f32[512,256]{1,0:T(8,128)S(1)} collective-permute-done((f32[512,256]{1,0:T(8,128)S(1)}, f32[512,256]{1,0:T(8,128)S(1)}, u32[]{:S(2)}, u32[]{:S(2)}) %collective-permute-start.8) | collective-permute-done | bytes 524320 | tf_op jit(solution)/shard_map/ppermute | solution.py:206
  66.3 1.0 %shard_map.62 = (f32[512,128]{1,0:T(8,128)S(1)}, f32[512,128]{1,0:T(8,128)S(1)}, f32[512,128]{1,0:T(8,128)S(1)}) custom-call(s32[1]{0:T(128)} %bitcast.own_row, f32[1040,128]{1,0:T(8,128)S(1)} %shard_map.58.refs_0_, f32[1040,128]{1,0:T(8,128)S(1)} %collective-permute-done.refs_1_, f32[1040,128]{1,0:T(8,128)S(1)} %collective-permute-done.9.refs_2_, ...), custom_call_target="tpu_custom_call" | custom-call | tf_op jit(solution)/shard_map/pallas_call | solution.py:210
  67.3 0.0 collective-permute-done.1.refs_0_
  67.3 1.5 %shard_map.63 = (f32[1,512,128]{2,1,0:T(8,128)}, f32[1,512,128]{2,1,0:T(8,128)}, f32[1,512,128]{2,1,0:T(8,128)}) custom-call(s32[1]{0:T(128)} %bitcast.own_row, f32[1040,128]{1,0:T(8,128)S(1)} %collective-permute-done.1.refs_0_, f32[512,256]{1,0:T(8,128)S(1)} %get-tuple-element.13.refs_3_.refs_1_, f32[512,256]{1,0:T(8,128)S(1)} %collective-permute-done.8.refs_4_.refs_2_, ...), custom_call_target="tpu_custom_call" | custom-call | tf_op jit(solution)/shard_map/pallas_call | solution.py:219
  (5 shorter events, 0.1 us)
Async XLA Ops:
  0.6 1.0 %copy-start.1 = (f32[2,512,128]{2,1,0:T(8,128)S(1)}, f32[2,512,128]{2,1,0:T(8,128)}, u32[]{:S(2)}) copy-start(f32[2,512,128]{2,1,0:T(8,128)} %refs_4_.1) | copy-start | bytes 1572868
  1.7 1.0 %copy-start.3 = (f32[2,512,128]{2,1,0:T(8,128)S(1)}, f32[2,512,128]{2,1,0:T(8,128)}, u32[]{:S(2)}) copy-start(f32[2,512,128]{2,1,0:T(8,128)} %refs_5_.2) | copy-start | bytes 1572868
  2.7 1.0 %copy-start = (f32[2,512,128]{2,1,0:T(8,128)S(1)}, f32[2,512,128]{2,1,0:T(8,128)}, u32[]{:S(2)}) copy-start(f32[2,512,128]{2,1,0:T(8,128)} %refs_5_.3) | copy-start | bytes 1572868
  3.8 49.6 %copy-start.4 = (f32[2,512,128]{2,1,0:T(8,128)S(1)}, f32[2,512,128]{2,1,0:T(8,128)}, u32[]{:S(2)}) copy-start(f32[2,512,128]{2,1,0:T(8,128)} %refs_5_.2) | copy-start | bytes 1572868
  3.9 49.5 %copy-start.2 = (f32[2,512,128]{2,1,0:T(8,128)S(1)}, f32[2,512,128]{2,1,0:T(8,128)}, u32[]{:S(2)}) copy-start(f32[2,512,128]{2,1,0:T(8,128)} %refs_4_.1) | copy-start | bytes 1572868
  3.9 3.1 %collective-permute-start.2 = (f32[8,128]{1,0:T(8,128)S(1)}, f32[8,128]{1,0:T(8,128)S(1)}, u32[]{:S(2)}, u32[]{:S(2)}) collective-permute-start(f32[8,128]{1,0:T(8,128)S(1)} %shard_map.59), channel_id=1, source_target_pairs={{0,4},{4,8},{8,12},{12,16},{16,20},{20,24},{24,28},{28,0},{1,5},{5... | collective-permute-start | bytes 12296 | tf_op jit(solution)/shard_map/ppermute | solution.py:163
  7.0 3.7 %collective-permute-start.3 = (f32[8,128]{1,0:T(8,128)S(1)}, f32[8,128]{1,0:T(8,128)S(1)}, u32[]{:S(2)}, u32[]{:S(2)}) collective-permute-start(f32[8,128]{1,0:T(8,128)S(1)} %max.9), channel_id=1, source_target_pairs={{0,8},{4,12},{8,16},{12,20},{16,24},{20,28},{24,0},{28,4},{1,9},{5... | collective-permute-start | bytes 12296 | tf_op jit(solution)/shard_map/ppermute | solution.py:163
  9.4 25.9 %collective-permute-start = (f32[1040,128]{1,0:T(8,128)S(1)}, f32[1040,128]{1,0:T(8,128)S(1)}, u32[]{:S(2)}, u32[]{:S(2)}) collective-permute-start(f32[1040,128]{1,0:T(8,128)S(1)} %shard_map.58.refs_0_), channel_id=1, source_target_pairs={{0,1},{1,2},{2,3},{3,0},{4,5},{5,6},{6,7},{7,4},{8,9},{9,10},{10,1... | collective-permute-start | bytes 1597448 | tf_op jit(solution)/shard_map/ppermute | solution.py:134
  10.7 3.6 %collective-permute-start.4 = (f32[8,128]{1,0:T(8,128)S(1)}, f32[8,128]{1,0:T(8,128)S(1)}, u32[]{:S(2)}, u32[]{:S(2)}) collective-permute-start(f32[8,128]{1,0:T(8,128)S(1)} %max.10), channel_id=1, source_target_pairs={{0,16},{4,20},{8,24},{12,28},{16,0},{20,4},{24,8},{28,12},{1,17},{... | collective-permute-start | bytes 12296 | tf_op jit(solution)/shard_map/ppermute | solution.py:163
  14.4 18.9 %collective-permute-start.5 = (f32[520,128]{1,0:T(8,128)S(1)}, f32[520,128]{1,0:T(8,128)S(1)}, u32[]{:S(2)}, u32[]{:S(2)}) collective-permute-start(f32[520,128]{1,0:T(8,128)S(1)} %shard_map.60.refs_0_), channel_id=1, source_target_pairs={{0,1},{1,2},{2,3},{3,0},{4,5},{5,6},{6,7},{7,4},{8,9},{9,10},{10,1... | collective-permute-start | bytes 798728 | tf_op jit(solution)/shard_map/ppermute | solution.py:134
  14.9 22.2 %collective-permute-start.7 = (f32[520,128]{1,0:T(8,128)S(1)}, f32[520,128]{1,0:T(8,128)S(1)}, u32[]{:S(2)}, u32[]{:S(2)}) collective-permute-start(f32[520,128]{1,0:T(8,128)S(1)} %shard_map.60.refs_0_), channel_id=1, source_target_pairs={{0,3},{1,0},{2,1},{3,2},{4,7},{5,4},{6,5},{7,6},{8,11},{9,8},{10,9... | collective-permute-start | bytes 798728 | tf_op jit(solution)/shard_map/ppermute | solution.py:134
  33.2 20.1 %collective-permute-start.6 = (f32[520,128]{1,0:T(8,128)S(1)}, f32[520,128]{1,0:T(8,128)S(1)}, u32[]{:S(2)}, u32[]{:S(2)}) collective-permute-start(f32[520,128]{1,0:T(8,128)S(1)} %collective-permute-done.5.refs_1_), channel_id=1, source_target_pairs={{0,1},{1,2},{2,3},{3,0},{4,5},{5,6},{6,7},{7,4},{8,9},{9,10},{10,1... | collective-permute-start | bytes 798728 | tf_op jit(solution)/shard_map/ppermute | solution.py:134
  33.2 24.5 %collective-permute-start.9 = (f32[1040,128]{1,0:T(8,128)S(1)}, f32[1040,128]{1,0:T(8,128)S(1)}, u32[]{:S(2)}, u32[]{:S(2)}) collective-permute-start(f32[1040,128]{1,0:T(8,128)S(1)} %shard_map.58.refs_0_), channel_id=1, source_target_pairs={{0,3},{1,0},{2,1},{3,2},{4,7},{5,4},{6,5},{7,6},{8,11},{9,8},{10,9... | collective-permute-start | bytes 1597448 | tf_op jit(solution)/shard_map/ppermute | solution.py:134
  35.3 32.0 %collective-permute-start.1 = (f32[1040,128]{1,0:T(8,128)S(1)}, f32[1040,128]{1,0:T(8,128)S(1)}, u32[]{:S(2)}, u32[]{:S(2)}) collective-permute-start(f32[1040,128]{1,0:T(8,128)S(1)} %collective-permute-done.refs_1_), channel_id=1, source_target_pairs={{0,1},{1,2},{2,3},{3,0},{4,5},{5,6},{6,7},{7,4},{8,9},{9,10},{10,1... | collective-permute-start | bytes 1597448 | tf_op jit(solution)/shard_map/ppermute | solution.py:134
  55.8 10.5 %collective-permute-start.8 = (f32[512,256]{1,0:T(8,128)S(1)}, f32[512,256]{1,0:T(8,128)S(1)}, u32[]{:S(2)}, u32[]{:S(2)}) collective-permute-start(f32[512,256]{1,0:T(8,128)S(1)} %get-tuple-element.13.refs_3_.refs_1_), channel_id=1, source_target_pairs={{0,4},{4,8},{8,12},{12,16},{16,20},{20,24},{24,28},{1,5},{5,9},{9,... | collective-permute-start | bytes 1572872 | tf_op jit(solution)/shard_map/ppermute | solution.py:206

commit v5 on v4

v5 whole, which is shorter than its diff:
```python
import functools

import jax
import jax.numpy as jnp
from jax import lax
from jax.experimental import pallas as pl
from jax.experimental.pallas import tpu as pltpu
from jax.sharding import PartitionSpec as P

SWEEPS = 2
PEAK_ROWS = 8
PAD_ROWS = 16
F32 = jnp.float32
BF16 = jnp.bfloat16
VMEM = pl.BlockSpec(memory_space=pltpu.VMEM)
ANY = pl.BlockSpec(memory_space=pl.ANY)
SMEM = pl.BlockSpec(memory_space=pltpu.SMEM)


def ring_offsets(shards):
    return [0, *[-d for d in range(1, shards // 2 + 1)], *range(1, (shards - 1) // 2 + 1)]


def split(x):
    high = x.astype(BF16)
    return high, (x - high.astype(F32)).astype(BF16)


def exact_dot(left, right):
    (left_high, left_low), (right_high, right_low) = left, right
    dot = lambda a, b: jnp.dot(a, b, preferred_element_type=F32)
    return dot(left_high, right_high) + (dot(left_high, right_low) + dot(left_low, right_high))


def on_diagonal(rows, cols):
    row = lax.broadcasted_iota(jnp.int32, (rows, cols), 0)
    return row == lax.broadcasted_iota(jnp.int32, (rows, cols), 1)


def send_kernel(up_ref, level_ref, down_ref, all_ref, odd_ref, even_ref, sems):
    _, phases, _ = level_ref.shape
    rows = lambda ref, part: ref.at[pl.ds(part * phases, phases), :]
    copies = [
        pltpu.make_async_copy(source, target, sems.at[at])
        for at, (source, target) in enumerate(
            (
                (level_ref.at[1], rows(all_ref, 0)),
                (up_ref.at[0], rows(all_ref, 1)),
                (down_ref.at[0], rows(all_ref, 2)),
                (level_ref.at[1], odd_ref),
                (up_ref.at[0], rows(even_ref, 0)),
                (down_ref.at[0], rows(even_ref, 1)),
            )
        )
    ]
    for copy in copies:
        copy.start()
    for copy in copies:
        copy.wait()


def peak_kernel(own_row, level_ref, peak_ref):
    cols = level_ref.shape[-1]
    own = level_ref[:, pl.ds(pl.multiple_of(own_row[0], cols), cols), :]
    lowest = jnp.min(jnp.where(on_diagonal(cols, cols)[None], own, 0.0))
    peak_ref[...] = jnp.full(peak_ref.shape, -lowest, F32)


def owner_row(own_row, offset, cols, shards):
    return pl.multiple_of(lax.rem(own_row[0] + (offset + shards) * cols, shards * cols), cols)


def solve_kernel(own_row, *refs):
    shards = len(refs) - 8
    blocks = [refs[0].at[0], *refs[1:shards]]
    up_ref, down_ref, solved_ref, inverse, high, low, s_high, s_low = refs[shards:]
    phases, cols = inverse.shape
    diagonal = on_diagonal(cols, cols)
    for slot, (offset, block) in enumerate(zip(ring_offsets(shards), blocks)):
        rows = pl.ds(owner_row(own_row, offset, cols, shards), cols)
        slot_cols = pl.ds(slot * cols, cols)
        high[:, slot_cols], low[:, slot_cols] = split(block[pl.ds(0, phases), :])
        square = block[rows, :]
        rate = -jnp.sum(jnp.where(diagonal, square, 0.0), axis=1, keepdims=True)
        inverse[rows, :] = jnp.broadcast_to(1.0 / rate, (cols, cols))
        high[rows, slot_cols], low[rows, slot_cols] = split(jnp.where(diagonal, 0.0, square))
    for side, ref in enumerate((up_ref, down_ref)):
        solved_ref[:, pl.ds(side * cols, cols)] = ref[0] * inverse[...]
    for _ in range(SWEEPS):
        for slot, offset in enumerate(ring_offsets(shards)):
            rows = pl.ds(owner_row(own_row, offset, cols, shards), cols)
            slot_rows = pl.ds(slot * cols, cols)
            s_high[slot_rows, :], s_low[slot_rows, :] = split(solved_ref[rows, :])
        product = exact_dot((high[...], low[...]), (s_high[...], s_low[...]))
        for side, ref in enumerate((up_ref, down_ref)):
            columns = slice(side * cols, (side + 1) * cols)
            solved_ref[:, columns] = (ref[0] + product[:, columns]) * inverse[...]


def gathered_product(own_row, blocks, offsets, shards, solved_ref):
    phases, cols = solved_ref.shape[0], blocks[0].shape[-1]
    left = split(jnp.concatenate([block[...] for block in blocks], axis=1))
    rows = [pl.ds(owner_row(own_row, offset, cols, shards), cols) for offset in offsets]
    right = split(jnp.concatenate([solved_ref[r, :] for r in rows], axis=0))
    return exact_dot(left, right)


def partial_kernel(first_rows, offsets, shards, own_row, up_ref, down_ref, *refs):
    *blocks, solved_ref, below_ref, level_ref, part_level, part_up, part_down = refs
    phases, cols = part_up.shape
    ups = [ref.at[pl.ds(first, phases), :] for first, ref in zip(first_rows, blocks)]
    downs = [ref.at[pl.ds(first + phases, phases), :] for first, ref in zip(first_rows, blocks)]
    upper = gathered_product(own_row, [up_ref.at[0], *ups], offsets, shards, solved_ref)
    part_up[...] = upper[:, :cols]
    lower = gathered_product(own_row, [down_ref.at[0], *downs], offsets, shards, below_ref)
    part_down[...] = lower[:, cols:]
    part_level[...] = level_ref[0] + upper[:, cols:] + lower[:, :cols]


def output_kernel(offset, shards, own_row, *refs):
    block, solved_ref, below_ref, part_level, part_up, part_down, peak_ref, new_level, new_up, new_down = refs
    phases, cols = part_up.shape
    scale = 1.0 / peak_ref[0:1, :]
    up, down = block.at[pl.ds(0, phases), :], block.at[pl.ds(phases, phases), :]
    upper = gathered_product(own_row, [up], [offset], shards, solved_ref)
    new_up[0] = (part_up[...] + upper[:, :cols]) * scale
    lower = gathered_product(own_row, [down], [offset], shards, below_ref)
    new_down[0] = (part_down[...] + lower[:, cols:]) * scale
    new_level[0] = (part_level[...] + upper[:, cols:] + lower[:, :cols]) * scale


def per_device(up_blocks, level_blocks, down_blocks):
    levels, phases, cols = level_blocks.shape
    assert levels == 2
    shards = lax.axis_size("col")
    ranges = lax.axis_size("lvl")
    own_row = (lax.axis_index("col") * cols).astype(jnp.int32).reshape(1)
    params = pltpu.CompilerParams(vmem_limit_bytes=32 * 2**20)
    shape = lambda *dims, kind=F32: jax.ShapeDtypeStruct(dims, kind)

    def shifted(block, distance):
        return lax.ppermute(block, "col", [(i, (i + distance) % shards) for i in range(shards)])

    def after(value, *earlier):
        return lax.optimization_barrier((value, *earlier))[0]

    def one_level(parity):
        return pl.BlockSpec((1, phases, cols), lambda step: (parity, 0, 0))

    odd, even = one_level(1), one_level(0)
    block, even_rows = shape(phases, cols), 2 * phases + PAD_ROWS
    everything, odd_block, even_blocks = pl.pallas_call(
        send_kernel,
        out_shape=(shape(phases + even_rows, cols), block, shape(even_rows, cols)),
        in_specs=[ANY] * 3,
        out_specs=(ANY,) * 3,
        scratch_shapes=[pltpu.SemaphoreType.DMA((6,))],
        grid=(1,),
        compiler_params=pltpu.CompilerParams(vmem_limit_bytes=60 * 2**20),
    )(up_blocks, level_blocks, down_blocks)
    peak = pl.pallas_call(
        peak_kernel,
        out_shape=shape(PEAK_ROWS, cols),
        in_specs=[SMEM, VMEM],
        out_specs=VMEM,
        grid=(1,),
        compiler_params=params,
    )(own_row, level_blocks)
    reach = 1
    while reach < ranges:
        route = [(i, (i + reach) % ranges) for i in range(ranges)]
        peak = jnp.maximum(peak, lax.ppermute(peak, "lvl", route))
        reach *= 2

    offsets = ring_offsets(shards)
    behind, ahead = range(1, shards // 2), range((shards - 1) // 2)
    first = shifted(everything, 1)
    level_parts, even_parts = {0: odd_block, -1: first[:phases]}, {0: even_blocks, -1: first[phases:]}

    def step(parts, reached, distance, *earlier):
        block = after(parts[reached], *earlier) if earlier else parts[reached]
        parts[reached - distance] = shifted(block, distance)

    for reached in ahead:
        step(level_parts, reached, -1)
    for reached in behind:
        step(level_parts, -reached, 1, peak)
    for reached in ahead:
        step(even_parts, reached, -1, first)
    for reached in behind:
        step(even_parts, -reached, 1)
    level_parts[0], level_parts[-1] = level_blocks, first
    for found in [shifted(peak, distance) for distance in range(1, shards)]:
        peak = jnp.maximum(peak, found)

    solved = pl.pallas_call(
        solve_kernel,
        out_shape=shape(phases, 2 * cols),
        in_specs=[SMEM, odd, *[VMEM] * (shards - 1), odd, odd],
        out_specs=VMEM,
        scratch_shapes=[
            pltpu.VMEM((phases, cols), F32),
            pltpu.VMEM((phases, phases), BF16),
            pltpu.VMEM((phases, phases), BF16),
            pltpu.VMEM((phases, 2 * cols), BF16),
            pltpu.VMEM((phases, 2 * cols), BF16),
        ],
        grid=(1,),
        compiler_params=params,
    )(own_row, *[level_parts[offset] for offset in offsets], up_blocks, down_blocks)
    from_below = lax.ppermute(solved, "lvl", [(i, i + 1) for i in range(ranges - 1)])

    last = -(shards // 2)
    early = [offset for offset in offsets[1:] if offset != last]
    first_rows = [phases if offset == -1 else 0 for offset in early]
    even_parts[-1] = first
    parts = pl.pallas_call(
        functools.partial(partial_kernel, first_rows, [0, *early], shards),
        out_shape=(block,) * 3,
        in_specs=[SMEM, even, even, *[VMEM] * (len(early) + 2), even],
        out_specs=(VMEM,) * 3,
        grid=(1,),
        compiler_params=params,
        cost_estimate=pl.CostEstimate(flops=0, bytes_accessed=0, transcendentals=0),
    )(own_row, up_blocks, down_blocks, *[even_parts[offset] for offset in early], solved, from_below, level_blocks)
    return pl.pallas_call(
        functools.partial(output_kernel, last, shards),
        out_shape=(shape(1, phases, cols),) * 3,
        in_specs=[SMEM, *[VMEM] * 7],
        out_specs=(VMEM,) * 3,
        grid=(1,),
        compiler_params=params,
    )(own_row, even_parts[last], solved, from_below, *parts, peak)


def solution(mesh):
    placed = (P("lvl", None, "col"),) * 3
    return jax.shard_map(per_device, mesh=mesh, in_specs=placed, out_specs=placed, check_vma=False)
```

time: 69 us -> 113 us (1.64)
  the two profiles are of different devices: /device:TPU:26 before, /device:TPU:0 now
where the time goes in v5:
time: 113 us; the launch traced here: 112 us
  Pallas kernels  53.8 us (48%)
  starting transfers between devices  31.2 us (28%)
  waiting for transfers between devices  26.6 us (24%)
    pallas_call x1, Pallas kernels, per_device(): pl.pallas_call(send_kernel, out_shape=(shape(phases + even_rows, cols), b...  48.8 us
    ppermute x8, starting transfers between devices, shifted(): lax.ppermute(block, 'col', [(i, (i + distance) % shards) for i in range(s...  27.7 us
    ppermute x8, waiting for transfers between devices, shifted(): lax.ppermute(block, 'col', [(i, (i + distance) % shards) for i in range(s...  18.7 us
    ppermute x3, waiting for transfers between devices, per_device(): peak = jnp.maximum(peak, lax.ppermute(peak, 'lvl', route))  7.83 us
    pallas_call x1, Pallas kernels, per_device(): pl.pallas_call(solve_kernel, out_shape=shape(phases, 2 * cols), in_specs=...  2.39 us
  transfers between devices with their start and end apart: 12, of which 6 were waited for; matrix products, arithmetic and copies ran while one was open for 0% of the time, Pallas kernels for 3%

profile of v5, /device:TPU:0, one launch (start us, length us, event | category | flops | bytes accessed | tf_op | source)
XLA Modules:
  0.0 112.4 jit_solution(170758207412567523)
XLA Ops:
  0.6 0.0 copy-start
  0.6 48.8 %shard_map.58 = (f32[1552,128]{1,0:T(8,128)}, f32[512,128]{1,0:T(8,128)}, f32[1040,128]{1,0:T(8,128)}) custom-call(f32[2,512,128]{2,1,0:T(8,128)} %up_ref.3, f32[2,512,128]{2,1,0:T(8,128)} %refs_4_.3, f32[2,512,128]{2,1,0:T(8,128)} %down_ref.3), custom_call_target="tpu_custom_call" | custom-call | tf_op jit(solution)/shard_map/pallas_call | solution.py:152
  49.4 3.1 %collective-permute-start = (f32[1552,128]{1,0:T(8,128)}, f32[1552,128]{1,0:T(8,128)S(1)}, u32[]{:S(2)}, u32[]{:S(2)}) collective-permute-start(f32[1552,128]{1,0:T(8,128)} %get-tuple-element.11), channel_id=1, source_target_pairs={{0,1},{1,2},{2,3},{3,0},{4,5},{5,6},{6,7},{7,4},{8,9},{9,10},{10,1... | collective-permute-start | bytes 2383880 | tf_op jit(solution)/shard_map/ppermute | solution.py:142
  52.5 0.0 copy-start.4
  52.5 0.0 copy-done
  52.5 0.0 copy-start.3
  52.5 0.1 shard_map.59
  52.7 0.1 collective-permute-start.2
  52.7 3.9 %collective-permute-done.2 = f32[8,128]{1,0:T(8,128)S(1)} collective-permute-done((f32[8,128]{1,0:T(8,128)S(1)}, f32[8,128]{1,0:T(8,128)S(1)}, u32[]{:S(2)}, u32[]{:S(2)}) %collective-permute-start.2) | collective-permute-done | bytes 4128 | tf_op jit(solution)/shard_map/ppermute | solution.py:172
  56.7 0.6 collective-permute-start.3
  57.3 3.9 %collective-permute-done.3 = f32[8,128]{1,0:T(8,128)S(1)} collective-permute-done((f32[8,128]{1,0:T(8,128)S(1)}, f32[8,128]{1,0:T(8,128)S(1)}, u32[]{:S(2)}, u32[]{:S(2)}) %collective-permute-start.3) | collective-permute-done | bytes 4128 | tf_op jit(solution)/shard_map/ppermute | solution.py:172
  61.2 1.5 %collective-permute-start.4 = (f32[8,128]{1,0:T(8,128)S(1)}, f32[8,128]{1,0:T(8,128)S(1)}, u32[]{:S(2)}, u32[]{:S(2)}) collective-permute-start(f32[8,128]{1,0:T(8,128)S(1)} %max.19), channel_id=1, source_target_pairs={{0,16},{4,20},{8,24},{12,28},{16,0},{20,4},{24,8},{28,12},{1,17},{... | collective-permute-start | bytes 12296 | tf_op jit(solution)/shard_map/ppermute | solution.py:172
  62.7 0.0 copy-done.4
  62.7 2.2 %collective-permute-start.6 = (f32[512,128]{1,0:T(8,128)S(1)}, f32[512,128]{1,0:T(8,128)S(1)}, u32[]{:S(2)}, u32[]{:S(2)}) collective-permute-start(f32[512,128]{1,0:T(8,128)S(1)} %copy-done.4), channel_id=1, source_target_pairs={{0,3},{1,0},{2,1},{3,2},{4,7},{5,4},{6,5},{7,6},{8,11},{9,8},{10,9... | collective-permute-start | bytes 786440 | tf_op jit(solution)/shard_map/ppermute | solution.py:142
  64.9 0.0 collective-permute-done.4
  65.0 8.4 %collective-permute-done.refs_1_.refs_0_ = f32[1552,128]{1,0:T(8,128)S(1)} collective-permute-done((f32[1552,128]{1,0:T(8,128)}, f32[1552,128]{1,0:T(8,128)S(1)}, u32[]{:S(2)}, u32[]{:S(2)}) %collective-permute-start) | collective-permute-done | bytes 794656 | tf_op jit(solution)/shard_map/ppermute | solution.py:142
  73.4 0.1 collective-permute-start.5
  73.4 0.0 copy-done.3
  73.4 0.0 copy-start.1
  73.5 0.0 copy-start.2
  73.5 5.6 %collective-permute-start.8 = (f32[1040,128]{1,0:T(8,128)S(1)}, f32[1040,128]{1,0:T(8,128)S(1)}, u32[]{:S(2)}, u32[]{:S(2)}) collective-permute-start(f32[1040,128]{1,0:T(8,128)S(1)} %copy-done.3), channel_id=1, source_target_pairs={{0,3},{1,0},{2,1},{3,2},{4,7},{5,4},{6,5},{7,6},{8,11},{9,8},{10,9... | collective-permute-start | bytes 1597448 | tf_op jit(solution)/shard_map/ppermute | solution.py:142
  79.1 0.1 collective-permute-start.1
  79.2 0.0 collective-permute-done.6.refs_3_
  79.2 7.0 %collective-permute-done.5.refs_2_ = f32[512,128]{1,0:T(8,128)S(1)} collective-permute-done((f32[512,128]{1,0:T(8,128)S(1)}, f32[512,128]{1,0:T(8,128)S(1)}, u32[]{:S(2)}, u32[]{:S(2)}) %collective-permute-start.5) | collective-permute-done | bytes 262176 | tf_op jit(solution)/shard_map/ppermute | solution.py:142
  86.2 0.0 copy-done.1
  86.2 0.0 copy-done.2
  86.2 2.4 %shard_map.60.refs_2_.refs_1_ = f32[512,256]{1,0:T(8,128)S(1)} custom-call(s32[1]{0:T(128)} %bitcast.own_row, f32[2,512,128]{2,1,0:T(8,128)S(1)} %copy-done, f32[1552,128]{1,0:T(8,128)S(1)} %collective-permute-done.refs_1_.refs_0_, f32[512,128]{1,0:T(8,128)S(1)} %collective-permute-done.5.refs_2_, f32[512,128]{1,0:T(8,128)S(1)} %collective-permute-done.6.refs_3_, ...), custom_call_target="tpu_custom_call" | custom-call | tf_op jit(solution)/shard_map/pallas_call | solution.py:196
  88.6 1.3 %collective-permute-start.7 = (f32[512,256]{1,0:T(8,128)S(1)}, f32[512,256]{1,0:T(8,128)S(1)}, u32[]{:S(2)}, u32[]{:S(2)}) collective-permute-start(f32[512,256]{1,0:T(8,128)S(1)} %shard_map.60.refs_2_.refs_1_), channel_id=1, source_target_pairs={{0,4},{4,8},{8,12},{12,16},{16,20},{20,24},{24,28},{1,5},{5,9},{9,... | collective-permute-start | bytes 1572872 | tf_op jit(solution)/shard_map/ppermute | solution.py:211
  89.9 12.4 %collective-permute-start.10 = (f32[8,128]{1,0:T(8,128)S(1)}, f32[8,128]{1,0:T(8,128)S(1)}, u32[]{:S(2)}, u32[]{:S(2)}) collective-permute-start(f32[8,128]{1,0:T(8,128)S(1)} %max.20), channel_id=1, source_target_pairs={{0,2},{1,3},{2,0},{3,1},{4,6},{5,7},{6,4},{7,5},{8,10},{9,11},{10,... | collective-permute-start | bytes 12296 | tf_op jit(solution)/shard_map/ppermute | solution.py:142
  102.3 1.2 %collective-permute-start.11 = (f32[8,128]{1,0:T(8,128)S(1)}, f32[8,128]{1,0:T(8,128)S(1)}, u32[]{:S(2)}, u32[]{:S(2)}) collective-permute-start(f32[8,128]{1,0:T(8,128)S(1)} %max.20), channel_id=1, source_target_pairs={{0,3},{1,0},{2,1},{3,2},{4,7},{5,4},{6,5},{7,6},{8,11},{9,8},{10,9... | collective-permute-start | bytes 12296 | tf_op jit(solution)/shard_map/ppermute | solution.py:142
  103.5 0.8 collective-permute-done.10
  104.2 3.1 %collective-permute-start.9 = (f32[8,128]{1,0:T(8,128)S(1)}, f32[8,128]{1,0:T(8,128)S(1)}, u32[]{:S(2)}, u32[]{:S(2)}) collective-permute-start(f32[8,128]{1,0:T(8,128)S(1)} %max.20), channel_id=1, source_target_pairs={{0,1},{1,2},{2,3},{3,0},{4,5},{5,6},{6,7},{7,4},{8,9},{9,10},{10,1... | collective-permute-start | bytes 12296 | tf_op jit(solution)/shard_map/ppermute | solution.py:142
  107.4 0.0 collective-permute-done.11
  107.4 2.5 %collective-permute-done.9 = f32[8,128]{1,0:T(8,128)S(1)} collective-permute-done((f32[8,128]{1,0:T(8,128)S(1)}, f32[8,128]{1,0:T(8,128)S(1)}, u32[]{:S(2)}, u32[]{:S(2)}) %collective-permute-start.9) | collective-permute-done | bytes 4128 | tf_op jit(solution)/shard_map/ppermute | solution.py:142
  109.9 0.0 collective-permute-done.8.refs_1_
  109.9 0.0 collective-permute-done.7.refs_3_.refs_2_
  109.9 1.0 shard_map.61
  110.9 0.0 collective-permute-done.1.refs_0_
  111.0 1.5 %shard_map.62 = (f32[1,512,128]{2,1,0:T(8,128)}, f32[1,512,128]{2,1,0:T(8,128)}, f32[1,512,128]{2,1,0:T(8,128)}) custom-call(s32[1]{0:T(128)} %bitcast.own_row, f32[1040,128]{1,0:T(8,128)S(1)} %collective-permute-done.1.refs_0_, f32[512,256]{1,0:T(8,128)S(1)} %shard_map.60.refs_2_.refs_1_, f32[512,256]{1,0:T(8,128)S(1)} %collective-permute-done.7.refs_3_.refs_2_, ...), custom_call_target="tpu_custom_call" | custom-call | tf_op jit(solution)/shard_map/pallas_call | solution.py:226
  (6 shorter events, 0.1 us)
Async XLA Ops:
  0.6 51.9 %copy-start = (f32[2,512,128]{2,1,0:T(8,128)S(1)}, f32[2,512,128]{2,1,0:T(8,128)}, u32[]{:S(2)}) copy-start(f32[2,512,128]{2,1,0:T(8,128)} %refs_4_.3) | copy-start | bytes 1572868
  49.4 23.9 %collective-permute-start = (f32[1552,128]{1,0:T(8,128)}, f32[1552,128]{1,0:T(8,128)S(1)}, u32[]{:S(2)}, u32[]{:S(2)}) collective-permute-start(f32[1552,128]{1,0:T(8,128)} %get-tuple-element.11), channel_id=1, source_target_pairs={{0,1},{1,2},{2,3},{3,0},{4,5},{5,6},{6,7},{7,4},{8,9},{9,10},{10,1... | collective-permute-start | bytes 2383880 | tf_op jit(solution)/shard_map/ppermute | solution.py:142
  52.5 10.2 %copy-start.4 = (f32[512,128]{1,0:T(8,128)S(1)}, f32[512,128]{1,0:T(8,128)}, u32[]{:S(2)}) copy-start(f32[512,128]{1,0:T(8,128)} %get-tuple-element.13) | copy-start | bytes 786436
  52.5 20.9 %copy-start.3 = (f32[1040,128]{1,0:T(8,128)S(1)}, f32[1040,128]{1,0:T(8,128)}, u32[]{:S(2)}) copy-start(f32[1040,128]{1,0:T(8,128)} %get-tuple-element.15) | copy-start | bytes 1597444
  52.7 4.0 %collective-permute-start.2 = (f32[8,128]{1,0:T(8,128)S(1)}, f32[8,128]{1,0:T(8,128)S(1)}, u32[]{:S(2)}, u32[]{:S(2)}) collective-permute-start(f32[8,128]{1,0:T(8,128)S(1)} %shard_map.59), channel_id=1, source_target_pairs={{0,4},{4,8},{8,12},{12,16},{16,20},{20,24},{24,28},{28,0},{1,5},{5... | collective-permute-start | bytes 12296 | tf_op jit(solution)/shard_map/ppermute | solution.py:172
  56.7 4.5 %collective-permute-start.3 = (f32[8,128]{1,0:T(8,128)S(1)}, f32[8,128]{1,0:T(8,128)S(1)}, u32[]{:S(2)}, u32[]{:S(2)}) collective-permute-start(f32[8,128]{1,0:T(8,128)S(1)} %max.18), channel_id=1, source_target_pairs={{0,8},{4,12},{8,16},{12,20},{16,24},{20,28},{24,0},{28,4},{1,9},{5... | collective-permute-start | bytes 12296 | tf_op jit(solution)/shard_map/ppermute | solution.py:172
  61.2 3.8 %collective-permute-start.4 = (f32[8,128]{1,0:T(8,128)S(1)}, f32[8,128]{1,0:T(8,128)S(1)}, u32[]{:S(2)}, u32[]{:S(2)}) collective-permute-start(f32[8,128]{1,0:T(8,128)S(1)} %max.19), channel_id=1, source_target_pairs={{0,16},{4,20},{8,24},{12,28},{16,0},{20,4},{24,8},{28,12},{1,17},{... | collective-permute-start | bytes 12296 | tf_op jit(solution)/shard_map/ppermute | solution.py:172
  62.7 16.5 %collective-permute-start.6 = (f32[512,128]{1,0:T(8,128)S(1)}, f32[512,128]{1,0:T(8,128)S(1)}, u32[]{:S(2)}, u32[]{:S(2)}) collective-permute-start(f32[512,128]{1,0:T(8,128)S(1)} %copy-done.4), channel_id=1, source_target_pairs={{0,3},{1,0},{2,1},{3,2},{4,7},{5,4},{6,5},{7,6},{8,11},{9,8},{10,9... | collective-permute-start | bytes 786440 | tf_op jit(solution)/shard_map/ppermute | solution.py:142
  73.4 12.8 %collective-permute-start.5 = (f32[512,128]{1,0:T(8,128)S(1)}, f32[512,128]{1,0:T(8,128)S(1)}, u32[]{:S(2)}, u32[]{:S(2)}) collective-permute-start(f32[512,128]{1,0:T(8,128)S(1)} %slice.9), channel_id=1, source_target_pairs={{0,1},{1,2},{2,3},{3,0},{4,5},{5,6},{6,7},{7,4},{8,9},{9,10},{10,1... | collective-permute-start | bytes 786440 | tf_op jit(solution)/shard_map/ppermute | solution.py:142
  73.4 12.7 %copy-start.1 = (f32[2,512,128]{2,1,0:T(8,128)S(1)}, f32[2,512,128]{2,1,0:T(8,128)}, u32[]{:S(2)}) copy-start(f32[2,512,128]{2,1,0:T(8,128)} %up_ref.3) | copy-start | bytes 1572868
  73.5 12.7 %copy-start.2 = (f32[2,512,128]{2,1,0:T(8,128)S(1)}, f32[2,512,128]{2,1,0:T(8,128)}, u32[]{:S(2)}) copy-start(f32[2,512,128]{2,1,0:T(8,128)} %down_ref.3) | copy-start | bytes 1572868
  73.5 36.4 %collective-permute-start.8 = (f32[1040,128]{1,0:T(8,128)S(1)}, f32[1040,128]{1,0:T(8,128)S(1)}, u32[]{:S(2)}, u32[]{:S(2)}) collective-permute-start(f32[1040,128]{1,0:T(8,128)S(1)} %copy-done.3), channel_id=1, source_target_pairs={{0,3},{1,0},{2,1},{3,2},{4,7},{5,4},{6,5},{7,6},{8,11},{9,8},{10,9... | collective-permute-start | bytes 1597448 | tf_op jit(solution)/shard_map/ppermute | solution.py:142
  79.1 31.9 %collective-permute-start.1 = (f32[1040,128]{1,0:T(8,128)S(1)}, f32[1040,128]{1,0:T(8,128)S(1)}, u32[]{:S(2)}, u32[]{:S(2)}) collective-permute-start(f32[1040,128]{1,0:T(8,128)S(1)} %slice.8), channel_id=1, source_target_pairs={{0,1},{1,2},{2,3},{3,0},{4,5},{5,6},{6,7},{7,4},{8,9},{9,10},{10,1... | collective-permute-start | bytes 1597448 | tf_op jit(solution)/shard_map/ppermute | solution.py:142
  88.6 21.3 %collective-permute-start.7 = (f32[512,256]{1,0:T(8,128)S(1)}, f32[512,256]{1,0:T(8,128)S(1)}, u32[]{:S(2)}, u32[]{:S(2)}) collective-permute-start(f32[512,256]{1,0:T(8,128)S(1)} %shard_map.60.refs_2_.refs_1_), channel_id=1, source_target_pairs={{0,4},{4,8},{8,12},{12,16},{16,20},{20,24},{24,28},{1,5},{5,9},{9,... | collective-permute-start | bytes 1572872 | tf_op jit(solution)/shard_map/ppermute | solution.py:211
  89.9 14.3 %collective-permute-start.10 = (f32[8,128]{1,0:T(8,128)S(1)}, f32[8,128]{1,0:T(8,128)S(1)}, u32[]{:S(2)}, u32[]{:S(2)}) collective-permute-start(f32[8,128]{1,0:T(8,128)S(1)} %max.20), channel_id=1, source_target_pairs={{0,2},{1,3},{2,0},{3,1},{4,6},{5,7},{6,4},{7,5},{8,10},{9,11},{10,... | collective-permute-start | bytes 12296 | tf_op jit(solution)/shard_map/ppermute | solution.py:142
  102.3 5.1 %collective-permute-start.11 = (f32[8,128]{1,0:T(8,128)S(1)}, f32[8,128]{1,0:T(8,128)S(1)}, u32[]{:S(2)}, u32[]{:S(2)}) collective-permute-start(f32[8,128]{1,0:T(8,128)S(1)} %max.20), channel_id=1, source_target_pairs={{0,3},{1,0},{2,1},{3,2},{4,7},{5,4},{6,5},{7,6},{8,11},{9,8},{10,9... | collective-permute-start | bytes 12296 | tf_op jit(solution)/shard_map/ppermute | solution.py:142
  104.2 5.7 %collective-permute-start.9 = (f32[8,128]{1,0:T(8,128)S(1)}, f32[8,128]{1,0:T(8,128)S(1)}, u32[]{:S(2)}, u32[]{:S(2)}) collective-permute-start(f32[8,128]{1,0:T(8,128)S(1)} %max.20), channel_id=1, source_target_pairs={{0,1},{1,2},{2,3},{3,0},{4,5},{5,6},{6,7},{7,4},{8,9},{9,10},{10,1... | collective-permute-start | bytes 12296 | tf_op jit(solution)/shard_map/ppermute | solution.py:142

commit v6 on v5

v6 whole, which is shorter than its diff:
```python
import functools

import jax
import jax.numpy as jnp
from jax import lax
from jax.experimental import pallas as pl
from jax.experimental.pallas import tpu as pltpu
from jax.sharding import PartitionSpec as P

SWEEPS = 2
PEAK_ROWS = 8
PAD_ROWS = 16
F32 = jnp.float32
BF16 = jnp.bfloat16
VMEM = pl.BlockSpec(memory_space=pltpu.VMEM)
ANY = pl.BlockSpec(memory_space=pl.ANY)
SMEM = pl.BlockSpec(memory_space=pltpu.SMEM)


def ring_offsets(shards):
    return [0, *[-d for d in range(1, shards // 2 + 1)], *range(1, (shards - 1) // 2 + 1)]


def split(x):
    high = x.astype(BF16)
    return high, (x - high.astype(F32)).astype(BF16)


def exact_dot(left, right):
    (left_high, left_low), (right_high, right_low) = left, right
    dot = lambda a, b: jnp.dot(a, b, preferred_element_type=F32)
    return dot(left_high, right_high) + (dot(left_high, right_low) + dot(left_low, right_high))


def on_diagonal(rows, cols):
    row = lax.broadcasted_iota(jnp.int32, (rows, cols), 0)
    return row == lax.broadcasted_iota(jnp.int32, (rows, cols), 1)


def prepare_kernel(own_row, up_ref, level_ref, down_ref, sent_ref, peak_ref, square, sems):
    _, phases, cols = level_ref.shape
    own = pl.ds(pl.multiple_of(own_row[0], cols), cols)
    sources = [level_ref.at[:, own, :], level_ref.at[1], up_ref.at[0], down_ref.at[0]]
    targets = [square, *[sent_ref.at[pl.ds(part * phases, phases), :] for part in range(3)]]
    copies = [
        pltpu.make_async_copy(source, target, sems.at[at])
        for at, (source, target) in enumerate(zip(sources, targets))
    ]
    for copy in copies:
        copy.start()
    copies[0].wait()
    lowest = jnp.min(jnp.where(on_diagonal(cols, cols)[None], square[...], 0.0))
    peak_ref[...] = jnp.full(peak_ref.shape, -lowest, F32)
    for copy in copies[1:]:
        copy.wait()


def with_peak_kernel(rows, block_row, peak_row, block_ref, peak_ref, out_ref):
    out_ref[pl.ds(0, rows), :] = block_ref[pl.ds(block_row, rows), :]
    for at in range(rows, out_ref.shape[0], PEAK_ROWS):
        out_ref[pl.ds(at, PEAK_ROWS), :] = peak_ref[pl.ds(peak_row, PEAK_ROWS), :]


def owner_row(own_row, offset, cols, shards):
    return pl.multiple_of(lax.rem(own_row[0] + (offset + shards) * cols, shards * cols), cols)


def solve_kernel(own_row, *refs):
    shards = len(refs) - 8
    blocks = [refs[0].at[0], *refs[1:shards]]
    up_ref, down_ref, solved_ref, inverse, high, low, s_high, s_low = refs[shards:]
    phases, cols = inverse.shape
    diagonal = on_diagonal(cols, cols)
    for slot, (offset, block) in enumerate(zip(ring_offsets(shards), blocks)):
        rows = pl.ds(owner_row(own_row, offset, cols, shards), cols)
        slot_cols = pl.ds(slot * cols, cols)
        high[:, slot_cols], low[:, slot_cols] = split(block[pl.ds(0, phases), :])
        square = block[rows, :]
        rate = -jnp.sum(jnp.where(diagonal, square, 0.0), axis=1, keepdims=True)
        inverse[rows, :] = jnp.broadcast_to(1.0 / rate, (cols, cols))
        high[rows, slot_cols], low[rows, slot_cols] = split(jnp.where(diagonal, 0.0, square))
    for side, ref in enumerate((up_ref, down_ref)):
        solved_ref[:, pl.ds(side * cols, cols)] = ref[0] * inverse[...]
    for _ in range(SWEEPS):
        for slot, offset in enumerate(ring_offsets(shards)):
            rows = pl.ds(owner_row(own_row, offset, cols, shards), cols)
            slot_rows = pl.ds(slot * cols, cols)
            s_high[slot_rows, :], s_low[slot_rows, :] = split(solved_ref[rows, :])
        product = exact_dot((high[...], low[...]), (s_high[...], s_low[...]))
        for side, ref in enumerate((up_ref, down_ref)):
            columns = slice(side * cols, (side + 1) * cols)
            solved_ref[:, columns] = (ref[0] + product[:, columns]) * inverse[...]


def gathered_product(own_row, blocks, offsets, shards, solved_ref):
    phases, cols = solved_ref.shape[0], blocks[0].shape[-1]
    left = split(jnp.concatenate([block[...] for block in blocks], axis=1))
    rows = [pl.ds(owner_row(own_row, offset, cols, shards), cols) for offset in offsets]
    right = split(jnp.concatenate([solved_ref[r, :] for r in rows], axis=0))
    return exact_dot(left, right)


def largest(peak, blocks, row):
    for block in blocks:
        peak = jnp.maximum(peak, block[pl.ds(row, PEAK_ROWS), :])
    return peak


def partial_kernel(shards, own_row, up_ref, down_ref, peak_ref, *refs):
    *blocks, solved_ref, below_ref, level_ref, part_level, part_up, part_down, part_peak = refs
    phases, cols = part_up.shape
    offsets = [offset for offset in ring_offsets(shards) if offset != -(shards // 2)]
    levels, evens = blocks[: shards // 2 - 1], blocks[shards // 2 - 1 :]
    peak = largest(peak_ref[...], levels, phases)
    part_peak[...] = largest(peak, evens[1:], 2 * phases)
    first_rows = [phases if offset == -1 else 0 for offset in offsets[1:]]
    ups = [ref.at[pl.ds(first, phases), :] for first, ref in zip(first_rows, evens)]
    downs = [ref.at[pl.ds(first + phases, phases), :] for first, ref in zip(first_rows, evens)]
    upper = gathered_product(own_row, [up_ref.at[0], *ups], offsets, shards, solved_ref)
    part_up[...] = upper[:, :cols]
    lower = gathered_product(own_row, [down_ref.at[0], *downs], offsets, shards, below_ref)
    part_down[...] = lower[:, cols:]
    part_level[...] = level_ref[0] + upper[:, cols:] + lower[:, :cols]


def output_kernel(shards, own_row, *refs):
    block, solved_ref, below_ref, part_level, part_up, part_down, part_peak, new_level, new_up, new_down = refs
    phases, cols = part_up.shape
    offsets = [-(shards // 2)]
    scale = 1.0 / largest(part_peak[...], [block], 2 * phases)[0:1, :]
    up, down = block.at[pl.ds(0, phases), :], block.at[pl.ds(phases, phases), :]
    upper = gathered_product(own_row, [up], offsets, shards, solved_ref)
    new_up[0] = (part_up[...] + upper[:, :cols]) * scale
    lower = gathered_product(own_row, [down], offsets, shards, below_ref)
    new_down[0] = (part_down[...] + lower[:, cols:]) * scale
    new_level[0] = (part_level[...] + upper[:, cols:] + lower[:, :cols]) * scale


def per_device(up_blocks, level_blocks, down_blocks):
    levels, phases, cols = level_blocks.shape
    shards = lax.axis_size("col")
    ranges = lax.axis_size("lvl")
    assert levels == 2 and shards >= 4
    own_row = (lax.axis_index("col") * cols).astype(jnp.int32).reshape(1)
    params = pltpu.CompilerParams(vmem_limit_bytes=32 * 2**20)
    shape = lambda *dims, kind=F32: jax.ShapeDtypeStruct(dims, kind)
    block = shape(phases, cols)

    def shifted(part, distance):
        return lax.ppermute(part, "col", [(i, (i + distance) % shards) for i in range(shards)])

    def one_level(parity):
        return pl.BlockSpec((1, phases, cols), lambda step: (parity, 0, 0))

    odd, even = one_level(1), one_level(0)
    sent, peak = pl.pallas_call(
        prepare_kernel,
        out_shape=(shape(3 * phases, cols), shape(PEAK_ROWS, cols)),
        in_specs=[SMEM] + [ANY] * 3,
        out_specs=(VMEM, VMEM),
        scratch_shapes=[pltpu.VMEM((levels, cols, cols), F32), pltpu.SemaphoreType.DMA((4,))],
        grid=(1,),
        compiler_params=params,
    )(own_row, *[pltpu.with_memory_space_constraint(x, pltpu.HBM) for x in (up_blocks, level_blocks, down_blocks)])

    first = shifted(sent, 1)
    reach = 1
    while reach < ranges:
        route = [(i, (i + reach) % ranges) for i in range(ranges)]
        peak = jnp.maximum(peak, lax.ppermute(peak, "lvl", route))
        reach *= 2

    def with_peak(rows, extra, part, block_row, rates, peak_row):
        return pl.pallas_call(
            functools.partial(with_peak_kernel, rows, block_row, peak_row),
            out_shape=shape(rows + extra, cols),
            in_specs=[VMEM, VMEM],
            out_specs=VMEM,
            grid=(1,),
            compiler_params=params,
        )(part, rates)

    level_parts = {-1: first}
    even_parts = {-1: first}
    rates, peak_row = peak, 0
    for reached in range(1, shards // 2):
        part = with_peak(phases, PEAK_ROWS, level_parts[-reached], 0, rates, peak_row)
        rates = level_parts[-reached - 1] = shifted(part, 1)
        peak_row = phases
    level_parts[1] = shifted(sent[: phases + 2 * PAD_ROWS], -1)
    even_now = lax.optimization_barrier((sent, first))[0]
    even_parts[1] = shifted(with_peak(2 * phases, PAD_ROWS, even_now, phases, peak, 0), -1)
    for reached in range(1, (shards - 1) // 2):
        level_parts[reached + 1] = shifted(level_parts[reached], -1)
        even_parts[reached + 1] = shifted(even_parts[reached], -1)
    for reached in range(1, shards // 2):
        block_row = phases if reached == 1 else 0
        part = with_peak(2 * phases, PAD_ROWS, even_parts[-reached], block_row, rates, peak_row)
        even_parts[-reached - 1] = shifted(part, 1)

    offsets = ring_offsets(shards)[1:]
    solved = pl.pallas_call(
        solve_kernel,
        out_shape=shape(phases, 2 * cols),
        in_specs=[SMEM, odd, *[VMEM] * (shards - 1), odd, odd],
        out_specs=VMEM,
        scratch_shapes=[
            pltpu.VMEM((phases, cols), F32),
            pltpu.VMEM((phases, phases), BF16),
            pltpu.VMEM((phases, phases), BF16),
            pltpu.VMEM((phases, 2 * cols), BF16),
            pltpu.VMEM((phases, 2 * cols), BF16),
        ],
        grid=(1,),
        compiler_params=params,
    )(own_row, level_blocks, *[level_parts[offset] for offset in offsets], up_blocks, down_blocks)
    from_below = lax.ppermute(solved, "lvl", [(i, i + 1) for i in range(ranges - 1)])

    last = -(shards // 2)
    early = [level_parts[offset] for offset in offsets if offset < -1]
    early += [even_parts[offset] for offset in offsets if offset != last]
    parts = pl.pallas_call(
        functools.partial(partial_kernel, shards),
        out_shape=(block, block, block, shape(PEAK_ROWS, cols)),
        in_specs=[SMEM, even, even, *[VMEM] * (len(early) + 3), even],
        out_specs=(VMEM,) * 4,
        grid=(1,),
        compiler_params=params,
        cost_estimate=pl.CostEstimate(flops=0, bytes_accessed=0, transcendentals=0),
    )(own_row, up_blocks, down_blocks, peak, *early, solved, from_below, level_blocks)
    return pl.pallas_call(
        functools.partial(output_kernel, shards),
        out_shape=(shape(1, phases, cols),) * 3,
        in_specs=[SMEM, *[VMEM] * 7],
        out_specs=(VMEM,) * 3,
        grid=(1,),
        compiler_params=params,
    )(own_row, even_parts[last], solved, from_below, *parts)


def solution(mesh):
    placed = (P("lvl", None, "col"),) * 3
    return jax.shard_map(per_device, mesh=mesh, in_specs=placed, out_specs=placed, check_vma=False)
```

time: 113 us -> 62.6 us (0.55)
  the two profiles are of different devices: /device:TPU:0 before, /device:TPU:20 now
where the time goes in v6:
time: 62.6 us; the launch traced here: 62.4 us
  waiting for transfers between devices  45.9 us (73%)
  starting transfers between devices  9.47 us (15%)
  Pallas kernels  6.2 us (10%)
  between operations  0.74 us (1%)
    ppermute x5, waiting for transfers between devices, shifted(): lax.ppermute(part, 'col', [(i, (i + distance) % shards) for i in range(sh...  26.1 us
    ppermute x3, waiting for transfers between devices, per_device(): peak = jnp.maximum(peak, lax.ppermute(peak, 'lvl', route))  10.4 us
    ppermute x1, waiting for transfers between devices, per_device(): lax.ppermute(solved, 'lvl', [(i, i + 1) for i in range(ranges - 1)])  9.46 us
    ppermute x5, starting transfers between devices, shifted(): lax.ppermute(part, 'col', [(i, (i + distance) % shards) for i in range(sh...  6.45 us
    pallas_call x1, Pallas kernels, per_device(): pl.pallas_call(solve_kernel, out_shape=shape(phases, 2 * cols), in_specs=...  2.39 us
    ppermute x1, starting transfers between devices, per_device(): lax.ppermute(solved, 'lvl', [(i, i + 1) for i in range(ranges - 1)])  1.92 us
    pallas_call x1, Pallas kernels, per_device(): pl.pallas_call(functools.partial(output_kernel, shards), out_shape=(shape...  1.46 us
  transfers between devices with their start and end apart: 9, of which 6 were waited for; matrix products, arithmetic and copies ran while one was open for 0% of the time, Pallas kernels for 6%

profile of v6, /device:TPU:20, one launch (start us, length us, event | category | flops | bytes accessed | tf_op | source)
XLA Modules:
  0.0 62.4 jit_solution(17509186879552082753)
XLA Ops:
  0.6 1.2 %shard_map.58 = (f32[1536,128]{1,0:T(8,128)S(1)}, f32[8,128]{1,0:T(8,128)S(1)}) custom-call(s32[1]{0:T(128)} %bitcast.own_row, f32[2,512,128]{2,1,0:T(8,128)} %up_ref.3, f32[2,512,128]{2,1,0:T(8,128)} %refs_5_.3, f32[2,512,128]{2,1,0:T(8,128)} %down_ref.3), custom_call_target="tpu_custom_call" | custom-call | tf_op jit(solution)/shard_map/pallas_call | solution.py:156
  1.9 1.6 %collective-permute-start = (f32[1536,128]{1,0:T(8,128)S(1)}, f32[1536,128]{1,0:T(8,128)S(1)}, u32[]{:S(2)}, u32[]{:S(2)}) collective-permute-start(f32[1536,128]{1,0:T(8,128)S(1)} %get-tuple-element.12.block_ref), channel_id=1, source_target_pairs={{0,1},{1,2},{2,3},{3,0},{4,5},{5,6},{6,7},{7,4},{8,9},{9,10},{10,1... | collective-permute-start | bytes 2359304 | tf_op jit(solution)/shard_map/ppermute | solution.py:150
  3.5 0.0 collective-permute-start.1
  3.5 3.9 %collective-permute-done.1 = f32[8,128]{1,0:T(8,128)S(1)} collective-permute-done((f32[8,128]{1,0:T(8,128)S(1)}, f32[8,128]{1,0:T(8,128)S(1)}, u32[]{:S(2)}, u32[]{:S(2)}) %collective-permute-start.1) | collective-permute-done | bytes 4128 | tf_op jit(solution)/shard_map/ppermute | solution.py:170
  7.4 0.6 collective-permute-start.2
  8.0 3.9 %collective-permute-done.2 = f32[8,128]{1,0:T(8,128)S(1)} collective-permute-done((f32[8,128]{1,0:T(8,128)S(1)}, f32[8,128]{1,0:T(8,128)S(1)}, u32[]{:S(2)}, u32[]{:S(2)}) %collective-permute-start.2) | collective-permute-done | bytes 4128 | tf_op jit(solution)/shard_map/ppermute | solution.py:170
  11.9 0.5 collective-permute-start.3
  12.5 0.5 collective-permute-start.6
  13.0 2.6 %collective-permute-done.3 = f32[8,128]{1,0:T(8,128)S(1)} collective-permute-done((f32[8,128]{1,0:T(8,128)S(1)}, f32[8,128]{1,0:T(8,128)S(1)}, u32[]{:S(2)}, u32[]{:S(2)}) %collective-permute-start.3) | collective-permute-done | bytes 4128 | tf_op jit(solution)/shard_map/ppermute | solution.py:170
  15.5 10.5 %collective-permute-done.block_ref.refs_1_ = f32[1536,128]{1,0:T(8,128)S(1)} collective-permute-done((f32[1536,128]{1,0:T(8,128)S(1)}, f32[1536,128]{1,0:T(8,128)S(1)}, u32[]{:S(2)}, u32[]{:S(2)}) %collective-permute-start) | collective-permute-done | bytes 786464 | tf_op jit(solution)/shard_map/ppermute | solution.py:150
  26.1 1.8 %collective-permute-start.4 = (f32[520,128]{1,0:T(8,128)S(1)}, f32[520,128]{1,0:T(8,128)S(1)}, u32[]{:S(2)}, u32[]{:S(2)}) collective-permute-start(f32[520,128]{1,0:T(8,128)S(1)} %shard_map.59), channel_id=1, source_target_pairs={{0,1},{1,2},{2,3},{3,0},{4,5},{5,6},{6,7},{7,4},{8,9},{9,10},{10,1... | collective-permute-start | bytes 798728 | tf_op jit(solution)/shard_map/ppermute | solution.py:150
  27.9 0.0 copy-start
  27.9 0.0 copy-start.1
  27.9 0.0 copy-start.2
  27.9 0.4 collective-permute-start.8
  28.3 15.5 %collective-permute-done.4.peak_ref.refs_2_.refs_0_ = f32[520,128]{1,0:T(8,128)S(1)} collective-permute-done((f32[520,128]{1,0:T(8,128)S(1)}, f32[520,128]{1,0:T(8,128)S(1)}, u32[]{:S(2)}, u32[]{:S(2)}) %collective-permute-start.4) | collective-permute-done | bytes 266272 | tf_op jit(solution)/shard_map/ppermute | solution.py:150
  43.9 2.2 %collective-permute-start.5 = (f32[1040,128]{1,0:T(8,128)S(1)}, f32[1040,128]{1,0:T(8,128)S(1)}, u32[]{:S(2)}, u32[]{:S(2)}) collective-permute-start(f32[1040,128]{1,0:T(8,128)S(1)} %shard_map.60), channel_id=1, source_target_pairs={{0,1},{1,2},{2,3},{3,0},{4,5},{5,6},{6,7},{7,4},{8,9},{9,10},{10,1... | collective-permute-start | bytes 1597448 | tf_op jit(solution)/shard_map/ppermute | solution.py:150
  46.1 0.0 collective-permute-done.6.refs_3_
  46.1 0.0 copy-done
  46.1 0.0 copy-done.1
  46.1 0.0 copy-done.2
  46.1 2.4 %shard_map.61.refs_3_.refs_1_ = f32[512,256]{1,0:T(8,128)S(1)} custom-call(s32[1]{0:T(128)} %bitcast.own_row, f32[2,512,128]{2,1,0:T(8,128)S(1)} %copy-done.1, f32[1536,128]{1,0:T(8,128)S(1)} %collective-permute-done.block_ref.refs_1_, f32[520,128]{1,0:T(8,128)S(1)} %collective-permute-done.4.peak_ref.refs_2_.refs_0_, ...), custom_call_target="tpu_custom_call" | custom-call | tf_op jit(solution)/shard_map/pallas_call | solution.py:202
  48.5 1.9 %collective-permute-start.7 = (f32[512,256]{1,0:T(8,128)S(1)}, f32[512,256]{1,0:T(8,128)S(1)}, u32[]{:S(2)}, u32[]{:S(2)}) collective-permute-start(f32[512,256]{1,0:T(8,128)S(1)} %shard_map.61.refs_3_.refs_1_), channel_id=1, source_target_pairs={{0,4},{4,8},{8,12},{12,16},{16,20},{20,24},{24,28},{1,5},{5,9},{9,... | collective-permute-start | bytes 1572872 | tf_op jit(solution)/shard_map/ppermute | solution.py:217
  50.4 0.0 collective-permute-done.8.refs_2_
  50.4 9.5 %collective-permute-done.7.refs_4_.refs_2_ = f32[512,256]{1,0:T(8,128)S(1)} collective-permute-done((f32[512,256]{1,0:T(8,128)S(1)}, f32[512,256]{1,0:T(8,128)S(1)}, u32[]{:S(2)}, u32[]{:S(2)}) %collective-permute-start.7) | collective-permute-done | bytes 524320 | tf_op jit(solution)/shard_map/ppermute | solution.py:217
  59.9 1.0 %shard_map.63 = (f32[512,128]{1,0:T(8,128)S(1)}, f32[512,128]{1,0:T(8,128)S(1)}, f32[512,128]{1,0:T(8,128)S(1)}, f32[8,128]{1,0:T(8,128)S(1)}) custom-call(s32[1]{0:T(128)} %bitcast.own_row, f32[2,512,128]{2,1,0:T(8,128)S(1)} %copy-done, f32[2,512,128]{2,1,0:T(8,128)S(1)} %copy-done.2, f32[8,128]{1,0:T(8,128)S(1)} %max.11.peak_ref, ...), custom_call_target="tpu_custom_call" | custom-call | tf_op jit(solution)/shard_map/pallas_call | solution.py:222
  60.9 0.0 collective-permute-done.5.refs_0_
  60.9 1.5 %shard_map.64 = (f32[1,512,128]{2,1,0:T(8,128)}, f32[1,512,128]{2,1,0:T(8,128)}, f32[1,512,128]{2,1,0:T(8,128)}) custom-call(s32[1]{0:T(128)} %bitcast.own_row, f32[1040,128]{1,0:T(8,128)S(1)} %collective-permute-done.5.refs_0_, f32[512,256]{1,0:T(8,128)S(1)} %shard_map.61.refs_3_.refs_1_, f32[512,256]{1,0:T(8,128)S(1)} %collective-permute-done.7.refs_4_.refs_2_, ...), custom_call_target="tpu_custom_call" | custom-call | tf_op jit(solution)/shard_map/pallas_call | solution.py:231
  (7 shorter events, 0.1 us)
Async XLA Ops:
  1.9 24.2 %collective-permute-start = (f32[1536,128]{1,0:T(8,128)S(1)}, f32[1536,128]{1,0:T(8,128)S(1)}, u32[]{:S(2)}, u32[]{:S(2)}) collective-permute-start(f32[1536,128]{1,0:T(8,128)S(1)} %get-tuple-element.12.block_ref), channel_id=1, source_target_pairs={{0,1},{1,2},{2,3},{3,0},{4,5},{5,6},{6,7},{7,4},{8,9},{9,10},{10,1... | collective-permute-start | bytes 2359304 | tf_op jit(solution)/shard_map/ppermute | solution.py:150
  3.5 3.9 %collective-permute-start.1 = (f32[8,128]{1,0:T(8,128)S(1)}, f32[8,128]{1,0:T(8,128)S(1)}, u32[]{:S(2)}, u32[]{:S(2)}) collective-permute-start(f32[8,128]{1,0:T(8,128)S(1)} %get-tuple-element.11), channel_id=1, source_target_pairs={{0,4},{4,8},{8,12},{12,16},{16,20},{20,24},{24,28},{28,0},{1,5},{5... | collective-permute-start | bytes 12296 | tf_op jit(solution)/shard_map/ppermute | solution.py:170
  7.4 4.5 %collective-permute-start.2 = (f32[8,128]{1,0:T(8,128)S(1)}, f32[8,128]{1,0:T(8,128)S(1)}, u32[]{:S(2)}, u32[]{:S(2)}) collective-permute-start(f32[8,128]{1,0:T(8,128)S(1)} %max.9), channel_id=1, source_target_pairs={{0,8},{4,12},{8,16},{12,20},{16,24},{20,28},{24,0},{28,4},{1,9},{5... | collective-permute-start | bytes 12296 | tf_op jit(solution)/shard_map/ppermute | solution.py:170
  11.9 3.6 %collective-permute-start.3 = (f32[8,128]{1,0:T(8,128)S(1)}, f32[8,128]{1,0:T(8,128)S(1)}, u32[]{:S(2)}, u32[]{:S(2)}) collective-permute-start(f32[8,128]{1,0:T(8,128)S(1)} %max.10), channel_id=1, source_target_pairs={{0,16},{4,20},{8,24},{12,28},{16,0},{20,4},{24,8},{28,12},{1,17},{... | collective-permute-start | bytes 12296 | tf_op jit(solution)/shard_map/ppermute | solution.py:170
  12.5 33.6 %collective-permute-start.6 = (f32[544,128]{1,0:T(8,128)S(1)}, f32[544,128]{1,0:T(8,128)S(1)}, u32[]{:S(2)}, u32[]{:S(2)}) collective-permute-start(f32[544,128]{1,0:T(8,128)S(1)} %slice.3), channel_id=1, source_target_pairs={{0,3},{1,0},{2,1},{3,2},{4,7},{5,4},{6,5},{7,6},{8,11},{9,8},{10,9... | collective-permute-start | bytes 835592 | tf_op jit(solution)/shard_map/ppermute | solution.py:150
  26.1 17.7 %collective-permute-start.4 = (f32[520,128]{1,0:T(8,128)S(1)}, f32[520,128]{1,0:T(8,128)S(1)}, u32[]{:S(2)}, u32[]{:S(2)}) collective-permute-start(f32[520,128]{1,0:T(8,128)S(1)} %shard_map.59), channel_id=1, source_target_pairs={{0,1},{1,2},{2,3},{3,0},{4,5},{5,6},{6,7},{7,4},{8,9},{9,10},{10,1... | collective-permute-start | bytes 798728 | tf_op jit(solution)/shard_map/ppermute | solution.py:150
  27.9 18.2 %copy-start = (f32[2,512,128]{2,1,0:T(8,128)S(1)}, f32[2,512,128]{2,1,0:T(8,128)}, u32[]{:S(2)}) copy-start(f32[2,512,128]{2,1,0:T(8,128)} %up_ref.3) | copy-start | bytes 1572868
  27.9 18.2 %copy-start.1 = (f32[2,512,128]{2,1,0:T(8,128)S(1)}, f32[2,512,128]{2,1,0:T(8,128)}, u32[]{:S(2)}) copy-start(f32[2,512,128]{2,1,0:T(8,128)} %refs_5_.3) | copy-start | bytes 1572868
  27.9 18.2 %copy-start.2 = (f32[2,512,128]{2,1,0:T(8,128)S(1)}, f32[2,512,128]{2,1,0:T(8,128)}, u32[]{:S(2)}) copy-start(f32[2,512,128]{2,1,0:T(8,128)} %down_ref.3) | copy-start | bytes 1572868
  27.9 22.5 %collective-permute-start.8 = (f32[1040,128]{1,0:T(8,128)S(1)}, f32[1040,128]{1,0:T(8,128)S(1)}, u32[]{:S(2)}, u32[]{:S(2)}) collective-permute-start(f32[1040,128]{1,0:T(8,128)S(1)} %shard_map.62), channel_id=1, source_target_pairs={{0,3},{1,0},{2,1},{3,2},{4,7},{5,4},{6,5},{7,6},{8,11},{9,8},{10,9... | collective-permute-start | bytes 1597448 | tf_op jit(solution)/shard_map/ppermute | solution.py:150
  43.9 17.1 %collective-permute-start.5 = (f32[1040,128]{1,0:T(8,128)S(1)}, f32[1040,128]{1,0:T(8,128)S(1)}, u32[]{:S(2)}, u32[]{:S(2)}) collective-permute-start(f32[1040,128]{1,0:T(8,128)S(1)} %shard_map.60), channel_id=1, source_target_pairs={{0,1},{1,2},{2,3},{3,0},{4,5},{5,6},{6,7},{7,4},{8,9},{9,10},{10,1... | collective-permute-start | bytes 1597448 | tf_op jit(solution)/shard_map/ppermute | solution.py:150
  48.5 11.4 %collective-permute-start.7 = (f32[512,256]{1,0:T(8,128)S(1)}, f32[512,256]{1,0:T(8,128)S(1)}, u32[]{:S(2)}, u32[]{:S(2)}) collective-permute-start(f32[512,256]{1,0:T(8,128)S(1)} %shard_map.61.refs_3_.refs_1_), channel_id=1, source_target_pairs={{0,4},{4,8},{8,12},{12,16},{16,20},{20,24},{24,28},{1,5},{5,9},{9,... | collective-permute-start | bytes 1572872 | tf_op jit(solution)/shard_map/ppermute | solution.py:217

commit v7 on v6

--- a/solution.py
+++ b/solution.py
@@ -187,8 +187,9 @@
         part = with_peak(phases, PEAK_ROWS, level_parts[-reached], 0, rates, peak_row)
         rates = level_parts[-reached - 1] = shifted(part, 1)
         peak_row = phases
-    level_parts[1] = shifted(sent[: phases + 2 * PAD_ROWS], -1)
-    even_now = lax.optimization_barrier((sent, first))[0]
+    level_now = lax.optimization_barrier((sent, peak))[0]
+    level_parts[1] = shifted(level_now[: phases + 2 * PAD_ROWS], -1)
+    even_now = lax.optimization_barrier((sent, level_parts[1]))[0]
     even_parts[1] = shifted(with_peak(2 * phases, PAD_ROWS, even_now, phases, peak, 0), -1)
     for reached in range(1, (shards - 1) // 2):
         level_parts[reached + 1] = shifted(level_parts[reached], -1)

time: 62.6 us -> 62.5 us (level)
  starting transfers between devices: 9.47 us -> 10.5 us
  waiting for transfers between devices: 45.9 us -> 44.9 us
    ppermute x5, waiting for transfers between devices: 26.1 us -> 24.5 us  [shifted(): lax.ppermute(part, 'col', [(i, (i + distance) % shards) for i in range(sh...]
    ppermute x5, starting transfers between devices: 6.45 us -> 7.51 us  [shifted(): lax.ppermute(part, 'col', [(i, (i + distance) % shards) for i in range(sh...]
  transfers between devices with their start and end apart: 9 -> 9, of which waited for: 6 -> 7; matrix products, arithmetic and copies ran while one was open for 0% -> 0% of each run, Pallas kernels for 6% -> 6%
where the time goes in v7:
time: 62.5 us; the launch traced here: 62.4 us
  waiting for transfers between devices  44.9 us (72%)
  starting transfers between devices  10.5 us (17%)
  Pallas kernels  6.19 us (10%)
  between operations  0.73 us (1%)
    ppermute x5, waiting for transfers between devices, shifted(): lax.ppermute(part, 'col', [(i, (i + distance) % shards) for i in range(sh...  24.5 us
    ppermute x3, waiting for transfers between devices, per_device(): peak = jnp.maximum(peak, lax.ppermute(peak, 'lvl', route))  10.9 us
    ppermute x1, waiting for transfers between devices, per_device(): lax.ppermute(solved, 'lvl', [(i, i + 1) for i in range(ranges - 1)])  9.46 us
    ppermute x5, starting transfers between devices, shifted(): lax.ppermute(part, 'col', [(i, (i + distance) % shards) for i in range(sh...  7.51 us
    pallas_call x1, Pallas kernels, per_device(): pl.pallas_call(solve_kernel, out_shape=shape(phases, 2 * cols), in_specs=...  2.39 us
    ppermute x1, starting transfers between devices, per_device(): lax.ppermute(solved, 'lvl', [(i, i + 1) for i in range(ranges - 1)])  1.92 us
    pallas_call x1, Pallas kernels, per_device(): pl.pallas_call(functools.partial(output_kernel, shards), out_shape=(shape...  1.46 us
  transfers between devices with their start and end apart: 9, of which 7 were waited for; matrix products, arithmetic and copies ran while one was open for 0% of the time, Pallas kernels for 6%

profile of v7, /device:TPU:20, one launch (start us, length us, event | category | flops | bytes accessed | tf_op | source)
XLA Modules:
  0.0 62.4 jit_solution(17707275630331692531)
XLA Ops:
  0.6 1.2 %shard_map.58 = (f32[1536,128]{1,0:T(8,128)S(1)}, f32[8,128]{1,0:T(8,128)S(1)}) custom-call(s32[1]{0:T(128)} %bitcast.own_row, f32[2,512,128]{2,1,0:T(8,128)} %up_ref.3, f32[2,512,128]{2,1,0:T(8,128)} %refs_5_.3, f32[2,512,128]{2,1,0:T(8,128)} %down_ref.3), custom_call_target="tpu_custom_call" | custom-call | tf_op jit(solution)/shard_map/pallas_call | solution.py:156
  1.9 1.6 %collective-permute-start = (f32[1536,128]{1,0:T(8,128)S(1)}, f32[1536,128]{1,0:T(8,128)S(1)}, u32[]{:S(2)}, u32[]{:S(2)}) collective-permute-start(f32[1536,128]{1,0:T(8,128)S(1)} %get-tuple-element.14.block_ref), channel_id=1, source_target_pairs={{0,1},{1,2},{2,3},{3,0},{4,5},{5,6},{6,7},{7,4},{8,9},{9,10},{10,1... | collective-permute-start | bytes 2359304 | tf_op jit(solution)/shard_map/ppermute | solution.py:150
  3.5 0.0 collective-permute-start.1
  3.5 3.9 %collective-permute-done.1 = f32[8,128]{1,0:T(8,128)S(1)} collective-permute-done((f32[8,128]{1,0:T(8,128)S(1)}, f32[8,128]{1,0:T(8,128)S(1)}, u32[]{:S(2)}, u32[]{:S(2)}) %collective-permute-start.1) | collective-permute-done | bytes 4128 | tf_op jit(solution)/shard_map/ppermute | solution.py:170
  7.4 0.6 collective-permute-start.2
  8.0 3.9 %collective-permute-done.2 = f32[8,128]{1,0:T(8,128)S(1)} collective-permute-done((f32[8,128]{1,0:T(8,128)S(1)}, f32[8,128]{1,0:T(8,128)S(1)}, u32[]{:S(2)}, u32[]{:S(2)}) %collective-permute-start.2) | collective-permute-done | bytes 4128 | tf_op jit(solution)/shard_map/ppermute | solution.py:170
  11.9 0.5 collective-permute-start.3
  12.4 3.1 %collective-permute-done.3 = f32[8,128]{1,0:T(8,128)S(1)} collective-permute-done((f32[8,128]{1,0:T(8,128)S(1)}, f32[8,128]{1,0:T(8,128)S(1)}, u32[]{:S(2)}, u32[]{:S(2)}) %collective-permute-start.3) | collective-permute-done | bytes 4128 | tf_op jit(solution)/shard_map/ppermute | solution.py:170
  15.6 0.5 collective-permute-start.6
  16.1 10.0 %collective-permute-done.block_ref.refs_1_ = f32[1536,128]{1,0:T(8,128)S(1)} collective-permute-done((f32[1536,128]{1,0:T(8,128)S(1)}, f32[1536,128]{1,0:T(8,128)S(1)}, u32[]{:S(2)}, u32[]{:S(2)}) %collective-permute-start) | collective-permute-done | bytes 786464 | tf_op jit(solution)/shard_map/ppermute | solution.py:150
  26.1 1.8 %collective-permute-start.4 = (f32[520,128]{1,0:T(8,128)S(1)}, f32[520,128]{1,0:T(8,128)S(1)}, u32[]{:S(2)}, u32[]{:S(2)}) collective-permute-start(f32[520,128]{1,0:T(8,128)S(1)} %shard_map.59), channel_id=1, source_target_pairs={{0,1},{1,2},{2,3},{3,0},{4,5},{5,6},{6,7},{7,4},{8,9},{9,10},{10,1... | collective-permute-start | bytes 798728 | tf_op jit(solution)/shard_map/ppermute | solution.py:150
  27.8 0.3 collective-permute-done.6.refs_3_
  28.2 0.0 copy-start
  28.2 0.0 copy-start.1
  28.2 0.0 copy-start.2
  28.2 1.4 %collective-permute-start.8 = (f32[1040,128]{1,0:T(8,128)S(1)}, f32[1040,128]{1,0:T(8,128)S(1)}, u32[]{:S(2)}, u32[]{:S(2)}) collective-permute-start(f32[1040,128]{1,0:T(8,128)S(1)} %shard_map.62), channel_id=1, source_target_pairs={{0,3},{1,0},{2,1},{3,2},{4,7},{5,4},{6,5},{7,6},{8,11},{9,8},{10,9... | collective-permute-start | bytes 1597448 | tf_op jit(solution)/shard_map/ppermute | solution.py:150
  29.6 14.2 %collective-permute-done.4.peak_ref.refs_2_.refs_0_ = f32[520,128]{1,0:T(8,128)S(1)} collective-permute-done((f32[520,128]{1,0:T(8,128)S(1)}, f32[520,128]{1,0:T(8,128)S(1)}, u32[]{:S(2)}, u32[]{:S(2)}) %collective-permute-start.4) | collective-permute-done | bytes 266272 | tf_op jit(solution)/shard_map/ppermute | solution.py:150
  43.9 2.2 %collective-permute-start.5 = (f32[1040,128]{1,0:T(8,128)S(1)}, f32[1040,128]{1,0:T(8,128)S(1)}, u32[]{:S(2)}, u32[]{:S(2)}) collective-permute-start(f32[1040,128]{1,0:T(8,128)S(1)} %shard_map.60), channel_id=1, source_target_pairs={{0,1},{1,2},{2,3},{3,0},{4,5},{5,6},{6,7},{7,4},{8,9},{9,10},{10,1... | collective-permute-start | bytes 1597448 | tf_op jit(solution)/shard_map/ppermute | solution.py:150
  46.1 0.0 copy-done
  46.1 0.0 copy-done.1
  46.1 0.0 copy-done.2
  46.1 2.4 %shard_map.61.refs_3_.refs_1_ = f32[512,256]{1,0:T(8,128)S(1)} custom-call(s32[1]{0:T(128)} %bitcast.own_row, f32[2,512,128]{2,1,0:T(8,128)S(1)} %copy-done.1, f32[1536,128]{1,0:T(8,128)S(1)} %collective-permute-done.block_ref.refs_1_, f32[520,128]{1,0:T(8,128)S(1)} %collective-permute-done.4.peak_ref.refs_2_.refs_0_, ...), custom_call_target="tpu_custom_call" | custom-call | tf_op jit(solution)/shard_map/pallas_call | solution.py:203
  48.5 1.9 %collective-permute-start.7 = (f32[512,256]{1,0:T(8,128)S(1)}, f32[512,256]{1,0:T(8,128)S(1)}, u32[]{:S(2)}, u32[]{:S(2)}) collective-permute-start(f32[512,256]{1,0:T(8,128)S(1)} %shard_map.61.refs_3_.refs_1_), channel_id=1, source_target_pairs={{0,4},{4,8},{8,12},{12,16},{16,20},{20,24},{24,28},{1,5},{5,9},{9,... | collective-permute-start | bytes 1572872 | tf_op jit(solution)/shard_map/ppermute | solution.py:218
  50.4 0.0 collective-permute-done.8.refs_2_
  50.4 9.5 %collective-permute-done.7.refs_4_.refs_2_ = f32[512,256]{1,0:T(8,128)S(1)} collective-permute-done((f32[512,256]{1,0:T(8,128)S(1)}, f32[512,256]{1,0:T(8,128)S(1)}, u32[]{:S(2)}, u32[]{:S(2)}) %collective-permute-start.7) | collective-permute-done | bytes 524320 | tf_op jit(solution)/shard_map/ppermute | solution.py:218
  59.9 1.0 %shard_map.63 = (f32[512,128]{1,0:T(8,128)S(1)}, f32[512,128]{1,0:T(8,128)S(1)}, f32[512,128]{1,0:T(8,128)S(1)}, f32[8,128]{1,0:T(8,128)S(1)}) custom-call(s32[1]{0:T(128)} %bitcast.own_row, f32[2,512,128]{2,1,0:T(8,128)S(1)} %copy-done, f32[2,512,128]{2,1,0:T(8,128)S(1)} %copy-done.2, f32[8,128]{1,0:T(8,128)S(1)} %max.11.peak_ref, ...), custom_call_target="tpu_custom_call" | custom-call | tf_op jit(solution)/shard_map/pallas_call | solution.py:223
  60.9 0.0 collective-permute-done.5.refs_0_
  60.9 1.5 %shard_map.64 = (f32[1,512,128]{2,1,0:T(8,128)}, f32[1,512,128]{2,1,0:T(8,128)}, f32[1,512,128]{2,1,0:T(8,128)}) custom-call(s32[1]{0:T(128)} %bitcast.own_row, f32[1040,128]{1,0:T(8,128)S(1)} %collective-permute-done.5.refs_0_, f32[512,256]{1,0:T(8,128)S(1)} %shard_map.61.refs_3_.refs_1_, f32[512,256]{1,0:T(8,128)S(1)} %collective-permute-done.7.refs_4_.refs_2_, ...), custom_call_target="tpu_custom_call" | custom-call | tf_op jit(solution)/shard_map/pallas_call | solution.py:232
  (7 shorter events, 0.1 us)
Async XLA Ops:
  1.9 24.2 %collective-permute-start = (f32[1536,128]{1,0:T(8,128)S(1)}, f32[1536,128]{1,0:T(8,128)S(1)}, u32[]{:S(2)}, u32[]{:S(2)}) collective-permute-start(f32[1536,128]{1,0:T(8,128)S(1)} %get-tuple-element.14.block_ref), channel_id=1, source_target_pairs={{0,1},{1,2},{2,3},{3,0},{4,5},{5,6},{6,7},{7,4},{8,9},{9,10},{10,1... | collective-permute-start | bytes 2359304 | tf_op jit(solution)/shard_map/ppermute | solution.py:150
  3.5 3.9 %collective-permute-start.1 = (f32[8,128]{1,0:T(8,128)S(1)}, f32[8,128]{1,0:T(8,128)S(1)}, u32[]{:S(2)}, u32[]{:S(2)}) collective-permute-start(f32[8,128]{1,0:T(8,128)S(1)} %get-tuple-element.12), channel_id=1, source_target_pairs={{0,4},{4,8},{8,12},{12,16},{16,20},{20,24},{24,28},{28,0},{1,5},{5... | collective-permute-start | bytes 12296 | tf_op jit(solution)/shard_map/ppermute | solution.py:170
  7.4 4.5 %collective-permute-start.2 = (f32[8,128]{1,0:T(8,128)S(1)}, f32[8,128]{1,0:T(8,128)S(1)}, u32[]{:S(2)}, u32[]{:S(2)}) collective-permute-start(f32[8,128]{1,0:T(8,128)S(1)} %max.9), channel_id=1, source_target_pairs={{0,8},{4,12},{8,16},{12,20},{16,24},{20,28},{24,0},{28,4},{1,9},{5... | collective-permute-start | bytes 12296 | tf_op jit(solution)/shard_map/ppermute | solution.py:170
  11.9 3.6 %collective-permute-start.3 = (f32[8,128]{1,0:T(8,128)S(1)}, f32[8,128]{1,0:T(8,128)S(1)}, u32[]{:S(2)}, u32[]{:S(2)}) collective-permute-start(f32[8,128]{1,0:T(8,128)S(1)} %max.10), channel_id=1, source_target_pairs={{0,16},{4,20},{8,24},{12,28},{16,0},{20,4},{24,8},{28,12},{1,17},{... | collective-permute-start | bytes 12296 | tf_op jit(solution)/shard_map/ppermute | solution.py:170
  15.6 12.5 %collective-permute-start.6 = (f32[544,128]{1,0:T(8,128)S(1)}, f32[544,128]{1,0:T(8,128)S(1)}, u32[]{:S(2)}, u32[]{:S(2)}) collective-permute-start(f32[544,128]{1,0:T(8,128)S(1)} %slice.3), channel_id=1, source_target_pairs={{0,3},{1,0},{2,1},{3,2},{4,7},{5,4},{6,5},{7,6},{8,11},{9,8},{10,9... | collective-permute-start | bytes 835592 | tf_op jit(solution)/shard_map/ppermute | solution.py:150
  26.1 17.7 %collective-permute-start.4 = (f32[520,128]{1,0:T(8,128)S(1)}, f32[520,128]{1,0:T(8,128)S(1)}, u32[]{:S(2)}, u32[]{:S(2)}) collective-permute-start(f32[520,128]{1,0:T(8,128)S(1)} %shard_map.59), channel_id=1, source_target_pairs={{0,1},{1,2},{2,3},{3,0},{4,5},{5,6},{6,7},{7,4},{8,9},{9,10},{10,1... | collective-permute-start | bytes 798728 | tf_op jit(solution)/shard_map/ppermute | solution.py:150
  28.2 17.9 %copy-start = (f32[2,512,128]{2,1,0:T(8,128)S(1)}, f32[2,512,128]{2,1,0:T(8,128)}, u32[]{:S(2)}) copy-start(f32[2,512,128]{2,1,0:T(8,128)} %up_ref.3) | copy-start | bytes 1572868
  28.2 17.9 %copy-start.1 = (f32[2,512,128]{2,1,0:T(8,128)S(1)}, f32[2,512,128]{2,1,0:T(8,128)}, u32[]{:S(2)}) copy-start(f32[2,512,128]{2,1,0:T(8,128)} %refs_5_.3) | copy-start | bytes 1572868
  28.2 17.9 %copy-start.2 = (f32[2,512,128]{2,1,0:T(8,128)S(1)}, f32[2,512,128]{2,1,0:T(8,128)}, u32[]{:S(2)}) copy-start(f32[2,512,128]{2,1,0:T(8,128)} %down_ref.3) | copy-start | bytes 1572868
  28.2 22.2 %collective-permute-start.8 = (f32[1040,128]{1,0:T(8,128)S(1)}, f32[1040,128]{1,0:T(8,128)S(1)}, u32[]{:S(2)}, u32[]{:S(2)}) collective-permute-start(f32[1040,128]{1,0:T(8,128)S(1)} %shard_map.62), channel_id=1, source_target_pairs={{0,3},{1,0},{2,1},{3,2},{4,7},{5,4},{6,5},{7,6},{8,11},{9,8},{10,9... | collective-permute-start | bytes 1597448 | tf_op jit(solution)/shard_map/ppermute | solution.py:150
  43.9 17.0 %collective-permute-start.5 = (f32[1040,128]{1,0:T(8,128)S(1)}, f32[1040,128]{1,0:T(8,128)S(1)}, u32[]{:S(2)}, u32[]{:S(2)}) collective-permute-start(f32[1040,128]{1,0:T(8,128)S(1)} %shard_map.60), channel_id=1, source_target_pairs={{0,1},{1,2},{2,3},{3,0},{4,5},{5,6},{6,7},{7,4},{8,9},{9,10},{10,1... | collective-permute-start | bytes 1597448 | tf_op jit(solution)/shard_map/ppermute | solution.py:150
  48.5 11.4 %collective-permute-start.7 = (f32[512,256]{1,0:T(8,128)S(1)}, f32[512,256]{1,0:T(8,128)S(1)}, u32[]{:S(2)}, u32[]{:S(2)}) collective-permute-start(f32[512,256]{1,0:T(8,128)S(1)} %shard_map.61.refs_3_.refs_1_), channel_id=1, source_target_pairs={{0,4},{4,8},{8,12},{12,16},{16,20},{20,24},{24,28},{1,5},{5,9},{9,... | collective-permute-start | bytes 1572872 | tf_op jit(solution)/shard_map/ppermute | solution.py:218

commit v8 on v6

v8 whole, which is shorter than its diff:
```python
import functools

import jax
import jax.numpy as jnp
from jax import lax
from jax.experimental import pallas as pl
from jax.experimental.pallas import tpu as pltpu
from jax.sharding import PartitionSpec as P

SWEEPS = 2
PEAK_ROWS = 8
F32 = jnp.float32
BF16 = jnp.bfloat16
VMEM = pl.BlockSpec(memory_space=pltpu.VMEM)
ANY = pl.BlockSpec(memory_space=pl.ANY)
SMEM = pl.BlockSpec(memory_space=pltpu.SMEM)


def split(x):
    high = x.astype(BF16)
    return high, (x - high.astype(F32)).astype(BF16)


def exact_dot(left, right):
    (left_high, left_low), (right_high, right_low) = left, right
    dot = lambda a, b: jnp.dot(a, b, preferred_element_type=F32)
    return dot(left_high, right_high) + (dot(left_high, right_low) + dot(left_low, right_high))


def on_diagonal(rows, cols):
    row = lax.broadcasted_iota(jnp.int32, (rows, cols), 0)
    return row == lax.broadcasted_iota(jnp.int32, (rows, cols), 1)


def prepare_kernel(place, up_ref, level_ref, down_ref, first_ref, down_out_ref, peak_ref, square, sems):
    _, phases, cols = level_ref.shape
    own = pl.ds(pl.multiple_of(place[0] * cols, cols), cols)
    sources = [level_ref.at[:, own, :], level_ref.at[1], up_ref.at[0], down_ref.at[0]]
    targets = [square, first_ref.at[pl.ds(0, phases), :], first_ref.at[pl.ds(phases, phases), :], down_out_ref]
    copies = [
        pltpu.make_async_copy(source, target, sems.at[at])
        for at, (source, target) in enumerate(zip(sources, targets))
    ]
    for copy in copies:
        copy.start()
    copies[0].wait()
    lowest = jnp.min(jnp.where(on_diagonal(cols, cols)[None], square[...], 0.0))
    peak_ref[...] = jnp.full(peak_ref.shape, -lowest, F32)
    for copy in copies[1:]:
        copy.wait()


def stack_kernel(ranges, *refs):
    *parts, out_ref = refs
    at = 0
    for (first, rows), ref in zip(ranges, parts):
        out_ref[pl.ds(at, rows), :] = ref[pl.ds(first, rows), :]
        at += rows


def either_kernel(place, right_ref, left_ref, out_ref):
    out_ref[...] = jnp.where(place[0] >= 2, right_ref[...], left_ref[...])


def rows_of(place, offset, cols, shards):
    owner = lax.rem(place[0] + (offset + shards), shards)
    return pl.ds(pl.multiple_of(owner * cols, cols), cols)


def solve_kernel(shards, place, own_ref, right_ref, left_ref, far_ref, end_ref, up_ref, down_ref, solved_ref, *scratch):
    inverse, high, low, s_high, s_low = scratch
    phases, cols = inverse.shape
    diagonal = on_diagonal(cols, cols)
    offsets = (0, -1, 1, 2)

    def block(slot, rows):
        if slot == 0:
            return own_ref[0, rows, :]
        if slot == 1:
            return jnp.where(place[0] == 0, end_ref[rows, :], right_ref[rows, :])
        if slot == 2:
            return jnp.where(place[0] == shards - 1, end_ref[rows, :], left_ref[rows, :])
        return far_ref[rows, :]

    for slot, offset in enumerate(offsets):
        rows = rows_of(place, offset, cols, shards)
        slot_cols = pl.ds(slot * cols, cols)
        high[:, slot_cols], low[:, slot_cols] = split(block(slot, pl.ds(0, phases)))
        square = block(slot, rows)
        rate = -jnp.sum(jnp.where(diagonal, square, 0.0), axis=1, keepdims=True)
        inverse[rows, :] = jnp.broadcast_to(1.0 / rate, (cols, cols))
        high[rows, slot_cols], low[rows, slot_cols] = split(jnp.where(diagonal, 0.0, square))
    for side, ref in enumerate((up_ref, down_ref)):
        solved_ref[:, pl.ds(side * cols, cols)] = ref[0] * inverse[...]
    for _ in range(SWEEPS):
        for slot, offset in enumerate(offsets):
            rows, slot_rows = rows_of(place, offset, cols, shards), pl.ds(slot * cols, cols)
            s_high[slot_rows, :], s_low[slot_rows, :] = split(solved_ref[rows, :])
        product = exact_dot((high[...], low[...]), (s_high[...], s_low[...]))
        for side, ref in enumerate((up_ref, down_ref)):
            columns = slice(side * cols, (side + 1) * cols)
            solved_ref[:, columns] = (ref[0] + product[:, columns]) * inverse[...]


def gathered_product(blocks, rows, solved_ref):
    left = split(jnp.concatenate(blocks, axis=1))
    right = split(jnp.concatenate([solved_ref[r, :] for r in rows], axis=0))
    return exact_dot(left, right)


def partial_kernel(shards, place, up_ref, down_ref, peak_ref, first_right, first_left, down_right, down_left, far_ref, *refs):
    solved_ref, below_ref, level_ref, part_level, part_up, part_down, part_peak = refs
    phases, cols = part_up.shape
    rows = [rows_of(place, offset, cols, shards) for offset in (0, -1, 1, 2)]
    top, middle = pl.ds(0, phases), pl.ds(phases, phases)
    ups = [up_ref[0], first_right[middle, :], first_left[middle, :], far_ref[top, :]]
    downs = [down_ref[0], down_right[top, :], down_left[top, :], far_ref[middle, :]]
    upper = gathered_product(ups, rows, solved_ref)
    part_up[...] = upper[:, :cols]
    lower = gathered_product(downs, rows, below_ref)
    part_down[...] = lower[:, cols:]
    part_level[...] = level_ref[0] + upper[:, cols:] + lower[:, :cols]
    peak = peak_ref[...]
    for ref, row in ((down_right, phases), (down_left, phases), (far_ref, 2 * phases)):
        peak = jnp.maximum(peak, ref[pl.ds(row, PEAK_ROWS), :])
    part_peak[...] = peak


def output_kernel(shards, place, end_ref, solved_ref, below_ref, *refs):
    part_level, part_up, part_down, part_peak, new_level, new_up, new_down = refs
    phases, cols = part_up.shape
    peak = jnp.maximum(part_peak[...], end_ref[pl.ds(2 * phases, PEAK_ROWS), :])
    scale = 1.0 / peak[0:1, :]
    last = pl.multiple_of(jnp.where(place[0] == 0, (shards - 1) * cols, 0), cols)
    rows = [pl.ds(last, cols)]
    upper = gathered_product([end_ref[pl.ds(0, phases), :]], rows, solved_ref)
    new_up[0] = (part_up[...] + upper[:, :cols]) * scale
    lower = gathered_product([end_ref[pl.ds(phases, phases), :]], rows, below_ref)
    new_down[0] = (part_down[...] + lower[:, cols:]) * scale
    new_level[0] = (part_level[...] + upper[:, cols:] + lower[:, :cols]) * scale


def per_device(up_blocks, level_blocks, down_blocks):
    levels, phases, cols = level_blocks.shape
    shards = lax.axis_size("col")
    ranges = lax.axis_size("lvl")
    assert levels == 2 and shards == 4
    place = lax.axis_index("col").astype(jnp.int32).reshape(1)
    params = pltpu.CompilerParams(vmem_limit_bytes=32 * 2**20)
    shape = lambda rows, columns=cols: jax.ShapeDtypeStruct((rows, columns), F32)

    def call(kernel, out_shape, in_specs, *operands, scratch=(), **options):
        out_specs = jax.tree.map(lambda _: VMEM, out_shape)
        return pl.pallas_call(
            kernel,
            out_shape=out_shape,
            in_specs=in_specs,
            out_specs=out_specs,
            scratch_shapes=scratch,
            grid=(1,),
            compiler_params=params,
            **options,
        )(*operands)

    def one_level(parity):
        return pl.BlockSpec((1, phases, cols), lambda step: (parity, 0, 0))

    def to_right(part, step):
        return lax.ppermute(part, "col", [(i, i + 1) for i in range(step - 1, shards - 1)])

    def to_left(part, step):
        return lax.ppermute(part, "col", [(i, i - 1) for i in range(1, shards - step + 1)])

    def to_ends(part):
        return lax.ppermute(part, "col", [(1, 0), (shards - 2, shards - 1)])

    def stack(*pieces):
        ranges_of = [(first, rows) for _, first, rows in pieces]
        kernel = functools.partial(stack_kernel, ranges_of)
        return call(kernel, shape(sum(rows for _, rows in ranges_of)), [VMEM] * len(pieces), *[p[0] for p in pieces])

    def either(right, left):
        return call(either_kernel, shape(right.shape[0]), [SMEM, VMEM, VMEM], place, right, left)

    odd, even = one_level(1), one_level(0)
    in_hbm = [pltpu.with_memory_space_constraint(x, pltpu.HBM) for x in (up_blocks, level_blocks, down_blocks)]
    first, down, peak = call(
        prepare_kernel,
        (shape(2 * phases), shape(phases), shape(PEAK_ROWS)),
        [SMEM] + [ANY] * 3,
        place,
        *in_hbm,
        scratch=[pltpu.VMEM((levels, cols, cols), F32), pltpu.SemaphoreType.DMA((4,))],
    )
    first_right, first_left = to_right(first, 1), to_left(first, 1)
    reach = 1
    while reach < ranges:
        route = [(i, (i + reach) % ranges) for i in range(ranges)]
        peak = jnp.maximum(peak, lax.ppermute(peak, "lvl", route))
        reach *= 2
    down = stack((down, 0, phases), (peak, 0, PEAK_ROWS))
    down_right, down_left = to_right(down, 1), to_left(down, 1)

    level_far = either(to_right(first_right[:phases], 2), to_left(first_left[:phases], 2))
    level_end = to_ends(level_far)
    even_right = stack((first_right, phases, phases), (down_right, 0, phases + PEAK_ROWS))
    even_left = stack((first_left, phases, phases), (down_left, 0, phases + PEAK_ROWS))
    even_far = either(to_right(even_right, 2), to_left(even_left, 2))
    even_end = to_ends(even_far)

    solved = call(
        functools.partial(solve_kernel, shards),
        shape(phases, 2 * cols),
        [SMEM, odd, *[VMEM] * 4, odd, odd],
        place,
        level_blocks,
        first_right,
        first_left,
        level_far,
        level_end,
        up_blocks,
        down_blocks,
        scratch=[
            pltpu.VMEM((phases, cols), F32),
            pltpu.VMEM((phases, phases), BF16),
            pltpu.VMEM((phases, phases), BF16),
            pltpu.VMEM((phases, 2 * cols), BF16),
            pltpu.VMEM((phases, 2 * cols), BF16),
        ],
    )
    from_below = lax.ppermute(solved, "lvl", [(i, i + 1) for i in range(ranges - 1)])

    parts = call(
        functools.partial(partial_kernel, shards),
        (shape(phases),) * 3 + (shape(PEAK_ROWS),),
        [SMEM, even, even, *[VMEM] * 8, even],
        place,
        up_blocks,
        down_blocks,
        peak,
        first_right,
        first_left,
        down_right,
        down_left,
        even_far,
        solved,
        from_below,
        level_blocks,
        cost_estimate=pl.CostEstimate(flops=0, bytes_accessed=0, transcendentals=0),
    )
    return call(
        functools.partial(output_kernel, shards),
        (jax.ShapeDtypeStruct((1, phases, cols), F32),) * 3,
        [SMEM] + [VMEM] * 7,
        place,
        even_end,
        solved,
        from_below,
        *parts,
    )


def solution(mesh):
    placed = (P("lvl", None, "col"),) * 3
    return jax.shard_map(per_device, mesh=mesh, in_specs=placed, out_specs=placed, check_vma=False)
```

time: 62.6 us -> 76.6 us (1.22)
  the two profiles are of different devices: /device:TPU:20 before, /device:TPU:4 now
where the time goes in v8:
time: 76.6 us; the launch traced here: 76.2 us
  waiting for transfers between devices  48.6 us (63%)
  starting transfers between devices  20.4 us (27%)
  Pallas kernels  6.26 us (8%)
  between operations  0.84 us (1%)
    ppermute x4, waiting for transfers between devices, to_left(): lax.ppermute(part, 'col', [(i, i - 1) for i in range(1, shards - step + 1)])  18.2 us
    ppermute x3, waiting for transfers between devices, per_device(): peak = jnp.maximum(peak, lax.ppermute(peak, 'lvl', route))  10.9 us
    ppermute x1, waiting for transfers between devices, per_device(): lax.ppermute(solved, 'lvl', [(i, i + 1) for i in range(ranges - 1)])  9.47 us
    ppermute x4, starting transfers between devices, to_right(): lax.ppermute(part, 'col', [(i, i + 1) for i in range(step - 1, shards - 1)])  9.45 us
    ppermute x2, waiting for transfers between devices, to_ends(): return lax.ppermute(part, 'col', [(1, 0), (shards - 2, shards - 1)])  7.38 us
    pallas_call x9, Pallas kernels, call(): pl.pallas_call(kernel, out_shape=out_shape, in_specs=in_specs, out_specs=...  6.26 us
    ppermute x4, starting transfers between devices, to_left(): lax.ppermute(part, 'col', [(i, i - 1) for i in range(1, shards - step + 1)])  5.17 us
    ppermute x2, starting transfers between devices, to_ends(): return lax.ppermute(part, 'col', [(1, 0), (shards - 2, shards - 1)])  2.72 us
  transfers between devices with their start and end apart: 14, of which 8 were waited for; matrix products, arithmetic and copies ran while one was open for 0% of the time, Pallas kernels for 5%

profile of v8, /device:TPU:4, one launch (start us, length us, event | category | flops | bytes accessed | tf_op | source)
XLA Modules:
  0.0 76.2 jit_solution(13965138296513438895)
XLA Ops:
  0.6 1.2 %shard_map.58 = (f32[1024,128]{1,0:T(8,128)S(1)}, f32[512,128]{1,0:T(8,128)S(1)}, f32[8,128]{1,0:T(8,128)S(1)}) custom-call(s32[1]{0:T(128)} %bitcast.place, f32[2,512,128]{2,1,0:T(8,128)} %up_ref.5, f32[2,512,128]{2,1,0:T(8,128)} %refs_2_.1, f32[2,512,128]{2,1,0:T(8,128)} %down_ref.5), custom_call_target="tpu_custom_call" | custom-call | tf_op jit(solution)/shard_map/pallas_call | solution.py:154
  1.9 3.5 %collective-permute-start = (f32[1024,128]{1,0:T(8,128)S(1)}, f32[1024,128]{1,0:T(8,128)S(1)}, u32[]{:S(2)}, u32[]{:S(2)}) collective-permute-start(f32[1024,128]{1,0:T(8,128)S(1)} %get-tuple-element.10), channel_id=1, source_target_pairs={{0,1},{1,2},{2,3},{4,5},{5,6},{6,7},{8,9},{9,10},{10,11},{12,13},{... | collective-permute-start | bytes 1572872 | tf_op jit(solution)/shard_map/ppermute | solution.py:169
  5.4 1.3 %collective-permute-start.6 = (f32[1024,128]{1,0:T(8,128)S(1)}, f32[1024,128]{1,0:T(8,128)S(1)}, u32[]{:S(2)}, u32[]{:S(2)}) collective-permute-start(f32[1024,128]{1,0:T(8,128)S(1)} %get-tuple-element.10), channel_id=1, source_target_pairs={{1,0},{2,1},{3,2},{5,4},{6,5},{7,6},{9,8},{10,9},{11,10},{13,12},{... | collective-permute-start | bytes 1572872 | tf_op jit(solution)/shard_map/ppermute | solution.py:172
  6.7 0.1 collective-permute-start.1
  6.7 3.9 %collective-permute-done.1 = f32[8,128]{1,0:T(8,128)S(1)} collective-permute-done((f32[8,128]{1,0:T(8,128)S(1)}, f32[8,128]{1,0:T(8,128)S(1)}, u32[]{:S(2)}, u32[]{:S(2)}) %collective-permute-start.1) | collective-permute-done | bytes 4128 | tf_op jit(solution)/shard_map/ppermute | solution.py:199
  10.7 0.6 collective-permute-start.2
  11.3 3.9 %collective-permute-done.2 = f32[8,128]{1,0:T(8,128)S(1)} collective-permute-done((f32[8,128]{1,0:T(8,128)S(1)}, f32[8,128]{1,0:T(8,128)S(1)}, u32[]{:S(2)}, u32[]{:S(2)}) %collective-permute-start.2) | collective-permute-done | bytes 4128 | tf_op jit(solution)/shard_map/ppermute | solution.py:199
  15.2 0.5 collective-permute-start.3
  15.7 3.1 %collective-permute-done.3 = f32[8,128]{1,0:T(8,128)S(1)} collective-permute-done((f32[8,128]{1,0:T(8,128)S(1)}, f32[8,128]{1,0:T(8,128)S(1)}, u32[]{:S(2)}, u32[]{:S(2)}) %collective-permute-start.3) | collective-permute-done | bytes 4128 | tf_op jit(solution)/shard_map/ppermute | solution.py:199
  18.8 4.6 %collective-permute-start.4 = (f32[520,128]{1,0:T(8,128)S(1)}, f32[520,128]{1,0:T(8,128)S(1)}, u32[]{:S(2)}, u32[]{:S(2)}) collective-permute-start(f32[520,128]{1,0:T(8,128)S(1)} %shard_map.59), channel_id=1, source_target_pairs={{0,1},{1,2},{2,3},{4,5},{5,6},{6,7},{8,9},{9,10},{10,11},{12,13},{... | collective-permute-start | bytes 798728 | tf_op jit(solution)/shard_map/ppermute | solution.py:169
  23.4 1.3 %collective-permute-start.7 = (f32[520,128]{1,0:T(8,128)S(1)}, f32[520,128]{1,0:T(8,128)S(1)}, u32[]{:S(2)}, u32[]{:S(2)}) collective-permute-start(f32[520,128]{1,0:T(8,128)S(1)} %shard_map.59), channel_id=1, source_target_pairs={{1,0},{2,1},{3,2},{5,4},{6,5},{7,6},{9,8},{10,9},{11,10},{13,12},{... | collective-permute-start | bytes 798728 | tf_op jit(solution)/shard_map/ppermute | solution.py:172
  24.7 2.6 %collective-permute-done.4.refs_1_.down_right = f32[520,128]{1,0:T(8,128)S(1)} collective-permute-done((f32[520,128]{1,0:T(8,128)S(1)}, f32[520,128]{1,0:T(8,128)S(1)}, u32[]{:S(2)}, u32[]{:S(2)}) %collective-permute-start.4) | collective-permute-done | bytes 266272 | tf_op jit(solution)/shard_map/ppermute | solution.py:169
  27.3 0.0 collective-permute-done.refs_0_.right_ref.first_right
  27.3 0.7 collective-permute-start.5
  28.0 4.0 %collective-permute-done.7.refs_1_.down_left = f32[520,128]{1,0:T(8,128)S(1)} collective-permute-done((f32[520,128]{1,0:T(8,128)S(1)}, f32[520,128]{1,0:T(8,128)S(1)}, u32[]{:S(2)}, u32[]{:S(2)}) %collective-permute-start.7) | collective-permute-done | bytes 266272 | tf_op jit(solution)/shard_map/ppermute | solution.py:172
  32.0 0.0 collective-permute-done.6.refs_0_.left_ref.first_left
  32.0 1.3 %collective-permute-start.8 = (f32[1032,128]{1,0:T(8,128)S(1)}, f32[1032,128]{1,0:T(8,128)S(1)}, u32[]{:S(2)}, u32[]{:S(2)}) collective-permute-start(f32[1032,128]{1,0:T(8,128)S(1)} %shard_map.61), channel_id=1, source_target_pairs={{1,0},{2,1},{5,4},{6,5},{9,8},{10,9},{13,12},{14,13},{17,16},{18,1... | collective-permute-start | bytes 1585160 | tf_op jit(solution)/shard_map/ppermute | solution.py:172
  33.4 1.3 %collective-permute-start.11 = (f32[512,128]{1,0:T(8,128)S(1)}, f32[512,128]{1,0:T(8,128)S(1)}, u32[]{:S(2)}, u32[]{:S(2)}) collective-permute-start(f32[512,128]{1,0:T(8,128)S(1)} %slice.9), channel_id=1, source_target_pairs={{1,0},{2,1},{5,4},{6,5},{9,8},{10,9},{13,12},{14,13},{17,16},{18,1... | collective-permute-start | bytes 786440 | tf_op jit(solution)/shard_map/ppermute | solution.py:172
  34.7 0.7 collective-permute-start.10
  35.4 14.2 %collective-permute-done.11.left_ref = f32[512,128]{1,0:T(8,128)S(1)} collective-permute-done((f32[512,128]{1,0:T(8,128)S(1)}, f32[512,128]{1,0:T(8,128)S(1)}, u32[]{:S(2)}, u32[]{:S(2)}) %collective-permute-start.11) | collective-permute-done | bytes 262176 | tf_op jit(solution)/shard_map/ppermute | solution.py:172
  49.6 0.0 collective-permute-done.10.right_ref
  49.7 0.0 copy-start
  49.7 0.0 copy-start.1
  49.7 0.0 copy-start.2
  49.7 1.4 %collective-permute-start.12 = (f32[512,128]{1,0:T(8,128)S(1)}, f32[512,128]{1,0:T(8,128)S(1)}, u32[]{:S(2)}, u32[]{:S(2)}) collective-permute-start(f32[512,128]{1,0:T(8,128)S(1)} %shard_map.63.far_ref), channel_id=1, source_target_pairs={{1,0},{2,3},{5,4},{6,7},{9,8},{10,11},{13,12},{14,15},{17,16},{18,... | collective-permute-start | bytes 786440 | tf_op jit(solution)/shard_map/ppermute | solution.py:175
  51.1 0.0 collective-permute-done.5.right_ref
  51.1 0.0 collective-permute-done.8.left_ref
  51.2 0.1 shard_map.62.far_ref
  51.2 1.3 %collective-permute-start.9 = (f32[1032,128]{1,0:T(8,128)S(1)}, f32[1032,128]{1,0:T(8,128)S(1)}, u32[]{:S(2)}, u32[]{:S(2)}) collective-permute-start(f32[1032,128]{1,0:T(8,128)S(1)} %shard_map.62.far_ref), channel_id=1, source_target_pairs={{1,0},{2,3},{5,4},{6,7},{9,8},{10,11},{13,12},{14,15},{17,16},{18,... | collective-permute-start | bytes 1585160 | tf_op jit(solution)/shard_map/ppermute | solution.py:175
  52.5 7.4 %collective-permute-done.12.end_ref = f32[512,128]{1,0:T(8,128)S(1)} collective-permute-done((f32[512,128]{1,0:T(8,128)S(1)}, f32[512,128]{1,0:T(8,128)S(1)}, u32[]{:S(2)}, u32[]{:S(2)}) %collective-permute-start.12) | collective-permute-done | bytes 262176 | tf_op jit(solution)/shard_map/ppermute | solution.py:175
  59.9 0.0 copy-done
  59.9 0.0 copy-done.1
  59.9 0.0 copy-done.2
  59.9 2.3 %shard_map.64.refs_0_.solved_ref = f32[512,256]{1,0:T(8,128)S(1)} custom-call(s32[1]{0:T(128)} %bitcast.place, f32[2,512,128]{2,1,0:T(8,128)S(1)} %copy-done.1, f32[1024,128]{1,0:T(8,128)S(1)} %collective-permute-done.refs_0_.right_ref.first_right, f32[1024,128]{1,0:T(8,128)S(1)} %collective-permute-done.6.refs_0_.left_ref.first_left, ...), custom_call_target="tpu_custom_call" | custom-call | tf_op jit(solution)/shard_map/pallas_call | solution.py:154
  62.2 1.9 %collective-permute-start.13 = (f32[512,256]{1,0:T(8,128)S(1)}, f32[512,256]{1,0:T(8,128)S(1)}, u32[]{:S(2)}, u32[]{:S(2)}) collective-permute-start(f32[512,256]{1,0:T(8,128)S(1)} %shard_map.64.refs_0_.solved_ref), channel_id=1, source_target_pairs={{0,4},{4,8},{8,12},{12,16},{16,20},{20,24},{24,28},{1,5},{5,9},{9,... | collective-permute-start | bytes 1572872 | tf_op jit(solution)/shard_map/ppermute | solution.py:231
  64.2 9.5 %collective-permute-done.13.refs_1_.below_ref = f32[512,256]{1,0:T(8,128)S(1)} collective-permute-done((f32[512,256]{1,0:T(8,128)S(1)}, f32[512,256]{1,0:T(8,128)S(1)}, u32[]{:S(2)}, u32[]{:S(2)}) %collective-permute-start.13) | collective-permute-done | bytes 524320 | tf_op jit(solution)/shard_map/ppermute | solution.py:231
  73.6 1.1 %shard_map.65 = (f32[512,128]{1,0:T(8,128)S(1)}, f32[512,128]{1,0:T(8,128)S(1)}, f32[512,128]{1,0:T(8,128)S(1)}, f32[8,128]{1,0:T(8,128)S(1)}) custom-call(s32[1]{0:T(128)} %bitcast.place, f32[2,512,128]{2,1,0:T(8,128)S(1)} %copy-done, f32[2,512,128]{2,1,0:T(8,128)S(1)} %copy-done.2, f32[8,128]{1,0:T(8,128)S(1)} %max.11.refs_1_.peak_ref, ...), custom_call_target="tpu_custom_call" | custom-call | tf_op jit(solution)/shard_map/pallas_call | solution.py:154
  74.7 0.0 collective-permute-done.9.end_ref
  74.7 1.5 %shard_map.66 = (f32[1,512,128]{2,1,0:T(8,128)}, f32[1,512,128]{2,1,0:T(8,128)}, f32[1,512,128]{2,1,0:T(8,128)}) custom-call(s32[1]{0:T(128)} %bitcast.place, f32[1032,128]{1,0:T(8,128)S(1)} %collective-permute-done.9.end_ref, f32[512,256]{1,0:T(8,128)S(1)} %shard_map.64.refs_0_.solved_ref, f32[512,256]{1,0:T(8,128)S(1)} %collective-permute-done.13.refs_1_.below_ref, ...), custom_call_target="tpu_custom_call" | custom-call | tf_op jit(solution)/shard_map/pallas_call | solution.py:154
  (9 shorter events, 0.2 us)
Async XLA Ops:
  1.9 25.4 %collective-permute-start = (f32[1024,128]{1,0:T(8,128)S(1)}, f32[1024,128]{1,0:T(8,128)S(1)}, u32[]{:S(2)}, u32[]{:S(2)}) collective-permute-start(f32[1024,128]{1,0:T(8,128)S(1)} %get-tuple-element.10), channel_id=1, source_target_pairs={{0,1},{1,2},{2,3},{4,5},{5,6},{6,7},{8,9},{9,10},{10,11},{12,13},{... | collective-permute-start | bytes 1572872 | tf_op jit(solution)/shard_map/ppermute | solution.py:169
  5.4 26.6 %collective-permute-start.6 = (f32[1024,128]{1,0:T(8,128)S(1)}, f32[1024,128]{1,0:T(8,128)S(1)}, u32[]{:S(2)}, u32[]{:S(2)}) collective-permute-start(f32[1024,128]{1,0:T(8,128)S(1)} %get-tuple-element.10), channel_id=1, source_target_pairs={{1,0},{2,1},{3,2},{5,4},{6,5},{7,6},{9,8},{10,9},{11,10},{13,12},{... | collective-permute-start | bytes 1572872 | tf_op jit(solution)/shard_map/ppermute | solution.py:172
  6.7 4.0 %collective-permute-start.1 = (f32[8,128]{1,0:T(8,128)S(1)}, f32[8,128]{1,0:T(8,128)S(1)}, u32[]{:S(2)}, u32[]{:S(2)}) collective-permute-start(f32[8,128]{1,0:T(8,128)S(1)} %get-tuple-element.12), channel_id=1, source_target_pairs={{0,4},{4,8},{8,12},{12,16},{16,20},{20,24},{24,28},{28,0},{1,5},{5... | collective-permute-start | bytes 12296 | tf_op jit(solution)/shard_map/ppermute | solution.py:199
  10.7 4.5 %collective-permute-start.2 = (f32[8,128]{1,0:T(8,128)S(1)}, f32[8,128]{1,0:T(8,128)S(1)}, u32[]{:S(2)}, u32[]{:S(2)}) collective-permute-start(f32[8,128]{1,0:T(8,128)S(1)} %max.9), channel_id=1, source_target_pairs={{0,8},{4,12},{8,16},{12,20},{16,24},{20,28},{24,0},{28,4},{1,9},{5... | collective-permute-start | bytes 12296 | tf_op jit(solution)/shard_map/ppermute | solution.py:199
  15.2 3.6 %collective-permute-start.3 = (f32[8,128]{1,0:T(8,128)S(1)}, f32[8,128]{1,0:T(8,128)S(1)}, u32[]{:S(2)}, u32[]{:S(2)}) collective-permute-start(f32[8,128]{1,0:T(8,128)S(1)} %max.10), channel_id=1, source_target_pairs={{0,16},{4,20},{8,24},{12,28},{16,0},{20,4},{24,8},{28,12},{1,17},{... | collective-permute-start | bytes 12296 | tf_op jit(solution)/shard_map/ppermute | solution.py:199
  18.8 8.5 %collective-permute-start.4 = (f32[520,128]{1,0:T(8,128)S(1)}, f32[520,128]{1,0:T(8,128)S(1)}, u32[]{:S(2)}, u32[]{:S(2)}) collective-permute-start(f32[520,128]{1,0:T(8,128)S(1)} %shard_map.59), channel_id=1, source_target_pairs={{0,1},{1,2},{2,3},{4,5},{5,6},{6,7},{8,9},{9,10},{10,11},{12,13},{... | collective-permute-start | bytes 798728 | tf_op jit(solution)/shard_map/ppermute | solution.py:169
  23.4 8.6 %collective-permute-start.7 = (f32[520,128]{1,0:T(8,128)S(1)}, f32[520,128]{1,0:T(8,128)S(1)}, u32[]{:S(2)}, u32[]{:S(2)}) collective-permute-start(f32[520,128]{1,0:T(8,128)S(1)} %shard_map.59), channel_id=1, source_target_pairs={{1,0},{2,1},{3,2},{5,4},{6,5},{7,6},{9,8},{10,9},{11,10},{13,12},{... | collective-permute-start | bytes 798728 | tf_op jit(solution)/shard_map/ppermute | solution.py:172
  27.3 23.8 %collective-permute-start.5 = (f32[1032,128]{1,0:T(8,128)S(1)}, f32[1032,128]{1,0:T(8,128)S(1)}, u32[]{:S(2)}, u32[]{:S(2)}) collective-permute-start(f32[1032,128]{1,0:T(8,128)S(1)} %shard_map.60), channel_id=1, source_target_pairs={{1,2},{2,3},{5,6},{6,7},{9,10},{10,11},{13,14},{14,15},{17,18},{18... | collective-permute-start | bytes 1585160 | tf_op jit(solution)/shard_map/ppermute | solution.py:169
  32.0 19.1 %collective-permute-start.8 = (f32[1032,128]{1,0:T(8,128)S(1)}, f32[1032,128]{1,0:T(8,128)S(1)}, u32[]{:S(2)}, u32[]{:S(2)}) collective-permute-start(f32[1032,128]{1,0:T(8,128)S(1)} %shard_map.61), channel_id=1, source_target_pairs={{1,0},{2,1},{5,4},{6,5},{9,8},{10,9},{13,12},{14,13},{17,16},{18,1... | collective-permute-start | bytes 1585160 | tf_op jit(solution)/shard_map/ppermute | solution.py:172
  33.4 16.3 %collective-permute-start.11 = (f32[512,128]{1,0:T(8,128)S(1)}, f32[512,128]{1,0:T(8,128)S(1)}, u32[]{:S(2)}, u32[]{:S(2)}) collective-permute-start(f32[512,128]{1,0:T(8,128)S(1)} %slice.9), channel_id=1, source_target_pairs={{1,0},{2,1},{5,4},{6,5},{9,8},{10,9},{13,12},{14,13},{17,16},{18,1... | collective-permute-start | bytes 786440 | tf_op jit(solution)/shard_map/ppermute | solution.py:172
  34.7 14.9 %collective-permute-start.10 = (f32[512,128]{1,0:T(8,128)S(1)}, f32[512,128]{1,0:T(8,128)S(1)}, u32[]{:S(2)}, u32[]{:S(2)}) collective-permute-start(f32[512,128]{1,0:T(8,128)S(1)} %slice.8), channel_id=1, source_target_pairs={{1,2},{2,3},{5,6},{6,7},{9,10},{10,11},{13,14},{14,15},{17,18},{18... | collective-permute-start | bytes 786440 | tf_op jit(solution)/shard_map/ppermute | solution.py:169
  49.7 10.2 %copy-start = (f32[2,512,128]{2,1,0:T(8,128)S(1)}, f32[2,512,128]{2,1,0:T(8,128)}, u32[]{:S(2)}) copy-start(f32[2,512,128]{2,1,0:T(8,128)} %up_ref.5) | copy-start | bytes 1572868
  49.7 10.2 %copy-start.1 = (f32[2,512,128]{2,1,0:T(8,128)S(1)}, f32[2,512,128]{2,1,0:T(8,128)}, u32[]{:S(2)}) copy-start(f32[2,512,128]{2,1,0:T(8,128)} %refs_2_.1) | copy-start | bytes 1572868
  49.7 10.2 %copy-start.2 = (f32[2,512,128]{2,1,0:T(8,128)S(1)}, f32[2,512,128]{2,1,0:T(8,128)}, u32[]{:S(2)}) copy-start(f32[2,512,128]{2,1,0:T(8,128)} %down_ref.5) | copy-start | bytes 1572868
  49.7 10.2 %collective-permute-start.12 = (f32[512,128]{1,0:T(8,128)S(1)}, f32[512,128]{1,0:T(8,128)S(1)}, u32[]{:S(2)}, u32[]{:S(2)}) collective-permute-start(f32[512,128]{1,0:T(8,128)S(1)} %shard_map.63.far_ref), channel_id=1, source_target_pairs={{1,0},{2,3},{5,4},{6,7},{9,8},{10,11},{13,12},{14,15},{17,16},{18,... | collective-permute-start | bytes 786440 | tf_op jit(solution)/shard_map/ppermute | solution.py:175
  51.2 23.5 %collective-permute-start.9 = (f32[1032,128]{1,0:T(8,128)S(1)}, f32[1032,128]{1,0:T(8,128)S(1)}, u32[]{:S(2)}, u32[]{:S(2)}) collective-permute-start(f32[1032,128]{1,0:T(8,128)S(1)} %shard_map.62.far_ref), channel_id=1, source_target_pairs={{1,0},{2,3},{5,4},{6,7},{9,8},{10,11},{13,12},{14,15},{17,16},{18,... | collective-permute-start | bytes 1585160 | tf_op jit(solution)/shard_map/ppermute | solution.py:175
  62.2 11.4 %collective-permute-start.13 = (f32[512,256]{1,0:T(8,128)S(1)}, f32[512,256]{1,0:T(8,128)S(1)}, u32[]{:S(2)}, u32[]{:S(2)}) collective-permute-start(f32[512,256]{1,0:T(8,128)S(1)} %shard_map.64.refs_0_.solved_ref), channel_id=1, source_target_pairs={{0,4},{4,8},{8,12},{12,16},{16,20},{20,24},{24,28},{1,5},{5,9},{9,... | collective-permute-start | bytes 1572872 | tf_op jit(solution)/shard_map/ppermute | solution.py:231

commit v9 on v8

v9 whole, which is shorter than its diff:
```python
import functools

import jax
import jax.numpy as jnp
from jax import lax
from jax.experimental import pallas as pl
from jax.experimental.pallas import tpu as pltpu
from jax.sharding import PartitionSpec as P

SWEEPS = 2
PEAK_ROWS = 8
SLOTS = 4
F32 = jnp.float32
BF16 = jnp.bfloat16
VMEM = pl.BlockSpec(memory_space=pltpu.VMEM)
ANY = pl.BlockSpec(memory_space=pl.ANY)
SMEM = pl.BlockSpec(memory_space=pltpu.SMEM)


def split(x):
    high = x.astype(BF16)
    return high, (x - high.astype(F32)).astype(BF16)


def exact_dot(left, right):
    (left_high, left_low), (right_high, right_low) = left, right
    dot = lambda a, b: jnp.dot(a, b, preferred_element_type=F32)
    return dot(left_high, right_high) + (dot(left_high, right_low) + dot(left_low, right_high))


def on_diagonal(rows, cols):
    row = lax.broadcasted_iota(jnp.int32, (rows, cols), 0)
    return row == lax.broadcasted_iota(jnp.int32, (rows, cols), 1)


def prepare_kernel(owners, up_ref, level_ref, down_ref, sent_ref, peak_ref, square, sems):
    _, phases, cols = level_ref.shape
    own = rows_of(owners, 0, cols)
    sources = [level_ref.at[:, own, :], level_ref.at[1], up_ref.at[0], down_ref.at[0]]
    targets = [square, *[sent_ref.at[pl.ds(part * phases, phases), :] for part in range(3)]]
    copies = [
        pltpu.make_async_copy(source, target, sems.at[at])
        for at, (source, target) in enumerate(zip(sources, targets))
    ]
    for copy in copies:
        copy.start()
    copies[0].wait()
    lowest = jnp.min(jnp.where(on_diagonal(cols, cols)[None], square[...], 0.0))
    peak_ref[...] = jnp.full(peak_ref.shape, -lowest, F32)
    for copy in copies[1:]:
        copy.wait()


def stack_kernel(ranges, *refs):
    *parts, out_ref = refs
    at = 0
    for (first, rows), ref in zip(ranges, parts):
        out_ref[pl.ds(at, rows), :] = ref[pl.ds(first, rows), :]
        at += rows


def rows_of(owners, slot, cols):
    return pl.ds(pl.multiple_of(owners[slot] * cols, cols), cols)


def solve_kernel(owners, own_ref, *refs):
    *others, up_ref, down_ref, solved_ref, inverse, high, low, s_high, s_low = refs
    phases, cols = inverse.shape
    diagonal = on_diagonal(cols, cols)
    blocks = [own_ref.at[0], *others]
    for slot, block in enumerate(blocks):
        rows, slot_cols = rows_of(owners, slot, cols), pl.ds(slot * cols, cols)
        high[:, slot_cols], low[:, slot_cols] = split(block[pl.ds(0, phases), :])
        square = block[rows, :]
        rate = -jnp.sum(jnp.where(diagonal, square, 0.0), axis=1, keepdims=True)
        inverse[rows, :] = jnp.broadcast_to(1.0 / rate, (cols, cols))
        high[rows, slot_cols], low[rows, slot_cols] = split(jnp.where(diagonal, 0.0, square))
    for side, ref in enumerate((up_ref, down_ref)):
        solved_ref[:, pl.ds(side * cols, cols)] = ref[0] * inverse[...]
    for _ in range(SWEEPS):
        for slot in range(len(blocks)):
            rows, slot_rows = rows_of(owners, slot, cols), pl.ds(slot * cols, cols)
            s_high[slot_rows, :], s_low[slot_rows, :] = split(solved_ref[rows, :])
        product = exact_dot((high[...], low[...]), (s_high[...], s_low[...]))
        for side, ref in enumerate((up_ref, down_ref)):
            columns = slice(side * cols, (side + 1) * cols)
            solved_ref[:, columns] = (ref[0] + product[:, columns]) * inverse[...]


def gathered_product(owners, blocks, first_slot, solved_ref):
    cols = blocks[0].shape[-1]
    left = split(jnp.concatenate(blocks, axis=1))
    rows = [rows_of(owners, first_slot + at, cols) for at in range(len(blocks))]
    right = split(jnp.concatenate([solved_ref[r, :] for r in rows], axis=0))
    return exact_dot(left, right)


def partial_kernel(owners, up_ref, down_ref, peak_ref, level_near, near_ref, far_ref, *refs):
    solved_ref, below_ref, level_ref, part_level, part_up, part_down, part_peak = refs
    phases, cols = part_up.shape
    part = lambda ref, at: ref[pl.ds(at * phases, phases), :]
    upper = gathered_product(owners, [up_ref[0], part(near_ref, 1), part(far_ref, 0)], 0, solved_ref)
    part_up[...] = upper[:, :cols]
    lower = gathered_product(owners, [down_ref[0], part(near_ref, 2), part(far_ref, 1)], 0, below_ref)
    part_down[...] = lower[:, cols:]
    part_level[...] = level_ref[0] + upper[:, cols:] + lower[:, :cols]
    others = [level_near[pl.ds(phases, PEAK_ROWS), :], far_ref[pl.ds(2 * phases, PEAK_ROWS), :]]
    part_peak[...] = jnp.maximum(peak_ref[...], jnp.maximum(*others))


def output_kernel(owners, last_ref, solved_ref, below_ref, *refs):
    part_level, part_up, part_down, part_peak, new_level, new_up, new_down = refs
    phases, cols = part_up.shape
    peak = jnp.maximum(part_peak[...], last_ref[pl.ds(2 * phases, PEAK_ROWS), :])
    scale = 1.0 / peak[0:1, :]
    last = SLOTS - 1
    upper = gathered_product(owners, [last_ref[pl.ds(0, phases), :]], last, solved_ref)
    new_up[0] = (part_up[...] + upper[:, :cols]) * scale
    lower = gathered_product(owners, [last_ref[pl.ds(phases, phases), :]], last, below_ref)
    new_down[0] = (part_down[...] + lower[:, cols:]) * scale
    new_level[0] = (part_level[...] + upper[:, cols:] + lower[:, :cols]) * scale


def per_device(up_blocks, level_blocks, down_blocks):
    levels, phases, cols = level_blocks.shape
    shards = lax.axis_size("col")
    ranges = lax.axis_size("lvl")
    assert levels == 2 and shards == SLOTS
    place = lax.axis_index("col").astype(jnp.int32)
    owners = jnp.stack([place ^ distance for distance in (0, 1, 3, 2)])
    params = pltpu.CompilerParams(vmem_limit_bytes=32 * 2**20)
    shape = lambda rows, columns=cols: jax.ShapeDtypeStruct((rows, columns), F32)

    def call(kernel, out_shape, in_specs, *operands, scratch=(), **options):
        return pl.pallas_call(
            kernel,
            out_shape=out_shape,
            in_specs=in_specs,
            out_specs=jax.tree.map(lambda _: VMEM, out_shape),
            scratch_shapes=scratch,
            grid=(1,),
            compiler_params=params,
            **options,
        )(*operands)

    def one_level(parity):
        return pl.BlockSpec((1, phases, cols), lambda step: (parity, 0, 0))

    def exchanged(part, distance):
        return lax.ppermute(part, "col", [(i, i ^ distance) for i in range(shards)])

    def stack(*pieces):
        ranges_of = [(first, rows) for _, first, rows in pieces]
        kernel = functools.partial(stack_kernel, ranges_of)
        return call(kernel, shape(sum(rows for _, rows in ranges_of)), [VMEM] * len(pieces), *[p[0] for p in pieces])

    odd, even = one_level(1), one_level(0)
    in_hbm = [pltpu.with_memory_space_constraint(x, pltpu.HBM) for x in (up_blocks, level_blocks, down_blocks)]
    sent, peak = call(
        prepare_kernel,
        (shape(3 * phases), shape(PEAK_ROWS)),
        [SMEM] + [ANY] * 3,
        owners,
        *in_hbm,
        scratch=[pltpu.VMEM((levels, cols, cols), F32), pltpu.SemaphoreType.DMA((4,))],
    )
    level_far = exchanged(sent[:phases], 3)
    near = exchanged(sent, 1)
    reach = 1
    while reach < ranges:
        route = [(i, (i + reach) % ranges) for i in range(ranges)]
        peak = jnp.maximum(peak, lax.ppermute(peak, "lvl", route))
        reach *= 2
    sent_now = lax.optimization_barrier((sent, level_far))[0]
    even_far = exchanged(stack((sent_now, phases, 2 * phases), (peak, 0, PEAK_ROWS)), 3)
    level_last = exchanged(stack((level_far, 0, phases), (peak, 0, PEAK_ROWS)), 1)
    even_last = exchanged(even_far, 1)

    solved = call(
        solve_kernel,
        shape(phases, 2 * cols),
        [SMEM, odd, *[VMEM] * 3, odd, odd],
        owners,
        level_blocks,
        near,
        level_far,
        level_last,
        up_blocks,
        down_blocks,
        scratch=[
            pltpu.VMEM((phases, cols), F32),
            pltpu.VMEM((phases, phases), BF16),
            pltpu.VMEM((phases, phases), BF16),
            pltpu.VMEM((phases, 2 * cols), BF16),
            pltpu.VMEM((phases, 2 * cols), BF16),
        ],
    )
    from_below = lax.ppermute(solved, "lvl", [(i, i + 1) for i in range(ranges - 1)])

    parts = call(
        partial_kernel,
        (shape(phases),) * 3 + (shape(PEAK_ROWS),),
        [SMEM, even, even, *[VMEM] * 6, even],
        owners,
        up_blocks,
        down_blocks,
        peak,
        level_last,
        near,
        even_far,
        solved,
        from_below,
        level_blocks,
        cost_estimate=pl.CostEstimate(flops=0, bytes_accessed=0, transcendentals=0),
    )
    return call(
        output_kernel,
        (jax.ShapeDtypeStruct((1, phases, cols), F32),) * 3,
        [SMEM] + [VMEM] * 7,
        owners,
        even_last,
        solved,
        from_below,
        *parts,
    )


def solution(mesh):
    placed = (P("lvl", None, "col"),) * 3
    return jax.shard_map(per_device, mesh=mesh, in_specs=placed, out_specs=placed, check_vma=False)
```

time: 76.6 us -> 65.8 us (0.86)
  the two profiles are of different devices: /device:TPU:4 before, /device:TPU:12 now
where the time goes in v9:
time: 65.8 us; the launch traced here: 65.6 us
  waiting for transfers between devices  46.7 us (71%)
  starting transfers between devices  9.75 us (15%)
  Pallas kernels  8.31 us (13%)
  between operations  0.74 us (1%)
    ppermute x5, waiting for transfers between devices, exchanged(): return lax.ppermute(part, 'col', [(i, i ^ distance) for i in range(shards)])  26.3 us
    ppermute x3, waiting for transfers between devices, per_device(): peak = jnp.maximum(peak, lax.ppermute(peak, 'lvl', route))  10.9 us
    ppermute x1, waiting for transfers between devices, per_device(): lax.ppermute(solved, 'lvl', [(i, i + 1) for i in range(ranges - 1)])  9.47 us
    pallas_call x6, Pallas kernels, call(): pl.pallas_call(kernel, out_shape=out_shape, in_specs=in_specs, out_specs=...  8.31 us
    ppermute x5, starting transfers between devices, exchanged(): return lax.ppermute(part, 'col', [(i, i ^ distance) for i in range(shards)])  6.73 us
    ppermute x1, starting transfers between devices, per_device(): lax.ppermute(solved, 'lvl', [(i, i + 1) for i in range(ranges - 1)])  1.92 us
  transfers between devices with their start and end apart: 9, of which 6 were waited for; matrix products, arithmetic and copies ran while one was open for 0% of the time, Pallas kernels for 7%

profile of v9, /device:TPU:12, one launch (start us, length us, event | category | flops | bytes accessed | tf_op | source)
XLA Modules:
  0.0 65.6 jit_solution(7118331195716822640)
XLA Ops:
  0.6 0.1 pad_add_fusion.owners
  0.7 1.8 %shard_map.58 = (f32[1536,128]{1,0:T(8,128)S(1)}, f32[8,128]{1,0:T(8,128)S(1)}) custom-call(s32[4]{0:T(128)S(1)} %pad_add_fusion.owners, f32[2,512,128]{2,1,0:T(8,128)} %up_ref.3, f32[2,512,128]{2,1,0:T(8,128)} %refs_2_.1, f32[2,512,128]{2,1,0:T(8,128)} %down_ref.3), custom_call_target="tpu_custom_call" | custom-call | tf_op jit(solution)/shard_map/pallas_call | solution.py:135
  2.5 1.6 %collective-permute-start = (f32[512,128]{1,0:T(8,128)S(1)}, f32[512,128]{1,0:T(8,128)S(1)}, u32[]{:S(2)}, u32[]{:S(2)}) collective-permute-start(f32[512,128]{1,0:T(8,128)S(1)} %slice.3), channel_id=1, source_target_pairs={{0,3},{1,2},{2,1},{3,0},{4,7},{5,6},{6,5},{7,4},{8,11},{9,10},{10,... | collective-permute-start | bytes 786440 | tf_op jit(solution)/shard_map/ppermute | solution.py:150
  4.1 2.5 %collective-permute-start.6 = (f32[1536,128]{1,0:T(8,128)S(1)}, f32[1536,128]{1,0:T(8,128)S(1)}, u32[]{:S(2)}, u32[]{:S(2)}) collective-permute-start(f32[1536,128]{1,0:T(8,128)S(1)} %get-tuple-element.11.refs_0_), channel_id=1, source_target_pairs={{0,1},{1,0},{2,3},{3,2},{4,5},{5,4},{6,7},{7,6},{8,9},{9,8},{10,11... | collective-permute-start | bytes 2359304 | tf_op jit(solution)/shard_map/ppermute | solution.py:150
  6.6 0.0 collective-permute-start.1
  6.6 3.9 %collective-permute-done.1 = f32[8,128]{1,0:T(8,128)S(1)} collective-permute-done((f32[8,128]{1,0:T(8,128)S(1)}, f32[8,128]{1,0:T(8,128)S(1)}, u32[]{:S(2)}, u32[]{:S(2)}) %collective-permute-start.1) | collective-permute-done | bytes 4128 | tf_op jit(solution)/shard_map/ppermute | solution.py:172
  10.6 0.6 collective-permute-start.2
  11.2 3.9 %collective-permute-done.2 = f32[8,128]{1,0:T(8,128)S(1)} collective-permute-done((f32[8,128]{1,0:T(8,128)S(1)}, f32[8,128]{1,0:T(8,128)S(1)}, u32[]{:S(2)}, u32[]{:S(2)}) %collective-permute-start.2) | collective-permute-done | bytes 4128 | tf_op jit(solution)/shard_map/ppermute | solution.py:172
  15.1 0.5 collective-permute-start.3
  15.6 3.1 %collective-permute-done.3 = f32[8,128]{1,0:T(8,128)S(1)} collective-permute-done((f32[8,128]{1,0:T(8,128)S(1)}, f32[8,128]{1,0:T(8,128)S(1)}, u32[]{:S(2)}, u32[]{:S(2)}) %collective-permute-start.3) | collective-permute-done | bytes 4128 | tf_op jit(solution)/shard_map/ppermute | solution.py:172
  18.7 0.0 collective-permute-done.refs_0_.refs_1_
  18.7 0.0 copy-start.1
  18.7 0.0 copy-start.2
  18.7 0.0 copy-start
  18.8 0.1 collective-permute-start.4
  18.9 0.9 %collective-permute-start.7 = (f32[520,128]{1,0:T(8,128)S(1)}, f32[520,128]{1,0:T(8,128)S(1)}, u32[]{:S(2)}, u32[]{:S(2)}) collective-permute-start(f32[520,128]{1,0:T(8,128)S(1)} %shard_map.60), channel_id=1, source_target_pairs={{0,1},{1,0},{2,3},{3,2},{4,5},{5,4},{6,7},{7,6},{8,9},{9,8},{10,11... | collective-permute-start | bytes 798728 | tf_op jit(solution)/shard_map/ppermute | solution.py:150
  19.8 20.9 %collective-permute-done.4.far_ref = f32[1032,128]{1,0:T(8,128)S(1)} collective-permute-done((f32[1032,128]{1,0:T(8,128)S(1)}, f32[1032,128]{1,0:T(8,128)S(1)}, u32[]{:S(2)}, u32[]{:S(2)}) %collective-permute-start.4) | collective-permute-done | bytes 528416 | tf_op jit(solution)/shard_map/ppermute | solution.py:150
  40.7 1.6 %collective-permute-start.5 = (f32[1032,128]{1,0:T(8,128)S(1)}, f32[1032,128]{1,0:T(8,128)S(1)}, u32[]{:S(2)}, u32[]{:S(2)}) collective-permute-start(f32[1032,128]{1,0:T(8,128)S(1)} %collective-permute-done.4.far_ref), channel_id=1, source_target_pairs={{0,1},{1,0},{2,3},{3,2},{4,5},{5,4},{6,7},{7,6},{8,9},{9,8},{10,11... | collective-permute-start | bytes 1585160 | tf_op jit(solution)/shard_map/ppermute | solution.py:150
  42.3 5.4 %collective-permute-done.7.refs_2_.level_near = f32[520,128]{1,0:T(8,128)S(1)} collective-permute-done((f32[520,128]{1,0:T(8,128)S(1)}, f32[520,128]{1,0:T(8,128)S(1)}, u32[]{:S(2)}, u32[]{:S(2)}) %collective-permute-start.7) | collective-permute-done | bytes 266272 | tf_op jit(solution)/shard_map/ppermute | solution.py:150
  47.7 0.0 collective-permute-done.6.refs_0_.near_ref
  47.7 0.0 copy-done.1
  47.7 0.0 copy-done.2
  47.7 0.0 copy-done
  47.7 2.9 %shard_map.61.refs_0_.solved_ref = f32[512,256]{1,0:T(8,128)S(1)} custom-call(s32[4]{0:T(128)S(1)} %pad_add_fusion.owners, f32[2,512,128]{2,1,0:T(8,128)S(1)} %copy-done.1, f32[1536,128]{1,0:T(8,128)S(1)} %collective-permute-done.6.refs_0_.near_ref, f32[512,128]{1,0:T(8,128)S(1)} %collective-permute-done.refs_0_.refs_1_, ...), custom_call_target="tpu_custom_call" | custom-call | tf_op jit(solution)/shard_map/pallas_call | solution.py:135
  50.6 1.9 %collective-permute-start.8 = (f32[512,256]{1,0:T(8,128)S(1)}, f32[512,256]{1,0:T(8,128)S(1)}, u32[]{:S(2)}, u32[]{:S(2)}) collective-permute-start(f32[512,256]{1,0:T(8,128)S(1)} %shard_map.61.refs_0_.solved_ref), channel_id=1, source_target_pairs={{0,4},{4,8},{8,12},{12,16},{16,20},{20,24},{24,28},{1,5},{5,9},{9,... | collective-permute-start | bytes 1572872 | tf_op jit(solution)/shard_map/ppermute | solution.py:198
  52.6 9.5 %collective-permute-done.8.refs_1_.below_ref = f32[512,256]{1,0:T(8,128)S(1)} collective-permute-done((f32[512,256]{1,0:T(8,128)S(1)}, f32[512,256]{1,0:T(8,128)S(1)}, u32[]{:S(2)}, u32[]{:S(2)}) %collective-permute-start.8) | collective-permute-done | bytes 524320 | tf_op jit(solution)/shard_map/ppermute | solution.py:198
  62.0 1.6 %shard_map.62 = (f32[512,128]{1,0:T(8,128)S(1)}, f32[512,128]{1,0:T(8,128)S(1)}, f32[512,128]{1,0:T(8,128)S(1)}, f32[8,128]{1,0:T(8,128)S(1)}) custom-call(s32[4]{0:T(128)S(1)} %pad_add_fusion.owners, f32[2,512,128]{2,1,0:T(8,128)S(1)} %copy-done, f32[2,512,128]{2,1,0:T(8,128)S(1)} %copy-done.2, f32[8,128]{1,0:T(8,128)S(1)} %max.11.refs_1_.peak_ref, ...), custom_call_target="tpu_custom_call" | custom-call | tf_op jit(solution)/shard_map/pallas_call | solution.py:135
  63.6 0.0 collective-permute-done.5.last_ref
  63.6 2.0 %shard_map.63 = (f32[1,512,128]{2,1,0:T(8,128)}, f32[1,512,128]{2,1,0:T(8,128)}, f32[1,512,128]{2,1,0:T(8,128)}) custom-call(s32[4]{0:T(128)S(1)} %pad_add_fusion.owners, f32[1032,128]{1,0:T(8,128)S(1)} %collective-permute-done.5.last_ref, f32[512,256]{1,0:T(8,128)S(1)} %shard_map.61.refs_0_.solved_ref, ...), custom_call_target="tpu_custom_call" | custom-call | tf_op jit(solution)/shard_map/pallas_call | solution.py:135
  (6 shorter events, 0.1 us)
Async XLA Ops:
  2.5 16.2 %collective-permute-start = (f32[512,128]{1,0:T(8,128)S(1)}, f32[512,128]{1,0:T(8,128)S(1)}, u32[]{:S(2)}, u32[]{:S(2)}) collective-permute-start(f32[512,128]{1,0:T(8,128)S(1)} %slice.3), channel_id=1, source_target_pairs={{0,3},{1,2},{2,1},{3,0},{4,7},{5,6},{6,5},{7,4},{8,11},{9,10},{10,... | collective-permute-start | bytes 786440 | tf_op jit(solution)/shard_map/ppermute | solution.py:150
  4.1 43.5 %collective-permute-start.6 = (f32[1536,128]{1,0:T(8,128)S(1)}, f32[1536,128]{1,0:T(8,128)S(1)}, u32[]{:S(2)}, u32[]{:S(2)}) collective-permute-start(f32[1536,128]{1,0:T(8,128)S(1)} %get-tuple-element.11.refs_0_), channel_id=1, source_target_pairs={{0,1},{1,0},{2,3},{3,2},{4,5},{5,4},{6,7},{7,6},{8,9},{9,8},{10,11... | collective-permute-start | bytes 2359304 | tf_op jit(solution)/shard_map/ppermute | solution.py:150
  6.6 3.9 %collective-permute-start.1 = (f32[8,128]{1,0:T(8,128)S(1)}, f32[8,128]{1,0:T(8,128)S(1)}, u32[]{:S(2)}, u32[]{:S(2)}) collective-permute-start(f32[8,128]{1,0:T(8,128)S(1)} %get-tuple-element.12), channel_id=1, source_target_pairs={{0,4},{4,8},{8,12},{12,16},{16,20},{20,24},{24,28},{28,0},{1,5},{5... | collective-permute-start | bytes 12296 | tf_op jit(solution)/shard_map/ppermute | solution.py:172
  10.6 4.5 %collective-permute-start.2 = (f32[8,128]{1,0:T(8,128)S(1)}, f32[8,128]{1,0:T(8,128)S(1)}, u32[]{:S(2)}, u32[]{:S(2)}) collective-permute-start(f32[8,128]{1,0:T(8,128)S(1)} %max.9), channel_id=1, source_target_pairs={{0,8},{4,12},{8,16},{12,20},{16,24},{20,28},{24,0},{28,4},{1,9},{5... | collective-permute-start | bytes 12296 | tf_op jit(solution)/shard_map/ppermute | solution.py:172
  15.1 3.6 %collective-permute-start.3 = (f32[8,128]{1,0:T(8,128)S(1)}, f32[8,128]{1,0:T(8,128)S(1)}, u32[]{:S(2)}, u32[]{:S(2)}) collective-permute-start(f32[8,128]{1,0:T(8,128)S(1)} %max.10), channel_id=1, source_target_pairs={{0,16},{4,20},{8,24},{12,28},{16,0},{20,4},{24,8},{28,12},{1,17},{... | collective-permute-start | bytes 12296 | tf_op jit(solution)/shard_map/ppermute | solution.py:172
  18.7 29.0 %copy-start.1 = (f32[2,512,128]{2,1,0:T(8,128)S(1)}, f32[2,512,128]{2,1,0:T(8,128)}, u32[]{:S(2)}) copy-start(f32[2,512,128]{2,1,0:T(8,128)} %refs_2_.1) | copy-start | bytes 1572868
  18.7 29.0 %copy-start.2 = (f32[2,512,128]{2,1,0:T(8,128)S(1)}, f32[2,512,128]{2,1,0:T(8,128)}, u32[]{:S(2)}) copy-start(f32[2,512,128]{2,1,0:T(8,128)} %down_ref.3) | copy-start | bytes 1572868
  18.7 28.9 %copy-start = (f32[2,512,128]{2,1,0:T(8,128)S(1)}, f32[2,512,128]{2,1,0:T(8,128)}, u32[]{:S(2)}) copy-start(f32[2,512,128]{2,1,0:T(8,128)} %up_ref.3) | copy-start | bytes 1572868
  18.8 21.9 %collective-permute-start.4 = (f32[1032,128]{1,0:T(8,128)S(1)}, f32[1032,128]{1,0:T(8,128)S(1)}, u32[]{:S(2)}, u32[]{:S(2)}) collective-permute-start(f32[1032,128]{1,0:T(8,128)S(1)} %shard_map.59), channel_id=1, source_target_pairs={{0,3},{1,2},{2,1},{3,0},{4,7},{5,6},{6,5},{7,4},{8,11},{9,10},{10,... | collective-permute-start | bytes 1585160 | tf_op jit(solution)/shard_map/ppermute | solution.py:150
  18.9 28.8 %collective-permute-start.7 = (f32[520,128]{1,0:T(8,128)S(1)}, f32[520,128]{1,0:T(8,128)S(1)}, u32[]{:S(2)}, u32[]{:S(2)}) collective-permute-start(f32[520,128]{1,0:T(8,128)S(1)} %shard_map.60), channel_id=1, source_target_pairs={{0,1},{1,0},{2,3},{3,2},{4,5},{5,4},{6,7},{7,6},{8,9},{9,8},{10,11... | collective-permute-start | bytes 798728 | tf_op jit(solution)/shard_map/ppermute | solution.py:150
  40.7 22.9 %collective-permute-start.5 = (f32[1032,128]{1,0:T(8,128)S(1)}, f32[1032,128]{1,0:T(8,128)S(1)}, u32[]{:S(2)}, u32[]{:S(2)}) collective-permute-start(f32[1032,128]{1,0:T(8,128)S(1)} %collective-permute-done.4.far_ref), channel_id=1, source_target_pairs={{0,1},{1,0},{2,3},{3,2},{4,5},{5,4},{6,7},{7,6},{8,9},{9,8},{10,11... | collective-permute-start | bytes 1585160 | tf_op jit(solution)/shard_map/ppermute | solution.py:150
  50.6 11.4 %collective-permute-start.8 = (f32[512,256]{1,0:T(8,128)S(1)}, f32[512,256]{1,0:T(8,128)S(1)}, u32[]{:S(2)}, u32[]{:S(2)}) collective-permute-start(f32[512,256]{1,0:T(8,128)S(1)} %shard_map.61.refs_0_.solved_ref), channel_id=1, source_target_pairs={{0,4},{4,8},{8,12},{12,16},{16,20},{20,24},{24,28},{1,5},{5,9},{9,... | collective-permute-start | bytes 1572872 | tf_op jit(solution)/shard_map/ppermute | solution.py:198

commit v10 on v9

v10 whole, which is shorter than its diff:
```python
import functools

import jax
import jax.numpy as jnp
from jax import lax
from jax.experimental import pallas as pl
from jax.experimental.pallas import tpu as pltpu
from jax.sharding import PartitionSpec as P

SWEEPS = 2
PEAK_ROWS = 8
DISTANCES = (0, 1, 3, 2)
F32 = jnp.float32
BF16 = jnp.bfloat16
VMEM = pl.BlockSpec(memory_space=pltpu.VMEM)
ANY = pl.BlockSpec(memory_space=pl.ANY)
SMEM = pl.BlockSpec(memory_space=pltpu.SMEM)


def split(x):
    high = x.astype(BF16)
    return high, (x - high.astype(F32)).astype(BF16)


def exact_dot(left, right):
    (left_high, left_low), (right_high, right_low) = left, right
    dot = lambda a, b: jnp.dot(a, b, preferred_element_type=F32)
    return dot(left_high, right_high) + (dot(left_high, right_low) + dot(left_low, right_high))


def on_diagonal(rows, cols):
    row = lax.broadcasted_iota(jnp.int32, (rows, cols), 0)
    return row == lax.broadcasted_iota(jnp.int32, (rows, cols), 1)


def prepare_kernel(place, up_ref, level_ref, down_ref, odd_ref, even_ref, square, sems):
    _, phases, cols = level_ref.shape
    own = rows_of(place, 0, cols)
    sources = [level_ref.at[:, own, :], level_ref.at[1], up_ref.at[0], down_ref.at[0]]
    top, middle = pl.ds(0, phases), pl.ds(phases, phases)
    targets = [square, odd_ref.at[top, :], even_ref.at[top, :], even_ref.at[middle, :]]
    copies = [
        pltpu.make_async_copy(source, target, sems.at[at])
        for at, (source, target) in enumerate(zip(sources, targets))
    ]
    for copy in copies:
        copy.start()
    copies[0].wait()
    lowest = jnp.min(jnp.where(on_diagonal(cols, cols)[None], square[...], 0.0))
    odd_ref[pl.ds(phases, PEAK_ROWS), :] = jnp.full((PEAK_ROWS, cols), -lowest, F32)
    for copy in copies[1:]:
        copy.wait()


def rows_of(place, slot, cols):
    return pl.ds(pl.multiple_of((place[0] ^ DISTANCES[slot]) * cols, cols), cols)


def solve_kernel(place, own_ref, *refs):
    *blocks, up_ref, down_ref, solved_ref, peak_ref, inverse, high, low, s_high, s_low = refs
    phases, cols = inverse.shape
    blocks = [own_ref, *blocks]
    peak = own_ref[pl.ds(phases, PEAK_ROWS), :]
    for block in blocks[1:]:
        peak = jnp.maximum(peak, block[pl.ds(phases, PEAK_ROWS), :])
    peak_ref[...] = peak
    diagonal = on_diagonal(cols, cols)
    for slot, block in enumerate(blocks):
        rows, slot_cols = rows_of(place, slot, cols), pl.ds(slot * cols, cols)
        high[:, slot_cols], low[:, slot_cols] = split(block[pl.ds(0, phases), :])
        square = block[rows, :]
        rate = -jnp.sum(jnp.where(diagonal, square, 0.0), axis=1, keepdims=True)
        inverse[rows, :] = jnp.broadcast_to(1.0 / rate, (cols, cols))
        high[rows, slot_cols], low[rows, slot_cols] = split(jnp.where(diagonal, 0.0, square))
    for side, ref in enumerate((up_ref, down_ref)):
        solved_ref[:, pl.ds(side * cols, cols)] = ref[0] * inverse[...]
    for _ in range(SWEEPS):
        for slot in range(len(blocks)):
            rows, slot_rows = rows_of(place, slot, cols), pl.ds(slot * cols, cols)
            s_high[slot_rows, :], s_low[slot_rows, :] = split(solved_ref[rows, :])
        product = exact_dot((high[...], low[...]), (s_high[...], s_low[...]))
        for side, ref in enumerate((up_ref, down_ref)):
            columns = slice(side * cols, (side + 1) * cols)
            solved_ref[:, columns] = (ref[0] + product[:, columns]) * inverse[...]


def gathered_product(place, blocks, first_slot, solved_ref):
    cols = blocks[0].shape[-1]
    left = split(jnp.concatenate(blocks, axis=1))
    rows = [rows_of(place, first_slot + at, cols) for at in range(len(blocks))]
    right = split(jnp.concatenate([solved_ref[r, :] for r in rows], axis=0))
    return exact_dot(left, right)


def partial_kernel(place, own_ref, near_ref, far_ref, solved_ref, below_ref, level_ref, part_level, part_up, part_down):
    phases, cols = part_up.shape
    top, middle = pl.ds(0, phases), pl.ds(phases, phases)
    blocks = (own_ref, near_ref, far_ref)
    upper = gathered_product(place, [ref[top, :] for ref in blocks], 0, solved_ref)
    part_up[...] = upper[:, :cols]
    lower = gathered_product(place, [ref[middle, :] for ref in blocks], 0, below_ref)
    part_down[...] = lower[:, cols:]
    part_level[...] = level_ref[0] + upper[:, cols:] + lower[:, :cols]


def output_kernel(place, last_ref, solved_ref, below_ref, *refs):
    part_level, part_up, part_down, peak_ref, new_level, new_up, new_down = refs
    phases, cols = part_up.shape
    scale = 1.0 / peak_ref[0:1, :]
    last = len(DISTANCES) - 1
    upper = gathered_product(place, [last_ref[pl.ds(0, phases), :]], last, solved_ref)
    new_up[0] = (part_up[...] + upper[:, :cols]) * scale
    lower = gathered_product(place, [last_ref[pl.ds(phases, phases), :]], last, below_ref)
    new_down[0] = (part_down[...] + lower[:, cols:]) * scale
    new_level[0] = (part_level[...] + upper[:, cols:] + lower[:, :cols]) * scale


def per_device(up_blocks, level_blocks, down_blocks):
    levels, phases, cols = level_blocks.shape
    shards = lax.axis_size("col")
    ranges = lax.axis_size("lvl")
    assert levels == 2 and shards == len(DISTANCES)
    place = lax.axis_index("col").astype(jnp.int32).reshape(1)
    params = pltpu.CompilerParams(vmem_limit_bytes=32 * 2**20)
    shape = lambda rows, columns=cols: jax.ShapeDtypeStruct((rows, columns), F32)

    def call(kernel, out_shape, in_specs, *operands, scratch=(), **options):
        return pl.pallas_call(
            kernel,
            out_shape=out_shape,
            in_specs=in_specs,
            out_specs=jax.tree.map(lambda _: VMEM, out_shape),
            scratch_shapes=scratch,
            grid=(1,),
            compiler_params=params,
            **options,
        )(*operands)

    def one_level(parity):
        return pl.BlockSpec((1, phases, cols), lambda step: (parity, 0, 0))

    def exchanged(part, distance):
        return lax.ppermute(part, "col", [(i, i ^ distance) for i in range(shards)])

    def after(value, *earlier):
        return lax.optimization_barrier((value, *earlier))[0]

    odd, even = one_level(1), one_level(0)
    in_hbm = [pltpu.with_memory_space_constraint(x, pltpu.HBM) for x in (up_blocks, level_blocks, down_blocks)]
    odd_block, even_blocks = call(
        prepare_kernel,
        (shape(phases + PEAK_ROWS), shape(2 * phases)),
        [SMEM] + [ANY] * 3,
        place,
        *in_hbm,
        scratch=[pltpu.VMEM((levels, cols, cols), F32), pltpu.SemaphoreType.DMA((4,))],
    )
    level_far, level_near = exchanged(odd_block, 3), exchanged(odd_block, 1)
    even_far, even_near = exchanged(even_blocks, 3), exchanged(even_blocks, 1)
    level_last, even_last = exchanged(level_far, 1), exchanged(even_far, 1)

    solved, peak = call(
        solve_kernel,
        (shape(phases, 2 * cols), shape(PEAK_ROWS)),
        [SMEM, *[VMEM] * 4, odd, odd],
        place,
        odd_block,
        level_near,
        level_far,
        level_last,
        up_blocks,
        down_blocks,
        scratch=[
            pltpu.VMEM((phases, cols), F32),
            pltpu.VMEM((phases, phases), BF16),
            pltpu.VMEM((phases, phases), BF16),
            pltpu.VMEM((phases, 2 * cols), BF16),
            pltpu.VMEM((phases, 2 * cols), BF16),
        ],
    )
    from_below = lax.ppermute(solved, "lvl", [(i, i + 1) for i in range(ranges - 1)])

    peak, reach = after(peak, even_far), 1
    while reach < ranges:
        route = [(i, (i + reach) % ranges) for i in range(ranges)]
        peak = jnp.maximum(peak, lax.ppermute(peak, "lvl", route))
        reach *= 2

    parts = call(
        partial_kernel,
        (shape(phases),) * 3,
        [SMEM, *[VMEM] * 5, even],
        place,
        even_blocks,
        even_near,
        even_far,
        solved,
        from_below,
        level_blocks,
        cost_estimate=pl.CostEstimate(flops=0, bytes_accessed=0, transcendentals=0),
    )
    return call(
        output_kernel,
        (jax.ShapeDtypeStruct((1, phases, cols), F32),) * 3,
        [SMEM] + [VMEM] * 7,
        place,
        even_last,
        solved,
        from_below,
        *parts,
        peak,
    )


def solution(mesh):
    placed = (P("lvl", None, "col"),) * 3
    return jax.shard_map(per_device, mesh=mesh, in_specs=placed, out_specs=placed, check_vma=False)
```

time: 65.8 us -> 62.5 us (0.950)
  the two profiles are of different devices: /device:TPU:12 before, /device:TPU:0 now
where the time goes in v10:
time: 62.5 us; the launch traced here: 62.4 us
  starting transfers between devices  34.7 us (56%)
  waiting for transfers between devices  20.8 us (33%)
  Pallas kernels  6.16 us (10%)
  between operations  0.72 us (1%)
    ppermute x6, starting transfers between devices, exchanged(): return lax.ppermute(part, 'col', [(i, i ^ distance) for i in range(shards)])  23.9 us
    ppermute x6, waiting for transfers between devices, exchanged(): return lax.ppermute(part, 'col', [(i, i ^ distance) for i in range(shards)])  14.6 us
    ppermute x3, starting transfers between devices, per_device(): peak = jnp.maximum(peak, lax.ppermute(peak, 'lvl', route))  9.48 us
    pallas_call x4, Pallas kernels, call(): pl.pallas_call(kernel, out_shape=out_shape, in_specs=in_specs, out_specs=...  6.16 us
    ppermute x3, waiting for transfers between devices, per_device(): peak = jnp.maximum(peak, lax.ppermute(peak, 'lvl', route))  6.14 us
    ppermute x1, starting transfers between devices, per_device(): lax.ppermute(solved, 'lvl', [(i, i + 1) for i in range(ranges - 1)])  1.32 us
  transfers between devices with their start and end apart: 10, of which 5 were waited for; matrix products, arithmetic and copies ran while one was open for 0% of the time, Pallas kernels for 5%

profile of v10, /device:TPU:0, one launch (start us, length us, event | category | flops | bytes accessed | tf_op | source)
XLA Modules:
  0.0 62.4 jit_solution(13560364354134709060)
XLA Ops:
  0.6 0.0 copy-start
  0.6 0.0 copy-start.1
  0.7 1.3 %shard_map.58 = (f32[520,128]{1,0:T(8,128)S(1)}, f32[1024,128]{1,0:T(8,128)S(1)}) custom-call(s32[1]{0:T(128)} %bitcast.place, f32[2,512,128]{2,1,0:T(8,128)} %refs_3_.1, f32[2,512,128]{2,1,0:T(8,128)} %level_ref.3, f32[2,512,128]{2,1,0:T(8,128)} %refs_4_.1), custom_call_target="tpu_custom_call" | custom-call | tf_op jit(solution)/shard_map/pallas_call | solution.py:128
  2.0 5.1 %collective-permute-start.3 = (f32[520,128]{1,0:T(8,128)S(1)}, f32[520,128]{1,0:T(8,128)S(1)}, u32[]{:S(2)}, u32[]{:S(2)}) collective-permute-start(f32[520,128]{1,0:T(8,128)S(1)} %get-tuple-element.12.own_ref), channel_id=1, source_target_pairs={{0,3},{1,2},{2,1},{3,0},{4,7},{5,6},{6,5},{7,4},{8,11},{9,10},{10,... | collective-permute-start | bytes 798728 | tf_op jit(solution)/shard_map/ppermute | solution.py:143
  7.1 0.0 copy-start.2
  7.1 0.1 collective-permute-start
  7.2 0.0 collective-permute-start.2
  7.2 7.3 %collective-permute-done.3.refs_1_ = f32[520,128]{1,0:T(8,128)S(1)} collective-permute-done((f32[520,128]{1,0:T(8,128)S(1)}, f32[520,128]{1,0:T(8,128)S(1)}, u32[]{:S(2)}, u32[]{:S(2)}) %collective-permute-start.3) | collective-permute-done | bytes 266272 | tf_op jit(solution)/shard_map/ppermute | solution.py:143
  14.5 16.6 %collective-permute-start.4 = (f32[520,128]{1,0:T(8,128)S(1)}, f32[520,128]{1,0:T(8,128)S(1)}, u32[]{:S(2)}, u32[]{:S(2)}) collective-permute-start(f32[520,128]{1,0:T(8,128)S(1)} %collective-permute-done.3.refs_1_), channel_id=1, source_target_pairs={{0,1},{1,0},{2,3},{3,2},{4,5},{5,4},{6,7},{7,6},{8,9},{9,8},{10,11... | collective-permute-start | bytes 798728 | tf_op jit(solution)/shard_map/ppermute | solution.py:143
  31.1 0.0 collective-permute-start.6
  31.1 0.0 collective-permute-done.2.refs_0_
  31.1 7.3 %collective-permute-done.4.refs_2_ = f32[520,128]{1,0:T(8,128)S(1)} collective-permute-done((f32[520,128]{1,0:T(8,128)S(1)}, f32[520,128]{1,0:T(8,128)S(1)}, u32[]{:S(2)}, u32[]{:S(2)}) %collective-permute-start.4) | collective-permute-done | bytes 266272 | tf_op jit(solution)/shard_map/ppermute | solution.py:143
  38.4 0.0 copy-done
  38.4 0.0 copy-done.1
  38.4 2.4 %shard_map.59 = (f32[512,256]{1,0:T(8,128)S(1)}, f32[8,128]{1,0:T(8,128)S(1)}) custom-call(s32[1]{0:T(128)} %bitcast.place, f32[520,128]{1,0:T(8,128)S(1)} %get-tuple-element.12.own_ref, f32[520,128]{1,0:T(8,128)S(1)} %collective-permute-done.2.refs_0_, f32[520,128]{1,0:T(8,128)S(1)} %collective-permute-done.3.refs_1_, ...), custom_call_target="tpu_custom_call" | custom-call | tf_op jit(solution)/shard_map/pallas_call | solution.py:128
  40.8 1.3 %collective-permute-start.5 = (f32[512,256]{1,0:T(8,128)S(1)}, f32[512,256]{1,0:T(8,128)S(1)}, u32[]{:S(2)}, u32[]{:S(2)}) collective-permute-start(f32[512,256]{1,0:T(8,128)S(1)} %get-tuple-element.13.solved_ref), channel_id=1, source_target_pairs={{0,4},{4,8},{8,12},{12,16},{16,20},{20,24},{24,28},{1,5},{5,9},{9,... | collective-permute-start | bytes 1572872 | tf_op jit(solution)/shard_map/ppermute | solution.py:181
  42.1 0.0 collective-permute-done.far_ref
  42.1 2.1 %collective-permute-start.1 = (f32[1024,128]{1,0:T(8,128)S(1)}, f32[1024,128]{1,0:T(8,128)S(1)}, u32[]{:S(2)}, u32[]{:S(2)}) collective-permute-start(f32[1024,128]{1,0:T(8,128)S(1)} %collective-permute-done.far_ref), channel_id=1, source_target_pairs={{0,1},{1,0},{2,3},{3,2},{4,5},{5,4},{6,7},{7,6},{8,9},{9,8},{10,11... | collective-permute-start | bytes 1572872 | tf_op jit(solution)/shard_map/ppermute | solution.py:143
  44.2 1.9 %collective-permute-start.7 = (f32[8,128]{1,0:T(8,128)S(1)}, f32[8,128]{1,0:T(8,128)S(1)}, u32[]{:S(2)}, u32[]{:S(2)}) collective-permute-start(f32[8,128]{1,0:T(8,128)S(1)} %get-tuple-element.18), channel_id=1, source_target_pairs={{0,4},{4,8},{8,12},{12,16},{16,20},{20,24},{24,28},{28,0},{1,5},{5... | collective-permute-start | bytes 12296 | tf_op jit(solution)/shard_map/ppermute | solution.py:186
  46.2 2.0 %collective-permute-done.7 = f32[8,128]{1,0:T(8,128)S(1)} collective-permute-done((f32[8,128]{1,0:T(8,128)S(1)}, f32[8,128]{1,0:T(8,128)S(1)}, u32[]{:S(2)}, u32[]{:S(2)}) %collective-permute-start.7) | collective-permute-done | bytes 4128 | tf_op jit(solution)/shard_map/ppermute | solution.py:186
  48.2 4.7 %collective-permute-start.8 = (f32[8,128]{1,0:T(8,128)S(1)}, f32[8,128]{1,0:T(8,128)S(1)}, u32[]{:S(2)}, u32[]{:S(2)}) collective-permute-start(f32[8,128]{1,0:T(8,128)S(1)} %max.9), channel_id=1, source_target_pairs={{0,8},{4,12},{8,16},{12,20},{16,24},{20,28},{24,0},{28,4},{1,9},{5... | collective-permute-start | bytes 12296 | tf_op jit(solution)/shard_map/ppermute | solution.py:186
  52.8 2.5 %collective-permute-done.8 = f32[8,128]{1,0:T(8,128)S(1)} collective-permute-done((f32[8,128]{1,0:T(8,128)S(1)}, f32[8,128]{1,0:T(8,128)S(1)}, u32[]{:S(2)}, u32[]{:S(2)}) %collective-permute-start.8) | collective-permute-done | bytes 4128 | tf_op jit(solution)/shard_map/ppermute | solution.py:186
  55.4 2.9 %collective-permute-start.9 = (f32[8,128]{1,0:T(8,128)S(1)}, f32[8,128]{1,0:T(8,128)S(1)}, u32[]{:S(2)}, u32[]{:S(2)}) collective-permute-start(f32[8,128]{1,0:T(8,128)S(1)} %max.10), channel_id=1, source_target_pairs={{0,16},{4,20},{8,24},{12,28},{16,0},{20,4},{24,8},{28,12},{1,17},{... | collective-permute-start | bytes 12296 | tf_op jit(solution)/shard_map/ppermute | solution.py:186
  58.3 1.6 %collective-permute-done.9 = f32[8,128]{1,0:T(8,128)S(1)} collective-permute-done((f32[8,128]{1,0:T(8,128)S(1)}, f32[8,128]{1,0:T(8,128)S(1)}, u32[]{:S(2)}, u32[]{:S(2)}) %collective-permute-start.9) | collective-permute-done | bytes 4128 | tf_op jit(solution)/shard_map/ppermute | solution.py:186
  59.9 0.0 collective-permute-done.6.near_ref
  59.9 0.0 collective-permute-done.5.below_ref
  59.9 0.0 copy-done.2
  59.9 1.0 %shard_map.60 = (f32[512,128]{1,0:T(8,128)S(1)}, f32[512,128]{1,0:T(8,128)S(1)}, f32[512,128]{1,0:T(8,128)S(1)}) custom-call(s32[1]{0:T(128)} %bitcast.place, f32[1024,128]{1,0:T(8,128)S(1)} %get-tuple-element.11.own_ref, f32[1024,128]{1,0:T(8,128)S(1)} %collective-permute-done.6.near_ref, f32[1024,128]{1,0:T(8,128)S(1)} %collective-permute-done.far_ref, ...), custom_call_target="tpu_custom_call" | custom-call | tf_op jit(solution)/shard_map/pallas_call | solution.py:128
  60.9 0.0 collective-permute-done.1.last_ref
  60.9 1.5 %shard_map.61 = (f32[1,512,128]{2,1,0:T(8,128)}, f32[1,512,128]{2,1,0:T(8,128)}, f32[1,512,128]{2,1,0:T(8,128)}) custom-call(s32[1]{0:T(128)} %bitcast.place, f32[1024,128]{1,0:T(8,128)S(1)} %collective-permute-done.1.last_ref, f32[512,256]{1,0:T(8,128)S(1)} %get-tuple-element.13.solved_ref, f32[512,256]{1,0:T(8,128)S(1)} %collective-permute-done.5.below_ref, ...), custom_call_target="tpu_custom_call" | custom-call | tf_op jit(solution)/shard_map/pallas_call | solution.py:128
  (3 shorter events, 0.0 us)
Async XLA Ops:
  0.6 37.8 %copy-start = (f32[2,512,128]{2,1,0:T(8,128)S(1)}, f32[2,512,128]{2,1,0:T(8,128)}, u32[]{:S(2)}) copy-start(f32[2,512,128]{2,1,0:T(8,128)} %refs_3_.1) | copy-start | bytes 1572868
  0.6 37.8 %copy-start.1 = (f32[2,512,128]{2,1,0:T(8,128)S(1)}, f32[2,512,128]{2,1,0:T(8,128)}, u32[]{:S(2)}) copy-start(f32[2,512,128]{2,1,0:T(8,128)} %refs_4_.1) | copy-start | bytes 1572868
  2.0 12.5 %collective-permute-start.3 = (f32[520,128]{1,0:T(8,128)S(1)}, f32[520,128]{1,0:T(8,128)S(1)}, u32[]{:S(2)}, u32[]{:S(2)}) collective-permute-start(f32[520,128]{1,0:T(8,128)S(1)} %get-tuple-element.12.own_ref), channel_id=1, source_target_pairs={{0,3},{1,2},{2,1},{3,0},{4,7},{5,6},{6,5},{7,4},{8,11},{9,10},{10,... | collective-permute-start | bytes 798728 | tf_op jit(solution)/shard_map/ppermute | solution.py:143
  7.1 52.8 %copy-start.2 = (f32[2,512,128]{2,1,0:T(8,128)S(1)}, f32[2,512,128]{2,1,0:T(8,128)}, u32[]{:S(2)}) copy-start(f32[2,512,128]{2,1,0:T(8,128)} %level_ref.3) | copy-start | bytes 1572868
  7.1 35.1 %collective-permute-start = (f32[1024,128]{1,0:T(8,128)S(1)}, f32[1024,128]{1,0:T(8,128)S(1)}, u32[]{:S(2)}, u32[]{:S(2)}) collective-permute-start(f32[1024,128]{1,0:T(8,128)S(1)} %get-tuple-element.11.own_ref), channel_id=1, source_target_pairs={{0,3},{1,2},{2,1},{3,0},{4,7},{5,6},{6,5},{7,4},{8,11},{9,10},{10,... | collective-permute-start | bytes 1572872 | tf_op jit(solution)/shard_map/ppermute | solution.py:143
  7.2 24.0 %collective-permute-start.2 = (f32[520,128]{1,0:T(8,128)S(1)}, f32[520,128]{1,0:T(8,128)S(1)}, u32[]{:S(2)}, u32[]{:S(2)}) collective-permute-start(f32[520,128]{1,0:T(8,128)S(1)} %get-tuple-element.12.own_ref), channel_id=1, source_target_pairs={{0,1},{1,0},{2,3},{3,2},{4,5},{5,4},{6,7},{7,6},{8,9},{9,8},{10,11... | collective-permute-start | bytes 798728 | tf_op jit(solution)/shard_map/ppermute | solution.py:143
  14.5 23.9 %collective-permute-start.4 = (f32[520,128]{1,0:T(8,128)S(1)}, f32[520,128]{1,0:T(8,128)S(1)}, u32[]{:S(2)}, u32[]{:S(2)}) collective-permute-start(f32[520,128]{1,0:T(8,128)S(1)} %collective-permute-done.3.refs_1_), channel_id=1, source_target_pairs={{0,1},{1,0},{2,3},{3,2},{4,5},{5,4},{6,7},{7,6},{8,9},{9,8},{10,11... | collective-permute-start | bytes 798728 | tf_op jit(solution)/shard_map/ppermute | solution.py:143
  31.1 28.8 %collective-permute-start.6 = (f32[1024,128]{1,0:T(8,128)S(1)}, f32[1024,128]{1,0:T(8,128)S(1)}, u32[]{:S(2)}, u32[]{:S(2)}) collective-permute-start(f32[1024,128]{1,0:T(8,128)S(1)} %get-tuple-element.11.own_ref), channel_id=1, source_target_pairs={{0,1},{1,0},{2,3},{3,2},{4,5},{5,4},{6,7},{7,6},{8,9},{9,8},{10,11... | collective-permute-start | bytes 1572872 | tf_op jit(solution)/shard_map/ppermute | solution.py:143
  40.8 19.1 %collective-permute-start.5 = (f32[512,256]{1,0:T(8,128)S(1)}, f32[512,256]{1,0:T(8,128)S(1)}, u32[]{:S(2)}, u32[]{:S(2)}) collective-permute-start(f32[512,256]{1,0:T(8,128)S(1)} %get-tuple-element.13.solved_ref), channel_id=1, source_target_pairs={{0,4},{4,8},{8,12},{12,16},{16,20},{20,24},{24,28},{1,5},{5,9},{9,... | collective-permute-start | bytes 1572872 | tf_op jit(solution)/shard_map/ppermute | solution.py:181
  42.1 18.8 %collective-permute-start.1 = (f32[1024,128]{1,0:T(8,128)S(1)}, f32[1024,128]{1,0:T(8,128)S(1)}, u32[]{:S(2)}, u32[]{:S(2)}) collective-permute-start(f32[1024,128]{1,0:T(8,128)S(1)} %collective-permute-done.far_ref), channel_id=1, source_target_pairs={{0,1},{1,0},{2,3},{3,2},{4,5},{5,4},{6,7},{7,6},{8,9},{9,8},{10,11... | collective-permute-start | bytes 1572872 | tf_op jit(solution)/shard_map/ppermute | solution.py:143
  44.2 3.9 %collective-permute-start.7 = (f32[8,128]{1,0:T(8,128)S(1)}, f32[8,128]{1,0:T(8,128)S(1)}, u32[]{:S(2)}, u32[]{:S(2)}) collective-permute-start(f32[8,128]{1,0:T(8,128)S(1)} %get-tuple-element.18), channel_id=1, source_target_pairs={{0,4},{4,8},{8,12},{12,16},{16,20},{20,24},{24,28},{28,0},{1,5},{5... | collective-permute-start | bytes 12296 | tf_op jit(solution)/shard_map/ppermute | solution.py:186
  48.2 7.2 %collective-permute-start.8 = (f32[8,128]{1,0:T(8,128)S(1)}, f32[8,128]{1,0:T(8,128)S(1)}, u32[]{:S(2)}, u32[]{:S(2)}) collective-permute-start(f32[8,128]{1,0:T(8,128)S(1)} %max.9), channel_id=1, source_target_pairs={{0,8},{4,12},{8,16},{12,20},{16,24},{20,28},{24,0},{28,4},{1,9},{5... | collective-permute-start | bytes 12296 | tf_op jit(solution)/shard_map/ppermute | solution.py:186
  55.4 4.5 %collective-permute-start.9 = (f32[8,128]{1,0:T(8,128)S(1)}, f32[8,128]{1,0:T(8,128)S(1)}, u32[]{:S(2)}, u32[]{:S(2)}) collective-permute-start(f32[8,128]{1,0:T(8,128)S(1)} %max.10), channel_id=1, source_target_pairs={{0,16},{4,20},{8,24},{12,28},{16,0},{20,4},{24,8},{28,12},{1,17},{... | collective-permute-start | bytes 12296 | tf_op jit(solution)/shard_map/ppermute | solution.py:186

commit v11 on v10

--- a/solution.py
+++ b/solution.py
@@ -33,12 +33,12 @@
     return row == lax.broadcasted_iota(jnp.int32, (rows, cols), 1)
 
 
-def prepare_kernel(place, up_ref, level_ref, down_ref, odd_ref, even_ref, square, sems):
+def prepare_kernel(place, up_ref, level_ref, down_ref, sent_ref, square, sems):
     _, phases, cols = level_ref.shape
     own = rows_of(place, 0, cols)
     sources = [level_ref.at[:, own, :], level_ref.at[1], up_ref.at[0], down_ref.at[0]]
-    top, middle = pl.ds(0, phases), pl.ds(phases, phases)
-    targets = [square, odd_ref.at[top, :], even_ref.at[top, :], even_ref.at[middle, :]]
+    starts = (0, phases + PEAK_ROWS, 2 * phases + PEAK_ROWS)
+    targets = [square, *[sent_ref.at[pl.ds(start, phases), :] for start in starts]]
     copies = [
         pltpu.make_async_copy(source, target, sems.at[at])
         for at, (source, target) in enumerate(zip(sources, targets))
@@ -47,23 +47,27 @@
         copy.start()
     copies[0].wait()
     lowest = jnp.min(jnp.where(on_diagonal(cols, cols)[None], square[...], 0.0))
-    odd_ref[pl.ds(phases, PEAK_ROWS), :] = jnp.full((PEAK_ROWS, cols), -lowest, F32)
+    sent_ref[pl.ds(phases, PEAK_ROWS), :] = jnp.full((PEAK_ROWS, cols), -lowest, F32)
     for copy in copies[1:]:
         copy.wait()
 
 
+def stack_kernel(ranges, *refs):
+    *parts, out_ref = refs
+    at = 0
+    for (first, rows), ref in zip(ranges, parts):
+        out_ref[pl.ds(at, rows), :] = ref[pl.ds(first, rows), :]
+        at += rows
+
+
 def rows_of(place, slot, cols):
     return pl.ds(pl.multiple_of((place[0] ^ DISTANCES[slot]) * cols, cols), cols)
 
 
 def solve_kernel(place, own_ref, *refs):
-    *blocks, up_ref, down_ref, solved_ref, peak_ref, inverse, high, low, s_high, s_low = refs
+    *blocks, up_ref, down_ref, solved_ref, inverse, high, low, s_high, s_low = refs
     phases, cols = inverse.shape
     blocks = [own_ref, *blocks]
-    peak = own_ref[pl.ds(phases, PEAK_ROWS), :]
-    for block in blocks[1:]:
-        peak = jnp.maximum(peak, block[pl.ds(phases, PEAK_ROWS), :])
-    peak_ref[...] = peak
     diagonal = on_diagonal(cols, cols)
     for slot, block in enumerate(blocks):
         rows, slot_cols = rows_of(place, slot, cols), pl.ds(slot * cols, cols)
@@ -92,13 +96,13 @@
     return exact_dot(left, right)
 
 
-def partial_kernel(place, own_ref, near_ref, far_ref, solved_ref, below_ref, level_ref, part_level, part_up, part_down):
+def partial_kernel(place, own_ref, near_ref, level_last_ref, far_ref, solved_ref, below_ref, level_ref, part_level, part_up, part_down):
     phases, cols = part_up.shape
     top, middle = pl.ds(0, phases), pl.ds(phases, phases)
-    blocks = (own_ref, near_ref, far_ref)
-    upper = gathered_product(place, [ref[top, :] for ref in blocks], 0, solved_ref)
+    own_up, own_down = (pl.ds(start + PEAK_ROWS, phases) for start in (phases, 2 * phases))
+    upper = gathered_product(place, [own_ref[own_up, :], near_ref[own_up, :], far_ref[top, :]], 0, solved_ref)
     part_up[...] = upper[:, :cols]
-    lower = gathered_product(place, [ref[middle, :] for ref in blocks], 0, below_ref)
+    lower = gathered_product(place, [own_ref[own_down, :], level_last_ref[middle, :], far_ref[middle, :]], 0, below_ref)
     part_down[...] = lower[:, cols:]
     part_level[...] = level_ref[0] + upper[:, cols:] + lower[:, :cols]
 
@@ -145,27 +149,43 @@
     def after(value, *earlier):
         return lax.optimization_barrier((value, *earlier))[0]
 
+    def stack(*pieces):
+        ranges_of = [(first, rows) for _, first, rows in pieces]
+        kernel = functools.partial(stack_kernel, ranges_of)
+        return call(kernel, shape(sum(rows for _, rows in ranges_of)), [VMEM] * len(pieces), *[p[0] for p in pieces])
+
     odd, even = one_level(1), one_level(0)
     in_hbm = [pltpu.with_memory_space_constraint(x, pltpu.HBM) for x in (up_blocks, level_blocks, down_blocks)]
-    odd_block, even_blocks = call(
+    sent = call(
         prepare_kernel,
-        (shape(phases + PEAK_ROWS), shape(2 * phases)),
+        shape(3 * phases + PEAK_ROWS),
         [SMEM] + [ANY] * 3,
         place,
         *in_hbm,
         scratch=[pltpu.VMEM((levels, cols, cols), F32), pltpu.SemaphoreType.DMA((4,))],
     )
-    level_far, level_near = exchanged(odd_block, 3), exchanged(odd_block, 1)
-    even_far, even_near = exchanged(even_blocks, 3), exchanged(even_blocks, 1)
-    level_last, even_last = exchanged(level_far, 1), exchanged(even_far, 1)
-
-    solved, peak = call(
+    up_row, down_row = phases + PEAK_ROWS, 2 * phases + PEAK_ROWS
+    level_far, near = exchanged(sent[:up_row], 3), exchanged(sent[:down_row], 1)
+    peak = exchanged(sent[phases:up_row], 2)
+    sent_now = after(sent, level_far, peak)
+    for part in (sent, level_far, near):
+        peak = jnp.maximum(peak, part[phases:up_row])
+    even_far = exchanged(sent_now[up_row:], 3)
+    level_last = exchanged(stack((level_far, 0, phases), (sent, down_row, phases)), 1)
+    even_last = exchanged(even_far, 1)
+    reach = 1
+    while reach < ranges:
+        route = [(i, (i + reach) % ranges) for i in range(ranges)]
+        peak = jnp.maximum(peak, lax.ppermute(peak, "lvl", route))
+        reach *= 2
+
+    solved = call(
         solve_kernel,
-        (shape(phases, 2 * cols), shape(PEAK_ROWS)),
+        shape(phases, 2 * cols),
         [SMEM, *[VMEM] * 4, odd, odd],
-        place,
-        odd_block,
-        level_near,
+        after(place, peak),
+        sent,
+        near,
         level_far,
         level_last,
         up_blocks,
@@ -180,19 +200,14 @@
     )
     from_below = lax.ppermute(solved, "lvl", [(i, i + 1) for i in range(ranges - 1)])
 
-    peak, reach = after(peak, even_far), 1
-    while reach < ranges:
-        route = [(i, (i + reach) % ranges) for i in range(ranges)]
-        peak = jnp.maximum(peak, lax.ppermute(peak, "lvl", route))
-        reach *= 2
-
     parts = call(
         partial_kernel,
         (shape(phases),) * 3,
-        [SMEM, *[VMEM] * 5, even],
+        [SMEM, *[VMEM] * 6, even],
         place,
-        even_blocks,
-        even_near,
+        sent,
+        near,
+        level_last,
         even_far,
         solved,
         from_below,

time: 62.5 us -> 62.1 us (level)
  starting transfers between devices: 34.7 us -> 17.1 us
  waiting for transfers between devices: 20.8 us -> 37.9 us
    ppermute x6, waiting for transfers between devices: 14.6 us -> 28.4 us  [exchanged(): return lax.ppermute(part, 'col', [(i, i ^ distance) for i in range(shards)])]
    ppermute x6, starting transfers between devices: 23.9 us -> 13.2 us  [exchanged(): return lax.ppermute(part, 'col', [(i, i ^ distance) for i in range(shards)])]
    ppermute x3, starting transfers between devices: 9.48 us -> 2.57 us  [per_device(): peak = jnp.maximum(peak, lax.ppermute(peak, 'lvl', route))]
    ppermute x3, waiting for transfers between devices: 6.14 us -> 9.51 us  [per_device(): peak = jnp.maximum(peak, lax.ppermute(peak, 'lvl', route))]
    pallas_call x4 -> x5, Pallas kernels: 6.16 us -> 6.1 us  [call(): pl.pallas_call(kernel, out_shape=out_shape, in_specs=in_specs, out_specs=...]
  transfers between devices with their start and end apart: 10 -> 10, of which waited for: 5 -> 7; matrix products, arithmetic and copies ran while one was open for 0% -> 0% of each run, Pallas kernels for 5% -> 6%
where the time goes in v11:
time: 62.1 us; the launch traced here: 62 us
  waiting for transfers between devices  37.9 us (61%)
  starting transfers between devices  17.1 us (28%)
  Pallas kernels  6.1 us (10%)
  between operations  0.75 us (1%)
    ppermute x6, waiting for transfers between devices, exchanged(): return lax.ppermute(part, 'col', [(i, i ^ distance) for i in range(shards)])  28.4 us
    ppermute x6, starting transfers between devices, exchanged(): return lax.ppermute(part, 'col', [(i, i ^ distance) for i in range(shards)])  13.2 us
    ppermute x3, waiting for transfers between devices, per_device(): peak = jnp.maximum(peak, lax.ppermute(peak, 'lvl', route))  9.51 us
    pallas_call x5, Pallas kernels, call(): pl.pallas_call(kernel, out_shape=out_shape, in_specs=in_specs, out_specs=...  6.1 us
    ppermute x3, starting transfers between devices, per_device(): peak = jnp.maximum(peak, lax.ppermute(peak, 'lvl', route))  2.57 us
    ppermute x1, starting transfers between devices, per_device(): lax.ppermute(solved, 'lvl', [(i, i + 1) for i in range(ranges - 1)])  1.32 us
  transfers between devices with their start and end apart: 10, of which 7 were waited for; matrix products, arithmetic and copies ran while one was open for 0% of the time, Pallas kernels for 6%

profile of v11, /device:TPU:0, one launch (start us, length us, event | category | flops | bytes accessed | tf_op | source)
XLA Modules:
  0.0 62.0 jit_solution(8813930470650591748)
XLA Ops:
  0.6 1.2 %shard_map.58.refs_1_.own_ref = f32[1544,128]{1,0:T(8,128)S(1)} custom-call(s32[1]{0:T(128)} %bitcast.place, f32[2,512,128]{2,1,0:T(8,128)} %refs_3_.1, f32[2,512,128]{2,1,0:T(8,128)} %level_ref.3, f32[2,512,128]{2,1,0:T(8,128)} %refs_4_.1), custom_call_target="tpu_custom_call" | custom-call | tf_op jit(solution)/shard_map/pallas_call | solution.py:132
  1.9 5.1 %collective-permute-start = (f32[520,128]{1,0:T(8,128)S(1)}, f32[520,128]{1,0:T(8,128)S(1)}, u32[]{:S(2)}, u32[]{:S(2)}) collective-permute-start(f32[520,128]{1,0:T(8,128)S(1)} %slice.25), channel_id=1, source_target_pairs={{0,3},{1,2},{2,1},{3,0},{4,7},{5,6},{6,5},{7,4},{8,11},{9,10},{10,... | collective-permute-start | bytes 798728 | tf_op jit(solution)/shard_map/ppermute | solution.py:147
  7.0 0.1 collective-permute-start.4
  7.1 0.6 collective-permute-start.1
  7.7 6.6 %collective-permute-done.refs_0_.refs_1_ = f32[520,128]{1,0:T(8,128)S(1)} collective-permute-done((f32[520,128]{1,0:T(8,128)S(1)}, f32[520,128]{1,0:T(8,128)S(1)}, u32[]{:S(2)}, u32[]{:S(2)}) %collective-permute-start) | collective-permute-done | bytes 266272 | tf_op jit(solution)/shard_map/ppermute | solution.py:147
  14.3 0.0 copy-start
  14.4 0.0 copy-start.1
  14.4 4.6 %collective-permute-start.8 = (f32[1024,128]{1,0:T(8,128)S(1)}, f32[1024,128]{1,0:T(8,128)S(1)}, u32[]{:S(2)}, u32[]{:S(2)}) collective-permute-start(f32[1024,128]{1,0:T(8,128)S(1)} %shard_map.59), channel_id=1, source_target_pairs={{0,1},{1,0},{2,3},{3,2},{4,5},{5,4},{6,7},{7,6},{8,9},{9,8},{10,11... | collective-permute-start | bytes 1572872 | tf_op jit(solution)/shard_map/ppermute | solution.py:147
  19.0 6.2 %collective-permute-done.1 = f32[8,128]{1,0:T(8,128)S(1)} collective-permute-done((f32[8,128]{1,0:T(8,128)S(1)}, f32[8,128]{1,0:T(8,128)S(1)}, u32[]{:S(2)}, u32[]{:S(2)}) %collective-permute-start.1) | collective-permute-done | bytes 4128 | tf_op jit(solution)/shard_map/ppermute | solution.py:147
  25.3 0.1 collective-permute-start.2
  25.4 0.0 collective-permute-done.4.refs_0_.near_ref
  25.4 0.1 collective-permute-start.5
  25.4 3.9 %collective-permute-done.5 = f32[8,128]{1,0:T(8,128)S(1)} collective-permute-done((f32[8,128]{1,0:T(8,128)S(1)}, f32[8,128]{1,0:T(8,128)S(1)}, u32[]{:S(2)}, u32[]{:S(2)}) %collective-permute-start.5) | collective-permute-done | bytes 4128 | tf_op jit(solution)/shard_map/ppermute | solution.py:179
  29.4 0.8 %collective-permute-start.6 = (f32[8,128]{1,0:T(8,128)S(1)}, f32[8,128]{1,0:T(8,128)S(1)}, u32[]{:S(2)}, u32[]{:S(2)}) collective-permute-start(f32[8,128]{1,0:T(8,128)S(1)} %max.21), channel_id=1, source_target_pairs={{0,8},{4,12},{8,16},{12,20},{16,24},{20,28},{24,0},{28,4},{1,9},{5... | collective-permute-start | bytes 12296 | tf_op jit(solution)/shard_map/ppermute | solution.py:179
  30.2 3.7 %collective-permute-done.6 = f32[8,128]{1,0:T(8,128)S(1)} collective-permute-done((f32[8,128]{1,0:T(8,128)S(1)}, f32[8,128]{1,0:T(8,128)S(1)}, u32[]{:S(2)}, u32[]{:S(2)}) %collective-permute-start.6) | collective-permute-done | bytes 4128 | tf_op jit(solution)/shard_map/ppermute | solution.py:179
  33.9 1.7 %collective-permute-start.7 = (f32[8,128]{1,0:T(8,128)S(1)}, f32[8,128]{1,0:T(8,128)S(1)}, u32[]{:S(2)}, u32[]{:S(2)}) collective-permute-start(f32[8,128]{1,0:T(8,128)S(1)} %max.22), channel_id=1, source_target_pairs={{0,16},{4,20},{8,24},{12,28},{16,0},{20,4},{24,8},{28,12},{1,17},{... | collective-permute-start | bytes 12296 | tf_op jit(solution)/shard_map/ppermute | solution.py:179
  35.6 1.9 %collective-permute-done.7 = f32[8,128]{1,0:T(8,128)S(1)} collective-permute-done((f32[8,128]{1,0:T(8,128)S(1)}, f32[8,128]{1,0:T(8,128)S(1)}, u32[]{:S(2)}, u32[]{:S(2)}) %collective-permute-start.7) | collective-permute-done | bytes 4128 | tf_op jit(solution)/shard_map/ppermute | solution.py:179
  37.5 0.0 copy-start.2
  37.5 0.0 collective-permute-done.8.refs_2_.level_last_ref
  37.5 0.0 copy-done
  37.5 0.0 copy-done.1
  37.5 2.4 %shard_map.60.solved_ref = f32[512,256]{1,0:T(8,128)S(1)} custom-call(s32[1]{0:T(128)} %bitcast.place, f32[1544,128]{1,0:T(8,128)S(1)} %shard_map.58.refs_1_.own_ref, f32[1032,128]{1,0:T(8,128)S(1)} %collective-permute-done.4.refs_0_.near_ref, f32[520,128]{1,0:T(8,128)S(1)} %collective-permute-done.refs_0_.refs_1_, ...), custom_call_target="tpu_custom_call" | custom-call | tf_op jit(solution)/shard_map/pallas_call | solution.py:132
  39.9 1.3 %collective-permute-start.9 = (f32[512,256]{1,0:T(8,128)S(1)}, f32[512,256]{1,0:T(8,128)S(1)}, u32[]{:S(2)}, u32[]{:S(2)}) collective-permute-start(f32[512,256]{1,0:T(8,128)S(1)} %shard_map.60.solved_ref), channel_id=1, source_target_pairs={{0,4},{4,8},{8,12},{12,16},{16,20},{20,24},{24,28},{1,5},{5,9},{9,... | collective-permute-start | bytes 1572872 | tf_op jit(solution)/shard_map/ppermute | solution.py:201
  41.2 6.2 %collective-permute-done.2.far_ref = f32[1024,128]{1,0:T(8,128)S(1)} collective-permute-done((f32[1024,128]{1,0:T(8,128)S(1)}, f32[1024,128]{1,0:T(8,128)S(1)}, u32[]{:S(2)}, u32[]{:S(2)}) %collective-permute-start.2) | collective-permute-done | bytes 524320 | tf_op jit(solution)/shard_map/ppermute | solution.py:147
  47.5 2.7 %collective-permute-start.3 = (f32[1024,128]{1,0:T(8,128)S(1)}, f32[1024,128]{1,0:T(8,128)S(1)}, u32[]{:S(2)}, u32[]{:S(2)}) collective-permute-start(f32[1024,128]{1,0:T(8,128)S(1)} %collective-permute-done.2.far_ref), channel_id=1, source_target_pairs={{0,1},{1,0},{2,3},{3,2},{4,5},{5,4},{6,7},{7,6},{8,9},{9,8},{10,11... | collective-permute-start | bytes 1572872 | tf_op jit(solution)/shard_map/ppermute | solution.py:147
  50.2 0.0 collective-permute-done.9.below_ref
  50.2 0.0 copy-done.2
  50.2 1.0 %shard_map.61 = (f32[512,128]{1,0:T(8,128)S(1)}, f32[512,128]{1,0:T(8,128)S(1)}, f32[512,128]{1,0:T(8,128)S(1)}) custom-call(s32[1]{0:T(128)} %bitcast.place, f32[1544,128]{1,0:T(8,128)S(1)} %shard_map.58.refs_1_.own_ref, f32[1032,128]{1,0:T(8,128)S(1)} %collective-permute-done.4.refs_0_.near_ref, ...), custom_call_target="tpu_custom_call" | custom-call | tf_op jit(solution)/shard_map/pallas_call | solution.py:132
  51.2 9.3 %collective-permute-done.3.last_ref = f32[1024,128]{1,0:T(8,128)S(1)} collective-permute-done((f32[1024,128]{1,0:T(8,128)S(1)}, f32[1024,128]{1,0:T(8,128)S(1)}, u32[]{:S(2)}, u32[]{:S(2)}) %collective-permute-start.3) | collective-permute-done | bytes 524320 | tf_op jit(solution)/shard_map/ppermute | solution.py:147
  60.5 1.4 %shard_map.62 = (f32[1,512,128]{2,1,0:T(8,128)}, f32[1,512,128]{2,1,0:T(8,128)}, f32[1,512,128]{2,1,0:T(8,128)}) custom-call(s32[1]{0:T(128)} %bitcast.place, f32[1024,128]{1,0:T(8,128)S(1)} %collective-permute-done.3.last_ref, f32[512,256]{1,0:T(8,128)S(1)} %shard_map.60.solved_ref, f32[512,256]{1,0:T(8,128)S(1)} %collective-permute-done.9.below_ref, ...), custom_call_target="tpu_custom_call" | custom-call | tf_op jit(solution)/shard_map/pallas_call | solution.py:132
  (9 shorter events, 0.1 us)
Async XLA Ops:
  1.9 12.4 %collective-permute-start = (f32[520,128]{1,0:T(8,128)S(1)}, f32[520,128]{1,0:T(8,128)S(1)}, u32[]{:S(2)}, u32[]{:S(2)}) collective-permute-start(f32[520,128]{1,0:T(8,128)S(1)} %slice.25), channel_id=1, source_target_pairs={{0,3},{1,2},{2,1},{3,0},{4,7},{5,6},{6,5},{7,4},{8,11},{9,10},{10,... | collective-permute-start | bytes 798728 | tf_op jit(solution)/shard_map/ppermute | solution.py:147
  7.0 18.3 %collective-permute-start.4 = (f32[1032,128]{1,0:T(8,128)S(1)}, f32[1032,128]{1,0:T(8,128)S(1)}, u32[]{:S(2)}, u32[]{:S(2)}) collective-permute-start(f32[1032,128]{1,0:T(8,128)S(1)} %slice.28), channel_id=1, source_target_pairs={{0,1},{1,0},{2,3},{3,2},{4,5},{5,4},{6,7},{7,6},{8,9},{9,8},{10,11... | collective-permute-start | bytes 1585160 | tf_op jit(solution)/shard_map/ppermute | solution.py:147
  7.1 18.1 %collective-permute-start.1 = (f32[8,128]{1,0:T(8,128)S(1)}, f32[8,128]{1,0:T(8,128)S(1)}, u32[]{:S(2)}, u32[]{:S(2)}) collective-permute-start(f32[8,128]{1,0:T(8,128)S(1)} %slice.26), channel_id=1, source_target_pairs={{0,2},{1,3},{2,0},{3,1},{4,6},{5,7},{6,4},{7,5},{8,10},{9,11},{10,... | collective-permute-start | bytes 12296 | tf_op jit(solution)/shard_map/ppermute | solution.py:147
  14.3 23.1 %copy-start = (f32[2,512,128]{2,1,0:T(8,128)S(1)}, f32[2,512,128]{2,1,0:T(8,128)}, u32[]{:S(2)}) copy-start(f32[2,512,128]{2,1,0:T(8,128)} %refs_3_.1) | copy-start | bytes 1572868
  14.4 23.1 %copy-start.1 = (f32[2,512,128]{2,1,0:T(8,128)S(1)}, f32[2,512,128]{2,1,0:T(8,128)}, u32[]{:S(2)}) copy-start(f32[2,512,128]{2,1,0:T(8,128)} %refs_4_.1) | copy-start | bytes 1572868
  14.4 23.1 %collective-permute-start.8 = (f32[1024,128]{1,0:T(8,128)S(1)}, f32[1024,128]{1,0:T(8,128)S(1)}, u32[]{:S(2)}, u32[]{:S(2)}) collective-permute-start(f32[1024,128]{1,0:T(8,128)S(1)} %shard_map.59), channel_id=1, source_target_pairs={{0,1},{1,0},{2,3},{3,2},{4,5},{5,4},{6,7},{7,6},{8,9},{9,8},{10,11... | collective-permute-start | bytes 1572872 | tf_op jit(solution)/shard_map/ppermute | solution.py:147
  25.3 22.2 %collective-permute-start.2 = (f32[1024,128]{1,0:T(8,128)S(1)}, f32[1024,128]{1,0:T(8,128)S(1)}, u32[]{:S(2)}, u32[]{:S(2)}) collective-permute-start(f32[1024,128]{1,0:T(8,128)S(1)} %slice.21), channel_id=1, source_target_pairs={{0,3},{1,2},{2,1},{3,0},{4,7},{5,6},{6,5},{7,4},{8,11},{9,10},{10,... | collective-permute-start | bytes 1572872 | tf_op jit(solution)/shard_map/ppermute | solution.py:147
  25.4 4.0 %collective-permute-start.5 = (f32[8,128]{1,0:T(8,128)S(1)}, f32[8,128]{1,0:T(8,128)S(1)}, u32[]{:S(2)}, u32[]{:S(2)}) collective-permute-start(f32[8,128]{1,0:T(8,128)S(1)} %slice_maximum_fusion), channel_id=1, source_target_pairs={{0,4},{4,8},{8,12},{12,16},{16,20},{20,24},{24,28},{28,0},{1,5},{5... | collective-permute-start | bytes 12296 | tf_op jit(solution)/shard_map/ppermute | solution.py:179
  29.4 4.5 %collective-permute-start.6 = (f32[8,128]{1,0:T(8,128)S(1)}, f32[8,128]{1,0:T(8,128)S(1)}, u32[]{:S(2)}, u32[]{:S(2)}) collective-permute-start(f32[8,128]{1,0:T(8,128)S(1)} %max.21), channel_id=1, source_target_pairs={{0,8},{4,12},{8,16},{12,20},{16,24},{20,28},{24,0},{28,4},{1,9},{5... | collective-permute-start | bytes 12296 | tf_op jit(solution)/shard_map/ppermute | solution.py:179
  33.9 3.6 %collective-permute-start.7 = (f32[8,128]{1,0:T(8,128)S(1)}, f32[8,128]{1,0:T(8,128)S(1)}, u32[]{:S(2)}, u32[]{:S(2)}) collective-permute-start(f32[8,128]{1,0:T(8,128)S(1)} %max.22), channel_id=1, source_target_pairs={{0,16},{4,20},{8,24},{12,28},{16,0},{20,4},{24,8},{28,12},{1,17},{... | collective-permute-start | bytes 12296 | tf_op jit(solution)/shard_map/ppermute | solution.py:179
  37.5 12.7 %copy-start.2 = (f32[2,512,128]{2,1,0:T(8,128)S(1)}, f32[2,512,128]{2,1,0:T(8,128)}, u32[]{:S(2)}) copy-start(f32[2,512,128]{2,1,0:T(8,128)} %level_ref.3) | copy-start | bytes 1572868
  39.9 10.3 %collective-permute-start.9 = (f32[512,256]{1,0:T(8,128)S(1)}, f32[512,256]{1,0:T(8,128)S(1)}, u32[]{:S(2)}, u32[]{:S(2)}) collective-permute-start(f32[512,256]{1,0:T(8,128)S(1)} %shard_map.60.solved_ref), channel_id=1, source_target_pairs={{0,4},{4,8},{8,12},{12,16},{16,20},{20,24},{24,28},{1,5},{5,9},{9,... | collective-permute-start | bytes 1572872 | tf_op jit(solution)/shard_map/ppermute | solution.py:201
  47.5 13.0 %collective-permute-start.3 = (f32[1024,128]{1,0:T(8,128)S(1)}, f32[1024,128]{1,0:T(8,128)S(1)}, u32[]{:S(2)}, u32[]{:S(2)}) collective-permute-start(f32[1024,128]{1,0:T(8,128)S(1)} %collective-permute-done.2.far_ref), channel_id=1, source_target_pairs={{0,1},{1,0},{2,3},{3,2},{4,5},{5,4},{6,7},{7,6},{8,9},{9,8},{10,11... | collective-permute-start | bytes 1572872 | tf_op jit(solution)/shard_map/ppermute | solution.py:147

commit v12 on v11

--- a/solution.py
+++ b/solution.py
@@ -110,7 +110,7 @@
 def output_kernel(place, last_ref, solved_ref, below_ref, *refs):
     part_level, part_up, part_down, peak_ref, new_level, new_up, new_down = refs
     phases, cols = part_up.shape
-    scale = 1.0 / peak_ref[0:1, :]
+    scale = 1.0 / jnp.maximum(peak_ref[...], last_ref[pl.ds(2 * phases, PEAK_ROWS), :])[0:1, :]
     last = len(DISTANCES) - 1
     upper = gathered_product(place, [last_ref[pl.ds(0, phases), :]], last, solved_ref)
     new_up[0] = (part_up[...] + upper[:, :cols]) * scale
@@ -166,18 +166,15 @@
     )
     up_row, down_row = phases + PEAK_ROWS, 2 * phases + PEAK_ROWS
     level_far, near = exchanged(sent[:up_row], 3), exchanged(sent[:down_row], 1)
-    peak = exchanged(sent[phases:up_row], 2)
-    sent_now = after(sent, level_far, peak)
-    for part in (sent, level_far, near):
-        peak = jnp.maximum(peak, part[phases:up_row])
-    even_far = exchanged(sent_now[up_row:], 3)
+    even_far = exchanged(after(sent, level_far)[up_row:], 3)
     level_last = exchanged(stack((level_far, 0, phases), (sent, down_row, phases)), 1)
-    even_last = exchanged(even_far, 1)
+    peak = jnp.maximum(sent[phases:up_row], level_far[phases:])
     reach = 1
     while reach < ranges:
         route = [(i, (i + reach) % ranges) for i in range(ranges)]
         peak = jnp.maximum(peak, lax.ppermute(peak, "lvl", route))
         reach *= 2
+    even_last = exchanged(stack((even_far, 0, 2 * phases), (peak, 0, PEAK_ROWS)), 1)
 
     solved = call(
         solve_kernel,

time: 62.1 us -> 63.6 us (1.024)
  the two profiles are of different devices: /device:TPU:0 before, /device:TPU:12 now
where the time goes in v12:
time: 63.6 us; the launch traced here: 63.5 us
  waiting for transfers between devices  47.3 us (74%)
  starting transfers between devices  9.04 us (14%)
  Pallas kernels  6.21 us (10%)
  between operations  0.75 us (1%)
    ppermute x5, waiting for transfers between devices, exchanged(): return lax.ppermute(part, 'col', [(i, i ^ distance) for i in range(shards)])  26.9 us
    ppermute x3, waiting for transfers between devices, per_device(): peak = jnp.maximum(peak, lax.ppermute(peak, 'lvl', route))  10.9 us
    ppermute x1, waiting for transfers between devices, per_device(): lax.ppermute(solved, 'lvl', [(i, i + 1) for i in range(ranges - 1)])  9.47 us
    pallas_call x6, Pallas kernels, call(): pl.pallas_call(kernel, out_shape=out_shape, in_specs=in_specs, out_specs=...  6.21 us
    ppermute x5, starting transfers between devices, exchanged(): return lax.ppermute(part, 'col', [(i, i ^ distance) for i in range(shards)])  5.97 us
    ppermute x1, starting transfers between devices, per_device(): lax.ppermute(solved, 'lvl', [(i, i + 1) for i in range(ranges - 1)])  1.92 us
  transfers between devices with their start and end apart: 9, of which 7 were waited for; matrix products, arithmetic and copies ran while one was open for 0% of the time, Pallas kernels for 6%

profile of v12, /device:TPU:12, one launch (start us, length us, event | category | flops | bytes accessed | tf_op | source)
XLA Modules:
  0.0 63.5 jit_solution(14745835344635293653)
XLA Ops:
  0.6 1.2 %shard_map.58.refs_1_.own_ref = f32[1544,128]{1,0:T(8,128)S(1)} custom-call(s32[1]{0:T(128)} %bitcast.place, f32[2,512,128]{2,1,0:T(8,128)} %refs_3_.1, f32[2,512,128]{2,1,0:T(8,128)} %level_ref.3, f32[2,512,128]{2,1,0:T(8,128)} %refs_4_.1), custom_call_target="tpu_custom_call" | custom-call | tf_op jit(solution)/shard_map/pallas_call | solution.py:132
  1.9 1.6 %collective-permute-start = (f32[520,128]{1,0:T(8,128)S(1)}, f32[520,128]{1,0:T(8,128)S(1)}, u32[]{:S(2)}, u32[]{:S(2)}) collective-permute-start(f32[520,128]{1,0:T(8,128)S(1)} %slice.20), channel_id=1, source_target_pairs={{0,3},{1,2},{2,1},{3,0},{4,7},{5,6},{6,5},{7,4},{8,11},{9,10},{10,... | collective-permute-start | bytes 798728 | tf_op jit(solution)/shard_map/ppermute | solution.py:147
  3.6 2.5 %collective-permute-start.6 = (f32[1032,128]{1,0:T(8,128)S(1)}, f32[1032,128]{1,0:T(8,128)S(1)}, u32[]{:S(2)}, u32[]{:S(2)}) collective-permute-start(f32[1032,128]{1,0:T(8,128)S(1)} %slice.23), channel_id=1, source_target_pairs={{0,1},{1,0},{2,3},{3,2},{4,5},{5,4},{6,7},{7,6},{8,9},{9,8},{10,11... | collective-permute-start | bytes 1585160 | tf_op jit(solution)/shard_map/ppermute | solution.py:147
  6.1 9.7 %collective-permute-done.refs_0_.refs_1_ = f32[520,128]{1,0:T(8,128)S(1)} collective-permute-done((f32[520,128]{1,0:T(8,128)S(1)}, f32[520,128]{1,0:T(8,128)S(1)}, u32[]{:S(2)}, u32[]{:S(2)}) %collective-permute-start) | collective-permute-done | bytes 266272 | tf_op jit(solution)/shard_map/ppermute | solution.py:147
  15.8 1.6 %collective-permute-start.1 = (f32[1024,128]{1,0:T(8,128)S(1)}, f32[1024,128]{1,0:T(8,128)S(1)}, u32[]{:S(2)}, u32[]{:S(2)}) collective-permute-start(f32[1024,128]{1,0:T(8,128)S(1)} %slice.16), channel_id=1, source_target_pairs={{0,3},{1,2},{2,1},{3,0},{4,7},{5,6},{6,5},{7,4},{8,11},{9,10},{10,... | collective-permute-start | bytes 1572872 | tf_op jit(solution)/shard_map/ppermute | solution.py:147
  17.5 0.1 collective-permute-start.7
  17.6 0.1 collective-permute-start.2
  17.7 3.9 %collective-permute-done.2 = f32[8,128]{1,0:T(8,128)S(1)} collective-permute-done((f32[8,128]{1,0:T(8,128)S(1)}, f32[8,128]{1,0:T(8,128)S(1)}, u32[]{:S(2)}, u32[]{:S(2)}) %collective-permute-start.2) | collective-permute-done | bytes 4128 | tf_op jit(solution)/shard_map/ppermute | solution.py:175
  21.6 0.6 collective-permute-start.3
  22.2 3.9 %collective-permute-done.3 = f32[8,128]{1,0:T(8,128)S(1)} collective-permute-done((f32[8,128]{1,0:T(8,128)S(1)}, f32[8,128]{1,0:T(8,128)S(1)}, u32[]{:S(2)}, u32[]{:S(2)}) %collective-permute-start.3) | collective-permute-done | bytes 4128 | tf_op jit(solution)/shard_map/ppermute | solution.py:175
  26.1 0.5 collective-permute-start.4
  26.6 3.1 %collective-permute-done.4 = f32[8,128]{1,0:T(8,128)S(1)} collective-permute-done((f32[8,128]{1,0:T(8,128)S(1)}, f32[8,128]{1,0:T(8,128)S(1)}, u32[]{:S(2)}, u32[]{:S(2)}) %collective-permute-start.4) | collective-permute-done | bytes 4128 | tf_op jit(solution)/shard_map/ppermute | solution.py:175
  29.7 0.0 copy-start
  29.7 0.0 copy-start.1
  29.7 10.4 %collective-permute-done.1.refs_0_.far_ref = f32[1024,128]{1,0:T(8,128)S(1)} collective-permute-done((f32[1024,128]{1,0:T(8,128)S(1)}, f32[1024,128]{1,0:T(8,128)S(1)}, u32[]{:S(2)}, u32[]{:S(2)}) %collective-permute-start.1) | collective-permute-done | bytes 524320 | tf_op jit(solution)/shard_map/ppermute | solution.py:147
  40.1 0.0 copy-start.2
  40.2 0.1 collective-permute-start.5
  40.2 0.0 collective-permute-done.6.refs_0_.near_ref
  40.2 6.9 %collective-permute-done.7.refs_2_.level_last_ref = f32[1024,128]{1,0:T(8,128)S(1)} collective-permute-done((f32[1024,128]{1,0:T(8,128)S(1)}, f32[1024,128]{1,0:T(8,128)S(1)}, u32[]{:S(2)}, u32[]{:S(2)}) %collective-permute-start.7) | collective-permute-done | bytes 524320 | tf_op jit(solution)/shard_map/ppermute | solution.py:147
  47.1 0.0 copy-done
  47.1 0.0 copy-done.1
  47.1 2.4 %shard_map.61.solved_ref = f32[512,256]{1,0:T(8,128)S(1)} custom-call(s32[1]{0:T(128)} %bitcast.place, f32[1544,128]{1,0:T(8,128)S(1)} %shard_map.58.refs_1_.own_ref, f32[1032,128]{1,0:T(8,128)S(1)} %collective-permute-done.6.refs_0_.near_ref, f32[520,128]{1,0:T(8,128)S(1)} %collective-permute-done.refs_0_.refs_1_, ...), custom_call_target="tpu_custom_call" | custom-call | tf_op jit(solution)/shard_map/pallas_call | solution.py:132
  49.5 1.9 %collective-permute-start.8 = (f32[512,256]{1,0:T(8,128)S(1)}, f32[512,256]{1,0:T(8,128)S(1)}, u32[]{:S(2)}, u32[]{:S(2)}) collective-permute-start(f32[512,256]{1,0:T(8,128)S(1)} %shard_map.61.solved_ref), channel_id=1, source_target_pairs={{0,4},{4,8},{8,12},{12,16},{16,20},{20,24},{24,28},{1,5},{5,9},{9,... | collective-permute-start | bytes 1572872 | tf_op jit(solution)/shard_map/ppermute | solution.py:198
  51.5 9.5 %collective-permute-done.8.below_ref = f32[512,256]{1,0:T(8,128)S(1)} collective-permute-done((f32[512,256]{1,0:T(8,128)S(1)}, f32[512,256]{1,0:T(8,128)S(1)}, u32[]{:S(2)}, u32[]{:S(2)}) %collective-permute-start.8) | collective-permute-done | bytes 524320 | tf_op jit(solution)/shard_map/ppermute | solution.py:198
  60.9 0.0 copy-done.2
  60.9 1.0 %shard_map.62 = (f32[512,128]{1,0:T(8,128)S(1)}, f32[512,128]{1,0:T(8,128)S(1)}, f32[512,128]{1,0:T(8,128)S(1)}) custom-call(s32[1]{0:T(128)} %bitcast.place, f32[1544,128]{1,0:T(8,128)S(1)} %shard_map.58.refs_1_.own_ref, f32[1032,128]{1,0:T(8,128)S(1)} %collective-permute-done.6.refs_0_.near_ref, ...), custom_call_target="tpu_custom_call" | custom-call | tf_op jit(solution)/shard_map/pallas_call | solution.py:132
  62.0 0.0 collective-permute-done.5.last_ref
  62.0 1.5 %shard_map.63 = (f32[1,512,128]{2,1,0:T(8,128)}, f32[1,512,128]{2,1,0:T(8,128)}, f32[1,512,128]{2,1,0:T(8,128)}) custom-call(s32[1]{0:T(128)} %bitcast.place, f32[1032,128]{1,0:T(8,128)S(1)} %collective-permute-done.5.last_ref, f32[512,256]{1,0:T(8,128)S(1)} %shard_map.61.solved_ref, f32[512,256]{1,0:T(8,128)S(1)} %collective-permute-done.8.below_ref, ...), custom_call_target="tpu_custom_call" | custom-call | tf_op jit(solution)/shard_map/pallas_call | solution.py:132
  (9 shorter events, 0.2 us)
Async XLA Ops:
  1.9 13.9 %collective-permute-start = (f32[520,128]{1,0:T(8,128)S(1)}, f32[520,128]{1,0:T(8,128)S(1)}, u32[]{:S(2)}, u32[]{:S(2)}) collective-permute-start(f32[520,128]{1,0:T(8,128)S(1)} %slice.20), channel_id=1, source_target_pairs={{0,3},{1,2},{2,1},{3,0},{4,7},{5,6},{6,5},{7,4},{8,11},{9,10},{10,... | collective-permute-start | bytes 798728 | tf_op jit(solution)/shard_map/ppermute | solution.py:147
  3.6 36.7 %collective-permute-start.6 = (f32[1032,128]{1,0:T(8,128)S(1)}, f32[1032,128]{1,0:T(8,128)S(1)}, u32[]{:S(2)}, u32[]{:S(2)}) collective-permute-start(f32[1032,128]{1,0:T(8,128)S(1)} %slice.23), channel_id=1, source_target_pairs={{0,1},{1,0},{2,3},{3,2},{4,5},{5,4},{6,7},{7,6},{8,9},{9,8},{10,11... | collective-permute-start | bytes 1585160 | tf_op jit(solution)/shard_map/ppermute | solution.py:147
  15.8 24.3 %collective-permute-start.1 = (f32[1024,128]{1,0:T(8,128)S(1)}, f32[1024,128]{1,0:T(8,128)S(1)}, u32[]{:S(2)}, u32[]{:S(2)}) collective-permute-start(f32[1024,128]{1,0:T(8,128)S(1)} %slice.16), channel_id=1, source_target_pairs={{0,3},{1,2},{2,1},{3,0},{4,7},{5,6},{6,5},{7,4},{8,11},{9,10},{10,... | collective-permute-start | bytes 1572872 | tf_op jit(solution)/shard_map/ppermute | solution.py:147
  17.5 29.6 %collective-permute-start.7 = (f32[1024,128]{1,0:T(8,128)S(1)}, f32[1024,128]{1,0:T(8,128)S(1)}, u32[]{:S(2)}, u32[]{:S(2)}) collective-permute-start(f32[1024,128]{1,0:T(8,128)S(1)} %shard_map.60), channel_id=1, source_target_pairs={{0,1},{1,0},{2,3},{3,2},{4,5},{5,4},{6,7},{7,6},{8,9},{9,8},{10,11... | collective-permute-start | bytes 1572872 | tf_op jit(solution)/shard_map/ppermute | solution.py:147
  17.6 4.0 %collective-permute-start.2 = (f32[8,128]{1,0:T(8,128)S(1)}, f32[8,128]{1,0:T(8,128)S(1)}, u32[]{:S(2)}, u32[]{:S(2)}) collective-permute-start(f32[8,128]{1,0:T(8,128)S(1)} %slice_maximum_fusion), channel_id=1, source_target_pairs={{0,4},{4,8},{8,12},{12,16},{16,20},{20,24},{24,28},{28,0},{1,5},{5... | collective-permute-start | bytes 12296 | tf_op jit(solution)/shard_map/ppermute | solution.py:175
  21.6 4.5 %collective-permute-start.3 = (f32[8,128]{1,0:T(8,128)S(1)}, f32[8,128]{1,0:T(8,128)S(1)}, u32[]{:S(2)}, u32[]{:S(2)}) collective-permute-start(f32[8,128]{1,0:T(8,128)S(1)} %max.13), channel_id=1, source_target_pairs={{0,8},{4,12},{8,16},{12,20},{16,24},{20,28},{24,0},{28,4},{1,9},{5... | collective-permute-start | bytes 12296 | tf_op jit(solution)/shard_map/ppermute | solution.py:175
  26.1 3.6 %collective-permute-start.4 = (f32[8,128]{1,0:T(8,128)S(1)}, f32[8,128]{1,0:T(8,128)S(1)}, u32[]{:S(2)}, u32[]{:S(2)}) collective-permute-start(f32[8,128]{1,0:T(8,128)S(1)} %max.14), channel_id=1, source_target_pairs={{0,16},{4,20},{8,24},{12,28},{16,0},{20,4},{24,8},{28,12},{1,17},{... | collective-permute-start | bytes 12296 | tf_op jit(solution)/shard_map/ppermute | solution.py:175
  29.7 17.4 %copy-start = (f32[2,512,128]{2,1,0:T(8,128)S(1)}, f32[2,512,128]{2,1,0:T(8,128)}, u32[]{:S(2)}) copy-start(f32[2,512,128]{2,1,0:T(8,128)} %refs_3_.1) | copy-start | bytes 1572868
  29.7 17.4 %copy-start.1 = (f32[2,512,128]{2,1,0:T(8,128)S(1)}, f32[2,512,128]{2,1,0:T(8,128)}, u32[]{:S(2)}) copy-start(f32[2,512,128]{2,1,0:T(8,128)} %refs_4_.1) | copy-start | bytes 1572868
  40.1 20.8 %copy-start.2 = (f32[2,512,128]{2,1,0:T(8,128)S(1)}, f32[2,512,128]{2,1,0:T(8,128)}, u32[]{:S(2)}) copy-start(f32[2,512,128]{2,1,0:T(8,128)} %level_ref.3) | copy-start | bytes 1572868
  40.2 21.8 %collective-permute-start.5 = (f32[1032,128]{1,0:T(8,128)S(1)}, f32[1032,128]{1,0:T(8,128)S(1)}, u32[]{:S(2)}, u32[]{:S(2)}) collective-permute-start(f32[1032,128]{1,0:T(8,128)S(1)} %shard_map.59), channel_id=1, source_target_pairs={{0,1},{1,0},{2,3},{3,2},{4,5},{5,4},{6,7},{7,6},{8,9},{9,8},{10,11... | collective-permute-start | bytes 1585160 | tf_op jit(solution)/shard_map/ppermute | solution.py:147
  49.5 11.4 %collective-permute-start.8 = (f32[512,256]{1,0:T(8,128)S(1)}, f32[512,256]{1,0:T(8,128)S(1)}, u32[]{:S(2)}, u32[]{:S(2)}) collective-permute-start(f32[512,256]{1,0:T(8,128)S(1)} %shard_map.61.solved_ref), channel_id=1, source_target_pairs={{0,4},{4,8},{8,12},{12,16},{16,20},{20,24},{24,28},{1,5},{5,9},{9,... | collective-permute-start | bytes 1572872 | tf_op jit(solution)/shard_map/ppermute | solution.py:198

commit v13 on v12

--- a/solution.py
+++ b/solution.py
@@ -9,6 +9,7 @@
 
 SWEEPS = 2
 PEAK_ROWS = 8
+PAD_ROWS = 24
 DISTANCES = (0, 1, 3, 2)
 F32 = jnp.float32
 BF16 = jnp.bfloat16
@@ -96,13 +97,13 @@
     return exact_dot(left, right)
 
 
-def partial_kernel(place, own_ref, near_ref, level_last_ref, far_ref, solved_ref, below_ref, level_ref, part_level, part_up, part_down):
+def partial_kernel(place, own_ref, near_ref, down_near_ref, far_ref, solved_ref, below_ref, level_ref, part_level, part_up, part_down):
     phases, cols = part_up.shape
     top, middle = pl.ds(0, phases), pl.ds(phases, phases)
     own_up, own_down = (pl.ds(start + PEAK_ROWS, phases) for start in (phases, 2 * phases))
     upper = gathered_product(place, [own_ref[own_up, :], near_ref[own_up, :], far_ref[top, :]], 0, solved_ref)
     part_up[...] = upper[:, :cols]
-    lower = gathered_product(place, [own_ref[own_down, :], level_last_ref[middle, :], far_ref[middle, :]], 0, below_ref)
+    lower = gathered_product(place, [own_ref[own_down, :], down_near_ref[...], far_ref[middle, :]], 0, below_ref)
     part_down[...] = lower[:, cols:]
     part_level[...] = level_ref[0] + upper[:, cols:] + lower[:, :cols]
 
@@ -165,16 +166,18 @@
         scratch=[pltpu.VMEM((levels, cols, cols), F32), pltpu.SemaphoreType.DMA((4,))],
     )
     up_row, down_row = phases + PEAK_ROWS, 2 * phases + PEAK_ROWS
-    level_far, near = exchanged(sent[:up_row], 3), exchanged(sent[:down_row], 1)
+    level_far, near = exchanged(sent[: up_row + PAD_ROWS], 3), exchanged(sent[:down_row], 1)
+    level_last = exchanged(level_far, 1)
     even_far = exchanged(after(sent, level_far)[up_row:], 3)
-    level_last = exchanged(stack((level_far, 0, phases), (sent, down_row, phases)), 1)
-    peak = jnp.maximum(sent[phases:up_row], level_far[phases:])
-    reach = 1
+    peak = jnp.maximum(sent[phases:up_row], level_far[phases:up_row])
+    peaks, reach = [peak], 1
     while reach < ranges:
         route = [(i, (i + reach) % ranges) for i in range(ranges)]
-        peak = jnp.maximum(peak, lax.ppermute(peak, "lvl", route))
+        peaks.append(jnp.maximum(peaks[-1], lax.ppermute(peaks[-1], "lvl", route)))
         reach *= 2
-    even_last = exchanged(stack((even_far, 0, 2 * phases), (peak, 0, PEAK_ROWS)), 1)
+    peak = peaks[-1]
+    down_near = exchanged(after(sent, peaks[1])[down_row:], 1)
+    even_last = exchanged(stack((after(even_far, down_near), 0, 2 * phases), (peak, 0, PEAK_ROWS)), 1)
 
     solved = call(
         solve_kernel,
@@ -204,7 +207,7 @@
         place,
         sent,
         near,
-        level_last,
+        down_near,
         even_far,
         solved,
         from_below,

time: 63.6 us -> 64.8 us (1.019)
  the two profiles are of different devices: /device:TPU:12 before, /device:TPU:4 now
where the time goes in v13:
time: 64.8 us; the launch traced here: 64.7 us
  waiting for transfers between devices  42.7 us (66%)
  starting transfers between devices  14.9 us (23%)
  Pallas kernels  6.18 us (10%)
  between operations  0.74 us (1%)
    ppermute x6, waiting for transfers between devices, exchanged(): return lax.ppermute(part, 'col', [(i, i ^ distance) for i in range(shards)])  22.3 us
    ppermute x6, starting transfers between devices, exchanged(): return lax.ppermute(part, 'col', [(i, i ^ distance) for i in range(shards)])  11.8 us
    ppermute x3, waiting for transfers between devices, per_device(): peaks.append(jnp.maximum(peaks[-1], lax.ppermute(peaks[-1], 'lvl', route)))  10.9 us
    ppermute x1, waiting for transfers between devices, per_device(): lax.ppermute(solved, 'lvl', [(i, i + 1) for i in range(ranges - 1)])  9.47 us
    pallas_call x5, Pallas kernels, call(): pl.pallas_call(kernel, out_shape=out_shape, in_specs=in_specs, out_specs=...  6.18 us
    ppermute x1, starting transfers between devices, per_device(): lax.ppermute(solved, 'lvl', [(i, i + 1) for i in range(ranges - 1)])  1.92 us
  transfers between devices with their start and end apart: 10, of which 6 were waited for; matrix products, arithmetic and copies ran while one was open for 0% of the time, Pallas kernels for 5%

profile of v13, /device:TPU:4, one launch (start us, length us, event | category | flops | bytes accessed | tf_op | source)
XLA Modules:
  0.0 64.7 jit_solution(17100492808917882446)
XLA Ops:
  0.6 1.2 %shard_map.58.own_ref = f32[1544,128]{1,0:T(8,128)S(1)} custom-call(s32[1]{0:T(128)} %bitcast.place, f32[2,512,128]{2,1,0:T(8,128)} %refs_3_.1, f32[2,512,128]{2,1,0:T(8,128)} %level_ref.3, f32[2,512,128]{2,1,0:T(8,128)} %refs_4_.1), custom_call_target="tpu_custom_call" | custom-call | tf_op jit(solution)/shard_map/pallas_call | solution.py:133
  1.9 3.7 %collective-permute-start = (f32[544,128]{1,0:T(8,128)S(1)}, f32[544,128]{1,0:T(8,128)S(1)}, u32[]{:S(2)}, u32[]{:S(2)}) collective-permute-start(f32[544,128]{1,0:T(8,128)S(1)} %slice.24), channel_id=1, source_target_pairs={{0,3},{1,2},{2,1},{3,0},{4,7},{5,6},{6,5},{7,4},{8,11},{9,10},{10,... | collective-permute-start | bytes 835592 | tf_op jit(solution)/shard_map/ppermute | solution.py:148
  5.6 0.1 collective-permute-start.7
  5.7 7.7 %collective-permute-done.refs_1_ = f32[544,128]{1,0:T(8,128)S(1)} collective-permute-done((f32[544,128]{1,0:T(8,128)S(1)}, f32[544,128]{1,0:T(8,128)S(1)}, u32[]{:S(2)}, u32[]{:S(2)}) %collective-permute-start) | collective-permute-done | bytes 278560 | tf_op jit(solution)/shard_map/ppermute | solution.py:148
  13.4 3.6 %collective-permute-start.1 = (f32[1024,128]{1,0:T(8,128)S(1)}, f32[1024,128]{1,0:T(8,128)S(1)}, u32[]{:S(2)}, u32[]{:S(2)}) collective-permute-start(f32[1024,128]{1,0:T(8,128)S(1)} %slice.19), channel_id=1, source_target_pairs={{0,3},{1,2},{2,1},{3,0},{4,7},{5,6},{6,5},{7,4},{8,11},{9,10},{10,... | collective-permute-start | bytes 1572872 | tf_op jit(solution)/shard_map/ppermute | solution.py:148
  17.0 2.6 %collective-permute-start.8 = (f32[544,128]{1,0:T(8,128)S(1)}, f32[544,128]{1,0:T(8,128)S(1)}, u32[]{:S(2)}, u32[]{:S(2)}) collective-permute-start(f32[544,128]{1,0:T(8,128)S(1)} %collective-permute-done.refs_1_), channel_id=1, source_target_pairs={{0,1},{1,0},{2,3},{3,2},{4,5},{5,4},{6,7},{7,6},{8,9},{9,8},{10,11... | collective-permute-start | bytes 835592 | tf_op jit(solution)/shard_map/ppermute | solution.py:148
  19.6 0.0 collective-permute-start.2
  19.6 3.9 %collective-permute-done.2 = f32[8,128]{1,0:T(8,128)S(1)} collective-permute-done((f32[8,128]{1,0:T(8,128)S(1)}, f32[8,128]{1,0:T(8,128)S(1)}, u32[]{:S(2)}, u32[]{:S(2)}) %collective-permute-start.2) | collective-permute-done | bytes 4128 | tf_op jit(solution)/shard_map/ppermute | solution.py:176
  23.5 0.1 collective-permute-start.3
  23.6 0.6 collective-permute-start.4
  24.3 3.9 %collective-permute-done.4 = f32[8,128]{1,0:T(8,128)S(1)} collective-permute-done((f32[8,128]{1,0:T(8,128)S(1)}, f32[8,128]{1,0:T(8,128)S(1)}, u32[]{:S(2)}, u32[]{:S(2)}) %collective-permute-start.4) | collective-permute-done | bytes 4128 | tf_op jit(solution)/shard_map/ppermute | solution.py:176
  28.2 0.5 collective-permute-start.5
  28.7 3.1 %collective-permute-done.5 = f32[8,128]{1,0:T(8,128)S(1)} collective-permute-done((f32[8,128]{1,0:T(8,128)S(1)}, f32[8,128]{1,0:T(8,128)S(1)}, u32[]{:S(2)}, u32[]{:S(2)}) %collective-permute-start.5) | collective-permute-done | bytes 4128 | tf_op jit(solution)/shard_map/ppermute | solution.py:176
  31.8 0.0 copy-start
  31.8 0.0 copy-start.1
  31.8 14.7 %collective-permute-done.3.down_near_ref = f32[512,128]{1,0:T(8,128)S(1)} collective-permute-done((f32[512,128]{1,0:T(8,128)S(1)}, f32[512,128]{1,0:T(8,128)S(1)}, u32[]{:S(2)}, u32[]{:S(2)}) %collective-permute-start.3) | collective-permute-done | bytes 262176 | tf_op jit(solution)/shard_map/ppermute | solution.py:148
  46.5 0.0 collective-permute-done.1.refs_0_.far_ref
  46.5 0.0 copy-start.2
  46.5 1.8 %collective-permute-start.6 = (f32[1032,128]{1,0:T(8,128)S(1)}, f32[1032,128]{1,0:T(8,128)S(1)}, u32[]{:S(2)}, u32[]{:S(2)}) collective-permute-start(f32[1032,128]{1,0:T(8,128)S(1)} %shard_map.59), channel_id=1, source_target_pairs={{0,1},{1,0},{2,3},{3,2},{4,5},{5,4},{6,7},{7,6},{8,9},{9,8},{10,11... | collective-permute-start | bytes 1585160 | tf_op jit(solution)/shard_map/ppermute | solution.py:148
  48.3 0.0 collective-permute-done.7.refs_0_.near_ref
  48.3 0.0 collective-permute-done.8.refs_2_
  48.3 0.0 copy-done
  48.3 0.0 copy-done.1
  48.3 2.4 %shard_map.60.solved_ref = f32[512,256]{1,0:T(8,128)S(1)} custom-call(s32[1]{0:T(128)} %bitcast.place, f32[1544,128]{1,0:T(8,128)S(1)} %shard_map.58.own_ref, f32[1032,128]{1,0:T(8,128)S(1)} %collective-permute-done.7.refs_0_.near_ref, f32[544,128]{1,0:T(8,128)S(1)} %collective-permute-done.refs_1_, f32[544,128]{1,0:T(8,128)S(1)} %collective-permute-done.8.refs_2_, ...), custom_call_target="tpu_custom_call" | custom-call | tf_op jit(solution)/shard_map/pallas_call | solution.py:133
  50.8 1.9 %collective-permute-start.9 = (f32[512,256]{1,0:T(8,128)S(1)}, f32[512,256]{1,0:T(8,128)S(1)}, u32[]{:S(2)}, u32[]{:S(2)}) collective-permute-start(f32[512,256]{1,0:T(8,128)S(1)} %shard_map.60.solved_ref), channel_id=1, source_target_pairs={{0,4},{4,8},{8,12},{12,16},{16,20},{20,24},{24,28},{1,5},{5,9},{9,... | collective-permute-start | bytes 1572872 | tf_op jit(solution)/shard_map/ppermute | solution.py:201
  52.7 9.5 %collective-permute-done.9.below_ref = f32[512,256]{1,0:T(8,128)S(1)} collective-permute-done((f32[512,256]{1,0:T(8,128)S(1)}, f32[512,256]{1,0:T(8,128)S(1)}, u32[]{:S(2)}, u32[]{:S(2)}) %collective-permute-start.9) | collective-permute-done | bytes 524320 | tf_op jit(solution)/shard_map/ppermute | solution.py:201
  62.2 0.0 copy-done.2
  62.2 1.0 %shard_map.61 = (f32[512,128]{1,0:T(8,128)S(1)}, f32[512,128]{1,0:T(8,128)S(1)}, f32[512,128]{1,0:T(8,128)S(1)}) custom-call(s32[1]{0:T(128)} %bitcast.place, f32[1544,128]{1,0:T(8,128)S(1)} %shard_map.58.own_ref, f32[1032,128]{1,0:T(8,128)S(1)} %collective-permute-done.7.refs_0_.near_ref, f32[512,128]{1,0:T(8,128)S(1)} %collective-permute-done.3.down_near_ref, ...), custom_call_target="tpu_custom_call" | custom-call | tf_op jit(solution)/shard_map/pallas_call | solution.py:133
  63.2 0.0 collective-permute-done.6.last_ref
  63.2 1.5 %shard_map.62 = (f32[1,512,128]{2,1,0:T(8,128)}, f32[1,512,128]{2,1,0:T(8,128)}, f32[1,512,128]{2,1,0:T(8,128)}) custom-call(s32[1]{0:T(128)} %bitcast.place, f32[1032,128]{1,0:T(8,128)S(1)} %collective-permute-done.6.last_ref, f32[512,256]{1,0:T(8,128)S(1)} %shard_map.60.solved_ref, f32[512,256]{1,0:T(8,128)S(1)} %collective-permute-done.9.below_ref, ...), custom_call_target="tpu_custom_call" | custom-call | tf_op jit(solution)/shard_map/pallas_call | solution.py:133
  (9 shorter events, 0.2 us)
Async XLA Ops:
  1.9 11.4 %collective-permute-start = (f32[544,128]{1,0:T(8,128)S(1)}, f32[544,128]{1,0:T(8,128)S(1)}, u32[]{:S(2)}, u32[]{:S(2)}) collective-permute-start(f32[544,128]{1,0:T(8,128)S(1)} %slice.24), channel_id=1, source_target_pairs={{0,3},{1,2},{2,1},{3,0},{4,7},{5,6},{6,5},{7,4},{8,11},{9,10},{10,... | collective-permute-start | bytes 835592 | tf_op jit(solution)/shard_map/ppermute | solution.py:148
  5.6 42.7 %collective-permute-start.7 = (f32[1032,128]{1,0:T(8,128)S(1)}, f32[1032,128]{1,0:T(8,128)S(1)}, u32[]{:S(2)}, u32[]{:S(2)}) collective-permute-start(f32[1032,128]{1,0:T(8,128)S(1)} %slice.27), channel_id=1, source_target_pairs={{0,1},{1,0},{2,3},{3,2},{4,5},{5,4},{6,7},{7,6},{8,9},{9,8},{10,11... | collective-permute-start | bytes 1585160 | tf_op jit(solution)/shard_map/ppermute | solution.py:148
  13.4 33.1 %collective-permute-start.1 = (f32[1024,128]{1,0:T(8,128)S(1)}, f32[1024,128]{1,0:T(8,128)S(1)}, u32[]{:S(2)}, u32[]{:S(2)}) collective-permute-start(f32[1024,128]{1,0:T(8,128)S(1)} %slice.19), channel_id=1, source_target_pairs={{0,3},{1,2},{2,1},{3,0},{4,7},{5,6},{6,5},{7,4},{8,11},{9,10},{10,... | collective-permute-start | bytes 1572872 | tf_op jit(solution)/shard_map/ppermute | solution.py:148
  17.0 31.3 %collective-permute-start.8 = (f32[544,128]{1,0:T(8,128)S(1)}, f32[544,128]{1,0:T(8,128)S(1)}, u32[]{:S(2)}, u32[]{:S(2)}) collective-permute-start(f32[544,128]{1,0:T(8,128)S(1)} %collective-permute-done.refs_1_), channel_id=1, source_target_pairs={{0,1},{1,0},{2,3},{3,2},{4,5},{5,4},{6,7},{7,6},{8,9},{9,8},{10,11... | collective-permute-start | bytes 835592 | tf_op jit(solution)/shard_map/ppermute | solution.py:148
  19.6 3.9 %collective-permute-start.2 = (f32[8,128]{1,0:T(8,128)S(1)}, f32[8,128]{1,0:T(8,128)S(1)}, u32[]{:S(2)}, u32[]{:S(2)}) collective-permute-start(f32[8,128]{1,0:T(8,128)S(1)} %slice_maximum_fusion), channel_id=1, source_target_pairs={{0,4},{4,8},{8,12},{12,16},{16,20},{20,24},{24,28},{28,0},{1,5},{5... | collective-permute-start | bytes 12296 | tf_op jit(solution)/shard_map/ppermute | solution.py:176
  23.5 22.9 %collective-permute-start.3 = (f32[512,128]{1,0:T(8,128)S(1)}, f32[512,128]{1,0:T(8,128)S(1)}, u32[]{:S(2)}, u32[]{:S(2)}) collective-permute-start(f32[512,128]{1,0:T(8,128)S(1)} %slice.22), channel_id=1, source_target_pairs={{0,1},{1,0},{2,3},{3,2},{4,5},{5,4},{6,7},{7,6},{8,9},{9,8},{10,11... | collective-permute-start | bytes 786440 | tf_op jit(solution)/shard_map/ppermute | solution.py:148
  23.6 4.6 %collective-permute-start.4 = (f32[8,128]{1,0:T(8,128)S(1)}, f32[8,128]{1,0:T(8,128)S(1)}, u32[]{:S(2)}, u32[]{:S(2)}) collective-permute-start(f32[8,128]{1,0:T(8,128)S(1)} %max.13), channel_id=1, source_target_pairs={{0,8},{4,12},{8,16},{12,20},{16,24},{20,28},{24,0},{28,4},{1,9},{5... | collective-permute-start | bytes 12296 | tf_op jit(solution)/shard_map/ppermute | solution.py:176
  28.2 3.6 %collective-permute-start.5 = (f32[8,128]{1,0:T(8,128)S(1)}, f32[8,128]{1,0:T(8,128)S(1)}, u32[]{:S(2)}, u32[]{:S(2)}) collective-permute-start(f32[8,128]{1,0:T(8,128)S(1)} %max.14), channel_id=1, source_target_pairs={{0,16},{4,20},{8,24},{12,28},{16,0},{20,4},{24,8},{28,12},{1,17},{... | collective-permute-start | bytes 12296 | tf_op jit(solution)/shard_map/ppermute | solution.py:176
  31.8 16.5 %copy-start = (f32[2,512,128]{2,1,0:T(8,128)S(1)}, f32[2,512,128]{2,1,0:T(8,128)}, u32[]{:S(2)}) copy-start(f32[2,512,128]{2,1,0:T(8,128)} %refs_3_.1) | copy-start | bytes 1572868
  31.8 16.5 %copy-start.1 = (f32[2,512,128]{2,1,0:T(8,128)S(1)}, f32[2,512,128]{2,1,0:T(8,128)}, u32[]{:S(2)}) copy-start(f32[2,512,128]{2,1,0:T(8,128)} %refs_4_.1) | copy-start | bytes 1572868
  46.5 15.7 %copy-start.2 = (f32[2,512,128]{2,1,0:T(8,128)S(1)}, f32[2,512,128]{2,1,0:T(8,128)}, u32[]{:S(2)}) copy-start(f32[2,512,128]{2,1,0:T(8,128)} %level_ref.3) | copy-start | bytes 1572868
  46.5 16.7 %collective-permute-start.6 = (f32[1032,128]{1,0:T(8,128)S(1)}, f32[1032,128]{1,0:T(8,128)S(1)}, u32[]{:S(2)}, u32[]{:S(2)}) collective-permute-start(f32[1032,128]{1,0:T(8,128)S(1)} %shard_map.59), channel_id=1, source_target_pairs={{0,1},{1,0},{2,3},{3,2},{4,5},{5,4},{6,7},{7,6},{8,9},{9,8},{10,11... | collective-permute-start | bytes 1585160 | tf_op jit(solution)/shard_map/ppermute | solution.py:148
  50.8 11.4 %collective-permute-start.9 = (f32[512,256]{1,0:T(8,128)S(1)}, f32[512,256]{1,0:T(8,128)S(1)}, u32[]{:S(2)}, u32[]{:S(2)}) collective-permute-start(f32[512,256]{1,0:T(8,128)S(1)} %shard_map.60.solved_ref), channel_id=1, source_target_pairs={{0,4},{4,8},{8,12},{12,16},{16,20},{20,24},{24,28},{1,5},{5,9},{9,... | collective-permute-start | bytes 1572872 | tf_op jit(solution)/shard_map/ppermute | solution.py:201

commit v14 on v13

--- a/solution.py
+++ b/solution.py
@@ -97,15 +97,21 @@
     return exact_dot(left, right)
 
 
-def partial_kernel(place, own_ref, near_ref, down_near_ref, far_ref, solved_ref, below_ref, level_ref, part_level, part_up, part_down):
+def upper_kernel(place, own_ref, near_ref, far_ref, solved_ref, level_ref, part_level, part_up):
     phases, cols = part_up.shape
-    top, middle = pl.ds(0, phases), pl.ds(phases, phases)
-    own_up, own_down = (pl.ds(start + PEAK_ROWS, phases) for start in (phases, 2 * phases))
-    upper = gathered_product(place, [own_ref[own_up, :], near_ref[own_up, :], far_ref[top, :]], 0, solved_ref)
+    up = pl.ds(phases + PEAK_ROWS, phases)
+    blocks = [own_ref[up, :], near_ref[up, :], far_ref[pl.ds(0, phases), :]]
+    upper = gathered_product(place, blocks, 0, solved_ref)
     part_up[...] = upper[:, :cols]
-    lower = gathered_product(place, [own_ref[own_down, :], down_near_ref[...], far_ref[middle, :]], 0, below_ref)
+    part_level[...] = level_ref[0] + upper[:, cols:]
+
+
+def lower_kernel(place, own_ref, near_ref, far_ref, below_ref, upper_level, part_level, part_down):
+    phases, cols = part_down.shape
+    blocks = [own_ref[pl.ds(2 * phases + PEAK_ROWS, phases), :], near_ref[...], far_ref[pl.ds(phases, phases), :]]
+    lower = gathered_product(place, blocks, 0, below_ref)
     part_down[...] = lower[:, cols:]
-    part_level[...] = level_ref[0] + upper[:, cols:] + lower[:, :cols]
+    part_level[...] = upper_level[...] + lower[:, :cols]
 
 
 def output_kernel(place, last_ref, solved_ref, below_ref, *refs):
@@ -176,8 +182,8 @@
         peaks.append(jnp.maximum(peaks[-1], lax.ppermute(peaks[-1], "lvl", route)))
         reach *= 2
     peak = peaks[-1]
-    down_near = exchanged(after(sent, peaks[1])[down_row:], 1)
-    even_last = exchanged(stack((after(even_far, down_near), 0, 2 * phases), (peak, 0, PEAK_ROWS)), 1)
+    down_near = exchanged(after(sent, level_far)[down_row:], 1)
+    even_last = exchanged(stack((even_far, 0, 2 * phases), (peak, 0, PEAK_ROWS)), 1)
 
     solved = call(
         solve_kernel,
@@ -198,21 +204,32 @@
             pltpu.VMEM((phases, 2 * cols), BF16),
         ],
     )
-    from_below = lax.ppermute(solved, "lvl", [(i, i + 1) for i in range(ranges - 1)])
-
-    parts = call(
-        partial_kernel,
-        (shape(phases),) * 3,
-        [SMEM, *[VMEM] * 6, even],
+    from_below = lax.ppermute(after(solved, down_near), "lvl", [(i, i + 1) for i in range(ranges - 1)])
+
+    free = pl.CostEstimate(flops=0, bytes_accessed=0, transcendentals=0)
+    upper_level, part_up = call(
+        upper_kernel,
+        (shape(phases),) * 2,
+        [SMEM, *[VMEM] * 4, even],
         place,
         sent,
         near,
+        even_far,
+        solved,
+        level_blocks,
+        cost_estimate=free,
+    )
+    part_level, part_down = call(
+        lower_kernel,
+        (shape(phases),) * 2,
+        [SMEM, *[VMEM] * 5],
+        place,
+        sent,
         down_near,
         even_far,
-        solved,
         from_below,
-        level_blocks,
-        cost_estimate=pl.CostEstimate(flops=0, bytes_accessed=0, transcendentals=0),
+        upper_level,
+        cost_estimate=free,
     )
     return call(
         output_kernel,
@@ -222,7 +239,9 @@
         even_last,
         solved,
         from_below,
-        *parts,
+        part_level,
+        part_up,
+        part_down,
         peak,
     )
 

time: 64.8 us -> 61.3 us (0.946)
  the two profiles are of different devices: /device:TPU:4 before, /device:TPU:0 now
where the time goes in v14:
time: 61.3 us; the launch traced here: 60.7 us
  waiting for transfers between devices  31.6 us (52%)
  starting transfers between devices  22 us (36%)
  Pallas kernels  6.24 us (10%)
  between operations  0.76 us (1%)
    ppermute x6, waiting for transfers between devices, exchanged(): return lax.ppermute(part, 'col', [(i, i ^ distance) for i in range(shards)])  20.8 us
    ppermute x6, starting transfers between devices, exchanged(): return lax.ppermute(part, 'col', [(i, i ^ distance) for i in range(shards)])  18.2 us
    ppermute x3, waiting for transfers between devices, per_device(): peaks.append(jnp.maximum(peaks[-1], lax.ppermute(peaks[-1], 'lvl', route)))  9.92 us
    pallas_call x6, Pallas kernels, call(): pl.pallas_call(kernel, out_shape=out_shape, in_specs=in_specs, out_specs=...  6.24 us
    ppermute x3, starting transfers between devices, per_device(): peaks.append(jnp.maximum(peaks[-1], lax.ppermute(peaks[-1], 'lvl', route)))  2.17 us
    ppermute x1, starting transfers between devices, per_device(): lax.ppermute(after(solved, down_near), 'lvl', [(i, i + 1) for i in range(...  1.59 us
  transfers between devices with their start and end apart: 10, of which 8 were waited for; matrix products, arithmetic and copies ran while one was open for 0% of the time, Pallas kernels for 6%

profile of v14, /device:TPU:0, one launch (start us, length us, event | category | flops | bytes accessed | tf_op | source)
XLA Modules:
  0.0 60.7 jit_solution(5741606449412234271)
XLA Ops:
  0.6 1.2 %shard_map.58.own_ref = f32[1544,128]{1,0:T(8,128)S(1)} custom-call(s32[1]{0:T(128)} %bitcast.place, f32[2,512,128]{2,1,0:T(8,128)} %refs_3_.1, f32[2,512,128]{2,1,0:T(8,128)} %level_ref.3, f32[2,512,128]{2,1,0:T(8,128)} %refs_4_.1), custom_call_target="tpu_custom_call" | custom-call | tf_op jit(solution)/shard_map/pallas_call | solution.py:139
  1.9 5.1 %collective-permute-start = (f32[544,128]{1,0:T(8,128)S(1)}, f32[544,128]{1,0:T(8,128)S(1)}, u32[]{:S(2)}, u32[]{:S(2)}) collective-permute-start(f32[544,128]{1,0:T(8,128)S(1)} %slice.24), channel_id=1, source_target_pairs={{0,3},{1,2},{2,1},{3,0},{4,7},{5,6},{6,5},{7,4},{8,11},{9,10},{10,... | collective-permute-start | bytes 835592 | tf_op jit(solution)/shard_map/ppermute | solution.py:154
  7.0 0.1 collective-permute-start.6
  7.1 7.5 %collective-permute-done.refs_1_ = f32[544,128]{1,0:T(8,128)S(1)} collective-permute-done((f32[544,128]{1,0:T(8,128)S(1)}, f32[544,128]{1,0:T(8,128)S(1)}, u32[]{:S(2)}, u32[]{:S(2)}) %collective-permute-start) | collective-permute-done | bytes 278560 | tf_op jit(solution)/shard_map/ppermute | solution.py:154
  14.6 3.8 %collective-permute-start.1 = (f32[1024,128]{1,0:T(8,128)S(1)}, f32[1024,128]{1,0:T(8,128)S(1)}, u32[]{:S(2)}, u32[]{:S(2)}) collective-permute-start(f32[1024,128]{1,0:T(8,128)S(1)} %slice.19), channel_id=1, source_target_pairs={{0,3},{1,2},{2,1},{3,0},{4,7},{5,6},{6,5},{7,4},{8,11},{9,10},{10,... | collective-permute-start | bytes 1572872 | tf_op jit(solution)/shard_map/ppermute | solution.py:154
  18.4 2.6 %collective-permute-start.7 = (f32[544,128]{1,0:T(8,128)S(1)}, f32[544,128]{1,0:T(8,128)S(1)}, u32[]{:S(2)}, u32[]{:S(2)}) collective-permute-start(f32[544,128]{1,0:T(8,128)S(1)} %collective-permute-done.refs_1_), channel_id=1, source_target_pairs={{0,1},{1,0},{2,3},{3,2},{4,5},{5,4},{6,7},{7,6},{8,9},{9,8},{10,11... | collective-permute-start | bytes 835592 | tf_op jit(solution)/shard_map/ppermute | solution.py:154
  21.0 0.1 collective-permute-start.8
  21.1 0.1 collective-permute-start.2
  21.2 3.9 %collective-permute-done.2 = f32[8,128]{1,0:T(8,128)S(1)} collective-permute-done((f32[8,128]{1,0:T(8,128)S(1)}, f32[8,128]{1,0:T(8,128)S(1)}, u32[]{:S(2)}, u32[]{:S(2)}) %collective-permute-start.2) | collective-permute-done | bytes 4128 | tf_op jit(solution)/shard_map/ppermute | solution.py:182
  25.1 0.6 collective-permute-start.3
  25.7 3.9 %collective-permute-done.3 = f32[8,128]{1,0:T(8,128)S(1)} collective-permute-done((f32[8,128]{1,0:T(8,128)S(1)}, f32[8,128]{1,0:T(8,128)S(1)}, u32[]{:S(2)}, u32[]{:S(2)}) %collective-permute-start.3) | collective-permute-done | bytes 4128 | tf_op jit(solution)/shard_map/ppermute | solution.py:182
  29.6 1.5 %collective-permute-start.4 = (f32[8,128]{1,0:T(8,128)S(1)}, f32[8,128]{1,0:T(8,128)S(1)}, u32[]{:S(2)}, u32[]{:S(2)}) collective-permute-start(f32[8,128]{1,0:T(8,128)S(1)} %max.14), channel_id=1, source_target_pairs={{0,16},{4,20},{8,24},{12,28},{16,0},{20,4},{24,8},{28,12},{1,17},{... | collective-permute-start | bytes 12296 | tf_op jit(solution)/shard_map/ppermute | solution.py:182
  31.2 2.1 %collective-permute-done.4 = f32[8,128]{1,0:T(8,128)S(1)} collective-permute-done((f32[8,128]{1,0:T(8,128)S(1)}, f32[8,128]{1,0:T(8,128)S(1)}, u32[]{:S(2)}, u32[]{:S(2)}) %collective-permute-start.4) | collective-permute-done | bytes 4128 | tf_op jit(solution)/shard_map/ppermute | solution.py:182
  33.2 0.0 copy-start.1
  33.2 0.0 copy-start.2
  33.2 3.9 %collective-permute-done.1.refs_0_.far_ref = f32[1024,128]{1,0:T(8,128)S(1)} collective-permute-done((f32[1024,128]{1,0:T(8,128)S(1)}, f32[1024,128]{1,0:T(8,128)S(1)}, u32[]{:S(2)}, u32[]{:S(2)}) %collective-permute-start.1) | collective-permute-done | bytes 524320 | tf_op jit(solution)/shard_map/ppermute | solution.py:154
  37.2 0.0 copy-start
  37.2 6.5 %collective-permute-start.5 = (f32[1032,128]{1,0:T(8,128)S(1)}, f32[1032,128]{1,0:T(8,128)S(1)}, u32[]{:S(2)}, u32[]{:S(2)}) collective-permute-start(f32[1032,128]{1,0:T(8,128)S(1)} %shard_map.59), channel_id=1, source_target_pairs={{0,1},{1,0},{2,3},{3,2},{4,5},{5,4},{6,7},{7,6},{8,9},{9,8},{10,11... | collective-permute-start | bytes 1585160 | tf_op jit(solution)/shard_map/ppermute | solution.py:154
  43.8 0.0 collective-permute-done.6.refs_0_.near_ref
  43.8 0.0 collective-permute-done.7.refs_2_
  43.8 0.0 copy-done.1
  43.8 0.0 copy-done.2
  43.8 2.4 %shard_map.60.solved_ref = f32[512,256]{1,0:T(8,128)S(1)} custom-call(s32[1]{0:T(128)} %bitcast.place, f32[1544,128]{1,0:T(8,128)S(1)} %shard_map.58.own_ref, f32[1032,128]{1,0:T(8,128)S(1)} %collective-permute-done.6.refs_0_.near_ref, f32[544,128]{1,0:T(8,128)S(1)} %collective-permute-done.refs_1_, f32[544,128]{1,0:T(8,128)S(1)} %collective-permute-done.7.refs_2_, ...), custom_call_target="tpu_custom_call" | custom-call | tf_op jit(solution)/shard_map/pallas_call | solution.py:139
  46.2 2.1 %collective-permute-done.8.near_ref = f32[512,128]{1,0:T(8,128)S(1)} collective-permute-done((f32[512,128]{1,0:T(8,128)S(1)}, f32[512,128]{1,0:T(8,128)S(1)}, u32[]{:S(2)}, u32[]{:S(2)}) %collective-permute-start.8) | collective-permute-done | bytes 262176 | tf_op jit(solution)/shard_map/ppermute | solution.py:154
  48.3 1.6 %collective-permute-start.9 = (f32[512,256]{1,0:T(8,128)S(1)}, f32[512,256]{1,0:T(8,128)S(1)}, u32[]{:S(2)}, u32[]{:S(2)}) collective-permute-start(f32[512,256]{1,0:T(8,128)S(1)} %shard_map.60.solved_ref), channel_id=1, source_target_pairs={{0,4},{4,8},{8,12},{12,16},{16,20},{20,24},{24,28},{1,5},{5,9},{9,... | collective-permute-start | bytes 1572872 | tf_op jit(solution)/shard_map/ppermute | solution.py:207
  49.9 0.0 copy-done
  49.9 0.6 shard_map.61
  50.4 0.9 %collective-permute-done.9.below_ref = f32[512,256]{1,0:T(8,128)S(1)} collective-permute-done((f32[512,256]{1,0:T(8,128)S(1)}, f32[512,256]{1,0:T(8,128)S(1)}, u32[]{:S(2)}, u32[]{:S(2)}) %collective-permute-start.9) | collective-permute-done | bytes 524320 | tf_op jit(solution)/shard_map/ppermute | solution.py:207
  51.3 0.6 shard_map.62
  51.9 7.3 %collective-permute-done.5.last_ref = f32[1032,128]{1,0:T(8,128)S(1)} collective-permute-done((f32[1032,128]{1,0:T(8,128)S(1)}, f32[1032,128]{1,0:T(8,128)S(1)}, u32[]{:S(2)}, u32[]{:S(2)}) %collective-permute-start.5) | collective-permute-done | bytes 528416 | tf_op jit(solution)/shard_map/ppermute | solution.py:154
  59.2 1.5 %shard_map.63 = (f32[1,512,128]{2,1,0:T(8,128)}, f32[1,512,128]{2,1,0:T(8,128)}, f32[1,512,128]{2,1,0:T(8,128)}) custom-call(s32[1]{0:T(128)} %bitcast.place, f32[1032,128]{1,0:T(8,128)S(1)} %collective-permute-done.5.last_ref, f32[512,256]{1,0:T(8,128)S(1)} %shard_map.60.solved_ref, f32[512,256]{1,0:T(8,128)S(1)} %collective-permute-done.9.below_ref, ...), custom_call_target="tpu_custom_call" | custom-call | tf_op jit(solution)/shard_map/pallas_call | solution.py:139
  (9 shorter events, 0.2 us)
Async XLA Ops:
  1.9 12.7 %collective-permute-start = (f32[544,128]{1,0:T(8,128)S(1)}, f32[544,128]{1,0:T(8,128)S(1)}, u32[]{:S(2)}, u32[]{:S(2)}) collective-permute-start(f32[544,128]{1,0:T(8,128)S(1)} %slice.24), channel_id=1, source_target_pairs={{0,3},{1,2},{2,1},{3,0},{4,7},{5,6},{6,5},{7,4},{8,11},{9,10},{10,... | collective-permute-start | bytes 835592 | tf_op jit(solution)/shard_map/ppermute | solution.py:154
  7.0 36.7 %collective-permute-start.6 = (f32[1032,128]{1,0:T(8,128)S(1)}, f32[1032,128]{1,0:T(8,128)S(1)}, u32[]{:S(2)}, u32[]{:S(2)}) collective-permute-start(f32[1032,128]{1,0:T(8,128)S(1)} %slice.27), channel_id=1, source_target_pairs={{0,1},{1,0},{2,3},{3,2},{4,5},{5,4},{6,7},{7,6},{8,9},{9,8},{10,11... | collective-permute-start | bytes 1585160 | tf_op jit(solution)/shard_map/ppermute | solution.py:154
  14.6 22.6 %collective-permute-start.1 = (f32[1024,128]{1,0:T(8,128)S(1)}, f32[1024,128]{1,0:T(8,128)S(1)}, u32[]{:S(2)}, u32[]{:S(2)}) collective-permute-start(f32[1024,128]{1,0:T(8,128)S(1)} %slice.19), channel_id=1, source_target_pairs={{0,3},{1,2},{2,1},{3,0},{4,7},{5,6},{6,5},{7,4},{8,11},{9,10},{10,... | collective-permute-start | bytes 1572872 | tf_op jit(solution)/shard_map/ppermute | solution.py:154
  18.4 25.3 %collective-permute-start.7 = (f32[544,128]{1,0:T(8,128)S(1)}, f32[544,128]{1,0:T(8,128)S(1)}, u32[]{:S(2)}, u32[]{:S(2)}) collective-permute-start(f32[544,128]{1,0:T(8,128)S(1)} %collective-permute-done.refs_1_), channel_id=1, source_target_pairs={{0,1},{1,0},{2,3},{3,2},{4,5},{5,4},{6,7},{7,6},{8,9},{9,8},{10,11... | collective-permute-start | bytes 835592 | tf_op jit(solution)/shard_map/ppermute | solution.py:154
  21.0 27.2 %collective-permute-start.8 = (f32[512,128]{1,0:T(8,128)S(1)}, f32[512,128]{1,0:T(8,128)S(1)}, u32[]{:S(2)}, u32[]{:S(2)}) collective-permute-start(f32[512,128]{1,0:T(8,128)S(1)} %slice.23), channel_id=1, source_target_pairs={{0,1},{1,0},{2,3},{3,2},{4,5},{5,4},{6,7},{7,6},{8,9},{9,8},{10,11... | collective-permute-start | bytes 786440 | tf_op jit(solution)/shard_map/ppermute | solution.py:154
  21.1 4.0 %collective-permute-start.2 = (f32[8,128]{1,0:T(8,128)S(1)}, f32[8,128]{1,0:T(8,128)S(1)}, u32[]{:S(2)}, u32[]{:S(2)}) collective-permute-start(f32[8,128]{1,0:T(8,128)S(1)} %slice_maximum_fusion), channel_id=1, source_target_pairs={{0,4},{4,8},{8,12},{12,16},{16,20},{20,24},{24,28},{28,0},{1,5},{5... | collective-permute-start | bytes 12296 | tf_op jit(solution)/shard_map/ppermute | solution.py:182
  25.1 4.5 %collective-permute-start.3 = (f32[8,128]{1,0:T(8,128)S(1)}, f32[8,128]{1,0:T(8,128)S(1)}, u32[]{:S(2)}, u32[]{:S(2)}) collective-permute-start(f32[8,128]{1,0:T(8,128)S(1)} %max.13), channel_id=1, source_target_pairs={{0,8},{4,12},{8,16},{12,20},{16,24},{20,28},{24,0},{28,4},{1,9},{5... | collective-permute-start | bytes 12296 | tf_op jit(solution)/shard_map/ppermute | solution.py:182
  29.6 3.6 %collective-permute-start.4 = (f32[8,128]{1,0:T(8,128)S(1)}, f32[8,128]{1,0:T(8,128)S(1)}, u32[]{:S(2)}, u32[]{:S(2)}) collective-permute-start(f32[8,128]{1,0:T(8,128)S(1)} %max.14), channel_id=1, source_target_pairs={{0,16},{4,20},{8,24},{12,28},{16,0},{20,4},{24,8},{28,12},{1,17},{... | collective-permute-start | bytes 12296 | tf_op jit(solution)/shard_map/ppermute | solution.py:182
  33.2 10.5 %copy-start.1 = (f32[2,512,128]{2,1,0:T(8,128)S(1)}, f32[2,512,128]{2,1,0:T(8,128)}, u32[]{:S(2)}) copy-start(f32[2,512,128]{2,1,0:T(8,128)} %refs_3_.1) | copy-start | bytes 1572868
  33.2 10.5 %copy-start.2 = (f32[2,512,128]{2,1,0:T(8,128)S(1)}, f32[2,512,128]{2,1,0:T(8,128)}, u32[]{:S(2)}) copy-start(f32[2,512,128]{2,1,0:T(8,128)} %refs_4_.1) | copy-start | bytes 1572868
  37.2 12.6 %copy-start = (f32[2,512,128]{2,1,0:T(8,128)S(1)}, f32[2,512,128]{2,1,0:T(8,128)}, u32[]{:S(2)}) copy-start(f32[2,512,128]{2,1,0:T(8,128)} %level_ref.3) | copy-start | bytes 1572868
  37.2 22.0 %collective-permute-start.5 = (f32[1032,128]{1,0:T(8,128)S(1)}, f32[1032,128]{1,0:T(8,128)S(1)}, u32[]{:S(2)}, u32[]{:S(2)}) collective-permute-start(f32[1032,128]{1,0:T(8,128)S(1)} %shard_map.59), channel_id=1, source_target_pairs={{0,1},{1,0},{2,3},{3,2},{4,5},{5,4},{6,7},{7,6},{8,9},{9,8},{10,11... | collective-permute-start | bytes 1585160 | tf_op jit(solution)/shard_map/ppermute | solution.py:154
  48.3 3.1 %collective-permute-start.9 = (f32[512,256]{1,0:T(8,128)S(1)}, f32[512,256]{1,0:T(8,128)S(1)}, u32[]{:S(2)}, u32[]{:S(2)}) collective-permute-start(f32[512,256]{1,0:T(8,128)S(1)} %shard_map.60.solved_ref), channel_id=1, source_target_pairs={{0,4},{4,8},{8,12},{12,16},{16,20},{20,24},{24,28},{1,5},{5,9},{9,... | collective-permute-start | bytes 1572872 | tf_op jit(solution)/shard_map/ppermute | solution.py:207

commit v15 on v14

--- a/solution.py
+++ b/solution.py
@@ -97,33 +97,29 @@
     return exact_dot(left, right)
 
 
-def upper_kernel(place, own_ref, near_ref, far_ref, solved_ref, level_ref, part_level, part_up):
+def upper_kernel(place, own_ref, near_ref, far_ref, last_ref, solved_ref, level_ref, part_level, part_up):
     phases, cols = part_up.shape
     up = pl.ds(phases + PEAK_ROWS, phases)
-    blocks = [own_ref[up, :], near_ref[up, :], far_ref[pl.ds(0, phases), :]]
-    upper = gathered_product(place, blocks, 0, solved_ref)
+    upper = gathered_product(place, [own_ref[up, :], near_ref[up, :], far_ref[...], last_ref[...]], 0, solved_ref)
     part_up[...] = upper[:, :cols]
     part_level[...] = level_ref[0] + upper[:, cols:]
 
 
 def lower_kernel(place, own_ref, near_ref, far_ref, below_ref, upper_level, part_level, part_down):
     phases, cols = part_down.shape
-    blocks = [own_ref[pl.ds(2 * phases + PEAK_ROWS, phases), :], near_ref[...], far_ref[pl.ds(phases, phases), :]]
+    blocks = [own_ref[pl.ds(2 * phases + PEAK_ROWS, phases), :], near_ref[...], far_ref[...]]
     lower = gathered_product(place, blocks, 0, below_ref)
     part_down[...] = lower[:, cols:]
     part_level[...] = upper_level[...] + lower[:, :cols]
 
 
-def output_kernel(place, last_ref, solved_ref, below_ref, *refs):
-    part_level, part_up, part_down, peak_ref, new_level, new_up, new_down = refs
+def output_kernel(place, last_ref, below_ref, part_level, part_up, part_down, peak_ref, new_level, new_up, new_down):
     phases, cols = part_up.shape
-    scale = 1.0 / jnp.maximum(peak_ref[...], last_ref[pl.ds(2 * phases, PEAK_ROWS), :])[0:1, :]
-    last = len(DISTANCES) - 1
-    upper = gathered_product(place, [last_ref[pl.ds(0, phases), :]], last, solved_ref)
-    new_up[0] = (part_up[...] + upper[:, :cols]) * scale
-    lower = gathered_product(place, [last_ref[pl.ds(phases, phases), :]], last, below_ref)
+    scale = 1.0 / jnp.maximum(peak_ref[...], last_ref[pl.ds(phases, PEAK_ROWS), :])[0:1, :]
+    new_up[0] = part_up[...] * scale
+    lower = gathered_product(place, [last_ref[pl.ds(0, phases), :]], len(DISTANCES) - 1, below_ref)
     new_down[0] = (part_down[...] + lower[:, cols:]) * scale
-    new_level[0] = (part_level[...] + upper[:, cols:] + lower[:, :cols]) * scale
+    new_level[0] = (part_level[...] + lower[:, :cols]) * scale
 
 
 def per_device(up_blocks, level_blocks, down_blocks):
@@ -174,7 +170,10 @@
     up_row, down_row = phases + PEAK_ROWS, 2 * phases + PEAK_ROWS
     level_far, near = exchanged(sent[: up_row + PAD_ROWS], 3), exchanged(sent[:down_row], 1)
     level_last = exchanged(level_far, 1)
-    even_far = exchanged(after(sent, level_far)[up_row:], 3)
+    up_far = exchanged(after(sent, level_far)[up_row:down_row], 3)
+    down_near = exchanged(after(sent, level_far)[down_row:], 1)
+    down_far = exchanged(after(sent, up_far)[down_row:], 3)
+    up_last = exchanged(up_far, 1)
     peak = jnp.maximum(sent[phases:up_row], level_far[phases:up_row])
     peaks, reach = [peak], 1
     while reach < ranges:
@@ -182,8 +181,7 @@
         peaks.append(jnp.maximum(peaks[-1], lax.ppermute(peaks[-1], "lvl", route)))
         reach *= 2
     peak = peaks[-1]
-    down_near = exchanged(after(sent, level_far)[down_row:], 1)
-    even_last = exchanged(stack((even_far, 0, 2 * phases), (peak, 0, PEAK_ROWS)), 1)
+    down_last = exchanged(stack((down_far, 0, phases), (peak, 0, PEAK_ROWS)), 1)
 
     solved = call(
         solve_kernel,
@@ -210,11 +208,12 @@
     upper_level, part_up = call(
         upper_kernel,
         (shape(phases),) * 2,
-        [SMEM, *[VMEM] * 4, even],
+        [SMEM, *[VMEM] * 5, even],
         place,
         sent,
         near,
-        even_far,
+        up_far,
+        up_last,
         solved,
         level_blocks,
         cost_estimate=free,
@@ -226,7 +225,7 @@
         place,
         sent,
         down_near,
-        even_far,
+        down_far,
         from_below,
         upper_level,
         cost_estimate=free,
@@ -234,10 +233,9 @@
     return call(
         output_kernel,
         (jax.ShapeDtypeStruct((1, phases, cols), F32),) * 3,
-        [SMEM] + [VMEM] * 7,
-        place,
-        even_last,
-        solved,
+        [SMEM] + [VMEM] * 6,
+        place,
+        down_last,
         from_below,
         part_level,
         part_up,

time: 61.3 us -> 64.2 us (1.047)
  waiting for transfers between devices: 31.6 us -> 35 us
    ppermute x6 -> x8, waiting for transfers between devices: 20.8 us -> 27.2 us  [exchanged(): return lax.ppermute(part, 'col', [(i, i ^ distance) for i in range(shards)])]
    ppermute x3, waiting for transfers between devices: 9.92 us -> 7.84 us  [per_device(): peaks.append(jnp.maximum(peaks[-1], lax.ppermute(peaks[-1], 'lvl', route)))]
    ppermute x1, waiting for transfers between devices: 0.89 us -> 0.01 us  [per_device(): lax.ppermute(after(solved, down_near), 'lvl', [(i, i + 1) for i in range(...]
    ppermute x6 -> x8, starting transfers between devices: 18.2 us -> 18.4 us  [exchanged(): return lax.ppermute(part, 'col', [(i, i ^ distance) for i in range(shards)])]
  transfers between devices with their start and end apart: 10 -> 12, of which waited for: 8 -> 6; matrix products, arithmetic and copies ran while one was open for 0% -> 0% of each run, Pallas kernels for 6% -> 6%
where the time goes in v15:
time: 64.2 us; the launch traced here: 64 us
  waiting for transfers between devices  35 us (55%)
  starting transfers between devices  22 us (34%)
  Pallas kernels  6.06 us (9%)
  between operations  0.79 us (1%)
    ppermute x8, waiting for transfers between devices, exchanged(): return lax.ppermute(part, 'col', [(i, i ^ distance) for i in range(shards)])  27.2 us
    ppermute x8, starting transfers between devices, exchanged(): return lax.ppermute(part, 'col', [(i, i ^ distance) for i in range(shards)])  18.4 us
    ppermute x3, waiting for transfers between devices, per_device(): peaks.append(jnp.maximum(peaks[-1], lax.ppermute(peaks[-1], 'lvl', route)))  7.84 us
    pallas_call x6, Pallas kernels, call(): pl.pallas_call(kernel, out_shape=out_shape, in_specs=in_specs, out_specs=...  6.06 us
    ppermute x3, starting transfers between devices, per_device(): peaks.append(jnp.maximum(peaks[-1], lax.ppermute(peaks[-1], 'lvl', route)))  2.11 us
    ppermute x1, starting transfers between devices, per_device(): lax.ppermute(after(solved, down_near), 'lvl', [(i, i + 1) for i in range(...  1.45 us
  transfers between devices with their start and end apart: 12, of which 6 were waited for; matrix products, arithmetic and copies ran while one was open for 0% of the time, Pallas kernels for 6%

profile of v15, /device:TPU:0, one launch (start us, length us, event | category | flops | bytes accessed | tf_op | source)
XLA Modules:
  0.0 64.0 jit_solution(9795833572899792669)
XLA Ops:
  0.6 1.2 %shard_map.58.own_ref = f32[1544,128]{1,0:T(8,128)S(1)} custom-call(s32[1]{0:T(128)} %bitcast.place, f32[2,512,128]{2,1,0:T(8,128)} %refs_3_.1, f32[2,512,128]{2,1,0:T(8,128)} %level_ref.3, f32[2,512,128]{2,1,0:T(8,128)} %refs_4_.1), custom_call_target="tpu_custom_call" | custom-call | tf_op jit(solution)/shard_map/pallas_call | solution.py:135
  1.9 5.1 %collective-permute-start = (f32[544,128]{1,0:T(8,128)S(1)}, f32[544,128]{1,0:T(8,128)S(1)}, u32[]{:S(2)}, u32[]{:S(2)}) collective-permute-start(f32[544,128]{1,0:T(8,128)S(1)} %slice.28), channel_id=1, source_target_pairs={{0,3},{1,2},{2,1},{3,0},{4,7},{5,6},{6,5},{7,4},{8,11},{9,10},{10,... | collective-permute-start | bytes 835592 | tf_op jit(solution)/shard_map/ppermute | solution.py:150
  7.0 0.1 collective-permute-start.7
  7.1 7.5 %collective-permute-done.refs_1_ = f32[544,128]{1,0:T(8,128)S(1)} collective-permute-done((f32[544,128]{1,0:T(8,128)S(1)}, f32[544,128]{1,0:T(8,128)S(1)}, u32[]{:S(2)}, u32[]{:S(2)}) %collective-permute-start) | collective-permute-done | bytes 278560 | tf_op jit(solution)/shard_map/ppermute | solution.py:150
  14.6 4.8 %collective-permute-start.8 = (f32[544,128]{1,0:T(8,128)S(1)}, f32[544,128]{1,0:T(8,128)S(1)}, u32[]{:S(2)}, u32[]{:S(2)}) collective-permute-start(f32[544,128]{1,0:T(8,128)S(1)} %collective-permute-done.refs_1_), channel_id=1, source_target_pairs={{0,1},{1,0},{2,3},{3,2},{4,5},{5,4},{6,7},{7,6},{8,9},{9,8},{10,11... | collective-permute-start | bytes 835592 | tf_op jit(solution)/shard_map/ppermute | solution.py:150
  19.4 0.0 copy-start.2
  19.4 0.0 copy-start.1
  19.4 2.5 %collective-permute-start.1 = (f32[512,128]{1,0:T(8,128)S(1)}, f32[512,128]{1,0:T(8,128)S(1)}, u32[]{:S(2)}, u32[]{:S(2)}) collective-permute-start(f32[512,128]{1,0:T(8,128)S(1)} %get-tuple-element.20), channel_id=1, source_target_pairs={{0,3},{1,2},{2,1},{3,0},{4,7},{5,6},{6,5},{7,4},{8,11},{9,10},{10,... | collective-permute-start | bytes 786440 | tf_op jit(solution)/shard_map/ppermute | solution.py:150
  21.9 0.0 collective-permute-start.9
  21.9 0.0 collective-permute-start.3
  21.9 3.9 %collective-permute-done.3 = f32[8,128]{1,0:T(8,128)S(1)} collective-permute-done((f32[8,128]{1,0:T(8,128)S(1)}, f32[8,128]{1,0:T(8,128)S(1)}, u32[]{:S(2)}, u32[]{:S(2)}) %collective-permute-start.3) | collective-permute-done | bytes 4128 | tf_op jit(solution)/shard_map/ppermute | solution.py:181
  25.9 0.6 collective-permute-start.4
  26.5 3.9 %collective-permute-done.4 = f32[8,128]{1,0:T(8,128)S(1)} collective-permute-done((f32[8,128]{1,0:T(8,128)S(1)}, f32[8,128]{1,0:T(8,128)S(1)}, u32[]{:S(2)}, u32[]{:S(2)}) %collective-permute-start.4) | collective-permute-done | bytes 4128 | tf_op jit(solution)/shard_map/ppermute | solution.py:181
  30.4 1.5 %collective-permute-start.5 = (f32[8,128]{1,0:T(8,128)S(1)}, f32[8,128]{1,0:T(8,128)S(1)}, u32[]{:S(2)}, u32[]{:S(2)}) collective-permute-start(f32[8,128]{1,0:T(8,128)S(1)} %max.14), channel_id=1, source_target_pairs={{0,16},{4,20},{8,24},{12,28},{16,0},{20,4},{24,8},{28,12},{1,17},{... | collective-permute-start | bytes 12296 | tf_op jit(solution)/shard_map/ppermute | solution.py:181
  31.9 5.7 %collective-permute-done.1.far_ref = f32[512,128]{1,0:T(8,128)S(1)} collective-permute-done((f32[512,128]{1,0:T(8,128)S(1)}, f32[512,128]{1,0:T(8,128)S(1)}, u32[]{:S(2)}, u32[]{:S(2)}) %collective-permute-start.1) | collective-permute-done | bytes 262176 | tf_op jit(solution)/shard_map/ppermute | solution.py:150
  37.6 3.8 %collective-permute-start.2 = (f32[512,128]{1,0:T(8,128)S(1)}, f32[512,128]{1,0:T(8,128)S(1)}, u32[]{:S(2)}, u32[]{:S(2)}) collective-permute-start(f32[512,128]{1,0:T(8,128)S(1)} %slice.23), channel_id=1, source_target_pairs={{0,3},{1,2},{2,1},{3,0},{4,7},{5,6},{6,5},{7,4},{8,11},{9,10},{10,... | collective-permute-start | bytes 786440 | tf_op jit(solution)/shard_map/ppermute | solution.py:150
  41.4 0.0 collective-permute-done.5
  41.4 0.0 collective-permute-done.7.refs_0_.near_ref
  41.4 0.0 collective-permute-done.8.refs_2_
  41.4 0.0 copy-done.2
  41.4 0.0 copy-done.1
  41.4 2.4 %shard_map.60.solved_ref = f32[512,256]{1,0:T(8,128)S(1)} custom-call(s32[1]{0:T(128)} %bitcast.place, f32[1544,128]{1,0:T(8,128)S(1)} %shard_map.58.own_ref, f32[1032,128]{1,0:T(8,128)S(1)} %collective-permute-done.7.refs_0_.near_ref, f32[544,128]{1,0:T(8,128)S(1)} %collective-permute-done.refs_1_, f32[544,128]{1,0:T(8,128)S(1)} %collective-permute-done.8.refs_2_, ...), custom_call_target="tpu_custom_call" | custom-call | tf_op jit(solution)/shard_map/pallas_call | solution.py:135
  43.9 0.0 copy-start
  43.9 0.0 collective-permute-done.9.near_ref
  43.9 1.5 %collective-permute-start.10 = (f32[512,256]{1,0:T(8,128)S(1)}, f32[512,256]{1,0:T(8,128)S(1)}, u32[]{:S(2)}, u32[]{:S(2)}) collective-permute-start(f32[512,256]{1,0:T(8,128)S(1)} %shard_map.60.solved_ref), channel_id=1, source_target_pairs={{0,4},{4,8},{8,12},{12,16},{16,20},{20,24},{24,28},{1,5},{5,9},{9,... | collective-permute-start | bytes 1572872 | tf_op jit(solution)/shard_map/ppermute | solution.py:205
  45.4 2.6 %collective-permute-done.2.refs_0_.far_ref = f32[512,128]{1,0:T(8,128)S(1)} collective-permute-done((f32[512,128]{1,0:T(8,128)S(1)}, f32[512,128]{1,0:T(8,128)S(1)}, u32[]{:S(2)}, u32[]{:S(2)}) %collective-permute-start.2) | collective-permute-done | bytes 262176 | tf_op jit(solution)/shard_map/ppermute | solution.py:150
  48.0 0.1 collective-permute-start.6
  48.1 2.0 %collective-permute-start.11 = (f32[512,128]{1,0:T(8,128)S(1)}, f32[512,128]{1,0:T(8,128)S(1)}, u32[]{:S(2)}, u32[]{:S(2)}) collective-permute-start(f32[512,128]{1,0:T(8,128)S(1)} %collective-permute-done.1.far_ref), channel_id=1, source_target_pairs={{0,1},{1,0},{2,3},{3,2},{4,5},{5,4},{6,7},{7,6},{8,9},{9,8},{10,11... | collective-permute-start | bytes 786440 | tf_op jit(solution)/shard_map/ppermute | solution.py:150
  50.1 11.5 %collective-permute-done.11.last_ref = f32[512,128]{1,0:T(8,128)S(1)} collective-permute-done((f32[512,128]{1,0:T(8,128)S(1)}, f32[512,128]{1,0:T(8,128)S(1)}, u32[]{:S(2)}, u32[]{:S(2)}) %collective-permute-start.11) | collective-permute-done | bytes 262176 | tf_op jit(solution)/shard_map/ppermute | solution.py:150
  61.6 0.0 copy-done
  61.6 0.6 shard_map.61
  62.2 0.0 collective-permute-done.10.below_ref
  62.2 0.6 shard_map.62
  62.8 0.0 collective-permute-done.6.last_ref
  62.8 1.2 %shard_map.63 = (f32[1,512,128]{2,1,0:T(8,128)}, f32[1,512,128]{2,1,0:T(8,128)}, f32[1,512,128]{2,1,0:T(8,128)}) custom-call(s32[1]{0:T(128)} %bitcast.place, f32[520,128]{1,0:T(8,128)S(1)} %collective-permute-done.6.last_ref, f32[512,256]{1,0:T(8,128)S(1)} %collective-permute-done.10.below_ref, f32[512,128]{1,0:T(8,128)S(1)} %get-tuple-element.16.part_level, ...), custom_call_target="tpu_custom_call" | custom-call | tf_op jit(solution)/shard_map/pallas_call | solution.py:135
  (9 shorter events, 0.1 us)
Async XLA Ops:
  1.9 12.7 %collective-permute-start = (f32[544,128]{1,0:T(8,128)S(1)}, f32[544,128]{1,0:T(8,128)S(1)}, u32[]{:S(2)}, u32[]{:S(2)}) collective-permute-start(f32[544,128]{1,0:T(8,128)S(1)} %slice.28), channel_id=1, source_target_pairs={{0,3},{1,2},{2,1},{3,0},{4,7},{5,6},{6,5},{7,4},{8,11},{9,10},{10,... | collective-permute-start | bytes 835592 | tf_op jit(solution)/shard_map/ppermute | solution.py:150
  7.0 34.4 %collective-permute-start.7 = (f32[1032,128]{1,0:T(8,128)S(1)}, f32[1032,128]{1,0:T(8,128)S(1)}, u32[]{:S(2)}, u32[]{:S(2)}) collective-permute-start(f32[1032,128]{1,0:T(8,128)S(1)} %slice.31), channel_id=1, source_target_pairs={{0,1},{1,0},{2,3},{3,2},{4,5},{5,4},{6,7},{7,6},{8,9},{9,8},{10,11... | collective-permute-start | bytes 1585160 | tf_op jit(solution)/shard_map/ppermute | solution.py:150
  14.6 26.8 %collective-permute-start.8 = (f32[544,128]{1,0:T(8,128)S(1)}, f32[544,128]{1,0:T(8,128)S(1)}, u32[]{:S(2)}, u32[]{:S(2)}) collective-permute-start(f32[544,128]{1,0:T(8,128)S(1)} %collective-permute-done.refs_1_), channel_id=1, source_target_pairs={{0,1},{1,0},{2,3},{3,2},{4,5},{5,4},{6,7},{7,6},{8,9},{9,8},{10,11... | collective-permute-start | bytes 835592 | tf_op jit(solution)/shard_map/ppermute | solution.py:150
  19.4 22.1 %copy-start.2 = (f32[2,512,128]{2,1,0:T(8,128)S(1)}, f32[2,512,128]{2,1,0:T(8,128)}, u32[]{:S(2)}) copy-start(f32[2,512,128]{2,1,0:T(8,128)} %refs_4_.1) | copy-start | bytes 1572868
  19.4 22.0 %copy-start.1 = (f32[2,512,128]{2,1,0:T(8,128)S(1)}, f32[2,512,128]{2,1,0:T(8,128)}, u32[]{:S(2)}) copy-start(f32[2,512,128]{2,1,0:T(8,128)} %refs_3_.1) | copy-start | bytes 1572868
  19.4 18.2 %collective-permute-start.1 = (f32[512,128]{1,0:T(8,128)S(1)}, f32[512,128]{1,0:T(8,128)S(1)}, u32[]{:S(2)}, u32[]{:S(2)}) collective-permute-start(f32[512,128]{1,0:T(8,128)S(1)} %get-tuple-element.20), channel_id=1, source_target_pairs={{0,3},{1,2},{2,1},{3,0},{4,7},{5,6},{6,5},{7,4},{8,11},{9,10},{10,... | collective-permute-start | bytes 786440 | tf_op jit(solution)/shard_map/ppermute | solution.py:150
  21.9 22.0 %collective-permute-start.9 = (f32[512,128]{1,0:T(8,128)S(1)}, f32[512,128]{1,0:T(8,128)S(1)}, u32[]{:S(2)}, u32[]{:S(2)}) collective-permute-start(f32[512,128]{1,0:T(8,128)S(1)} %get-tuple-element.19), channel_id=1, source_target_pairs={{0,1},{1,0},{2,3},{3,2},{4,5},{5,4},{6,7},{7,6},{8,9},{9,8},{10,11... | collective-permute-start | bytes 786440 | tf_op jit(solution)/shard_map/ppermute | solution.py:150
  21.9 3.9 %collective-permute-start.3 = (f32[8,128]{1,0:T(8,128)S(1)}, f32[8,128]{1,0:T(8,128)S(1)}, u32[]{:S(2)}, u32[]{:S(2)}) collective-permute-start(f32[8,128]{1,0:T(8,128)S(1)} %slice_maximum_fusion), channel_id=1, source_target_pairs={{0,4},{4,8},{8,12},{12,16},{16,20},{20,24},{24,28},{28,0},{1,5},{5... | collective-permute-start | bytes 12296 | tf_op jit(solution)/shard_map/ppermute | solution.py:181
  25.9 4.5 %collective-permute-start.4 = (f32[8,128]{1,0:T(8,128)S(1)}, f32[8,128]{1,0:T(8,128)S(1)}, u32[]{:S(2)}, u32[]{:S(2)}) collective-permute-start(f32[8,128]{1,0:T(8,128)S(1)} %max.13), channel_id=1, source_target_pairs={{0,8},{4,12},{8,16},{12,20},{16,24},{20,28},{24,0},{28,4},{1,9},{5... | collective-permute-start | bytes 12296 | tf_op jit(solution)/shard_map/ppermute | solution.py:181
  30.4 11.0 %collective-permute-start.5 = (f32[8,128]{1,0:T(8,128)S(1)}, f32[8,128]{1,0:T(8,128)S(1)}, u32[]{:S(2)}, u32[]{:S(2)}) collective-permute-start(f32[8,128]{1,0:T(8,128)S(1)} %max.14), channel_id=1, source_target_pairs={{0,16},{4,20},{8,24},{12,28},{16,0},{20,4},{24,8},{28,12},{1,17},{... | collective-permute-start | bytes 12296 | tf_op jit(solution)/shard_map/ppermute | solution.py:181
  37.6 10.4 %collective-permute-start.2 = (f32[512,128]{1,0:T(8,128)S(1)}, f32[512,128]{1,0:T(8,128)S(1)}, u32[]{:S(2)}, u32[]{:S(2)}) collective-permute-start(f32[512,128]{1,0:T(8,128)S(1)} %slice.23), channel_id=1, source_target_pairs={{0,3},{1,2},{2,1},{3,0},{4,7},{5,6},{6,5},{7,4},{8,11},{9,10},{10,... | collective-permute-start | bytes 786440 | tf_op jit(solution)/shard_map/ppermute | solution.py:150
  43.9 17.7 %copy-start = (f32[2,512,128]{2,1,0:T(8,128)S(1)}, f32[2,512,128]{2,1,0:T(8,128)}, u32[]{:S(2)}) copy-start(f32[2,512,128]{2,1,0:T(8,128)} %level_ref.3) | copy-start | bytes 1572868
  43.9 18.3 %collective-permute-start.10 = (f32[512,256]{1,0:T(8,128)S(1)}, f32[512,256]{1,0:T(8,128)S(1)}, u32[]{:S(2)}, u32[]{:S(2)}) collective-permute-start(f32[512,256]{1,0:T(8,128)S(1)} %shard_map.60.solved_ref), channel_id=1, source_target_pairs={{0,4},{4,8},{8,12},{12,16},{16,20},{20,24},{24,28},{1,5},{5,9},{9,... | collective-permute-start | bytes 1572872 | tf_op jit(solution)/shard_map/ppermute | solution.py:205
  48.0 14.8 %collective-permute-start.6 = (f32[520,128]{1,0:T(8,128)S(1)}, f32[520,128]{1,0:T(8,128)S(1)}, u32[]{:S(2)}, u32[]{:S(2)}) collective-permute-start(f32[520,128]{1,0:T(8,128)S(1)} %shard_map.59), channel_id=1, source_target_pairs={{0,1},{1,0},{2,3},{3,2},{4,5},{5,4},{6,7},{7,6},{8,9},{9,8},{10,11... | collective-permute-start | bytes 798728 | tf_op jit(solution)/shard_map/ppermute | solution.py:150
  48.1 13.5 %collective-permute-start.11 = (f32[512,128]{1,0:T(8,128)S(1)}, f32[512,128]{1,0:T(8,128)S(1)}, u32[]{:S(2)}, u32[]{:S(2)}) collective-permute-start(f32[512,128]{1,0:T(8,128)S(1)} %collective-permute-done.1.far_ref), channel_id=1, source_target_pairs={{0,1},{1,0},{2,3},{3,2},{4,5},{5,4},{6,7},{7,6},{8,9},{9,8},{10,11... | collective-permute-start | bytes 786440 | tf_op jit(solution)/shard_map/ppermute | solution.py:150

commit v16 on v15

--- a/solution.py
+++ b/solution.py
@@ -173,7 +173,6 @@
     up_far = exchanged(after(sent, level_far)[up_row:down_row], 3)
     down_near = exchanged(after(sent, level_far)[down_row:], 1)
     down_far = exchanged(after(sent, up_far)[down_row:], 3)
-    up_last = exchanged(up_far, 1)
     peak = jnp.maximum(sent[phases:up_row], level_far[phases:up_row])
     peaks, reach = [peak], 1
     while reach < ranges:
@@ -181,6 +180,7 @@
         peaks.append(jnp.maximum(peaks[-1], lax.ppermute(peaks[-1], "lvl", route)))
         reach *= 2
     peak = peaks[-1]
+    up_last = exchanged(after(up_far, peak), 1)
     down_last = exchanged(stack((down_far, 0, phases), (peak, 0, PEAK_ROWS)), 1)
 
     solved = call(
@@ -202,7 +202,7 @@
             pltpu.VMEM((phases, 2 * cols), BF16),
         ],
     )
-    from_below = lax.ppermute(after(solved, down_near), "lvl", [(i, i + 1) for i in range(ranges - 1)])
+    from_below = lax.ppermute(after(solved, down_near, up_last), "lvl", [(i, i + 1) for i in range(ranges - 1)])
 
     free = pl.CostEstimate(flops=0, bytes_accessed=0, transcendentals=0)
     upper_level, part_up = call(

time: 64.2 us -> 62.6 us (0.975)
  starting transfers between devices: 22 us -> 17.9 us
  waiting for transfers between devices: 35 us -> 37.6 us
    ppermute x8, starting transfers between devices: 18.4 us -> 13.9 us  [exchanged(): return lax.ppermute(part, 'col', [(i, i ^ distance) for i in range(shards)])]
    ppermute x3, waiting for transfers between devices: 7.84 us -> 9.93 us  [per_device(): peaks.append(jnp.maximum(peaks[-1], lax.ppermute(peaks[-1], 'lvl', route)))]
  transfers between devices with their start and end apart: 12 -> 12, of which waited for: 6 -> 9; matrix products, arithmetic and copies ran while one was open for 0% -> 0% of each run, Pallas kernels for 6% -> 6%
where the time goes in v16:
time: 62.6 us; the launch traced here: 62.4 us
  waiting for transfers between devices  37.6 us (60%)
  starting transfers between devices  17.9 us (29%)
  Pallas kernels  6.05 us (10%)
  between operations  0.76 us (1%)
    ppermute x8, waiting for transfers between devices, exchanged(): return lax.ppermute(part, 'col', [(i, i ^ distance) for i in range(shards)])  27.7 us
    ppermute x8, starting transfers between devices, exchanged(): return lax.ppermute(part, 'col', [(i, i ^ distance) for i in range(shards)])  13.9 us
    ppermute x3, waiting for transfers between devices, per_device(): peaks.append(jnp.maximum(peaks[-1], lax.ppermute(peaks[-1], 'lvl', route)))  9.93 us
    pallas_call x6, Pallas kernels, call(): pl.pallas_call(kernel, out_shape=out_shape, in_specs=in_specs, out_specs=...  6.05 us
    ppermute x3, starting transfers between devices, per_device(): peaks.append(jnp.maximum(peaks[-1], lax.ppermute(peaks[-1], 'lvl', route)))  2.11 us
    ppermute x1, starting transfers between devices, per_device(): lax.ppermute(after(solved, down_near, up_last), 'lvl', [(i, i + 1) for i...  1.84 us
  transfers between devices with their start and end apart: 12, of which 9 were waited for; matrix products, arithmetic and copies ran while one was open for 0% of the time, Pallas kernels for 6%

profile of v16, /device:TPU:0, one launch (start us, length us, event | category | flops | bytes accessed | tf_op | source)
XLA Modules:
  0.0 62.4 jit_solution(6590491084535054685)
XLA Ops:
  0.6 1.2 %shard_map.58.own_ref = f32[1544,128]{1,0:T(8,128)S(1)} custom-call(s32[1]{0:T(128)} %bitcast.place, f32[2,512,128]{2,1,0:T(8,128)} %refs_3_.1, f32[2,512,128]{2,1,0:T(8,128)} %level_ref.3, f32[2,512,128]{2,1,0:T(8,128)} %refs_4_.1), custom_call_target="tpu_custom_call" | custom-call | tf_op jit(solution)/shard_map/pallas_call | solution.py:135
  1.9 5.1 %collective-permute-start = (f32[544,128]{1,0:T(8,128)S(1)}, f32[544,128]{1,0:T(8,128)S(1)}, u32[]{:S(2)}, u32[]{:S(2)}) collective-permute-start(f32[544,128]{1,0:T(8,128)S(1)} %slice.28), channel_id=1, source_target_pairs={{0,3},{1,2},{2,1},{3,0},{4,7},{5,6},{6,5},{7,4},{8,11},{9,10},{10,... | collective-permute-start | bytes 835592 | tf_op jit(solution)/shard_map/ppermute | solution.py:150
  7.0 0.1 collective-permute-start.7
  7.1 7.5 %collective-permute-done.refs_1_ = f32[544,128]{1,0:T(8,128)S(1)} collective-permute-done((f32[544,128]{1,0:T(8,128)S(1)}, f32[544,128]{1,0:T(8,128)S(1)}, u32[]{:S(2)}, u32[]{:S(2)}) %collective-permute-start) | collective-permute-done | bytes 278560 | tf_op jit(solution)/shard_map/ppermute | solution.py:150
  14.6 0.0 copy-start.2
  14.6 0.0 copy-start.1
  14.6 3.8 %collective-permute-start.1 = (f32[512,128]{1,0:T(8,128)S(1)}, f32[512,128]{1,0:T(8,128)S(1)}, u32[]{:S(2)}, u32[]{:S(2)}) collective-permute-start(f32[512,128]{1,0:T(8,128)S(1)} %get-tuple-element.22), channel_id=1, source_target_pairs={{0,3},{1,2},{2,1},{3,0},{4,7},{5,6},{6,5},{7,4},{8,11},{9,10},{10,... | collective-permute-start | bytes 786440 | tf_op jit(solution)/shard_map/ppermute | solution.py:150
  18.5 2.6 %collective-permute-start.8 = (f32[544,128]{1,0:T(8,128)S(1)}, f32[544,128]{1,0:T(8,128)S(1)}, u32[]{:S(2)}, u32[]{:S(2)}) collective-permute-start(f32[544,128]{1,0:T(8,128)S(1)} %collective-permute-done.refs_1_), channel_id=1, source_target_pairs={{0,1},{1,0},{2,3},{3,2},{4,5},{5,4},{6,7},{7,6},{8,9},{9,8},{10,11... | collective-permute-start | bytes 835592 | tf_op jit(solution)/shard_map/ppermute | solution.py:150
  21.0 0.0 collective-permute-start.3
  21.0 3.9 %collective-permute-done.3 = f32[8,128]{1,0:T(8,128)S(1)} collective-permute-done((f32[8,128]{1,0:T(8,128)S(1)}, f32[8,128]{1,0:T(8,128)S(1)}, u32[]{:S(2)}, u32[]{:S(2)}) %collective-permute-start.3) | collective-permute-done | bytes 4128 | tf_op jit(solution)/shard_map/ppermute | solution.py:180
  25.0 0.6 collective-permute-start.4
  25.6 3.9 %collective-permute-done.4 = f32[8,128]{1,0:T(8,128)S(1)} collective-permute-done((f32[8,128]{1,0:T(8,128)S(1)}, f32[8,128]{1,0:T(8,128)S(1)}, u32[]{:S(2)}, u32[]{:S(2)}) %collective-permute-start.4) | collective-permute-done | bytes 4128 | tf_op jit(solution)/shard_map/ppermute | solution.py:180
  29.5 1.5 %collective-permute-start.5 = (f32[8,128]{1,0:T(8,128)S(1)}, f32[8,128]{1,0:T(8,128)S(1)}, u32[]{:S(2)}, u32[]{:S(2)}) collective-permute-start(f32[8,128]{1,0:T(8,128)S(1)} %max.14), channel_id=1, source_target_pairs={{0,16},{4,20},{8,24},{12,28},{16,0},{20,4},{24,8},{28,12},{1,17},{... | collective-permute-start | bytes 12296 | tf_op jit(solution)/shard_map/ppermute | solution.py:180
  31.0 0.0 collective-permute-start.9
  31.0 2.1 %collective-permute-done.5 = f32[8,128]{1,0:T(8,128)S(1)} collective-permute-done((f32[8,128]{1,0:T(8,128)S(1)}, f32[8,128]{1,0:T(8,128)S(1)}, u32[]{:S(2)}, u32[]{:S(2)}) %collective-permute-start.5) | collective-permute-done | bytes 4128 | tf_op jit(solution)/shard_map/ppermute | solution.py:180
  33.1 0.0 collective-permute-done.1.far_ref
  33.1 0.0 collective-permute-start.10
  33.2 2.2 %collective-permute-start.2 = (f32[512,128]{1,0:T(8,128)S(1)}, f32[512,128]{1,0:T(8,128)S(1)}, u32[]{:S(2)}, u32[]{:S(2)}) collective-permute-start(f32[512,128]{1,0:T(8,128)S(1)} %slice.23), channel_id=1, source_target_pairs={{0,3},{1,2},{2,1},{3,0},{4,7},{5,6},{6,5},{7,4},{8,11},{9,10},{10,... | collective-permute-start | bytes 786440 | tf_op jit(solution)/shard_map/ppermute | solution.py:150
  35.4 0.0 collective-permute-done.7.refs_0_.near_ref
  35.4 1.6 %collective-permute-done.8.refs_2_ = f32[544,128]{1,0:T(8,128)S(1)} collective-permute-done((f32[544,128]{1,0:T(8,128)S(1)}, f32[544,128]{1,0:T(8,128)S(1)}, u32[]{:S(2)}, u32[]{:S(2)}) %collective-permute-start.8) | collective-permute-done | bytes 278560 | tf_op jit(solution)/shard_map/ppermute | solution.py:150
  37.0 0.0 copy-done.2
  37.0 0.0 copy-done.1
  37.0 2.4 %shard_map.60.solved_ref = f32[512,256]{1,0:T(8,128)S(1)} custom-call(s32[1]{0:T(128)} %bitcast.place, f32[1544,128]{1,0:T(8,128)S(1)} %shard_map.58.own_ref, f32[1032,128]{1,0:T(8,128)S(1)} %collective-permute-done.7.refs_0_.near_ref, f32[544,128]{1,0:T(8,128)S(1)} %collective-permute-done.refs_1_, f32[544,128]{1,0:T(8,128)S(1)} %collective-permute-done.8.refs_2_, ...), custom_call_target="tpu_custom_call" | custom-call | tf_op jit(solution)/shard_map/pallas_call | solution.py:135
  39.4 0.0 copy-start
  39.4 3.2 %collective-permute-done.9.near_ref = f32[512,128]{1,0:T(8,128)S(1)} collective-permute-done((f32[512,128]{1,0:T(8,128)S(1)}, f32[512,128]{1,0:T(8,128)S(1)}, u32[]{:S(2)}, u32[]{:S(2)}) %collective-permute-start.9) | collective-permute-done | bytes 262176 | tf_op jit(solution)/shard_map/ppermute | solution.py:150
  42.6 6.1 %collective-permute-done.10.last_ref = f32[512,128]{1,0:T(8,128)S(1)} collective-permute-done((f32[512,128]{1,0:T(8,128)S(1)}, f32[512,128]{1,0:T(8,128)S(1)}, u32[]{:S(2)}, u32[]{:S(2)}) %collective-permute-start.10) | collective-permute-done | bytes 262176 | tf_op jit(solution)/shard_map/ppermute | solution.py:150
  48.7 1.8 %collective-permute-start.11 = (f32[512,256]{1,0:T(8,128)S(1)}, f32[512,256]{1,0:T(8,128)S(1)}, u32[]{:S(2)}, u32[]{:S(2)}) collective-permute-start(f32[512,256]{1,0:T(8,128)S(1)} %shard_map.60.solved_ref), channel_id=1, source_target_pairs={{0,4},{4,8},{8,12},{12,16},{16,20},{20,24},{24,28},{1,5},{5,9},{9,... | collective-permute-start | bytes 1572872 | tf_op jit(solution)/shard_map/ppermute | solution.py:205
  50.5 3.0 %collective-permute-done.2.refs_0_.far_ref = f32[512,128]{1,0:T(8,128)S(1)} collective-permute-done((f32[512,128]{1,0:T(8,128)S(1)}, f32[512,128]{1,0:T(8,128)S(1)}, u32[]{:S(2)}, u32[]{:S(2)}) %collective-permute-start.2) | collective-permute-done | bytes 262176 | tf_op jit(solution)/shard_map/ppermute | solution.py:150
  53.6 0.1 collective-permute-start.6
  53.7 0.0 copy-done
  53.7 0.6 shard_map.61
  54.3 0.0 collective-permute-done.11.below_ref
  54.3 0.6 shard_map.62
  54.9 6.3 %collective-permute-done.6.last_ref = f32[520,128]{1,0:T(8,128)S(1)} collective-permute-done((f32[520,128]{1,0:T(8,128)S(1)}, f32[520,128]{1,0:T(8,128)S(1)}, u32[]{:S(2)}, u32[]{:S(2)}) %collective-permute-start.6) | collective-permute-done | bytes 266272 | tf_op jit(solution)/shard_map/ppermute | solution.py:150
  61.2 1.2 %shard_map.63 = (f32[1,512,128]{2,1,0:T(8,128)}, f32[1,512,128]{2,1,0:T(8,128)}, f32[1,512,128]{2,1,0:T(8,128)}) custom-call(s32[1]{0:T(128)} %bitcast.place, f32[520,128]{1,0:T(8,128)S(1)} %collective-permute-done.6.last_ref, f32[512,256]{1,0:T(8,128)S(1)} %collective-permute-done.11.below_ref, f32[512,128]{1,0:T(8,128)S(1)} %get-tuple-element.18.part_level, ...), custom_call_target="tpu_custom_call" | custom-call | tf_op jit(solution)/shard_map/pallas_call | solution.py:135
  (9 shorter events, 0.1 us)
Async XLA Ops:
  1.9 12.7 %collective-permute-start = (f32[544,128]{1,0:T(8,128)S(1)}, f32[544,128]{1,0:T(8,128)S(1)}, u32[]{:S(2)}, u32[]{:S(2)}) collective-permute-start(f32[544,128]{1,0:T(8,128)S(1)} %slice.28), channel_id=1, source_target_pairs={{0,3},{1,2},{2,1},{3,0},{4,7},{5,6},{6,5},{7,4},{8,11},{9,10},{10,... | collective-permute-start | bytes 835592 | tf_op jit(solution)/shard_map/ppermute | solution.py:150
  7.0 28.3 %collective-permute-start.7 = (f32[1032,128]{1,0:T(8,128)S(1)}, f32[1032,128]{1,0:T(8,128)S(1)}, u32[]{:S(2)}, u32[]{:S(2)}) collective-permute-start(f32[1032,128]{1,0:T(8,128)S(1)} %slice.31), channel_id=1, source_target_pairs={{0,1},{1,0},{2,3},{3,2},{4,5},{5,4},{6,7},{7,6},{8,9},{9,8},{10,11... | collective-permute-start | bytes 1585160 | tf_op jit(solution)/shard_map/ppermute | solution.py:150
  14.6 22.4 %copy-start.2 = (f32[2,512,128]{2,1,0:T(8,128)S(1)}, f32[2,512,128]{2,1,0:T(8,128)}, u32[]{:S(2)}) copy-start(f32[2,512,128]{2,1,0:T(8,128)} %refs_4_.1) | copy-start | bytes 1572868
  14.6 22.4 %copy-start.1 = (f32[2,512,128]{2,1,0:T(8,128)S(1)}, f32[2,512,128]{2,1,0:T(8,128)}, u32[]{:S(2)}) copy-start(f32[2,512,128]{2,1,0:T(8,128)} %refs_3_.1) | copy-start | bytes 1572868
  14.6 18.5 %collective-permute-start.1 = (f32[512,128]{1,0:T(8,128)S(1)}, f32[512,128]{1,0:T(8,128)S(1)}, u32[]{:S(2)}, u32[]{:S(2)}) collective-permute-start(f32[512,128]{1,0:T(8,128)S(1)} %get-tuple-element.22), channel_id=1, source_target_pairs={{0,3},{1,2},{2,1},{3,0},{4,7},{5,6},{6,5},{7,4},{8,11},{9,10},{10,... | collective-permute-start | bytes 786440 | tf_op jit(solution)/shard_map/ppermute | solution.py:150
  18.5 18.5 %collective-permute-start.8 = (f32[544,128]{1,0:T(8,128)S(1)}, f32[544,128]{1,0:T(8,128)S(1)}, u32[]{:S(2)}, u32[]{:S(2)}) collective-permute-start(f32[544,128]{1,0:T(8,128)S(1)} %collective-permute-done.refs_1_), channel_id=1, source_target_pairs={{0,1},{1,0},{2,3},{3,2},{4,5},{5,4},{6,7},{7,6},{8,9},{9,8},{10,11... | collective-permute-start | bytes 835592 | tf_op jit(solution)/shard_map/ppermute | solution.py:150
  21.0 3.9 %collective-permute-start.3 = (f32[8,128]{1,0:T(8,128)S(1)}, f32[8,128]{1,0:T(8,128)S(1)}, u32[]{:S(2)}, u32[]{:S(2)}) collective-permute-start(f32[8,128]{1,0:T(8,128)S(1)} %slice_maximum_fusion), channel_id=1, source_target_pairs={{0,4},{4,8},{8,12},{12,16},{16,20},{20,24},{24,28},{28,0},{1,5},{5... | collective-permute-start | bytes 12296 | tf_op jit(solution)/shard_map/ppermute | solution.py:180
  25.0 4.5 %collective-permute-start.4 = (f32[8,128]{1,0:T(8,128)S(1)}, f32[8,128]{1,0:T(8,128)S(1)}, u32[]{:S(2)}, u32[]{:S(2)}) collective-permute-start(f32[8,128]{1,0:T(8,128)S(1)} %max.13), channel_id=1, source_target_pairs={{0,8},{4,12},{8,16},{12,20},{16,24},{20,28},{24,0},{28,4},{1,9},{5... | collective-permute-start | bytes 12296 | tf_op jit(solution)/shard_map/ppermute | solution.py:180
  29.5 3.6 %collective-permute-start.5 = (f32[8,128]{1,0:T(8,128)S(1)}, f32[8,128]{1,0:T(8,128)S(1)}, u32[]{:S(2)}, u32[]{:S(2)}) collective-permute-start(f32[8,128]{1,0:T(8,128)S(1)} %max.14), channel_id=1, source_target_pairs={{0,16},{4,20},{8,24},{12,28},{16,0},{20,4},{24,8},{28,12},{1,17},{... | collective-permute-start | bytes 12296 | tf_op jit(solution)/shard_map/ppermute | solution.py:180
  31.0 11.6 %collective-permute-start.9 = (f32[512,128]{1,0:T(8,128)S(1)}, f32[512,128]{1,0:T(8,128)S(1)}, u32[]{:S(2)}, u32[]{:S(2)}) collective-permute-start(f32[512,128]{1,0:T(8,128)S(1)} %get-tuple-element.21), channel_id=1, source_target_pairs={{0,1},{1,0},{2,3},{3,2},{4,5},{5,4},{6,7},{7,6},{8,9},{9,8},{10,11... | collective-permute-start | bytes 786440 | tf_op jit(solution)/shard_map/ppermute | solution.py:150
  33.1 15.6 %collective-permute-start.10 = (f32[512,128]{1,0:T(8,128)S(1)}, f32[512,128]{1,0:T(8,128)S(1)}, u32[]{:S(2)}, u32[]{:S(2)}) collective-permute-start(f32[512,128]{1,0:T(8,128)S(1)} %collective-permute-done.1.far_ref), channel_id=1, source_target_pairs={{0,1},{1,0},{2,3},{3,2},{4,5},{5,4},{6,7},{7,6},{8,9},{9,8},{10,11... | collective-permute-start | bytes 786440 | tf_op jit(solution)/shard_map/ppermute | solution.py:150
  33.2 20.4 %collective-permute-start.2 = (f32[512,128]{1,0:T(8,128)S(1)}, f32[512,128]{1,0:T(8,128)S(1)}, u32[]{:S(2)}, u32[]{:S(2)}) collective-permute-start(f32[512,128]{1,0:T(8,128)S(1)} %slice.23), channel_id=1, source_target_pairs={{0,3},{1,2},{2,1},{3,0},{4,7},{5,6},{6,5},{7,4},{8,11},{9,10},{10,... | collective-permute-start | bytes 786440 | tf_op jit(solution)/shard_map/ppermute | solution.py:150
  39.4 14.2 %copy-start = (f32[2,512,128]{2,1,0:T(8,128)S(1)}, f32[2,512,128]{2,1,0:T(8,128)}, u32[]{:S(2)}) copy-start(f32[2,512,128]{2,1,0:T(8,128)} %level_ref.3) | copy-start | bytes 1572868
  48.7 5.6 %collective-permute-start.11 = (f32[512,256]{1,0:T(8,128)S(1)}, f32[512,256]{1,0:T(8,128)S(1)}, u32[]{:S(2)}, u32[]{:S(2)}) collective-permute-start(f32[512,256]{1,0:T(8,128)S(1)} %shard_map.60.solved_ref), channel_id=1, source_target_pairs={{0,4},{4,8},{8,12},{12,16},{16,20},{20,24},{24,28},{1,5},{5,9},{9,... | collective-permute-start | bytes 1572872 | tf_op jit(solution)/shard_map/ppermute | solution.py:205
  53.6 7.6 %collective-permute-start.6 = (f32[520,128]{1,0:T(8,128)S(1)}, f32[520,128]{1,0:T(8,128)S(1)}, u32[]{:S(2)}, u32[]{:S(2)}) collective-permute-start(f32[520,128]{1,0:T(8,128)S(1)} %shard_map.59), channel_id=1, source_target_pairs={{0,1},{1,0},{2,3},{3,2},{4,5},{5,4},{6,7},{7,6},{8,9},{9,8},{10,11... | collective-permute-start | bytes 798728 | tf_op jit(solution)/shard_map/ppermute | solution.py:150

commit v17 on v14

--- a/solution.py
+++ b/solution.py
@@ -9,8 +9,6 @@
 
 SWEEPS = 2
 PEAK_ROWS = 8
-PAD_ROWS = 24
-DISTANCES = (0, 1, 3, 2)
 F32 = jnp.float32
 BF16 = jnp.bfloat16
 VMEM = pl.BlockSpec(memory_space=pltpu.VMEM)
@@ -62,18 +60,24 @@
 
 
 def rows_of(place, slot, cols):
-    return pl.ds(pl.multiple_of((place[0] ^ DISTANCES[slot]) * cols, cols), cols)
-
-
-def solve_kernel(place, own_ref, *refs):
-    *blocks, up_ref, down_ref, solved_ref, inverse, high, low, s_high, s_low = refs
+    z = place[0]
+    inner = (z ^ (z >> 1)) & 1
+    return pl.ds(pl.multiple_of((z ^ (0, 1, 2 + inner, 3 - inner)[slot]) * cols, cols), cols)
+
+
+def solve_kernel(place, own_ref, near_ref, inner_ref, hand_ref, cross_ref, last_ref, up_ref, down_ref, solved_ref, *scratch):
+    inverse, high, low, s_high, s_low = scratch
     phases, cols = inverse.shape
-    blocks = [own_ref, *blocks]
     diagonal = on_diagonal(cols, cols)
-    for slot, block in enumerate(blocks):
+    blocks = [(own_ref,), (near_ref,), (inner_ref, hand_ref), (cross_ref, last_ref)]
+
+    def part(refs, rows):
+        return sum(ref[rows, :] for ref in refs[1:]) + refs[0][rows, :] if len(refs) > 1 else refs[0][rows, :]
+
+    for slot, refs in enumerate(blocks):
         rows, slot_cols = rows_of(place, slot, cols), pl.ds(slot * cols, cols)
-        high[:, slot_cols], low[:, slot_cols] = split(block[pl.ds(0, phases), :])
-        square = block[rows, :]
+        high[:, slot_cols], low[:, slot_cols] = split(part(refs, pl.ds(0, phases)))
+        square = part(refs, rows)
         rate = -jnp.sum(jnp.where(diagonal, square, 0.0), axis=1, keepdims=True)
         inverse[rows, :] = jnp.broadcast_to(1.0 / rate, (cols, cols))
         high[rows, slot_cols], low[rows, slot_cols] = split(jnp.where(diagonal, 0.0, square))
@@ -97,31 +101,33 @@
     return exact_dot(left, right)
 
 
-def upper_kernel(place, own_ref, near_ref, far_ref, solved_ref, level_ref, part_level, part_up):
+def upper_kernel(place, own_ref, near_ref, inner_ref, hand_ref, cross_ref, solved_ref, level_ref, part_level, part_up):
     phases, cols = part_up.shape
-    up = pl.ds(phases + PEAK_ROWS, phases)
-    blocks = [own_ref[up, :], near_ref[up, :], far_ref[pl.ds(0, phases), :]]
+    up, top = pl.ds(phases + PEAK_ROWS, phases), pl.ds(0, phases)
+    blocks = [own_ref[up, :], near_ref[up, :], inner_ref[up, :] + hand_ref[up, :], cross_ref[top, :]]
     upper = gathered_product(place, blocks, 0, solved_ref)
     part_up[...] = upper[:, :cols]
     part_level[...] = level_ref[0] + upper[:, cols:]
 
 
-def lower_kernel(place, own_ref, near_ref, far_ref, below_ref, upper_level, part_level, part_down):
+def lower_kernel(place, own_ref, near_ref, inner_ref, hand_ref, cross_ref, below_ref, upper_level, peak_ref, *parts):
+    part_level, part_down, part_peak = parts
     phases, cols = part_down.shape
-    blocks = [own_ref[pl.ds(2 * phases + PEAK_ROWS, phases), :], near_ref[...], far_ref[pl.ds(phases, phases), :]]
+    down, middle = pl.ds(2 * phases + PEAK_ROWS, phases), pl.ds(phases, phases)
+    blocks = [own_ref[down, :], near_ref[down, :], inner_ref[down, :] + hand_ref[down, :], cross_ref[middle, :]]
     lower = gathered_product(place, blocks, 0, below_ref)
     part_down[...] = lower[:, cols:]
     part_level[...] = upper_level[...] + lower[:, :cols]
-
-
-def output_kernel(place, last_ref, solved_ref, below_ref, *refs):
-    part_level, part_up, part_down, peak_ref, new_level, new_up, new_down = refs
+    part_peak[...] = jnp.maximum(peak_ref[...], cross_ref[pl.ds(2 * phases, PEAK_ROWS), :])
+
+
+def output_kernel(place, last_ref, solved_ref, below_ref, part_level, part_up, part_down, peak_ref, *outs):
+    new_level, new_up, new_down = outs
     phases, cols = part_up.shape
     scale = 1.0 / jnp.maximum(peak_ref[...], last_ref[pl.ds(2 * phases, PEAK_ROWS), :])[0:1, :]
-    last = len(DISTANCES) - 1
-    upper = gathered_product(place, [last_ref[pl.ds(0, phases), :]], last, solved_ref)
+    upper = gathered_product(place, [last_ref[pl.ds(0, phases), :]], 3, solved_ref)
     new_up[0] = (part_up[...] + upper[:, :cols]) * scale
-    lower = gathered_product(place, [last_ref[pl.ds(phases, phases), :]], last, below_ref)
+    lower = gathered_product(place, [last_ref[pl.ds(phases, phases), :]], 3, below_ref)
     new_down[0] = (part_down[...] + lower[:, cols:]) * scale
     new_level[0] = (part_level[...] + upper[:, cols:] + lower[:, :cols]) * scale
 
@@ -130,7 +136,7 @@
     levels, phases, cols = level_blocks.shape
     shards = lax.axis_size("col")
     ranges = lax.axis_size("lvl")
-    assert levels == 2 and shards == len(DISTANCES)
+    assert levels == 2 and shards == 4
     place = lax.axis_index("col").astype(jnp.int32).reshape(1)
     params = pltpu.CompilerParams(vmem_limit_bytes=32 * 2**20)
     shape = lambda rows, columns=cols: jax.ShapeDtypeStruct((rows, columns), F32)
@@ -150,8 +156,14 @@
     def one_level(parity):
         return pl.BlockSpec((1, phases, cols), lambda step: (parity, 0, 0))
 
-    def exchanged(part, distance):
-        return lax.ppermute(part, "col", [(i, i ^ distance) for i in range(shards)])
+    def near(part):
+        return lax.ppermute(part, "col", [(i, i ^ 1) for i in range(shards)])
+
+    def inner(part):
+        return lax.ppermute(part, "col", [(1, 2), (2, 1)])
+
+    def to_ends(part):
+        return lax.ppermute(part, "col", [(1, 0), (shards - 2, shards - 1)])
 
     def after(value, *earlier):
         return lax.optimization_barrier((value, *earlier))[0]
@@ -171,28 +183,30 @@
         *in_hbm,
         scratch=[pltpu.VMEM((levels, cols, cols), F32), pltpu.SemaphoreType.DMA((4,))],
     )
-    up_row, down_row = phases + PEAK_ROWS, 2 * phases + PEAK_ROWS
-    level_far, near = exchanged(sent[: up_row + PAD_ROWS], 3), exchanged(sent[:down_row], 1)
-    level_last = exchanged(level_far, 1)
-    even_far = exchanged(after(sent, level_far)[up_row:], 3)
-    peak = jnp.maximum(sent[phases:up_row], level_far[phases:up_row])
-    peaks, reach = [peak], 1
+    up_row = phases + PEAK_ROWS
+    near_blocks, inner_blocks = near(sent), inner(sent)
+    peak, reach = sent[phases:up_row], 1
     while reach < ranges:
         route = [(i, (i + reach) % ranges) for i in range(ranges)]
-        peaks.append(jnp.maximum(peaks[-1], lax.ppermute(peaks[-1], "lvl", route)))
+        peak = jnp.maximum(peak, lax.ppermute(peak, "lvl", route))
         reach *= 2
-    peak = peaks[-1]
-    down_near = exchanged(after(sent, level_far)[down_row:], 1)
-    even_last = exchanged(stack((even_far, 0, 2 * phases), (peak, 0, PEAK_ROWS)), 1)
+    hand_blocks = to_ends(after(inner_blocks, peak))
+    peak = jnp.maximum(peak, near(peak))
+    level_cross = inner(after(near_blocks, peak)[:phases])
+    level_last = to_ends(level_cross)
+    even_cross = inner(stack((after(near_blocks, level_cross), up_row, 2 * phases), (peak, 0, PEAK_ROWS)))
+    even_last = to_ends(even_cross)
 
     solved = call(
         solve_kernel,
         shape(phases, 2 * cols),
-        [SMEM, *[VMEM] * 4, odd, odd],
-        after(place, peak),
+        [SMEM, *[VMEM] * 6, odd, odd],
+        place,
         sent,
-        near,
-        level_far,
+        near_blocks,
+        inner_blocks,
+        hand_blocks,
+        level_cross,
         level_last,
         up_blocks,
         down_blocks,
@@ -204,31 +218,29 @@
             pltpu.VMEM((phases, 2 * cols), BF16),
         ],
     )
-    from_below = lax.ppermute(after(solved, down_near), "lvl", [(i, i + 1) for i in range(ranges - 1)])
+    from_below = lax.ppermute(solved, "lvl", [(i, i + 1) for i in range(ranges - 1)])
 
     free = pl.CostEstimate(flops=0, bytes_accessed=0, transcendentals=0)
+    evens = (sent, near_blocks, inner_blocks, hand_blocks, even_cross)
     upper_level, part_up = call(
         upper_kernel,
         (shape(phases),) * 2,
-        [SMEM, *[VMEM] * 4, even],
-        place,
-        sent,
-        near,
-        even_far,
+        [SMEM, *[VMEM] * 6, even],
+        place,
+        *evens,
         solved,
         level_blocks,
         cost_estimate=free,
     )
-    part_level, part_down = call(
+    part_level, part_down, part_peak = call(
         lower_kernel,
-        (shape(phases),) * 2,
-        [SMEM, *[VMEM] * 5],
-        place,
-        sent,
-        down_near,
-        even_far,
+        (shape(phases), shape(phases), shape(PEAK_ROWS)),
+        [SMEM, *[VMEM] * 8],
+        place,
+        *evens,
         from_below,
         upper_level,
+        peak,
         cost_estimate=free,
     )
     return call(
@@ -242,7 +254,7 @@
         part_level,
         part_up,
         part_down,
-        peak,
+        part_peak,
     )
 
 

time: 61.3 us -> 68.3 us (1.11)
  the two profiles are of different devices: /device:TPU:0 before, /device:TPU:4 now
where the time goes in v17:
time: 68.3 us; the launch traced here: 68 us
  waiting for transfers between devices  45.5 us (67%)
  starting transfers between devices  15.3 us (22%)
  Pallas kernels  6.36 us (9%)
  between operations  0.82 us (1%)
    ppermute x3, waiting for transfers between devices, to_ends(): return lax.ppermute(part, 'col', [(1, 0), (shards - 2, shards - 1)])  24.1 us
    ppermute x3, waiting for transfers between devices, per_device(): peak = jnp.maximum(peak, lax.ppermute(peak, 'lvl', route))  10.9 us
    ppermute x1, waiting for transfers between devices, per_device(): lax.ppermute(solved, 'lvl', [(i, i + 1) for i in range(ranges - 1)])  8.84 us
    pallas_call x6, Pallas kernels, call(): pl.pallas_call(kernel, out_shape=out_shape, in_specs=in_specs, out_specs=...  6.36 us
    ppermute x2, starting transfers between devices, near(): return lax.ppermute(part, 'col', [(i, i ^ 1) for i in range(shards)])  5.99 us
    ppermute x3, starting transfers between devices, to_ends(): return lax.ppermute(part, 'col', [(1, 0), (shards - 2, shards - 1)])  3.88 us
    ppermute x3, starting transfers between devices, inner(): return lax.ppermute(part, 'col', [(1, 2), (2, 1)])  2.33 us
    ppermute x1, starting transfers between devices, per_device(): lax.ppermute(solved, 'lvl', [(i, i + 1) for i in range(ranges - 1)])  1.92 us
  transfers between devices with their start and end apart: 12, of which 6 were waited for; matrix products, arithmetic and copies ran while one was open for 0% of the time, Pallas kernels for 5%

profile of v17, /device:TPU:4, one launch (start us, length us, event | category | flops | bytes accessed | tf_op | source)
XLA Modules:
  0.0 68.0 jit_solution(5782720179252433634)
XLA Ops:
  0.6 1.2 %shard_map.58.own_ref = f32[1544,128]{1,0:T(8,128)S(1)} custom-call(s32[1]{0:T(128)} %bitcast.place, f32[2,512,128]{2,1,0:T(8,128)} %up_ref.3, f32[2,512,128]{2,1,0:T(8,128)} %level_ref.3, f32[2,512,128]{2,1,0:T(8,128)} %down_ref.3), custom_call_target="tpu_custom_call" | custom-call | tf_op jit(solution)/shard_map/pallas_call | solution.py:145
  1.9 1.6 %collective-permute-start = (f32[1544,128]{1,0:T(8,128)S(1)}, f32[1544,128]{1,0:T(8,128)S(1)}, u32[]{:S(2)}, u32[]{:S(2)}) collective-permute-start(f32[1544,128]{1,0:T(8,128)S(1)} %shard_map.58.own_ref), channel_id=1, source_target_pairs={{0,1},{1,0},{2,3},{3,2},{4,5},{5,4},{6,7},{7,6},{8,9},{9,8},{10,11... | collective-permute-start | bytes 2371592 | tf_op jit(solution)/shard_map/ppermute | solution.py:160
  3.5 0.7 %collective-permute-start.8 = (f32[1544,128]{1,0:T(8,128)S(1)}, f32[1544,128]{1,0:T(8,128)S(1)}, u32[]{:S(2)}, u32[]{:S(2)}) collective-permute-start(f32[1544,128]{1,0:T(8,128)S(1)} %shard_map.58.own_ref), channel_id=1, source_target_pairs={{1,2},{2,1},{5,6},{6,5},{9,10},{10,9},{13,14},{14,13},{17,18},{18,... | collective-permute-start | bytes 2371592 | tf_op jit(solution)/shard_map/ppermute | solution.py:163
  4.2 0.1 collective-permute-start.1
  4.3 3.9 %collective-permute-done.1 = f32[8,128]{1,0:T(8,128)S(1)} collective-permute-done((f32[8,128]{1,0:T(8,128)S(1)}, f32[8,128]{1,0:T(8,128)S(1)}, u32[]{:S(2)}, u32[]{:S(2)}) %collective-permute-start.1) | collective-permute-done | bytes 4128 | tf_op jit(solution)/shard_map/ppermute | solution.py:191
  8.2 0.6 collective-permute-start.2
  8.8 3.9 %collective-permute-done.2 = f32[8,128]{1,0:T(8,128)S(1)} collective-permute-done((f32[8,128]{1,0:T(8,128)S(1)}, f32[8,128]{1,0:T(8,128)S(1)}, u32[]{:S(2)}, u32[]{:S(2)}) %collective-permute-start.2) | collective-permute-done | bytes 4128 | tf_op jit(solution)/shard_map/ppermute | solution.py:191
  12.7 0.5 collective-permute-start.3
  13.2 3.1 %collective-permute-done.3 = f32[8,128]{1,0:T(8,128)S(1)} collective-permute-done((f32[8,128]{1,0:T(8,128)S(1)}, f32[8,128]{1,0:T(8,128)S(1)}, u32[]{:S(2)}, u32[]{:S(2)}) %collective-permute-start.3) | collective-permute-done | bytes 4128 | tf_op jit(solution)/shard_map/ppermute | solution.py:191
  16.3 4.3 %collective-permute-start.4 = (f32[8,128]{1,0:T(8,128)S(1)}, f32[8,128]{1,0:T(8,128)S(1)}, u32[]{:S(2)}, u32[]{:S(2)}) collective-permute-start(f32[8,128]{1,0:T(8,128)S(1)} %max.14), channel_id=1, source_target_pairs={{0,1},{1,0},{2,3},{3,2},{4,5},{5,4},{6,7},{7,6},{8,9},{9,8},{10,11... | collective-permute-start | bytes 12296 | tf_op jit(solution)/shard_map/ppermute | solution.py:160
  20.7 1.6 %collective-permute-done.4 = f32[8,128]{1,0:T(8,128)S(1)} collective-permute-done((f32[8,128]{1,0:T(8,128)S(1)}, f32[8,128]{1,0:T(8,128)S(1)}, u32[]{:S(2)}, u32[]{:S(2)}) %collective-permute-start.4) | collective-permute-done | bytes 4128 | tf_op jit(solution)/shard_map/ppermute | solution.py:160
  22.3 0.0 collective-permute-done.refs_0_.near_ref
  22.3 0.0 copy-start
  22.3 0.0 copy-start.1
  22.3 0.8 %collective-permute-start.5 = (f32[512,128]{1,0:T(8,128)S(1)}, f32[512,128]{1,0:T(8,128)S(1)}, u32[]{:S(2)}, u32[]{:S(2)}) collective-permute-start(f32[512,128]{1,0:T(8,128)S(1)} %slice.7), channel_id=1, source_target_pairs={{1,2},{2,1},{5,6},{6,5},{9,10},{10,9},{13,14},{14,13},{17,18},{18,... | collective-permute-start | bytes 786440 | tf_op jit(solution)/shard_map/ppermute | solution.py:163
  23.1 0.0 collective-permute-done.8.inner_ref
  23.1 1.3 %collective-permute-start.9 = (f32[1544,128]{1,0:T(8,128)S(1)}, f32[1544,128]{1,0:T(8,128)S(1)}, u32[]{:S(2)}, u32[]{:S(2)}) collective-permute-start(f32[1544,128]{1,0:T(8,128)S(1)} %collective-permute-done.8.inner_ref), channel_id=1, source_target_pairs={{1,0},{2,3},{5,4},{6,7},{9,8},{10,11},{13,12},{14,15},{17,16},{18,... | collective-permute-start | bytes 2371592 | tf_op jit(solution)/shard_map/ppermute | solution.py:166
  24.4 0.0 collective-permute-done.5.cross_ref
  24.5 0.0 copy-start.2
  24.5 0.8 %collective-permute-start.6 = (f32[1032,128]{1,0:T(8,128)S(1)}, f32[1032,128]{1,0:T(8,128)S(1)}, u32[]{:S(2)}, u32[]{:S(2)}) collective-permute-start(f32[1032,128]{1,0:T(8,128)S(1)} %shard_map.59), channel_id=1, source_target_pairs={{1,2},{2,1},{5,6},{6,5},{9,10},{10,9},{13,14},{14,13},{17,18},{18,... | collective-permute-start | bytes 1585160 | tf_op jit(solution)/shard_map/ppermute | solution.py:163
  25.3 1.3 %collective-permute-start.10 = (f32[512,128]{1,0:T(8,128)S(1)}, f32[512,128]{1,0:T(8,128)S(1)}, u32[]{:S(2)}, u32[]{:S(2)}) collective-permute-start(f32[512,128]{1,0:T(8,128)S(1)} %collective-permute-done.5.cross_ref), channel_id=1, source_target_pairs={{1,0},{2,3},{5,4},{6,7},{9,8},{10,11},{13,12},{14,15},{17,16},{18,... | collective-permute-start | bytes 786440 | tf_op jit(solution)/shard_map/ppermute | solution.py:166
  26.6 0.0 collective-permute-done.6.cross_ref
  26.7 1.3 %collective-permute-start.7 = (f32[1032,128]{1,0:T(8,128)S(1)}, f32[1032,128]{1,0:T(8,128)S(1)}, u32[]{:S(2)}, u32[]{:S(2)}) collective-permute-start(f32[1032,128]{1,0:T(8,128)S(1)} %collective-permute-done.6.cross_ref), channel_id=1, source_target_pairs={{1,0},{2,3},{5,4},{6,7},{9,8},{10,11},{13,12},{14,15},{17,16},{18,... | collective-permute-start | bytes 1585160 | tf_op jit(solution)/shard_map/ppermute | solution.py:166
  28.0 24.1 %collective-permute-done.10.last_ref = f32[512,128]{1,0:T(8,128)S(1)} collective-permute-done((f32[512,128]{1,0:T(8,128)S(1)}, f32[512,128]{1,0:T(8,128)S(1)}, u32[]{:S(2)}, u32[]{:S(2)}) %collective-permute-start.10) | collective-permute-done | bytes 262176 | tf_op jit(solution)/shard_map/ppermute | solution.py:166
  52.1 0.0 collective-permute-done.9.hand_ref
  52.1 0.0 copy-done
  52.1 0.0 copy-done.1
  52.1 2.4 %shard_map.60.solved_ref = f32[512,256]{1,0:T(8,128)S(1)} custom-call(s32[1]{0:T(128)} %bitcast.place, f32[1544,128]{1,0:T(8,128)S(1)} %shard_map.58.own_ref, f32[1544,128]{1,0:T(8,128)S(1)} %collective-permute-done.refs_0_.near_ref, f32[1544,128]{1,0:T(8,128)S(1)} %collective-permute-done.8.inner_ref, f32[1544,128]{1,0:T(8,128)S(1)} %collective-permute-done.9.hand_ref, ...), custom_call_target="tpu_custom_call" | custom-call | tf_op jit(solution)/shard_map/pallas_call | solution.py:145
  54.5 1.9 %collective-permute-start.11 = (f32[512,256]{1,0:T(8,128)S(1)}, f32[512,256]{1,0:T(8,128)S(1)}, u32[]{:S(2)}, u32[]{:S(2)}) collective-permute-start(f32[512,256]{1,0:T(8,128)S(1)} %shard_map.60.solved_ref), channel_id=1, source_target_pairs={{0,4},{4,8},{8,12},{12,16},{16,20},{20,24},{24,28},{1,5},{5,9},{9,... | collective-permute-start | bytes 1572872 | tf_op jit(solution)/shard_map/ppermute | solution.py:221
  56.5 0.0 copy-done.2
  56.5 0.6 shard_map.61
  57.1 8.8 %collective-permute-done.11.below_ref = f32[512,256]{1,0:T(8,128)S(1)} collective-permute-done((f32[512,256]{1,0:T(8,128)S(1)}, f32[512,256]{1,0:T(8,128)S(1)}, u32[]{:S(2)}, u32[]{:S(2)}) %collective-permute-start.11) | collective-permute-done | bytes 524320 | tf_op jit(solution)/shard_map/ppermute | solution.py:221
  65.9 0.6 shard_map.62
  66.5 0.0 collective-permute-done.7.last_ref
  66.6 1.5 %shard_map.63 = (f32[1,512,128]{2,1,0:T(8,128)}, f32[1,512,128]{2,1,0:T(8,128)}, f32[1,512,128]{2,1,0:T(8,128)}) custom-call(s32[1]{0:T(128)} %bitcast.place, f32[1032,128]{1,0:T(8,128)S(1)} %collective-permute-done.7.last_ref, f32[512,256]{1,0:T(8,128)S(1)} %shard_map.60.solved_ref, f32[512,256]{1,0:T(8,128)S(1)} %collective-permute-done.11.below_ref, ...), custom_call_target="tpu_custom_call" | custom-call | tf_op jit(solution)/shard_map/pallas_call | solution.py:145
  (7 shorter events, 0.1 us)
Async XLA Ops:
  1.9 20.4 %collective-permute-start = (f32[1544,128]{1,0:T(8,128)S(1)}, f32[1544,128]{1,0:T(8,128)S(1)}, u32[]{:S(2)}, u32[]{:S(2)}) collective-permute-start(f32[1544,128]{1,0:T(8,128)S(1)} %shard_map.58.own_ref), channel_id=1, source_target_pairs={{0,1},{1,0},{2,3},{3,2},{4,5},{5,4},{6,7},{7,6},{8,9},{9,8},{10,11... | collective-permute-start | bytes 2371592 | tf_op jit(solution)/shard_map/ppermute | solution.py:160
  3.5 19.6 %collective-permute-start.8 = (f32[1544,128]{1,0:T(8,128)S(1)}, f32[1544,128]{1,0:T(8,128)S(1)}, u32[]{:S(2)}, u32[]{:S(2)}) collective-permute-start(f32[1544,128]{1,0:T(8,128)S(1)} %shard_map.58.own_ref), channel_id=1, source_target_pairs={{1,2},{2,1},{5,6},{6,5},{9,10},{10,9},{13,14},{14,13},{17,18},{18,... | collective-permute-start | bytes 2371592 | tf_op jit(solution)/shard_map/ppermute | solution.py:163
  4.2 4.0 %collective-permute-start.1 = (f32[8,128]{1,0:T(8,128)S(1)}, f32[8,128]{1,0:T(8,128)S(1)}, u32[]{:S(2)}, u32[]{:S(2)}) collective-permute-start(f32[8,128]{1,0:T(8,128)S(1)} %slice.8), channel_id=1, source_target_pairs={{0,4},{4,8},{8,12},{12,16},{16,20},{20,24},{24,28},{28,0},{1,5},{5... | collective-permute-start | bytes 12296 | tf_op jit(solution)/shard_map/ppermute | solution.py:191
  8.2 4.5 %collective-permute-start.2 = (f32[8,128]{1,0:T(8,128)S(1)}, f32[8,128]{1,0:T(8,128)S(1)}, u32[]{:S(2)}, u32[]{:S(2)}) collective-permute-start(f32[8,128]{1,0:T(8,128)S(1)} %slice_maximum_fusion), channel_id=1, source_target_pairs={{0,8},{4,12},{8,16},{12,20},{16,24},{20,28},{24,0},{28,4},{1,9},{5... | collective-permute-start | bytes 12296 | tf_op jit(solution)/shard_map/ppermute | solution.py:191
  12.7 3.6 %collective-permute-start.3 = (f32[8,128]{1,0:T(8,128)S(1)}, f32[8,128]{1,0:T(8,128)S(1)}, u32[]{:S(2)}, u32[]{:S(2)}) collective-permute-start(f32[8,128]{1,0:T(8,128)S(1)} %max.13), channel_id=1, source_target_pairs={{0,16},{4,20},{8,24},{12,28},{16,0},{20,4},{24,8},{28,12},{1,17},{... | collective-permute-start | bytes 12296 | tf_op jit(solution)/shard_map/ppermute | solution.py:191
  16.3 5.9 %collective-permute-start.4 = (f32[8,128]{1,0:T(8,128)S(1)}, f32[8,128]{1,0:T(8,128)S(1)}, u32[]{:S(2)}, u32[]{:S(2)}) collective-permute-start(f32[8,128]{1,0:T(8,128)S(1)} %max.14), channel_id=1, source_target_pairs={{0,1},{1,0},{2,3},{3,2},{4,5},{5,4},{6,7},{7,6},{8,9},{9,8},{10,11... | collective-permute-start | bytes 12296 | tf_op jit(solution)/shard_map/ppermute | solution.py:160
  22.3 29.8 %copy-start = (f32[2,512,128]{2,1,0:T(8,128)S(1)}, f32[2,512,128]{2,1,0:T(8,128)}, u32[]{:S(2)}) copy-start(f32[2,512,128]{2,1,0:T(8,128)} %up_ref.3) | copy-start | bytes 1572868
  22.3 29.8 %copy-start.1 = (f32[2,512,128]{2,1,0:T(8,128)S(1)}, f32[2,512,128]{2,1,0:T(8,128)}, u32[]{:S(2)}) copy-start(f32[2,512,128]{2,1,0:T(8,128)} %down_ref.3) | copy-start | bytes 1572868
  22.3 2.1 %collective-permute-start.5 = (f32[512,128]{1,0:T(8,128)S(1)}, f32[512,128]{1,0:T(8,128)S(1)}, u32[]{:S(2)}, u32[]{:S(2)}) collective-permute-start(f32[512,128]{1,0:T(8,128)S(1)} %slice.7), channel_id=1, source_target_pairs={{1,2},{2,1},{5,6},{6,5},{9,10},{10,9},{13,14},{14,13},{17,18},{18,... | collective-permute-start | bytes 786440 | tf_op jit(solution)/shard_map/ppermute | solution.py:163
  23.1 28.9 %collective-permute-start.9 = (f32[1544,128]{1,0:T(8,128)S(1)}, f32[1544,128]{1,0:T(8,128)S(1)}, u32[]{:S(2)}, u32[]{:S(2)}) collective-permute-start(f32[1544,128]{1,0:T(8,128)S(1)} %collective-permute-done.8.inner_ref), channel_id=1, source_target_pairs={{1,0},{2,3},{5,4},{6,7},{9,8},{10,11},{13,12},{14,15},{17,16},{18,... | collective-permute-start | bytes 2371592 | tf_op jit(solution)/shard_map/ppermute | solution.py:166
  24.5 32.0 %copy-start.2 = (f32[2,512,128]{2,1,0:T(8,128)S(1)}, f32[2,512,128]{2,1,0:T(8,128)}, u32[]{:S(2)}) copy-start(f32[2,512,128]{2,1,0:T(8,128)} %level_ref.3) | copy-start | bytes 1572868
  24.5 2.1 %collective-permute-start.6 = (f32[1032,128]{1,0:T(8,128)S(1)}, f32[1032,128]{1,0:T(8,128)S(1)}, u32[]{:S(2)}, u32[]{:S(2)}) collective-permute-start(f32[1032,128]{1,0:T(8,128)S(1)} %shard_map.59), channel_id=1, source_target_pairs={{1,2},{2,1},{5,6},{6,5},{9,10},{10,9},{13,14},{14,13},{17,18},{18,... | collective-permute-start | bytes 1585160 | tf_op jit(solution)/shard_map/ppermute | solution.py:163
  25.3 26.7 %collective-permute-start.10 = (f32[512,128]{1,0:T(8,128)S(1)}, f32[512,128]{1,0:T(8,128)S(1)}, u32[]{:S(2)}, u32[]{:S(2)}) collective-permute-start(f32[512,128]{1,0:T(8,128)S(1)} %collective-permute-done.5.cross_ref), channel_id=1, source_target_pairs={{1,0},{2,3},{5,4},{6,7},{9,8},{10,11},{13,12},{14,15},{17,16},{18,... | collective-permute-start | bytes 786440 | tf_op jit(solution)/shard_map/ppermute | solution.py:166
  26.7 39.9 %collective-permute-start.7 = (f32[1032,128]{1,0:T(8,128)S(1)}, f32[1032,128]{1,0:T(8,128)S(1)}, u32[]{:S(2)}, u32[]{:S(2)}) collective-permute-start(f32[1032,128]{1,0:T(8,128)S(1)} %collective-permute-done.6.cross_ref), channel_id=1, source_target_pairs={{1,0},{2,3},{5,4},{6,7},{9,8},{10,11},{13,12},{14,15},{17,16},{18,... | collective-permute-start | bytes 1585160 | tf_op jit(solution)/shard_map/ppermute | solution.py:166
  54.5 11.4 %collective-permute-start.11 = (f32[512,256]{1,0:T(8,128)S(1)}, f32[512,256]{1,0:T(8,128)S(1)}, u32[]{:S(2)}, u32[]{:S(2)}) collective-permute-start(f32[512,256]{1,0:T(8,128)S(1)} %shard_map.60.solved_ref), channel_id=1, source_target_pairs={{0,4},{4,8},{8,12},{12,16},{16,20},{20,24},{24,28},{1,5},{5,9},{9,... | collective-permute-start | bytes 1572872 | tf_op jit(solution)/shard_map/ppermute | solution.py:221

commit v18 on v17

--- a/solution.py
+++ b/solution.py
@@ -104,7 +104,7 @@
 def upper_kernel(place, own_ref, near_ref, inner_ref, hand_ref, cross_ref, solved_ref, level_ref, part_level, part_up):
     phases, cols = part_up.shape
     up, top = pl.ds(phases + PEAK_ROWS, phases), pl.ds(0, phases)
-    blocks = [own_ref[up, :], near_ref[up, :], inner_ref[up, :] + hand_ref[up, :], cross_ref[top, :]]
+    blocks = [own_ref[up, :], near_ref[top, :], inner_ref[top, :] + hand_ref[top, :], cross_ref[top, :]]
     upper = gathered_product(place, blocks, 0, solved_ref)
     part_up[...] = upper[:, :cols]
     part_level[...] = level_ref[0] + upper[:, cols:]
@@ -114,7 +114,7 @@
     part_level, part_down, part_peak = parts
     phases, cols = part_down.shape
     down, middle = pl.ds(2 * phases + PEAK_ROWS, phases), pl.ds(phases, phases)
-    blocks = [own_ref[down, :], near_ref[down, :], inner_ref[down, :] + hand_ref[down, :], cross_ref[middle, :]]
+    blocks = [own_ref[down, :], near_ref[middle, :], inner_ref[middle, :] + hand_ref[middle, :], cross_ref[middle, :]]
     lower = gathered_product(place, blocks, 0, below_ref)
     part_down[...] = lower[:, cols:]
     part_level[...] = upper_level[...] + lower[:, :cols]
@@ -184,18 +184,18 @@
         scratch=[pltpu.VMEM((levels, cols, cols), F32), pltpu.SemaphoreType.DMA((4,))],
     )
     up_row = phases + PEAK_ROWS
-    near_blocks, inner_blocks = near(sent), inner(sent)
-    peak, reach = sent[phases:up_row], 1
+    level_near, level_inner = near(sent[:up_row]), inner(sent[:up_row])
+    even_near = near(after(sent, level_near, level_inner)[up_row:])
+    level_cross, level_hand = inner(level_near), to_ends(level_inner)
+    even_inner = inner(after(sent, level_cross, level_hand)[up_row:])
+    level_last = to_ends(level_cross)
+    peak, reach = jnp.maximum(after(sent, level_inner)[phases:up_row], level_near[phases:]), 1
     while reach < ranges:
         route = [(i, (i + reach) % ranges) for i in range(ranges)]
         peak = jnp.maximum(peak, lax.ppermute(peak, "lvl", route))
         reach *= 2
-    hand_blocks = to_ends(after(inner_blocks, peak))
-    peak = jnp.maximum(peak, near(peak))
-    level_cross = inner(after(near_blocks, peak)[:phases])
-    level_last = to_ends(level_cross)
-    even_cross = inner(stack((after(near_blocks, level_cross), up_row, 2 * phases), (peak, 0, PEAK_ROWS)))
-    even_last = to_ends(even_cross)
+    even_hand = to_ends(even_inner)
+    even_cross = inner(stack((after(even_near, even_inner, level_last), 0, 2 * phases), (peak, 0, PEAK_ROWS)))
 
     solved = call(
         solve_kernel,
@@ -203,9 +203,9 @@
         [SMEM, *[VMEM] * 6, odd, odd],
         place,
         sent,
-        near_blocks,
-        inner_blocks,
-        hand_blocks,
+        level_near,
+        level_inner,
+        level_hand,
         level_cross,
         level_last,
         up_blocks,
@@ -218,10 +218,11 @@
             pltpu.VMEM((phases, 2 * cols), BF16),
         ],
     )
-    from_below = lax.ppermute(solved, "lvl", [(i, i + 1) for i in range(ranges - 1)])
+    even_last = to_ends(after(even_cross, solved))
+    from_below = lax.ppermute(after(solved, even_hand), "lvl", [(i, i + 1) for i in range(ranges - 1)])
 
     free = pl.CostEstimate(flops=0, bytes_accessed=0, transcendentals=0)
-    evens = (sent, near_blocks, inner_blocks, hand_blocks, even_cross)
+    evens = (sent, even_near, even_inner, even_hand, even_cross)
     upper_level, part_up = call(
         upper_kernel,
         (shape(phases),) * 2,

time: 68.3 us -> 68.8 us (level)
  starting transfers between devices: 15.3 us -> 20.1 us
  waiting for transfers between devices: 45.5 us -> 41.1 us
    ppermute x3 -> x4, waiting for transfers between devices: 24.1 us -> 16.4 us  [to_ends(): return lax.ppermute(part, 'col', [(1, 0), (shards - 2, shards - 1)])]
    ppermute x2, waiting for transfers between devices: 1.59 us -> 4.82 us  [near(): return lax.ppermute(part, 'col', [(i, i ^ 1) for i in range(shards)])]
    ppermute x2, starting transfers between devices: 5.99 us -> 9 us  [near(): return lax.ppermute(part, 'col', [(i, i ^ 1) for i in range(shards)])]
    ppermute x3 -> x4, starting transfers between devices: 3.88 us -> 5.16 us  [to_ends(): return lax.ppermute(part, 'col', [(1, 0), (shards - 2, shards - 1)])]
    ppermute x3 -> x4, starting transfers between devices: 2.33 us -> 2.86 us  [inner(): return lax.ppermute(part, 'col', [(1, 2), (2, 1)])]
  transfers between devices with their start and end apart: 12 -> 14, of which waited for: 6 -> 8; matrix products, arithmetic and copies ran while one was open for 0% -> 0% of each run, Pallas kernels for 5% -> 5%
where the time goes in v18:
time: 68.8 us; the launch traced here: 68.4 us
  waiting for transfers between devices  41.1 us (60%)
  starting transfers between devices  20.1 us (29%)
  Pallas kernels  6.34 us (9%)
  between operations  0.84 us (1%)
    ppermute x4, waiting for transfers between devices, to_ends(): return lax.ppermute(part, 'col', [(1, 0), (shards - 2, shards - 1)])  16.4 us
    ppermute x3, waiting for transfers between devices, per_device(): peak = jnp.maximum(peak, lax.ppermute(peak, 'lvl', route))  10.9 us
    ppermute x2, starting transfers between devices, near(): return lax.ppermute(part, 'col', [(i, i ^ 1) for i in range(shards)])  9 us
    ppermute x1, waiting for transfers between devices, per_device(): lax.ppermute(after(solved, even_hand), 'lvl', [(i, i + 1) for i in range(...  8.86 us
    pallas_call x6, Pallas kernels, call(): pl.pallas_call(kernel, out_shape=out_shape, in_specs=in_specs, out_specs=...  6.34 us
    ppermute x4, starting transfers between devices, to_ends(): return lax.ppermute(part, 'col', [(1, 0), (shards - 2, shards - 1)])  5.16 us
    ppermute x2, waiting for transfers between devices, near(): return lax.ppermute(part, 'col', [(i, i ^ 1) for i in range(shards)])  4.82 us
    ppermute x4, starting transfers between devices, inner(): return lax.ppermute(part, 'col', [(1, 2), (2, 1)])  2.86 us
  transfers between devices with their start and end apart: 14, of which 8 were waited for; matrix products, arithmetic and copies ran while one was open for 0% of the time, Pallas kernels for 5%

profile of v18, /device:TPU:4, one launch (start us, length us, event | category | flops | bytes accessed | tf_op | source)
XLA Modules:
  0.0 68.4 jit_solution(9623465167022564059)
XLA Ops:
  0.6 1.2 %shard_map.58.own_ref = f32[1544,128]{1,0:T(8,128)S(1)} custom-call(s32[1]{0:T(128)} %bitcast.place, f32[2,512,128]{2,1,0:T(8,128)} %up_ref.3, f32[2,512,128]{2,1,0:T(8,128)} %level_ref.3, f32[2,512,128]{2,1,0:T(8,128)} %down_ref.3), custom_call_target="tpu_custom_call" | custom-call | tf_op jit(solution)/shard_map/pallas_call | solution.py:145
  1.9 0.7 collective-permute-start.1
  2.6 4.4 %collective-permute-start = (f32[520,128]{1,0:T(8,128)S(1)}, f32[520,128]{1,0:T(8,128)S(1)}, u32[]{:S(2)}, u32[]{:S(2)}) collective-permute-start(f32[520,128]{1,0:T(8,128)S(1)} %slice.21), channel_id=1, source_target_pairs={{0,1},{1,0},{2,3},{3,2},{4,5},{5,4},{6,7},{7,6},{8,9},{9,8},{10,11... | collective-permute-start | bytes 798728 | tf_op jit(solution)/shard_map/ppermute | solution.py:160
  7.0 0.0 collective-permute-done.1.inner_ref
  7.0 1.3 %collective-permute-start.4 = (f32[520,128]{1,0:T(8,128)S(1)}, f32[520,128]{1,0:T(8,128)S(1)}, u32[]{:S(2)}, u32[]{:S(2)}) collective-permute-start(f32[520,128]{1,0:T(8,128)S(1)} %collective-permute-done.1.inner_ref), channel_id=1, source_target_pairs={{1,0},{2,3},{5,4},{6,7},{9,8},{10,11},{13,12},{14,15},{17,16},{18,... | collective-permute-start | bytes 798728 | tf_op jit(solution)/shard_map/ppermute | solution.py:166
  8.3 4.8 %collective-permute-done.near_ref = f32[520,128]{1,0:T(8,128)S(1)} collective-permute-done((f32[520,128]{1,0:T(8,128)S(1)}, f32[520,128]{1,0:T(8,128)S(1)}, u32[]{:S(2)}, u32[]{:S(2)}) %collective-permute-start) | collective-permute-done | bytes 266272 | tf_op jit(solution)/shard_map/ppermute | solution.py:160
  13.1 0.7 collective-permute-start.3
  13.9 4.6 %collective-permute-start.2 = (f32[1024,128]{1,0:T(8,128)S(1)}, f32[1024,128]{1,0:T(8,128)S(1)}, u32[]{:S(2)}, u32[]{:S(2)}) collective-permute-start(f32[1024,128]{1,0:T(8,128)S(1)} %slice.17), channel_id=1, source_target_pairs={{0,1},{1,0},{2,3},{3,2},{4,5},{5,4},{6,7},{7,6},{8,9},{9,8},{10,11... | collective-permute-start | bytes 1572872 | tf_op jit(solution)/shard_map/ppermute | solution.py:160
  18.4 3.7 %collective-permute-done.4.hand_ref = f32[520,128]{1,0:T(8,128)S(1)} collective-permute-done((f32[520,128]{1,0:T(8,128)S(1)}, f32[520,128]{1,0:T(8,128)S(1)}, u32[]{:S(2)}, u32[]{:S(2)}) %collective-permute-start.4) | collective-permute-done | bytes 266272 | tf_op jit(solution)/shard_map/ppermute | solution.py:166
  22.1 0.0 collective-permute-done.3.cross_ref
  22.1 0.7 %collective-permute-start.5 = (f32[1024,128]{1,0:T(8,128)S(1)}, f32[1024,128]{1,0:T(8,128)S(1)}, u32[]{:S(2)}, u32[]{:S(2)}) collective-permute-start(f32[1024,128]{1,0:T(8,128)S(1)} %slice.18), channel_id=1, source_target_pairs={{1,2},{2,1},{5,6},{6,5},{9,10},{10,9},{13,14},{14,13},{17,18},{18,... | collective-permute-start | bytes 1572872 | tf_op jit(solution)/shard_map/ppermute | solution.py:163
  22.8 1.3 %collective-permute-start.6 = (f32[520,128]{1,0:T(8,128)S(1)}, f32[520,128]{1,0:T(8,128)S(1)}, u32[]{:S(2)}, u32[]{:S(2)}) collective-permute-start(f32[520,128]{1,0:T(8,128)S(1)} %collective-permute-done.3.cross_ref), channel_id=1, source_target_pairs={{1,0},{2,3},{5,4},{6,7},{9,8},{10,11},{13,12},{14,15},{17,16},{18,... | collective-permute-start | bytes 798728 | tf_op jit(solution)/shard_map/ppermute | solution.py:166
  24.1 0.1 collective-permute-start.7
  24.2 3.9 %collective-permute-done.7 = f32[8,128]{1,0:T(8,128)S(1)} collective-permute-done((f32[8,128]{1,0:T(8,128)S(1)}, f32[8,128]{1,0:T(8,128)S(1)}, u32[]{:S(2)}, u32[]{:S(2)}) %collective-permute-start.7) | collective-permute-done | bytes 4128 | tf_op jit(solution)/shard_map/ppermute | solution.py:195
  28.1 0.6 collective-permute-start.8
  28.7 3.9 %collective-permute-done.8 = f32[8,128]{1,0:T(8,128)S(1)} collective-permute-done((f32[8,128]{1,0:T(8,128)S(1)}, f32[8,128]{1,0:T(8,128)S(1)}, u32[]{:S(2)}, u32[]{:S(2)}) %collective-permute-start.8) | collective-permute-done | bytes 4128 | tf_op jit(solution)/shard_map/ppermute | solution.py:195
  32.6 0.5 collective-permute-start.9
  33.1 3.1 %collective-permute-done.9 = f32[8,128]{1,0:T(8,128)S(1)} collective-permute-done((f32[8,128]{1,0:T(8,128)S(1)}, f32[8,128]{1,0:T(8,128)S(1)}, u32[]{:S(2)}, u32[]{:S(2)}) %collective-permute-start.9) | collective-permute-done | bytes 4128 | tf_op jit(solution)/shard_map/ppermute | solution.py:195
  36.2 0.0 copy-start.1
  36.2 0.0 copy-start.2
  36.2 0.0 collective-permute-done.2.refs_0_.near_ref
  36.2 1.0 %collective-permute-done.6.last_ref = f32[520,128]{1,0:T(8,128)S(1)} collective-permute-done((f32[520,128]{1,0:T(8,128)S(1)}, f32[520,128]{1,0:T(8,128)S(1)}, u32[]{:S(2)}, u32[]{:S(2)}) %collective-permute-start.6) | collective-permute-done | bytes 266272 | tf_op jit(solution)/shard_map/ppermute | solution.py:166
  37.2 0.0 collective-permute-done.5.inner_ref
  37.3 0.0 copy-start
  37.3 0.8 %collective-permute-start.10 = (f32[1032,128]{1,0:T(8,128)S(1)}, f32[1032,128]{1,0:T(8,128)S(1)}, u32[]{:S(2)}, u32[]{:S(2)}) collective-permute-start(f32[1032,128]{1,0:T(8,128)S(1)} %shard_map.59), channel_id=1, source_target_pairs={{1,2},{2,1},{5,6},{6,5},{9,10},{10,9},{13,14},{14,13},{17,18},{18,... | collective-permute-start | bytes 1585160 | tf_op jit(solution)/shard_map/ppermute | solution.py:163
  38.1 1.3 %collective-permute-start.12 = (f32[1024,128]{1,0:T(8,128)S(1)}, f32[1024,128]{1,0:T(8,128)S(1)}, u32[]{:S(2)}, u32[]{:S(2)}) collective-permute-start(f32[1024,128]{1,0:T(8,128)S(1)} %collective-permute-done.5.inner_ref), channel_id=1, source_target_pairs={{1,0},{2,3},{5,4},{6,7},{9,8},{10,11},{13,12},{14,15},{17,16},{18,... | collective-permute-start | bytes 1572872 | tf_op jit(solution)/shard_map/ppermute | solution.py:166
  39.4 0.0 copy-done.1
  39.4 0.0 copy-done.2
  39.4 2.4 %shard_map.60.solved_ref = f32[512,256]{1,0:T(8,128)S(1)} custom-call(s32[1]{0:T(128)} %bitcast.place, f32[1544,128]{1,0:T(8,128)S(1)} %shard_map.58.own_ref, f32[520,128]{1,0:T(8,128)S(1)} %collective-permute-done.near_ref, f32[520,128]{1,0:T(8,128)S(1)} %collective-permute-done.1.inner_ref, f32[520,128]{1,0:T(8,128)S(1)} %collective-permute-done.4.hand_ref, ...), custom_call_target="tpu_custom_call" | custom-call | tf_op jit(solution)/shard_map/pallas_call | solution.py:145
  41.9 0.0 collective-permute-done.10.cross_ref
  41.9 1.3 %collective-permute-start.11 = (f32[1032,128]{1,0:T(8,128)S(1)}, f32[1032,128]{1,0:T(8,128)S(1)}, u32[]{:S(2)}, u32[]{:S(2)}) collective-permute-start(f32[1032,128]{1,0:T(8,128)S(1)} %collective-permute-done.10.cross_ref), channel_id=1, source_target_pairs={{1,0},{2,3},{5,4},{6,7},{9,8},{10,11},{13,12},{14,15},{17,16},{18,... | collective-permute-start | bytes 1585160 | tf_op jit(solution)/shard_map/ppermute | solution.py:166
  43.2 11.8 %collective-permute-done.12.hand_ref = f32[1024,128]{1,0:T(8,128)S(1)} collective-permute-done((f32[1024,128]{1,0:T(8,128)S(1)}, f32[1024,128]{1,0:T(8,128)S(1)}, u32[]{:S(2)}, u32[]{:S(2)}) %collective-permute-start.12) | collective-permute-done | bytes 524320 | tf_op jit(solution)/shard_map/ppermute | solution.py:166
  55.0 1.9 %collective-permute-start.13 = (f32[512,256]{1,0:T(8,128)S(1)}, f32[512,256]{1,0:T(8,128)S(1)}, u32[]{:S(2)}, u32[]{:S(2)}) collective-permute-start(f32[512,256]{1,0:T(8,128)S(1)} %shard_map.60.solved_ref), channel_id=1, source_target_pairs={{0,4},{4,8},{8,12},{12,16},{16,20},{20,24},{24,28},{1,5},{5,9},{9,... | collective-permute-start | bytes 1572872 | tf_op jit(solution)/shard_map/ppermute | solution.py:222
  56.9 0.0 copy-done
  56.9 0.6 shard_map.61
  57.5 8.9 %collective-permute-done.13.below_ref = f32[512,256]{1,0:T(8,128)S(1)} collective-permute-done((f32[512,256]{1,0:T(8,128)S(1)}, f32[512,256]{1,0:T(8,128)S(1)}, u32[]{:S(2)}, u32[]{:S(2)}) %collective-permute-start.13) | collective-permute-done | bytes 524320 | tf_op jit(solution)/shard_map/ppermute | solution.py:222
  66.4 0.6 shard_map.62
  67.0 0.0 collective-permute-done.11.last_ref
  67.0 1.5 %shard_map.63 = (f32[1,512,128]{2,1,0:T(8,128)}, f32[1,512,128]{2,1,0:T(8,128)}, f32[1,512,128]{2,1,0:T(8,128)}) custom-call(s32[1]{0:T(128)} %bitcast.place, f32[1032,128]{1,0:T(8,128)S(1)} %collective-permute-done.11.last_ref, f32[512,256]{1,0:T(8,128)S(1)} %shard_map.60.solved_ref, f32[512,256]{1,0:T(8,128)S(1)} %collective-permute-done.13.below_ref, ...), custom_call_target="tpu_custom_call" | custom-call | tf_op jit(solution)/shard_map/pallas_call | solution.py:145
  (8 shorter events, 0.1 us)
Async XLA Ops:
  1.9 5.1 %collective-permute-start.1 = (f32[520,128]{1,0:T(8,128)S(1)}, f32[520,128]{1,0:T(8,128)S(1)}, u32[]{:S(2)}, u32[]{:S(2)}) collective-permute-start(f32[520,128]{1,0:T(8,128)S(1)} %slice.21), channel_id=1, source_target_pairs={{1,2},{2,1},{5,6},{6,5},{9,10},{10,9},{13,14},{14,13},{17,18},{18,... | collective-permute-start | bytes 798728 | tf_op jit(solution)/shard_map/ppermute | solution.py:163
  2.6 10.6 %collective-permute-start = (f32[520,128]{1,0:T(8,128)S(1)}, f32[520,128]{1,0:T(8,128)S(1)}, u32[]{:S(2)}, u32[]{:S(2)}) collective-permute-start(f32[520,128]{1,0:T(8,128)S(1)} %slice.21), channel_id=1, source_target_pairs={{0,1},{1,0},{2,3},{3,2},{4,5},{5,4},{6,7},{7,6},{8,9},{9,8},{10,11... | collective-permute-start | bytes 798728 | tf_op jit(solution)/shard_map/ppermute | solution.py:160
  7.0 15.0 %collective-permute-start.4 = (f32[520,128]{1,0:T(8,128)S(1)}, f32[520,128]{1,0:T(8,128)S(1)}, u32[]{:S(2)}, u32[]{:S(2)}) collective-permute-start(f32[520,128]{1,0:T(8,128)S(1)} %collective-permute-done.1.inner_ref), channel_id=1, source_target_pairs={{1,0},{2,3},{5,4},{6,7},{9,8},{10,11},{13,12},{14,15},{17,16},{18,... | collective-permute-start | bytes 798728 | tf_op jit(solution)/shard_map/ppermute | solution.py:166
  13.1 8.9 %collective-permute-start.3 = (f32[520,128]{1,0:T(8,128)S(1)}, f32[520,128]{1,0:T(8,128)S(1)}, u32[]{:S(2)}, u32[]{:S(2)}) collective-permute-start(f32[520,128]{1,0:T(8,128)S(1)} %collective-permute-done.near_ref), channel_id=1, source_target_pairs={{1,2},{2,1},{5,6},{6,5},{9,10},{10,9},{13,14},{14,13},{17,18},{18,... | collective-permute-start | bytes 798728 | tf_op jit(solution)/shard_map/ppermute | solution.py:163
  13.9 22.4 %collective-permute-start.2 = (f32[1024,128]{1,0:T(8,128)S(1)}, f32[1024,128]{1,0:T(8,128)S(1)}, u32[]{:S(2)}, u32[]{:S(2)}) collective-permute-start(f32[1024,128]{1,0:T(8,128)S(1)} %slice.17), channel_id=1, source_target_pairs={{0,1},{1,0},{2,3},{3,2},{4,5},{5,4},{6,7},{7,6},{8,9},{9,8},{10,11... | collective-permute-start | bytes 1572872 | tf_op jit(solution)/shard_map/ppermute | solution.py:160
  22.1 15.1 %collective-permute-start.5 = (f32[1024,128]{1,0:T(8,128)S(1)}, f32[1024,128]{1,0:T(8,128)S(1)}, u32[]{:S(2)}, u32[]{:S(2)}) collective-permute-start(f32[1024,128]{1,0:T(8,128)S(1)} %slice.18), channel_id=1, source_target_pairs={{1,2},{2,1},{5,6},{6,5},{9,10},{10,9},{13,14},{14,13},{17,18},{18,... | collective-permute-start | bytes 1572872 | tf_op jit(solution)/shard_map/ppermute | solution.py:163
  22.8 14.4 %collective-permute-start.6 = (f32[520,128]{1,0:T(8,128)S(1)}, f32[520,128]{1,0:T(8,128)S(1)}, u32[]{:S(2)}, u32[]{:S(2)}) collective-permute-start(f32[520,128]{1,0:T(8,128)S(1)} %collective-permute-done.3.cross_ref), channel_id=1, source_target_pairs={{1,0},{2,3},{5,4},{6,7},{9,8},{10,11},{13,12},{14,15},{17,16},{18,... | collective-permute-start | bytes 798728 | tf_op jit(solution)/shard_map/ppermute | solution.py:166
  24.1 4.0 %collective-permute-start.7 = (f32[8,128]{1,0:T(8,128)S(1)}, f32[8,128]{1,0:T(8,128)S(1)}, u32[]{:S(2)}, u32[]{:S(2)}) collective-permute-start(f32[8,128]{1,0:T(8,128)S(1)} %slice_maximum_fusion), channel_id=1, source_target_pairs={{0,4},{4,8},{8,12},{12,16},{16,20},{20,24},{24,28},{28,0},{1,5},{5... | collective-permute-start | bytes 12296 | tf_op jit(solution)/shard_map/ppermute | solution.py:195
  28.1 4.5 %collective-permute-start.8 = (f32[8,128]{1,0:T(8,128)S(1)}, f32[8,128]{1,0:T(8,128)S(1)}, u32[]{:S(2)}, u32[]{:S(2)}) collective-permute-start(f32[8,128]{1,0:T(8,128)S(1)} %max.13), channel_id=1, source_target_pairs={{0,8},{4,12},{8,16},{12,20},{16,24},{20,28},{24,0},{28,4},{1,9},{5... | collective-permute-start | bytes 12296 | tf_op jit(solution)/shard_map/ppermute | solution.py:195
  32.6 3.6 %collective-permute-start.9 = (f32[8,128]{1,0:T(8,128)S(1)}, f32[8,128]{1,0:T(8,128)S(1)}, u32[]{:S(2)}, u32[]{:S(2)}) collective-permute-start(f32[8,128]{1,0:T(8,128)S(1)} %max.14), channel_id=1, source_target_pairs={{0,16},{4,20},{8,24},{12,28},{16,0},{20,4},{24,8},{28,12},{1,17},{... | collective-permute-start | bytes 12296 | tf_op jit(solution)/shard_map/ppermute | solution.py:195
  36.2 3.2 %copy-start.1 = (f32[2,512,128]{2,1,0:T(8,128)S(1)}, f32[2,512,128]{2,1,0:T(8,128)}, u32[]{:S(2)}) copy-start(f32[2,512,128]{2,1,0:T(8,128)} %up_ref.3) | copy-start | bytes 1572868
  36.2 3.2 %copy-start.2 = (f32[2,512,128]{2,1,0:T(8,128)S(1)}, f32[2,512,128]{2,1,0:T(8,128)}, u32[]{:S(2)}) copy-start(f32[2,512,128]{2,1,0:T(8,128)} %down_ref.3) | copy-start | bytes 1572868
  37.3 19.6 %copy-start = (f32[2,512,128]{2,1,0:T(8,128)S(1)}, f32[2,512,128]{2,1,0:T(8,128)}, u32[]{:S(2)}) copy-start(f32[2,512,128]{2,1,0:T(8,128)} %level_ref.3) | copy-start | bytes 1572868
  37.3 4.6 %collective-permute-start.10 = (f32[1032,128]{1,0:T(8,128)S(1)}, f32[1032,128]{1,0:T(8,128)S(1)}, u32[]{:S(2)}, u32[]{:S(2)}) collective-permute-start(f32[1032,128]{1,0:T(8,128)S(1)} %shard_map.59), channel_id=1, source_target_pairs={{1,2},{2,1},{5,6},{6,5},{9,10},{10,9},{13,14},{14,13},{17,18},{18,... | collective-permute-start | bytes 1585160 | tf_op jit(solution)/shard_map/ppermute | solution.py:163
  38.1 16.9 %collective-permute-start.12 = (f32[1024,128]{1,0:T(8,128)S(1)}, f32[1024,128]{1,0:T(8,128)S(1)}, u32[]{:S(2)}, u32[]{:S(2)}) collective-permute-start(f32[1024,128]{1,0:T(8,128)S(1)} %collective-permute-done.5.inner_ref), channel_id=1, source_target_pairs={{1,0},{2,3},{5,4},{6,7},{9,8},{10,11},{13,12},{14,15},{17,16},{18,... | collective-permute-start | bytes 1572872 | tf_op jit(solution)/shard_map/ppermute | solution.py:166
  41.9 25.1 %collective-permute-start.11 = (f32[1032,128]{1,0:T(8,128)S(1)}, f32[1032,128]{1,0:T(8,128)S(1)}, u32[]{:S(2)}, u32[]{:S(2)}) collective-permute-start(f32[1032,128]{1,0:T(8,128)S(1)} %collective-permute-done.10.cross_ref), channel_id=1, source_target_pairs={{1,0},{2,3},{5,4},{6,7},{9,8},{10,11},{13,12},{14,15},{17,16},{18,... | collective-permute-start | bytes 1585160 | tf_op jit(solution)/shard_map/ppermute | solution.py:166
  55.0 11.4 %collective-permute-start.13 = (f32[512,256]{1,0:T(8,128)S(1)}, f32[512,256]{1,0:T(8,128)S(1)}, u32[]{:S(2)}, u32[]{:S(2)}) collective-permute-start(f32[512,256]{1,0:T(8,128)S(1)} %shard_map.60.solved_ref), channel_id=1, source_target_pairs={{0,4},{4,8},{8,12},{12,16},{16,20},{20,24},{24,28},{1,5},{5,9},{9,... | collective-permute-start | bytes 1572872 | tf_op jit(solution)/shard_map/ppermute | solution.py:222

commit v19 on v16

--- a/solution.py
+++ b/solution.py
@@ -172,7 +172,6 @@
     level_last = exchanged(level_far, 1)
     up_far = exchanged(after(sent, level_far)[up_row:down_row], 3)
     down_near = exchanged(after(sent, level_far)[down_row:], 1)
-    down_far = exchanged(after(sent, up_far)[down_row:], 3)
     peak = jnp.maximum(sent[phases:up_row], level_far[phases:up_row])
     peaks, reach = [peak], 1
     while reach < ranges:
@@ -180,8 +179,9 @@
         peaks.append(jnp.maximum(peaks[-1], lax.ppermute(peaks[-1], "lvl", route)))
         reach *= 2
     peak = peaks[-1]
+    down_far = exchanged(after(sent, peaks[2 % len(peaks)])[down_row:], 3)
     up_last = exchanged(after(up_far, peak), 1)
-    down_last = exchanged(stack((down_far, 0, phases), (peak, 0, PEAK_ROWS)), 1)
+    down_last = exchanged(stack((after(down_far, up_last), 0, phases), (peak, 0, PEAK_ROWS)), 1)
 
     solved = call(
         solve_kernel,
@@ -202,7 +202,7 @@
             pltpu.VMEM((phases, 2 * cols), BF16),
         ],
     )
-    from_below = lax.ppermute(after(solved, down_near, up_last), "lvl", [(i, i + 1) for i in range(ranges - 1)])
+    from_below = lax.ppermute(after(solved, down_near), "lvl", [(i, i + 1) for i in range(ranges - 1)])
 
     free = pl.CostEstimate(flops=0, bytes_accessed=0, transcendentals=0)
     upper_level, part_up = call(

time: 62.6 us -> 63.3 us (1.011)
  starting transfers between devices: 17.9 us -> 19.5 us
  waiting for transfers between devices: 37.6 us -> 36.7 us
    ppermute x8, starting transfers between devices: 13.9 us -> 15.7 us  [exchanged(): return lax.ppermute(part, 'col', [(i, i ^ distance) for i in range(shards)])]
    ppermute x8, waiting for transfers between devices: 27.7 us -> 26.8 us  [exchanged(): return lax.ppermute(part, 'col', [(i, i ^ distance) for i in range(shards)])]
where the time goes in v19:
time: 63.3 us; the launch traced here: 63.1 us
  waiting for transfers between devices  36.7 us (58%)
  starting transfers between devices  19.5 us (31%)
  Pallas kernels  6.05 us (10%)
  between operations  0.76 us (1%)
    ppermute x8, waiting for transfers between devices, exchanged(): return lax.ppermute(part, 'col', [(i, i ^ distance) for i in range(shards)])  26.8 us
    ppermute x8, starting transfers between devices, exchanged(): return lax.ppermute(part, 'col', [(i, i ^ distance) for i in range(shards)])  15.7 us
    ppermute x3, waiting for transfers between devices, per_device(): peaks.append(jnp.maximum(peaks[-1], lax.ppermute(peaks[-1], 'lvl', route)))  9.9 us
    pallas_call x6, Pallas kernels, call(): pl.pallas_call(kernel, out_shape=out_shape, in_specs=in_specs, out_specs=...  6.05 us
    ppermute x3, starting transfers between devices, per_device(): peaks.append(jnp.maximum(peaks[-1], lax.ppermute(peaks[-1], 'lvl', route)))  2.11 us
    ppermute x1, starting transfers between devices, per_device(): lax.ppermute(after(solved, down_near), 'lvl', [(i, i + 1) for i in range(...  1.72 us
  transfers between devices with their start and end apart: 12, of which 9 were waited for; matrix products, arithmetic and copies ran while one was open for 0% of the time, Pallas kernels for 6%

profile of v19, /device:TPU:0, one launch (start us, length us, event | category | flops | bytes accessed | tf_op | source)
XLA Modules:
  0.0 63.1 jit_solution(10675190913429329751)
XLA Ops:
  0.6 1.2 %shard_map.58.own_ref = f32[1544,128]{1,0:T(8,128)S(1)} custom-call(s32[1]{0:T(128)} %bitcast.place, f32[2,512,128]{2,1,0:T(8,128)} %refs_3_.1, f32[2,512,128]{2,1,0:T(8,128)} %level_ref.3, f32[2,512,128]{2,1,0:T(8,128)} %refs_4_.1), custom_call_target="tpu_custom_call" | custom-call | tf_op jit(solution)/shard_map/pallas_call | solution.py:135
  1.9 5.1 %collective-permute-start = (f32[544,128]{1,0:T(8,128)S(1)}, f32[544,128]{1,0:T(8,128)S(1)}, u32[]{:S(2)}, u32[]{:S(2)}) collective-permute-start(f32[544,128]{1,0:T(8,128)S(1)} %slice.29), channel_id=1, source_target_pairs={{0,3},{1,2},{2,1},{3,0},{4,7},{5,6},{6,5},{7,4},{8,11},{9,10},{10,... | collective-permute-start | bytes 835592 | tf_op jit(solution)/shard_map/ppermute | solution.py:150
  7.0 0.1 collective-permute-start.8
  7.1 7.5 %collective-permute-done.refs_1_ = f32[544,128]{1,0:T(8,128)S(1)} collective-permute-done((f32[544,128]{1,0:T(8,128)S(1)}, f32[544,128]{1,0:T(8,128)S(1)}, u32[]{:S(2)}, u32[]{:S(2)}) %collective-permute-start) | collective-permute-done | bytes 278560 | tf_op jit(solution)/shard_map/ppermute | solution.py:150
  14.6 4.8 %collective-permute-start.9 = (f32[544,128]{1,0:T(8,128)S(1)}, f32[544,128]{1,0:T(8,128)S(1)}, u32[]{:S(2)}, u32[]{:S(2)}) collective-permute-start(f32[544,128]{1,0:T(8,128)S(1)} %collective-permute-done.refs_1_), channel_id=1, source_target_pairs={{0,1},{1,0},{2,3},{3,2},{4,5},{5,4},{6,7},{7,6},{8,9},{9,8},{10,11... | collective-permute-start | bytes 835592 | tf_op jit(solution)/shard_map/ppermute | solution.py:150
  19.4 0.0 copy-start.2
  19.4 0.0 copy-start.1
  19.4 2.5 %collective-permute-start.4 = (f32[512,128]{1,0:T(8,128)S(1)}, f32[512,128]{1,0:T(8,128)S(1)}, u32[]{:S(2)}, u32[]{:S(2)}) collective-permute-start(f32[512,128]{1,0:T(8,128)S(1)} %get-tuple-element.24), channel_id=1, source_target_pairs={{0,3},{1,2},{2,1},{3,0},{4,7},{5,6},{6,5},{7,4},{8,11},{9,10},{10,... | collective-permute-start | bytes 786440 | tf_op jit(solution)/shard_map/ppermute | solution.py:150
  21.9 0.0 collective-permute-start.10
  21.9 0.0 collective-permute-start.1
  21.9 3.9 %collective-permute-done.1 = f32[8,128]{1,0:T(8,128)S(1)} collective-permute-done((f32[8,128]{1,0:T(8,128)S(1)}, f32[8,128]{1,0:T(8,128)S(1)}, u32[]{:S(2)}, u32[]{:S(2)}) %collective-permute-start.1) | collective-permute-done | bytes 4128 | tf_op jit(solution)/shard_map/ppermute | solution.py:179
  25.9 0.6 collective-permute-start.2
  26.5 3.9 %collective-permute-done.2 = f32[8,128]{1,0:T(8,128)S(1)} collective-permute-done((f32[8,128]{1,0:T(8,128)S(1)}, f32[8,128]{1,0:T(8,128)S(1)}, u32[]{:S(2)}, u32[]{:S(2)}) %collective-permute-start.2) | collective-permute-done | bytes 4128 | tf_op jit(solution)/shard_map/ppermute | solution.py:179
  30.4 1.5 %collective-permute-start.5 = (f32[8,128]{1,0:T(8,128)S(1)}, f32[8,128]{1,0:T(8,128)S(1)}, u32[]{:S(2)}, u32[]{:S(2)}) collective-permute-start(f32[8,128]{1,0:T(8,128)S(1)} %max.14), channel_id=1, source_target_pairs={{0,16},{4,20},{8,24},{12,28},{16,0},{20,4},{24,8},{28,12},{1,17},{... | collective-permute-start | bytes 12296 | tf_op jit(solution)/shard_map/ppermute | solution.py:179
  31.9 2.1 %collective-permute-done.5 = f32[8,128]{1,0:T(8,128)S(1)} collective-permute-done((f32[8,128]{1,0:T(8,128)S(1)}, f32[8,128]{1,0:T(8,128)S(1)}, u32[]{:S(2)}, u32[]{:S(2)}) %collective-permute-start.5) | collective-permute-done | bytes 4128 | tf_op jit(solution)/shard_map/ppermute | solution.py:179
  34.0 1.4 %collective-permute-start.3 = (f32[512,128]{1,0:T(8,128)S(1)}, f32[512,128]{1,0:T(8,128)S(1)}, u32[]{:S(2)}, u32[]{:S(2)}) collective-permute-start(f32[512,128]{1,0:T(8,128)S(1)} %slice.24), channel_id=1, source_target_pairs={{0,3},{1,2},{2,1},{3,0},{4,7},{5,6},{6,5},{7,4},{8,11},{9,10},{10,... | collective-permute-start | bytes 786440 | tf_op jit(solution)/shard_map/ppermute | solution.py:150
  35.4 2.1 %collective-permute-done.4.far_ref = f32[512,128]{1,0:T(8,128)S(1)} collective-permute-done((f32[512,128]{1,0:T(8,128)S(1)}, f32[512,128]{1,0:T(8,128)S(1)}, u32[]{:S(2)}, u32[]{:S(2)}) %collective-permute-start.4) | collective-permute-done | bytes 262176 | tf_op jit(solution)/shard_map/ppermute | solution.py:150
  37.5 0.0 collective-permute-start.6
  37.5 0.0 collective-permute-done.8.refs_0_.near_ref
  37.5 0.0 collective-permute-done.9.refs_2_
  37.5 0.0 copy-done.2
  37.5 0.0 copy-done.1
  37.5 2.4 %shard_map.60.solved_ref = f32[512,256]{1,0:T(8,128)S(1)} custom-call(s32[1]{0:T(128)} %bitcast.place, f32[1544,128]{1,0:T(8,128)S(1)} %shard_map.58.own_ref, f32[1032,128]{1,0:T(8,128)S(1)} %collective-permute-done.8.refs_0_.near_ref, f32[544,128]{1,0:T(8,128)S(1)} %collective-permute-done.refs_1_, f32[544,128]{1,0:T(8,128)S(1)} %collective-permute-done.9.refs_2_, ...), custom_call_target="tpu_custom_call" | custom-call | tf_op jit(solution)/shard_map/pallas_call | solution.py:135
  40.0 0.0 copy-start
  40.0 3.2 %collective-permute-done.10.near_ref = f32[512,128]{1,0:T(8,128)S(1)} collective-permute-done((f32[512,128]{1,0:T(8,128)S(1)}, f32[512,128]{1,0:T(8,128)S(1)}, u32[]{:S(2)}, u32[]{:S(2)}) %collective-permute-start.10) | collective-permute-done | bytes 262176 | tf_op jit(solution)/shard_map/ppermute | solution.py:150
  43.2 1.7 %collective-permute-start.11 = (f32[512,256]{1,0:T(8,128)S(1)}, f32[512,256]{1,0:T(8,128)S(1)}, u32[]{:S(2)}, u32[]{:S(2)}) collective-permute-start(f32[512,256]{1,0:T(8,128)S(1)} %shard_map.60.solved_ref), channel_id=1, source_target_pairs={{0,4},{4,8},{8,12},{12,16},{16,20},{20,24},{24,28},{1,5},{5,9},{9,... | collective-permute-start | bytes 1572872 | tf_op jit(solution)/shard_map/ppermute | solution.py:205
  44.9 3.8 %collective-permute-done.3.refs_0_.far_ref = f32[512,128]{1,0:T(8,128)S(1)} collective-permute-done((f32[512,128]{1,0:T(8,128)S(1)}, f32[512,128]{1,0:T(8,128)S(1)}, u32[]{:S(2)}, u32[]{:S(2)}) %collective-permute-start.3) | collective-permute-done | bytes 262176 | tf_op jit(solution)/shard_map/ppermute | solution.py:150
  48.8 4.8 %collective-permute-done.6.last_ref = f32[512,128]{1,0:T(8,128)S(1)} collective-permute-done((f32[512,128]{1,0:T(8,128)S(1)}, f32[512,128]{1,0:T(8,128)S(1)}, u32[]{:S(2)}, u32[]{:S(2)}) %collective-permute-start.6) | collective-permute-done | bytes 262176 | tf_op jit(solution)/shard_map/ppermute | solution.py:150
  53.5 1.8 %collective-permute-start.7 = (f32[520,128]{1,0:T(8,128)S(1)}, f32[520,128]{1,0:T(8,128)S(1)}, u32[]{:S(2)}, u32[]{:S(2)}) collective-permute-start(f32[520,128]{1,0:T(8,128)S(1)} %shard_map.59), channel_id=1, source_target_pairs={{0,1},{1,0},{2,3},{3,2},{4,5},{5,4},{6,7},{7,6},{8,9},{9,8},{10,11... | collective-permute-start | bytes 798728 | tf_op jit(solution)/shard_map/ppermute | solution.py:150
  55.3 0.0 copy-done
  55.3 0.6 shard_map.61
  55.9 0.0 collective-permute-done.11.below_ref
  56.0 0.6 shard_map.62
  56.6 5.4 %collective-permute-done.7.last_ref = f32[520,128]{1,0:T(8,128)S(1)} collective-permute-done((f32[520,128]{1,0:T(8,128)S(1)}, f32[520,128]{1,0:T(8,128)S(1)}, u32[]{:S(2)}, u32[]{:S(2)}) %collective-permute-start.7) | collective-permute-done | bytes 266272 | tf_op jit(solution)/shard_map/ppermute | solution.py:150
  61.9 1.2 %shard_map.63 = (f32[1,512,128]{2,1,0:T(8,128)}, f32[1,512,128]{2,1,0:T(8,128)}, f32[1,512,128]{2,1,0:T(8,128)}) custom-call(s32[1]{0:T(128)} %bitcast.place, f32[520,128]{1,0:T(8,128)S(1)} %collective-permute-done.7.last_ref, f32[512,256]{1,0:T(8,128)S(1)} %collective-permute-done.11.below_ref, f32[512,128]{1,0:T(8,128)S(1)} %get-tuple-element.20.part_level, ...), custom_call_target="tpu_custom_call" | custom-call | tf_op jit(solution)/shard_map/pallas_call | solution.py:135
  (9 shorter events, 0.1 us)
Async XLA Ops:
  1.9 12.7 %collective-permute-start = (f32[544,128]{1,0:T(8,128)S(1)}, f32[544,128]{1,0:T(8,128)S(1)}, u32[]{:S(2)}, u32[]{:S(2)}) collective-permute-start(f32[544,128]{1,0:T(8,128)S(1)} %slice.29), channel_id=1, source_target_pairs={{0,3},{1,2},{2,1},{3,0},{4,7},{5,6},{6,5},{7,4},{8,11},{9,10},{10,... | collective-permute-start | bytes 835592 | tf_op jit(solution)/shard_map/ppermute | solution.py:150
  7.0 30.5 %collective-permute-start.8 = (f32[1032,128]{1,0:T(8,128)S(1)}, f32[1032,128]{1,0:T(8,128)S(1)}, u32[]{:S(2)}, u32[]{:S(2)}) collective-permute-start(f32[1032,128]{1,0:T(8,128)S(1)} %slice.31), channel_id=1, source_target_pairs={{0,1},{1,0},{2,3},{3,2},{4,5},{5,4},{6,7},{7,6},{8,9},{9,8},{10,11... | collective-permute-start | bytes 1585160 | tf_op jit(solution)/shard_map/ppermute | solution.py:150
  14.6 23.0 %collective-permute-start.9 = (f32[544,128]{1,0:T(8,128)S(1)}, f32[544,128]{1,0:T(8,128)S(1)}, u32[]{:S(2)}, u32[]{:S(2)}) collective-permute-start(f32[544,128]{1,0:T(8,128)S(1)} %collective-permute-done.refs_1_), channel_id=1, source_target_pairs={{0,1},{1,0},{2,3},{3,2},{4,5},{5,4},{6,7},{7,6},{8,9},{9,8},{10,11... | collective-permute-start | bytes 835592 | tf_op jit(solution)/shard_map/ppermute | solution.py:150
  19.4 18.2 %copy-start.2 = (f32[2,512,128]{2,1,0:T(8,128)S(1)}, f32[2,512,128]{2,1,0:T(8,128)}, u32[]{:S(2)}) copy-start(f32[2,512,128]{2,1,0:T(8,128)} %refs_4_.1) | copy-start | bytes 1572868
  19.4 18.1 %copy-start.1 = (f32[2,512,128]{2,1,0:T(8,128)S(1)}, f32[2,512,128]{2,1,0:T(8,128)}, u32[]{:S(2)}) copy-start(f32[2,512,128]{2,1,0:T(8,128)} %refs_3_.1) | copy-start | bytes 1572868
  19.4 18.1 %collective-permute-start.4 = (f32[512,128]{1,0:T(8,128)S(1)}, f32[512,128]{1,0:T(8,128)S(1)}, u32[]{:S(2)}, u32[]{:S(2)}) collective-permute-start(f32[512,128]{1,0:T(8,128)S(1)} %get-tuple-element.24), channel_id=1, source_target_pairs={{0,3},{1,2},{2,1},{3,0},{4,7},{5,6},{6,5},{7,4},{8,11},{9,10},{10,... | collective-permute-start | bytes 786440 | tf_op jit(solution)/shard_map/ppermute | solution.py:150
  21.9 21.3 %collective-permute-start.10 = (f32[512,128]{1,0:T(8,128)S(1)}, f32[512,128]{1,0:T(8,128)S(1)}, u32[]{:S(2)}, u32[]{:S(2)}) collective-permute-start(f32[512,128]{1,0:T(8,128)S(1)} %get-tuple-element.23), channel_id=1, source_target_pairs={{0,1},{1,0},{2,3},{3,2},{4,5},{5,4},{6,7},{7,6},{8,9},{9,8},{10,11... | collective-permute-start | bytes 786440 | tf_op jit(solution)/shard_map/ppermute | solution.py:150
  21.9 3.9 %collective-permute-start.1 = (f32[8,128]{1,0:T(8,128)S(1)}, f32[8,128]{1,0:T(8,128)S(1)}, u32[]{:S(2)}, u32[]{:S(2)}) collective-permute-start(f32[8,128]{1,0:T(8,128)S(1)} %slice_maximum_fusion), channel_id=1, source_target_pairs={{0,4},{4,8},{8,12},{12,16},{16,20},{20,24},{24,28},{28,0},{1,5},{5... | collective-permute-start | bytes 12296 | tf_op jit(solution)/shard_map/ppermute | solution.py:179
  25.9 4.5 %collective-permute-start.2 = (f32[8,128]{1,0:T(8,128)S(1)}, f32[8,128]{1,0:T(8,128)S(1)}, u32[]{:S(2)}, u32[]{:S(2)}) collective-permute-start(f32[8,128]{1,0:T(8,128)S(1)} %max.13), channel_id=1, source_target_pairs={{0,8},{4,12},{8,16},{12,20},{16,24},{20,28},{24,0},{28,4},{1,9},{5... | collective-permute-start | bytes 12296 | tf_op jit(solution)/shard_map/ppermute | solution.py:179
  30.4 3.6 %collective-permute-start.5 = (f32[8,128]{1,0:T(8,128)S(1)}, f32[8,128]{1,0:T(8,128)S(1)}, u32[]{:S(2)}, u32[]{:S(2)}) collective-permute-start(f32[8,128]{1,0:T(8,128)S(1)} %max.14), channel_id=1, source_target_pairs={{0,16},{4,20},{8,24},{12,28},{16,0},{20,4},{24,8},{28,12},{1,17},{... | collective-permute-start | bytes 12296 | tf_op jit(solution)/shard_map/ppermute | solution.py:179
  34.0 14.8 %collective-permute-start.3 = (f32[512,128]{1,0:T(8,128)S(1)}, f32[512,128]{1,0:T(8,128)S(1)}, u32[]{:S(2)}, u32[]{:S(2)}) collective-permute-start(f32[512,128]{1,0:T(8,128)S(1)} %slice.24), channel_id=1, source_target_pairs={{0,3},{1,2},{2,1},{3,0},{4,7},{5,6},{6,5},{7,4},{8,11},{9,10},{10,... | collective-permute-start | bytes 786440 | tf_op jit(solution)/shard_map/ppermute | solution.py:150
  37.5 16.0 %collective-permute-start.6 = (f32[512,128]{1,0:T(8,128)S(1)}, f32[512,128]{1,0:T(8,128)S(1)}, u32[]{:S(2)}, u32[]{:S(2)}) collective-permute-start(f32[512,128]{1,0:T(8,128)S(1)} %collective-permute-done.4.far_ref), channel_id=1, source_target_pairs={{0,1},{1,0},{2,3},{3,2},{4,5},{5,4},{6,7},{7,6},{8,9},{9,8},{10,11... | collective-permute-start | bytes 786440 | tf_op jit(solution)/shard_map/ppermute | solution.py:150
  40.0 15.3 %copy-start = (f32[2,512,128]{2,1,0:T(8,128)S(1)}, f32[2,512,128]{2,1,0:T(8,128)}, u32[]{:S(2)}) copy-start(f32[2,512,128]{2,1,0:T(8,128)} %level_ref.3) | copy-start | bytes 1572868
  43.2 12.7 %collective-permute-start.11 = (f32[512,256]{1,0:T(8,128)S(1)}, f32[512,256]{1,0:T(8,128)S(1)}, u32[]{:S(2)}, u32[]{:S(2)}) collective-permute-start(f32[512,256]{1,0:T(8,128)S(1)} %shard_map.60.solved_ref), channel_id=1, source_target_pairs={{0,4},{4,8},{8,12},{12,16},{16,20},{20,24},{24,28},{1,5},{5,9},{9,... | collective-permute-start | bytes 1572872 | tf_op jit(solution)/shard_map/ppermute | solution.py:205
  53.5 8.4 %collective-permute-start.7 = (f32[520,128]{1,0:T(8,128)S(1)}, f32[520,128]{1,0:T(8,128)S(1)}, u32[]{:S(2)}, u32[]{:S(2)}) collective-permute-start(f32[520,128]{1,0:T(8,128)S(1)} %shard_map.59), channel_id=1, source_target_pairs={{0,1},{1,0},{2,3},{3,2},{4,5},{5,4},{6,7},{7,6},{8,9},{9,8},{10,11... | collective-permute-start | bytes 798728 | tf_op jit(solution)/shard_map/ppermute | solution.py:150

commit v20 on v16

--- a/solution.py
+++ b/solution.py
@@ -172,7 +172,6 @@
     level_last = exchanged(level_far, 1)
     up_far = exchanged(after(sent, level_far)[up_row:down_row], 3)
     down_near = exchanged(after(sent, level_far)[down_row:], 1)
-    down_far = exchanged(after(sent, up_far)[down_row:], 3)
     peak = jnp.maximum(sent[phases:up_row], level_far[phases:up_row])
     peaks, reach = [peak], 1
     while reach < ranges:
@@ -180,6 +179,7 @@
         peaks.append(jnp.maximum(peaks[-1], lax.ppermute(peaks[-1], "lvl", route)))
         reach *= 2
     peak = peaks[-1]
+    down_far = exchanged(after(sent, peaks[2 % len(peaks)])[down_row:], 3)
     up_last = exchanged(after(up_far, peak), 1)
     down_last = exchanged(stack((down_far, 0, phases), (peak, 0, PEAK_ROWS)), 1)
 

time: 62.6 us -> 62.6 us (level)
  no operation moved by 1% of the time
where the time goes in v20:
time: 62.6 us; the launch traced here: 62.4 us
  waiting for transfers between devices  37.6 us (60%)
  starting transfers between devices  17.9 us (29%)
  Pallas kernels  6.05 us (10%)
  between operations  0.76 us (1%)
    ppermute x8, waiting for transfers between devices, exchanged(): return lax.ppermute(part, 'col', [(i, i ^ distance) for i in range(shards)])  27.7 us
    ppermute x8, starting transfers between devices, exchanged(): return lax.ppermute(part, 'col', [(i, i ^ distance) for i in range(shards)])  13.9 us
    ppermute x3, waiting for transfers between devices, per_device(): peaks.append(jnp.maximum(peaks[-1], lax.ppermute(peaks[-1], 'lvl', route)))  9.93 us
    pallas_call x6, Pallas kernels, call(): pl.pallas_call(kernel, out_shape=out_shape, in_specs=in_specs, out_specs=...  6.05 us
    ppermute x3, starting transfers between devices, per_device(): peaks.append(jnp.maximum(peaks[-1], lax.ppermute(peaks[-1], 'lvl', route)))  2.11 us
    ppermute x1, starting transfers between devices, per_device(): lax.ppermute(after(solved, down_near, up_last), 'lvl', [(i, i + 1) for i...  1.84 us
  transfers between devices with their start and end apart: 12, of which 9 were waited for; matrix products, arithmetic and copies ran while one was open for 0% of the time, Pallas kernels for 6%

profile of v20, /device:TPU:0, one launch (start us, length us, event | category | flops | bytes accessed | tf_op | source)
XLA Modules:
  0.0 62.4 jit_solution(3637739865577221502)
XLA Ops:
  0.6 1.2 %shard_map.58.own_ref = f32[1544,128]{1,0:T(8,128)S(1)} custom-call(s32[1]{0:T(128)} %bitcast.place, f32[2,512,128]{2,1,0:T(8,128)} %refs_3_.1, f32[2,512,128]{2,1,0:T(8,128)} %level_ref.3, f32[2,512,128]{2,1,0:T(8,128)} %refs_4_.1), custom_call_target="tpu_custom_call" | custom-call | tf_op jit(solution)/shard_map/pallas_call | solution.py:135
  1.9 5.1 %collective-permute-start = (f32[544,128]{1,0:T(8,128)S(1)}, f32[544,128]{1,0:T(8,128)S(1)}, u32[]{:S(2)}, u32[]{:S(2)}) collective-permute-start(f32[544,128]{1,0:T(8,128)S(1)} %slice.29), channel_id=1, source_target_pairs={{0,3},{1,2},{2,1},{3,0},{4,7},{5,6},{6,5},{7,4},{8,11},{9,10},{10,... | collective-permute-start | bytes 835592 | tf_op jit(solution)/shard_map/ppermute | solution.py:150
  7.0 0.1 collective-permute-start.6
  7.1 7.5 %collective-permute-done.refs_1_ = f32[544,128]{1,0:T(8,128)S(1)} collective-permute-done((f32[544,128]{1,0:T(8,128)S(1)}, f32[544,128]{1,0:T(8,128)S(1)}, u32[]{:S(2)}, u32[]{:S(2)}) %collective-permute-start) | collective-permute-done | bytes 278560 | tf_op jit(solution)/shard_map/ppermute | solution.py:150
  14.6 0.0 copy-start.2
  14.6 0.0 copy-start.1
  14.6 3.8 %collective-permute-start.9 = (f32[512,128]{1,0:T(8,128)S(1)}, f32[512,128]{1,0:T(8,128)S(1)}, u32[]{:S(2)}, u32[]{:S(2)}) collective-permute-start(f32[512,128]{1,0:T(8,128)S(1)} %get-tuple-element.21), channel_id=1, source_target_pairs={{0,3},{1,2},{2,1},{3,0},{4,7},{5,6},{6,5},{7,4},{8,11},{9,10},{10,... | collective-permute-start | bytes 786440 | tf_op jit(solution)/shard_map/ppermute | solution.py:150
  18.5 2.6 %collective-permute-start.7 = (f32[544,128]{1,0:T(8,128)S(1)}, f32[544,128]{1,0:T(8,128)S(1)}, u32[]{:S(2)}, u32[]{:S(2)}) collective-permute-start(f32[544,128]{1,0:T(8,128)S(1)} %collective-permute-done.refs_1_), channel_id=1, source_target_pairs={{0,1},{1,0},{2,3},{3,2},{4,5},{5,4},{6,7},{7,6},{8,9},{9,8},{10,11... | collective-permute-start | bytes 835592 | tf_op jit(solution)/shard_map/ppermute | solution.py:150
  21.0 0.0 collective-permute-start.1
  21.0 3.9 %collective-permute-done.1 = f32[8,128]{1,0:T(8,128)S(1)} collective-permute-done((f32[8,128]{1,0:T(8,128)S(1)}, f32[8,128]{1,0:T(8,128)S(1)}, u32[]{:S(2)}, u32[]{:S(2)}) %collective-permute-start.1) | collective-permute-done | bytes 4128 | tf_op jit(solution)/shard_map/ppermute | solution.py:179
  25.0 0.6 collective-permute-start.2
  25.6 3.9 %collective-permute-done.2 = f32[8,128]{1,0:T(8,128)S(1)} collective-permute-done((f32[8,128]{1,0:T(8,128)S(1)}, f32[8,128]{1,0:T(8,128)S(1)}, u32[]{:S(2)}, u32[]{:S(2)}) %collective-permute-start.2) | collective-permute-done | bytes 4128 | tf_op jit(solution)/shard_map/ppermute | solution.py:179
  29.5 1.5 %collective-permute-start.4 = (f32[8,128]{1,0:T(8,128)S(1)}, f32[8,128]{1,0:T(8,128)S(1)}, u32[]{:S(2)}, u32[]{:S(2)}) collective-permute-start(f32[8,128]{1,0:T(8,128)S(1)} %max.14), channel_id=1, source_target_pairs={{0,16},{4,20},{8,24},{12,28},{16,0},{20,4},{24,8},{28,12},{1,17},{... | collective-permute-start | bytes 12296 | tf_op jit(solution)/shard_map/ppermute | solution.py:179
  31.0 0.0 collective-permute-start.8
  31.0 2.1 %collective-permute-done.4 = f32[8,128]{1,0:T(8,128)S(1)} collective-permute-done((f32[8,128]{1,0:T(8,128)S(1)}, f32[8,128]{1,0:T(8,128)S(1)}, u32[]{:S(2)}, u32[]{:S(2)}) %collective-permute-start.4) | collective-permute-done | bytes 4128 | tf_op jit(solution)/shard_map/ppermute | solution.py:179
  33.1 0.0 collective-permute-done.9.far_ref
  33.1 0.0 collective-permute-start.10
  33.2 2.2 %collective-permute-start.3 = (f32[512,128]{1,0:T(8,128)S(1)}, f32[512,128]{1,0:T(8,128)S(1)}, u32[]{:S(2)}, u32[]{:S(2)}) collective-permute-start(f32[512,128]{1,0:T(8,128)S(1)} %slice.24), channel_id=1, source_target_pairs={{0,3},{1,2},{2,1},{3,0},{4,7},{5,6},{6,5},{7,4},{8,11},{9,10},{10,... | collective-permute-start | bytes 786440 | tf_op jit(solution)/shard_map/ppermute | solution.py:150
  35.4 0.0 collective-permute-done.6.refs_0_.near_ref
  35.4 1.6 %collective-permute-done.7.refs_2_ = f32[544,128]{1,0:T(8,128)S(1)} collective-permute-done((f32[544,128]{1,0:T(8,128)S(1)}, f32[544,128]{1,0:T(8,128)S(1)}, u32[]{:S(2)}, u32[]{:S(2)}) %collective-permute-start.7) | collective-permute-done | bytes 278560 | tf_op jit(solution)/shard_map/ppermute | solution.py:150
  37.0 0.0 copy-done.2
  37.0 0.0 copy-done.1
  37.0 2.4 %shard_map.60.solved_ref = f32[512,256]{1,0:T(8,128)S(1)} custom-call(s32[1]{0:T(128)} %bitcast.place, f32[1544,128]{1,0:T(8,128)S(1)} %shard_map.58.own_ref, f32[1032,128]{1,0:T(8,128)S(1)} %collective-permute-done.6.refs_0_.near_ref, f32[544,128]{1,0:T(8,128)S(1)} %collective-permute-done.refs_1_, f32[544,128]{1,0:T(8,128)S(1)} %collective-permute-done.7.refs_2_, ...), custom_call_target="tpu_custom_call" | custom-call | tf_op jit(solution)/shard_map/pallas_call | solution.py:135
  39.4 0.0 copy-start
  39.4 3.2 %collective-permute-done.8.near_ref = f32[512,128]{1,0:T(8,128)S(1)} collective-permute-done((f32[512,128]{1,0:T(8,128)S(1)}, f32[512,128]{1,0:T(8,128)S(1)}, u32[]{:S(2)}, u32[]{:S(2)}) %collective-permute-start.8) | collective-permute-done | bytes 262176 | tf_op jit(solution)/shard_map/ppermute | solution.py:150
  42.6 6.1 %collective-permute-done.10.last_ref = f32[512,128]{1,0:T(8,128)S(1)} collective-permute-done((f32[512,128]{1,0:T(8,128)S(1)}, f32[512,128]{1,0:T(8,128)S(1)}, u32[]{:S(2)}, u32[]{:S(2)}) %collective-permute-start.10) | collective-permute-done | bytes 262176 | tf_op jit(solution)/shard_map/ppermute | solution.py:150
  48.7 1.8 %collective-permute-start.11 = (f32[512,256]{1,0:T(8,128)S(1)}, f32[512,256]{1,0:T(8,128)S(1)}, u32[]{:S(2)}, u32[]{:S(2)}) collective-permute-start(f32[512,256]{1,0:T(8,128)S(1)} %shard_map.60.solved_ref), channel_id=1, source_target_pairs={{0,4},{4,8},{8,12},{12,16},{16,20},{20,24},{24,28},{1,5},{5,9},{9,... | collective-permute-start | bytes 1572872 | tf_op jit(solution)/shard_map/ppermute | solution.py:205
  50.5 3.0 %collective-permute-done.3.refs_0_.far_ref = f32[512,128]{1,0:T(8,128)S(1)} collective-permute-done((f32[512,128]{1,0:T(8,128)S(1)}, f32[512,128]{1,0:T(8,128)S(1)}, u32[]{:S(2)}, u32[]{:S(2)}) %collective-permute-start.3) | collective-permute-done | bytes 262176 | tf_op jit(solution)/shard_map/ppermute | solution.py:150
  53.6 0.1 collective-permute-start.5
  53.7 0.0 copy-done
  53.7 0.6 shard_map.61
  54.3 0.0 collective-permute-done.11.below_ref
  54.3 0.6 shard_map.62
  54.9 6.3 %collective-permute-done.5.last_ref = f32[520,128]{1,0:T(8,128)S(1)} collective-permute-done((f32[520,128]{1,0:T(8,128)S(1)}, f32[520,128]{1,0:T(8,128)S(1)}, u32[]{:S(2)}, u32[]{:S(2)}) %collective-permute-start.5) | collective-permute-done | bytes 266272 | tf_op jit(solution)/shard_map/ppermute | solution.py:150
  61.2 1.2 %shard_map.63 = (f32[1,512,128]{2,1,0:T(8,128)}, f32[1,512,128]{2,1,0:T(8,128)}, f32[1,512,128]{2,1,0:T(8,128)}) custom-call(s32[1]{0:T(128)} %bitcast.place, f32[520,128]{1,0:T(8,128)S(1)} %collective-permute-done.5.last_ref, f32[512,256]{1,0:T(8,128)S(1)} %collective-permute-done.11.below_ref, f32[512,128]{1,0:T(8,128)S(1)} %get-tuple-element.18.part_level, ...), custom_call_target="tpu_custom_call" | custom-call | tf_op jit(solution)/shard_map/pallas_call | solution.py:135
  (9 shorter events, 0.1 us)
Async XLA Ops:
  1.9 12.7 %collective-permute-start = (f32[544,128]{1,0:T(8,128)S(1)}, f32[544,128]{1,0:T(8,128)S(1)}, u32[]{:S(2)}, u32[]{:S(2)}) collective-permute-start(f32[544,128]{1,0:T(8,128)S(1)} %slice.29), channel_id=1, source_target_pairs={{0,3},{1,2},{2,1},{3,0},{4,7},{5,6},{6,5},{7,4},{8,11},{9,10},{10,... | collective-permute-start | bytes 835592 | tf_op jit(solution)/shard_map/ppermute | solution.py:150
  7.0 28.3 %collective-permute-start.6 = (f32[1032,128]{1,0:T(8,128)S(1)}, f32[1032,128]{1,0:T(8,128)S(1)}, u32[]{:S(2)}, u32[]{:S(2)}) collective-permute-start(f32[1032,128]{1,0:T(8,128)S(1)} %slice.31), channel_id=1, source_target_pairs={{0,1},{1,0},{2,3},{3,2},{4,5},{5,4},{6,7},{7,6},{8,9},{9,8},{10,11... | collective-permute-start | bytes 1585160 | tf_op jit(solution)/shard_map/ppermute | solution.py:150
  14.6 22.4 %copy-start.2 = (f32[2,512,128]{2,1,0:T(8,128)S(1)}, f32[2,512,128]{2,1,0:T(8,128)}, u32[]{:S(2)}) copy-start(f32[2,512,128]{2,1,0:T(8,128)} %refs_4_.1) | copy-start | bytes 1572868
  14.6 22.4 %copy-start.1 = (f32[2,512,128]{2,1,0:T(8,128)S(1)}, f32[2,512,128]{2,1,0:T(8,128)}, u32[]{:S(2)}) copy-start(f32[2,512,128]{2,1,0:T(8,128)} %refs_3_.1) | copy-start | bytes 1572868
  14.6 18.5 %collective-permute-start.9 = (f32[512,128]{1,0:T(8,128)S(1)}, f32[512,128]{1,0:T(8,128)S(1)}, u32[]{:S(2)}, u32[]{:S(2)}) collective-permute-start(f32[512,128]{1,0:T(8,128)S(1)} %get-tuple-element.21), channel_id=1, source_target_pairs={{0,3},{1,2},{2,1},{3,0},{4,7},{5,6},{6,5},{7,4},{8,11},{9,10},{10,... | collective-permute-start | bytes 786440 | tf_op jit(solution)/shard_map/ppermute | solution.py:150
  18.5 18.5 %collective-permute-start.7 = (f32[544,128]{1,0:T(8,128)S(1)}, f32[544,128]{1,0:T(8,128)S(1)}, u32[]{:S(2)}, u32[]{:S(2)}) collective-permute-start(f32[544,128]{1,0:T(8,128)S(1)} %collective-permute-done.refs_1_), channel_id=1, source_target_pairs={{0,1},{1,0},{2,3},{3,2},{4,5},{5,4},{6,7},{7,6},{8,9},{9,8},{10,11... | collective-permute-start | bytes 835592 | tf_op jit(solution)/shard_map/ppermute | solution.py:150
  21.0 3.9 %collective-permute-start.1 = (f32[8,128]{1,0:T(8,128)S(1)}, f32[8,128]{1,0:T(8,128)S(1)}, u32[]{:S(2)}, u32[]{:S(2)}) collective-permute-start(f32[8,128]{1,0:T(8,128)S(1)} %slice_maximum_fusion), channel_id=1, source_target_pairs={{0,4},{4,8},{8,12},{12,16},{16,20},{20,24},{24,28},{28,0},{1,5},{5... | collective-permute-start | bytes 12296 | tf_op jit(solution)/shard_map/ppermute | solution.py:179
  25.0 4.5 %collective-permute-start.2 = (f32[8,128]{1,0:T(8,128)S(1)}, f32[8,128]{1,0:T(8,128)S(1)}, u32[]{:S(2)}, u32[]{:S(2)}) collective-permute-start(f32[8,128]{1,0:T(8,128)S(1)} %max.13), channel_id=1, source_target_pairs={{0,8},{4,12},{8,16},{12,20},{16,24},{20,28},{24,0},{28,4},{1,9},{5... | collective-permute-start | bytes 12296 | tf_op jit(solution)/shard_map/ppermute | solution.py:179
  29.5 3.6 %collective-permute-start.4 = (f32[8,128]{1,0:T(8,128)S(1)}, f32[8,128]{1,0:T(8,128)S(1)}, u32[]{:S(2)}, u32[]{:S(2)}) collective-permute-start(f32[8,128]{1,0:T(8,128)S(1)} %max.14), channel_id=1, source_target_pairs={{0,16},{4,20},{8,24},{12,28},{16,0},{20,4},{24,8},{28,12},{1,17},{... | collective-permute-start | bytes 12296 | tf_op jit(solution)/shard_map/ppermute | solution.py:179
  31.0 11.6 %collective-permute-start.8 = (f32[512,128]{1,0:T(8,128)S(1)}, f32[512,128]{1,0:T(8,128)S(1)}, u32[]{:S(2)}, u32[]{:S(2)}) collective-permute-start(f32[512,128]{1,0:T(8,128)S(1)} %get-tuple-element.22), channel_id=1, source_target_pairs={{0,1},{1,0},{2,3},{3,2},{4,5},{5,4},{6,7},{7,6},{8,9},{9,8},{10,11... | collective-permute-start | bytes 786440 | tf_op jit(solution)/shard_map/ppermute | solution.py:150
  33.1 15.6 %collective-permute-start.10 = (f32[512,128]{1,0:T(8,128)S(1)}, f32[512,128]{1,0:T(8,128)S(1)}, u32[]{:S(2)}, u32[]{:S(2)}) collective-permute-start(f32[512,128]{1,0:T(8,128)S(1)} %collective-permute-done.9.far_ref), channel_id=1, source_target_pairs={{0,1},{1,0},{2,3},{3,2},{4,5},{5,4},{6,7},{7,6},{8,9},{9,8},{10,11... | collective-permute-start | bytes 786440 | tf_op jit(solution)/shard_map/ppermute | solution.py:150
  33.2 20.4 %collective-permute-start.3 = (f32[512,128]{1,0:T(8,128)S(1)}, f32[512,128]{1,0:T(8,128)S(1)}, u32[]{:S(2)}, u32[]{:S(2)}) collective-permute-start(f32[512,128]{1,0:T(8,128)S(1)} %slice.24), channel_id=1, source_target_pairs={{0,3},{1,2},{2,1},{3,0},{4,7},{5,6},{6,5},{7,4},{8,11},{9,10},{10,... | collective-permute-start | bytes 786440 | tf_op jit(solution)/shard_map/ppermute | solution.py:150
  39.4 14.2 %copy-start = (f32[2,512,128]{2,1,0:T(8,128)S(1)}, f32[2,512,128]{2,1,0:T(8,128)}, u32[]{:S(2)}) copy-start(f32[2,512,128]{2,1,0:T(8,128)} %level_ref.3) | copy-start | bytes 1572868
  48.7 5.6 %collective-permute-start.11 = (f32[512,256]{1,0:T(8,128)S(1)}, f32[512,256]{1,0:T(8,128)S(1)}, u32[]{:S(2)}, u32[]{:S(2)}) collective-permute-start(f32[512,256]{1,0:T(8,128)S(1)} %shard_map.60.solved_ref), channel_id=1, source_target_pairs={{0,4},{4,8},{8,12},{12,16},{16,20},{20,24},{24,28},{1,5},{5,9},{9,... | collective-permute-start | bytes 1572872 | tf_op jit(solution)/shard_map/ppermute | solution.py:205
  53.6 7.6 %collective-permute-start.5 = (f32[520,128]{1,0:T(8,128)S(1)}, f32[520,128]{1,0:T(8,128)S(1)}, u32[]{:S(2)}, u32[]{:S(2)}) collective-permute-start(f32[520,128]{1,0:T(8,128)S(1)} %shard_map.59), channel_id=1, source_target_pairs={{0,1},{1,0},{2,3},{3,2},{4,5},{5,4},{6,7},{7,6},{8,9},{9,8},{10,11... | collective-permute-start | bytes 798728 | tf_op jit(solution)/shard_map/ppermute | solution.py:150

commit v21 on v14

--- a/solution.py
+++ b/solution.py
@@ -9,7 +9,7 @@
 
 SWEEPS = 2
 PEAK_ROWS = 8
-PAD_ROWS = 24
+PAD_ROWS = 16
 DISTANCES = (0, 1, 3, 2)
 F32 = jnp.float32
 BF16 = jnp.bfloat16
@@ -114,16 +114,22 @@
     part_level[...] = upper_level[...] + lower[:, :cols]
 
 
-def output_kernel(place, last_ref, solved_ref, below_ref, *refs):
-    part_level, part_up, part_down, peak_ref, new_level, new_up, new_down = refs
+def output_kernel(place, last_ref, solved_ref, below_ref, part_level, part_up, part_down, peak_ref, *refs):
+    *outs, made, sems = refs
     phases, cols = part_up.shape
     scale = 1.0 / jnp.maximum(peak_ref[...], last_ref[pl.ds(2 * phases, PEAK_ROWS), :])[0:1, :]
+    copies = [pltpu.make_async_copy(made.at[at], out.at[0], sems.at[at]) for at, out in enumerate(outs)]
     last = len(DISTANCES) - 1
     upper = gathered_product(place, [last_ref[pl.ds(0, phases), :]], last, solved_ref)
-    new_up[0] = (part_up[...] + upper[:, :cols]) * scale
+    made[1] = (part_up[...] + upper[:, :cols]) * scale
+    copies[1].start()
     lower = gathered_product(place, [last_ref[pl.ds(phases, phases), :]], last, below_ref)
-    new_down[0] = (part_down[...] + lower[:, cols:]) * scale
-    new_level[0] = (part_level[...] + upper[:, cols:] + lower[:, :cols]) * scale
+    made[2] = (part_down[...] + lower[:, cols:]) * scale
+    copies[2].start()
+    made[0] = (part_level[...] + upper[:, cols:] + lower[:, :cols]) * scale
+    copies[0].start()
+    for copy in copies:
+        copy.wait()
 
 
 def per_device(up_blocks, level_blocks, down_blocks):
@@ -135,12 +141,12 @@
     params = pltpu.CompilerParams(vmem_limit_bytes=32 * 2**20)
     shape = lambda rows, columns=cols: jax.ShapeDtypeStruct((rows, columns), F32)
 
-    def call(kernel, out_shape, in_specs, *operands, scratch=(), **options):
+    def call(kernel, out_shape, in_specs, *operands, scratch=(), out_spec=VMEM, **options):
         return pl.pallas_call(
             kernel,
             out_shape=out_shape,
             in_specs=in_specs,
-            out_specs=jax.tree.map(lambda _: VMEM, out_shape),
+            out_specs=jax.tree.map(lambda _: out_spec, out_shape),
             scratch_shapes=scratch,
             grid=(1,),
             compiler_params=params,
@@ -243,6 +249,8 @@
         part_up,
         part_down,
         peak,
+        scratch=[pltpu.VMEM((3, phases, cols), F32), pltpu.SemaphoreType.DMA((3,))],
+        out_spec=ANY,
     )
 
 

time: 61.3 us -> 61.2 us (level)
  no operation moved by 1% of the time
where the time goes in v21:
time: 61.2 us; the launch traced here: 60.5 us
  waiting for transfers between devices  31.6 us (52%)
  starting transfers between devices  21.8 us (36%)
  Pallas kernels  6.29 us (10%)
  between operations  0.76 us (1%)
    ppermute x6, waiting for transfers between devices, exchanged(): return lax.ppermute(part, 'col', [(i, i ^ distance) for i in range(shards)])  20.8 us
    ppermute x6, starting transfers between devices, exchanged(): return lax.ppermute(part, 'col', [(i, i ^ distance) for i in range(shards)])  18 us
    ppermute x3, waiting for transfers between devices, per_device(): peaks.append(jnp.maximum(peaks[-1], lax.ppermute(peaks[-1], 'lvl', route)))  9.92 us
    pallas_call x6, Pallas kernels, call(): pl.pallas_call(kernel, out_shape=out_shape, in_specs=in_specs, out_specs=...  6.29 us
    ppermute x3, starting transfers between devices, per_device(): peaks.append(jnp.maximum(peaks[-1], lax.ppermute(peaks[-1], 'lvl', route)))  2.17 us
    ppermute x1, starting transfers between devices, per_device(): lax.ppermute(after(solved, down_near), 'lvl', [(i, i + 1) for i in range(...  1.59 us
  transfers between devices with their start and end apart: 10, of which 8 were waited for; matrix products, arithmetic and copies ran while one was open for 0% of the time, Pallas kernels for 6%

profile of v21, /device:TPU:0, one launch (start us, length us, event | category | flops | bytes accessed | tf_op | source)
XLA Modules:
  0.0 60.5 jit_solution(5256527410937253609)
XLA Ops:
  0.6 1.2 %shard_map.58.own_ref = f32[1544,128]{1,0:T(8,128)S(1)} custom-call(s32[1]{0:T(128)} %bitcast.place, f32[2,512,128]{2,1,0:T(8,128)} %refs_3_.1, f32[2,512,128]{2,1,0:T(8,128)} %level_ref.3, f32[2,512,128]{2,1,0:T(8,128)} %refs_4_.1), custom_call_target="tpu_custom_call" | custom-call | tf_op jit(solution)/shard_map/pallas_call | solution.py:145
  1.9 5.1 %collective-permute-start = (f32[536,128]{1,0:T(8,128)S(1)}, f32[536,128]{1,0:T(8,128)S(1)}, u32[]{:S(2)}, u32[]{:S(2)}) collective-permute-start(f32[536,128]{1,0:T(8,128)S(1)} %slice.24), channel_id=1, source_target_pairs={{0,3},{1,2},{2,1},{3,0},{4,7},{5,6},{6,5},{7,4},{8,11},{9,10},{10,... | collective-permute-start | bytes 823304 | tf_op jit(solution)/shard_map/ppermute | solution.py:160
  7.0 0.1 collective-permute-start.6
  7.1 7.4 %collective-permute-done.refs_1_ = f32[536,128]{1,0:T(8,128)S(1)} collective-permute-done((f32[536,128]{1,0:T(8,128)S(1)}, f32[536,128]{1,0:T(8,128)S(1)}, u32[]{:S(2)}, u32[]{:S(2)}) %collective-permute-start) | collective-permute-done | bytes 274464 | tf_op jit(solution)/shard_map/ppermute | solution.py:160
  14.5 3.8 %collective-permute-start.1 = (f32[1024,128]{1,0:T(8,128)S(1)}, f32[1024,128]{1,0:T(8,128)S(1)}, u32[]{:S(2)}, u32[]{:S(2)}) collective-permute-start(f32[1024,128]{1,0:T(8,128)S(1)} %slice.19), channel_id=1, source_target_pairs={{0,3},{1,2},{2,1},{3,0},{4,7},{5,6},{6,5},{7,4},{8,11},{9,10},{10,... | collective-permute-start | bytes 1572872 | tf_op jit(solution)/shard_map/ppermute | solution.py:160
  18.4 2.5 %collective-permute-start.7 = (f32[536,128]{1,0:T(8,128)S(1)}, f32[536,128]{1,0:T(8,128)S(1)}, u32[]{:S(2)}, u32[]{:S(2)}) collective-permute-start(f32[536,128]{1,0:T(8,128)S(1)} %collective-permute-done.refs_1_), channel_id=1, source_target_pairs={{0,1},{1,0},{2,3},{3,2},{4,5},{5,4},{6,7},{7,6},{8,9},{9,8},{10,11... | collective-permute-start | bytes 823304 | tf_op jit(solution)/shard_map/ppermute | solution.py:160
  20.9 0.1 collective-permute-start.8
  21.0 0.1 collective-permute-start.2
  21.0 3.9 %collective-permute-done.2 = f32[8,128]{1,0:T(8,128)S(1)} collective-permute-done((f32[8,128]{1,0:T(8,128)S(1)}, f32[8,128]{1,0:T(8,128)S(1)}, u32[]{:S(2)}, u32[]{:S(2)}) %collective-permute-start.2) | collective-permute-done | bytes 4128 | tf_op jit(solution)/shard_map/ppermute | solution.py:188
  24.9 0.6 collective-permute-start.3
  25.5 3.9 %collective-permute-done.3 = f32[8,128]{1,0:T(8,128)S(1)} collective-permute-done((f32[8,128]{1,0:T(8,128)S(1)}, f32[8,128]{1,0:T(8,128)S(1)}, u32[]{:S(2)}, u32[]{:S(2)}) %collective-permute-start.3) | collective-permute-done | bytes 4128 | tf_op jit(solution)/shard_map/ppermute | solution.py:188
  29.5 1.5 %collective-permute-start.4 = (f32[8,128]{1,0:T(8,128)S(1)}, f32[8,128]{1,0:T(8,128)S(1)}, u32[]{:S(2)}, u32[]{:S(2)}) collective-permute-start(f32[8,128]{1,0:T(8,128)S(1)} %max.14), channel_id=1, source_target_pairs={{0,16},{4,20},{8,24},{12,28},{16,0},{20,4},{24,8},{28,12},{1,17},{... | collective-permute-start | bytes 12296 | tf_op jit(solution)/shard_map/ppermute | solution.py:188
  31.0 2.1 %collective-permute-done.4 = f32[8,128]{1,0:T(8,128)S(1)} collective-permute-done((f32[8,128]{1,0:T(8,128)S(1)}, f32[8,128]{1,0:T(8,128)S(1)}, u32[]{:S(2)}, u32[]{:S(2)}) %collective-permute-start.4) | collective-permute-done | bytes 4128 | tf_op jit(solution)/shard_map/ppermute | solution.py:188
  33.1 0.0 copy-start.1
  33.1 0.0 copy-start.2
  33.1 4.0 %collective-permute-done.1.refs_0_.far_ref = f32[1024,128]{1,0:T(8,128)S(1)} collective-permute-done((f32[1024,128]{1,0:T(8,128)S(1)}, f32[1024,128]{1,0:T(8,128)S(1)}, u32[]{:S(2)}, u32[]{:S(2)}) %collective-permute-start.1) | collective-permute-done | bytes 524320 | tf_op jit(solution)/shard_map/ppermute | solution.py:160
  37.1 0.0 copy-start
  37.1 6.5 %collective-permute-start.5 = (f32[1032,128]{1,0:T(8,128)S(1)}, f32[1032,128]{1,0:T(8,128)S(1)}, u32[]{:S(2)}, u32[]{:S(2)}) collective-permute-start(f32[1032,128]{1,0:T(8,128)S(1)} %shard_map.59), channel_id=1, source_target_pairs={{0,1},{1,0},{2,3},{3,2},{4,5},{5,4},{6,7},{7,6},{8,9},{9,8},{10,11... | collective-permute-start | bytes 1585160 | tf_op jit(solution)/shard_map/ppermute | solution.py:160
  43.6 0.0 collective-permute-done.6.refs_0_.near_ref
  43.6 0.0 collective-permute-done.7.refs_2_
  43.6 0.0 copy-done.1
  43.6 0.0 copy-done.2
  43.6 2.4 %shard_map.60.solved_ref = f32[512,256]{1,0:T(8,128)S(1)} custom-call(s32[1]{0:T(128)} %bitcast.place, f32[1544,128]{1,0:T(8,128)S(1)} %shard_map.58.own_ref, f32[1032,128]{1,0:T(8,128)S(1)} %collective-permute-done.6.refs_0_.near_ref, f32[536,128]{1,0:T(8,128)S(1)} %collective-permute-done.refs_1_, f32[536,128]{1,0:T(8,128)S(1)} %collective-permute-done.7.refs_2_, ...), custom_call_target="tpu_custom_call" | custom-call | tf_op jit(solution)/shard_map/pallas_call | solution.py:145
  46.0 2.1 %collective-permute-done.8.near_ref = f32[512,128]{1,0:T(8,128)S(1)} collective-permute-done((f32[512,128]{1,0:T(8,128)S(1)}, f32[512,128]{1,0:T(8,128)S(1)}, u32[]{:S(2)}, u32[]{:S(2)}) %collective-permute-start.8) | collective-permute-done | bytes 262176 | tf_op jit(solution)/shard_map/ppermute | solution.py:160
  48.1 1.6 %collective-permute-start.9 = (f32[512,256]{1,0:T(8,128)S(1)}, f32[512,256]{1,0:T(8,128)S(1)}, u32[]{:S(2)}, u32[]{:S(2)}) collective-permute-start(f32[512,256]{1,0:T(8,128)S(1)} %shard_map.60.solved_ref), channel_id=1, source_target_pairs={{0,4},{4,8},{8,12},{12,16},{16,20},{20,24},{24,28},{1,5},{5,9},{9,... | collective-permute-start | bytes 1572872 | tf_op jit(solution)/shard_map/ppermute | solution.py:213
  49.7 0.0 copy-done
  49.7 0.6 shard_map.61
  50.3 0.9 %collective-permute-done.9.below_ref = f32[512,256]{1,0:T(8,128)S(1)} collective-permute-done((f32[512,256]{1,0:T(8,128)S(1)}, f32[512,256]{1,0:T(8,128)S(1)}, u32[]{:S(2)}, u32[]{:S(2)}) %collective-permute-start.9) | collective-permute-done | bytes 524320 | tf_op jit(solution)/shard_map/ppermute | solution.py:213
  51.2 0.6 shard_map.62
  51.7 7.3 %collective-permute-done.5.last_ref = f32[1032,128]{1,0:T(8,128)S(1)} collective-permute-done((f32[1032,128]{1,0:T(8,128)S(1)}, f32[1032,128]{1,0:T(8,128)S(1)}, u32[]{:S(2)}, u32[]{:S(2)}) %collective-permute-start.5) | collective-permute-done | bytes 528416 | tf_op jit(solution)/shard_map/ppermute | solution.py:160
  59.1 1.5 %shard_map.63 = (f32[1,512,128]{2,1,0:T(8,128)}, f32[1,512,128]{2,1,0:T(8,128)}, f32[1,512,128]{2,1,0:T(8,128)}) custom-call(s32[1]{0:T(128)} %bitcast.place, f32[1032,128]{1,0:T(8,128)S(1)} %collective-permute-done.5.last_ref, f32[512,256]{1,0:T(8,128)S(1)} %shard_map.60.solved_ref, f32[512,256]{1,0:T(8,128)S(1)} %collective-permute-done.9.below_ref, ...), custom_call_target="tpu_custom_call" | custom-call | tf_op jit(solution)/shard_map/pallas_call | solution.py:145
  (9 shorter events, 0.2 us)
Async XLA Ops:
  1.9 12.6 %collective-permute-start = (f32[536,128]{1,0:T(8,128)S(1)}, f32[536,128]{1,0:T(8,128)S(1)}, u32[]{:S(2)}, u32[]{:S(2)}) collective-permute-start(f32[536,128]{1,0:T(8,128)S(1)} %slice.24), channel_id=1, source_target_pairs={{0,3},{1,2},{2,1},{3,0},{4,7},{5,6},{6,5},{7,4},{8,11},{9,10},{10,... | collective-permute-start | bytes 823304 | tf_op jit(solution)/shard_map/ppermute | solution.py:160
  7.0 36.6 %collective-permute-start.6 = (f32[1032,128]{1,0:T(8,128)S(1)}, f32[1032,128]{1,0:T(8,128)S(1)}, u32[]{:S(2)}, u32[]{:S(2)}) collective-permute-start(f32[1032,128]{1,0:T(8,128)S(1)} %slice.27), channel_id=1, source_target_pairs={{0,1},{1,0},{2,3},{3,2},{4,5},{5,4},{6,7},{7,6},{8,9},{9,8},{10,11... | collective-permute-start | bytes 1585160 | tf_op jit(solution)/shard_map/ppermute | solution.py:160
  14.5 22.6 %collective-permute-start.1 = (f32[1024,128]{1,0:T(8,128)S(1)}, f32[1024,128]{1,0:T(8,128)S(1)}, u32[]{:S(2)}, u32[]{:S(2)}) collective-permute-start(f32[1024,128]{1,0:T(8,128)S(1)} %slice.19), channel_id=1, source_target_pairs={{0,3},{1,2},{2,1},{3,0},{4,7},{5,6},{6,5},{7,4},{8,11},{9,10},{10,... | collective-permute-start | bytes 1572872 | tf_op jit(solution)/shard_map/ppermute | solution.py:160
  18.4 25.2 %collective-permute-start.7 = (f32[536,128]{1,0:T(8,128)S(1)}, f32[536,128]{1,0:T(8,128)S(1)}, u32[]{:S(2)}, u32[]{:S(2)}) collective-permute-start(f32[536,128]{1,0:T(8,128)S(1)} %collective-permute-done.refs_1_), channel_id=1, source_target_pairs={{0,1},{1,0},{2,3},{3,2},{4,5},{5,4},{6,7},{7,6},{8,9},{9,8},{10,11... | collective-permute-start | bytes 823304 | tf_op jit(solution)/shard_map/ppermute | solution.py:160
  20.9 27.2 %collective-permute-start.8 = (f32[512,128]{1,0:T(8,128)S(1)}, f32[512,128]{1,0:T(8,128)S(1)}, u32[]{:S(2)}, u32[]{:S(2)}) collective-permute-start(f32[512,128]{1,0:T(8,128)S(1)} %slice.23), channel_id=1, source_target_pairs={{0,1},{1,0},{2,3},{3,2},{4,5},{5,4},{6,7},{7,6},{8,9},{9,8},{10,11... | collective-permute-start | bytes 786440 | tf_op jit(solution)/shard_map/ppermute | solution.py:160
  21.0 4.0 %collective-permute-start.2 = (f32[8,128]{1,0:T(8,128)S(1)}, f32[8,128]{1,0:T(8,128)S(1)}, u32[]{:S(2)}, u32[]{:S(2)}) collective-permute-start(f32[8,128]{1,0:T(8,128)S(1)} %slice_maximum_fusion), channel_id=1, source_target_pairs={{0,4},{4,8},{8,12},{12,16},{16,20},{20,24},{24,28},{28,0},{1,5},{5... | collective-permute-start | bytes 12296 | tf_op jit(solution)/shard_map/ppermute | solution.py:188
  24.9 4.5 %collective-permute-start.3 = (f32[8,128]{1,0:T(8,128)S(1)}, f32[8,128]{1,0:T(8,128)S(1)}, u32[]{:S(2)}, u32[]{:S(2)}) collective-permute-start(f32[8,128]{1,0:T(8,128)S(1)} %max.13), channel_id=1, source_target_pairs={{0,8},{4,12},{8,16},{12,20},{16,24},{20,28},{24,0},{28,4},{1,9},{5... | collective-permute-start | bytes 12296 | tf_op jit(solution)/shard_map/ppermute | solution.py:188
  29.5 3.6 %collective-permute-start.4 = (f32[8,128]{1,0:T(8,128)S(1)}, f32[8,128]{1,0:T(8,128)S(1)}, u32[]{:S(2)}, u32[]{:S(2)}) collective-permute-start(f32[8,128]{1,0:T(8,128)S(1)} %max.14), channel_id=1, source_target_pairs={{0,16},{4,20},{8,24},{12,28},{16,0},{20,4},{24,8},{28,12},{1,17},{... | collective-permute-start | bytes 12296 | tf_op jit(solution)/shard_map/ppermute | solution.py:188
  33.1 10.5 %copy-start.1 = (f32[2,512,128]{2,1,0:T(8,128)S(1)}, f32[2,512,128]{2,1,0:T(8,128)}, u32[]{:S(2)}) copy-start(f32[2,512,128]{2,1,0:T(8,128)} %refs_3_.1) | copy-start | bytes 1572868
  33.1 10.5 %copy-start.2 = (f32[2,512,128]{2,1,0:T(8,128)S(1)}, f32[2,512,128]{2,1,0:T(8,128)}, u32[]{:S(2)}) copy-start(f32[2,512,128]{2,1,0:T(8,128)} %refs_4_.1) | copy-start | bytes 1572868
  37.1 12.5 %copy-start = (f32[2,512,128]{2,1,0:T(8,128)S(1)}, f32[2,512,128]{2,1,0:T(8,128)}, u32[]{:S(2)}) copy-start(f32[2,512,128]{2,1,0:T(8,128)} %level_ref.3) | copy-start | bytes 1572868
  37.1 21.9 %collective-permute-start.5 = (f32[1032,128]{1,0:T(8,128)S(1)}, f32[1032,128]{1,0:T(8,128)S(1)}, u32[]{:S(2)}, u32[]{:S(2)}) collective-permute-start(f32[1032,128]{1,0:T(8,128)S(1)} %shard_map.59), channel_id=1, source_target_pairs={{0,1},{1,0},{2,3},{3,2},{4,5},{5,4},{6,7},{7,6},{8,9},{9,8},{10,11... | collective-permute-start | bytes 1585160 | tf_op jit(solution)/shard_map/ppermute | solution.py:160
  48.1 3.1 %collective-permute-start.9 = (f32[512,256]{1,0:T(8,128)S(1)}, f32[512,256]{1,0:T(8,128)S(1)}, u32[]{:S(2)}, u32[]{:S(2)}) collective-permute-start(f32[512,256]{1,0:T(8,128)S(1)} %shard_map.60.solved_ref), channel_id=1, source_target_pairs={{0,4},{4,8},{8,12},{12,16},{16,20},{20,24},{24,28},{1,5},{5,9},{9,... | collective-permute-start | bytes 1572872 | tf_op jit(solution)/shard_map/ppermute | solution.py:213

commit v22 on v21

--- a/solution.py
+++ b/solution.py
@@ -27,6 +27,13 @@
     (left_high, left_low), (right_high, right_low) = left, right
     dot = lambda a, b: jnp.dot(a, b, preferred_element_type=F32)
     return dot(left_high, right_high) + (dot(left_high, right_low) + dot(left_low, right_high))
+
+
+def joined_dot(left, right):
+    (left_high, left_low), (right_high, right_low) = left, right
+    joined_left = jnp.concatenate([left_high, left_high, left_low], axis=1)
+    joined_right = jnp.concatenate([right_high, right_low, right_high], axis=0)
+    return jnp.dot(joined_left, joined_right, preferred_element_type=F32)
 
 
 def on_diagonal(rows, cols):
@@ -94,7 +101,7 @@
     left = split(jnp.concatenate(blocks, axis=1))
     rows = [rows_of(place, first_slot + at, cols) for at in range(len(blocks))]
     right = split(jnp.concatenate([solved_ref[r, :] for r in rows], axis=0))
-    return exact_dot(left, right)
+    return joined_dot(left, right)
 
 
 def upper_kernel(place, own_ref, near_ref, far_ref, solved_ref, level_ref, part_level, part_up):

time: 61.2 us -> 61 us (level)
  no operation moved by 1% of the time
where the time goes in v22:
time: 61 us; the launch traced here: 60.4 us
  waiting for transfers between devices  31.7 us (52%)
  starting transfers between devices  21.8 us (36%)
  Pallas kernels  6.06 us (10%)
  between operations  0.76 us (1%)
    ppermute x6, waiting for transfers between devices, exchanged(): return lax.ppermute(part, 'col', [(i, i ^ distance) for i in range(shards)])  20.8 us
    ppermute x6, starting transfers between devices, exchanged(): return lax.ppermute(part, 'col', [(i, i ^ distance) for i in range(shards)])  18 us
    ppermute x3, waiting for transfers between devices, per_device(): peaks.append(jnp.maximum(peaks[-1], lax.ppermute(peaks[-1], 'lvl', route)))  9.92 us
    pallas_call x6, Pallas kernels, call(): pl.pallas_call(kernel, out_shape=out_shape, in_specs=in_specs, out_specs=...  6.06 us
    ppermute x3, starting transfers between devices, per_device(): peaks.append(jnp.maximum(peaks[-1], lax.ppermute(peaks[-1], 'lvl', route)))  2.17 us
    ppermute x1, starting transfers between devices, per_device(): lax.ppermute(after(solved, down_near), 'lvl', [(i, i + 1) for i in range(...  1.59 us
  transfers between devices with their start and end apart: 10, of which 8 were waited for; matrix products, arithmetic and copies ran while one was open for 0% of the time, Pallas kernels for 6%

profile of v22, /device:TPU:0, one launch (start us, length us, event | category | flops | bytes accessed | tf_op | source)
XLA Modules:
  0.0 60.4 jit_solution(16126592418975751513)
XLA Ops:
  0.6 1.2 %shard_map.58.own_ref = f32[1544,128]{1,0:T(8,128)S(1)} custom-call(s32[1]{0:T(128)} %bitcast.place, f32[2,512,128]{2,1,0:T(8,128)} %refs_3_.1, f32[2,512,128]{2,1,0:T(8,128)} %level_ref.3, f32[2,512,128]{2,1,0:T(8,128)} %refs_4_.1), custom_call_target="tpu_custom_call" | custom-call | tf_op jit(solution)/shard_map/pallas_call | solution.py:152
  1.9 5.1 %collective-permute-start = (f32[536,128]{1,0:T(8,128)S(1)}, f32[536,128]{1,0:T(8,128)S(1)}, u32[]{:S(2)}, u32[]{:S(2)}) collective-permute-start(f32[536,128]{1,0:T(8,128)S(1)} %slice.24), channel_id=1, source_target_pairs={{0,3},{1,2},{2,1},{3,0},{4,7},{5,6},{6,5},{7,4},{8,11},{9,10},{10,... | collective-permute-start | bytes 823304 | tf_op jit(solution)/shard_map/ppermute | solution.py:167
  7.0 0.1 collective-permute-start.6
  7.1 7.4 %collective-permute-done.refs_1_ = f32[536,128]{1,0:T(8,128)S(1)} collective-permute-done((f32[536,128]{1,0:T(8,128)S(1)}, f32[536,128]{1,0:T(8,128)S(1)}, u32[]{:S(2)}, u32[]{:S(2)}) %collective-permute-start) | collective-permute-done | bytes 274464 | tf_op jit(solution)/shard_map/ppermute | solution.py:167
  14.5 3.8 %collective-permute-start.1 = (f32[1024,128]{1,0:T(8,128)S(1)}, f32[1024,128]{1,0:T(8,128)S(1)}, u32[]{:S(2)}, u32[]{:S(2)}) collective-permute-start(f32[1024,128]{1,0:T(8,128)S(1)} %slice.19), channel_id=1, source_target_pairs={{0,3},{1,2},{2,1},{3,0},{4,7},{5,6},{6,5},{7,4},{8,11},{9,10},{10,... | collective-permute-start | bytes 1572872 | tf_op jit(solution)/shard_map/ppermute | solution.py:167
  18.4 2.5 %collective-permute-start.7 = (f32[536,128]{1,0:T(8,128)S(1)}, f32[536,128]{1,0:T(8,128)S(1)}, u32[]{:S(2)}, u32[]{:S(2)}) collective-permute-start(f32[536,128]{1,0:T(8,128)S(1)} %collective-permute-done.refs_1_), channel_id=1, source_target_pairs={{0,1},{1,0},{2,3},{3,2},{4,5},{5,4},{6,7},{7,6},{8,9},{9,8},{10,11... | collective-permute-start | bytes 823304 | tf_op jit(solution)/shard_map/ppermute | solution.py:167
  20.9 0.1 collective-permute-start.8
  21.0 0.1 collective-permute-start.2
  21.0 3.9 %collective-permute-done.2 = f32[8,128]{1,0:T(8,128)S(1)} collective-permute-done((f32[8,128]{1,0:T(8,128)S(1)}, f32[8,128]{1,0:T(8,128)S(1)}, u32[]{:S(2)}, u32[]{:S(2)}) %collective-permute-start.2) | collective-permute-done | bytes 4128 | tf_op jit(solution)/shard_map/ppermute | solution.py:195
  24.9 0.6 collective-permute-start.3
  25.5 3.9 %collective-permute-done.3 = f32[8,128]{1,0:T(8,128)S(1)} collective-permute-done((f32[8,128]{1,0:T(8,128)S(1)}, f32[8,128]{1,0:T(8,128)S(1)}, u32[]{:S(2)}, u32[]{:S(2)}) %collective-permute-start.3) | collective-permute-done | bytes 4128 | tf_op jit(solution)/shard_map/ppermute | solution.py:195
  29.5 1.5 %collective-permute-start.4 = (f32[8,128]{1,0:T(8,128)S(1)}, f32[8,128]{1,0:T(8,128)S(1)}, u32[]{:S(2)}, u32[]{:S(2)}) collective-permute-start(f32[8,128]{1,0:T(8,128)S(1)} %max.14), channel_id=1, source_target_pairs={{0,16},{4,20},{8,24},{12,28},{16,0},{20,4},{24,8},{28,12},{1,17},{... | collective-permute-start | bytes 12296 | tf_op jit(solution)/shard_map/ppermute | solution.py:195
  31.0 2.1 %collective-permute-done.4 = f32[8,128]{1,0:T(8,128)S(1)} collective-permute-done((f32[8,128]{1,0:T(8,128)S(1)}, f32[8,128]{1,0:T(8,128)S(1)}, u32[]{:S(2)}, u32[]{:S(2)}) %collective-permute-start.4) | collective-permute-done | bytes 4128 | tf_op jit(solution)/shard_map/ppermute | solution.py:195
  33.1 0.0 copy-start.1
  33.1 0.0 copy-start.2
  33.1 4.0 %collective-permute-done.1.refs_0_.far_ref = f32[1024,128]{1,0:T(8,128)S(1)} collective-permute-done((f32[1024,128]{1,0:T(8,128)S(1)}, f32[1024,128]{1,0:T(8,128)S(1)}, u32[]{:S(2)}, u32[]{:S(2)}) %collective-permute-start.1) | collective-permute-done | bytes 524320 | tf_op jit(solution)/shard_map/ppermute | solution.py:167
  37.1 0.0 copy-start
  37.1 6.5 %collective-permute-start.5 = (f32[1032,128]{1,0:T(8,128)S(1)}, f32[1032,128]{1,0:T(8,128)S(1)}, u32[]{:S(2)}, u32[]{:S(2)}) collective-permute-start(f32[1032,128]{1,0:T(8,128)S(1)} %shard_map.59), channel_id=1, source_target_pairs={{0,1},{1,0},{2,3},{3,2},{4,5},{5,4},{6,7},{7,6},{8,9},{9,8},{10,11... | collective-permute-start | bytes 1585160 | tf_op jit(solution)/shard_map/ppermute | solution.py:167
  43.6 0.0 collective-permute-done.6.refs_0_.near_ref
  43.6 0.0 collective-permute-done.7.refs_2_
  43.6 0.0 copy-done.1
  43.6 0.0 copy-done.2
  43.6 2.4 %shard_map.60.solved_ref = f32[512,256]{1,0:T(8,128)S(1)} custom-call(s32[1]{0:T(128)} %bitcast.place, f32[1544,128]{1,0:T(8,128)S(1)} %shard_map.58.own_ref, f32[1032,128]{1,0:T(8,128)S(1)} %collective-permute-done.6.refs_0_.near_ref, f32[536,128]{1,0:T(8,128)S(1)} %collective-permute-done.refs_1_, f32[536,128]{1,0:T(8,128)S(1)} %collective-permute-done.7.refs_2_, ...), custom_call_target="tpu_custom_call" | custom-call | tf_op jit(solution)/shard_map/pallas_call | solution.py:152
  46.0 2.1 %collective-permute-done.8.near_ref = f32[512,128]{1,0:T(8,128)S(1)} collective-permute-done((f32[512,128]{1,0:T(8,128)S(1)}, f32[512,128]{1,0:T(8,128)S(1)}, u32[]{:S(2)}, u32[]{:S(2)}) %collective-permute-start.8) | collective-permute-done | bytes 262176 | tf_op jit(solution)/shard_map/ppermute | solution.py:167
  48.1 1.6 %collective-permute-start.9 = (f32[512,256]{1,0:T(8,128)S(1)}, f32[512,256]{1,0:T(8,128)S(1)}, u32[]{:S(2)}, u32[]{:S(2)}) collective-permute-start(f32[512,256]{1,0:T(8,128)S(1)} %shard_map.60.solved_ref), channel_id=1, source_target_pairs={{0,4},{4,8},{8,12},{12,16},{16,20},{20,24},{24,28},{1,5},{5,9},{9,... | collective-permute-start | bytes 1572872 | tf_op jit(solution)/shard_map/ppermute | solution.py:220
  49.7 0.0 copy-done
  49.7 0.5 shard_map.61
  50.2 0.9 %collective-permute-done.9.below_ref = f32[512,256]{1,0:T(8,128)S(1)} collective-permute-done((f32[512,256]{1,0:T(8,128)S(1)}, f32[512,256]{1,0:T(8,128)S(1)}, u32[]{:S(2)}, u32[]{:S(2)}) %collective-permute-start.9) | collective-permute-done | bytes 524320 | tf_op jit(solution)/shard_map/ppermute | solution.py:220
  51.2 0.5 shard_map.62
  51.7 7.4 %collective-permute-done.5.last_ref = f32[1032,128]{1,0:T(8,128)S(1)} collective-permute-done((f32[1032,128]{1,0:T(8,128)S(1)}, f32[1032,128]{1,0:T(8,128)S(1)}, u32[]{:S(2)}, u32[]{:S(2)}) %collective-permute-start.5) | collective-permute-done | bytes 528416 | tf_op jit(solution)/shard_map/ppermute | solution.py:167
  59.1 1.4 %shard_map.63 = (f32[1,512,128]{2,1,0:T(8,128)}, f32[1,512,128]{2,1,0:T(8,128)}, f32[1,512,128]{2,1,0:T(8,128)}) custom-call(s32[1]{0:T(128)} %bitcast.place, f32[1032,128]{1,0:T(8,128)S(1)} %collective-permute-done.5.last_ref, f32[512,256]{1,0:T(8,128)S(1)} %shard_map.60.solved_ref, f32[512,256]{1,0:T(8,128)S(1)} %collective-permute-done.9.below_ref, ...), custom_call_target="tpu_custom_call" | custom-call | tf_op jit(solution)/shard_map/pallas_call | solution.py:152
  (9 shorter events, 0.2 us)
Async XLA Ops:
  1.9 12.6 %collective-permute-start = (f32[536,128]{1,0:T(8,128)S(1)}, f32[536,128]{1,0:T(8,128)S(1)}, u32[]{:S(2)}, u32[]{:S(2)}) collective-permute-start(f32[536,128]{1,0:T(8,128)S(1)} %slice.24), channel_id=1, source_target_pairs={{0,3},{1,2},{2,1},{3,0},{4,7},{5,6},{6,5},{7,4},{8,11},{9,10},{10,... | collective-permute-start | bytes 823304 | tf_op jit(solution)/shard_map/ppermute | solution.py:167
  7.0 36.6 %collective-permute-start.6 = (f32[1032,128]{1,0:T(8,128)S(1)}, f32[1032,128]{1,0:T(8,128)S(1)}, u32[]{:S(2)}, u32[]{:S(2)}) collective-permute-start(f32[1032,128]{1,0:T(8,128)S(1)} %slice.27), channel_id=1, source_target_pairs={{0,1},{1,0},{2,3},{3,2},{4,5},{5,4},{6,7},{7,6},{8,9},{9,8},{10,11... | collective-permute-start | bytes 1585160 | tf_op jit(solution)/shard_map/ppermute | solution.py:167
  14.5 22.6 %collective-permute-start.1 = (f32[1024,128]{1,0:T(8,128)S(1)}, f32[1024,128]{1,0:T(8,128)S(1)}, u32[]{:S(2)}, u32[]{:S(2)}) collective-permute-start(f32[1024,128]{1,0:T(8,128)S(1)} %slice.19), channel_id=1, source_target_pairs={{0,3},{1,2},{2,1},{3,0},{4,7},{5,6},{6,5},{7,4},{8,11},{9,10},{10,... | collective-permute-start | bytes 1572872 | tf_op jit(solution)/shard_map/ppermute | solution.py:167
  18.4 25.2 %collective-permute-start.7 = (f32[536,128]{1,0:T(8,128)S(1)}, f32[536,128]{1,0:T(8,128)S(1)}, u32[]{:S(2)}, u32[]{:S(2)}) collective-permute-start(f32[536,128]{1,0:T(8,128)S(1)} %collective-permute-done.refs_1_), channel_id=1, source_target_pairs={{0,1},{1,0},{2,3},{3,2},{4,5},{5,4},{6,7},{7,6},{8,9},{9,8},{10,11... | collective-permute-start | bytes 823304 | tf_op jit(solution)/shard_map/ppermute | solution.py:167
  20.9 27.2 %collective-permute-start.8 = (f32[512,128]{1,0:T(8,128)S(1)}, f32[512,128]{1,0:T(8,128)S(1)}, u32[]{:S(2)}, u32[]{:S(2)}) collective-permute-start(f32[512,128]{1,0:T(8,128)S(1)} %slice.23), channel_id=1, source_target_pairs={{0,1},{1,0},{2,3},{3,2},{4,5},{5,4},{6,7},{7,6},{8,9},{9,8},{10,11... | collective-permute-start | bytes 786440 | tf_op jit(solution)/shard_map/ppermute | solution.py:167
  21.0 4.0 %collective-permute-start.2 = (f32[8,128]{1,0:T(8,128)S(1)}, f32[8,128]{1,0:T(8,128)S(1)}, u32[]{:S(2)}, u32[]{:S(2)}) collective-permute-start(f32[8,128]{1,0:T(8,128)S(1)} %slice_maximum_fusion), channel_id=1, source_target_pairs={{0,4},{4,8},{8,12},{12,16},{16,20},{20,24},{24,28},{28,0},{1,5},{5... | collective-permute-start | bytes 12296 | tf_op jit(solution)/shard_map/ppermute | solution.py:195
  24.9 4.5 %collective-permute-start.3 = (f32[8,128]{1,0:T(8,128)S(1)}, f32[8,128]{1,0:T(8,128)S(1)}, u32[]{:S(2)}, u32[]{:S(2)}) collective-permute-start(f32[8,128]{1,0:T(8,128)S(1)} %max.13), channel_id=1, source_target_pairs={{0,8},{4,12},{8,16},{12,20},{16,24},{20,28},{24,0},{28,4},{1,9},{5... | collective-permute-start | bytes 12296 | tf_op jit(solution)/shard_map/ppermute | solution.py:195
  29.5 3.6 %collective-permute-start.4 = (f32[8,128]{1,0:T(8,128)S(1)}, f32[8,128]{1,0:T(8,128)S(1)}, u32[]{:S(2)}, u32[]{:S(2)}) collective-permute-start(f32[8,128]{1,0:T(8,128)S(1)} %max.14), channel_id=1, source_target_pairs={{0,16},{4,20},{8,24},{12,28},{16,0},{20,4},{24,8},{28,12},{1,17},{... | collective-permute-start | bytes 12296 | tf_op jit(solution)/shard_map/ppermute | solution.py:195
  33.1 10.5 %copy-start.1 = (f32[2,512,128]{2,1,0:T(8,128)S(1)}, f32[2,512,128]{2,1,0:T(8,128)}, u32[]{:S(2)}) copy-start(f32[2,512,128]{2,1,0:T(8,128)} %refs_3_.1) | copy-start | bytes 1572868
  33.1 10.5 %copy-start.2 = (f32[2,512,128]{2,1,0:T(8,128)S(1)}, f32[2,512,128]{2,1,0:T(8,128)}, u32[]{:S(2)}) copy-start(f32[2,512,128]{2,1,0:T(8,128)} %refs_4_.1) | copy-start | bytes 1572868
  37.1 12.5 %copy-start = (f32[2,512,128]{2,1,0:T(8,128)S(1)}, f32[2,512,128]{2,1,0:T(8,128)}, u32[]{:S(2)}) copy-start(f32[2,512,128]{2,1,0:T(8,128)} %level_ref.3) | copy-start | bytes 1572868
  37.1 21.9 %collective-permute-start.5 = (f32[1032,128]{1,0:T(8,128)S(1)}, f32[1032,128]{1,0:T(8,128)S(1)}, u32[]{:S(2)}, u32[]{:S(2)}) collective-permute-start(f32[1032,128]{1,0:T(8,128)S(1)} %shard_map.59), channel_id=1, source_target_pairs={{0,1},{1,0},{2,3},{3,2},{4,5},{5,4},{6,7},{7,6},{8,9},{9,8},{10,11... | collective-permute-start | bytes 1585160 | tf_op jit(solution)/shard_map/ppermute | solution.py:167
  48.1 3.1 %collective-permute-start.9 = (f32[512,256]{1,0:T(8,128)S(1)}, f32[512,256]{1,0:T(8,128)S(1)}, u32[]{:S(2)}, u32[]{:S(2)}) collective-permute-start(f32[512,256]{1,0:T(8,128)S(1)} %shard_map.60.solved_ref), channel_id=1, source_target_pairs={{0,4},{4,8},{8,12},{12,16},{16,20},{20,24},{24,28},{1,5},{5,9},{9,... | collective-permute-start | bytes 1572872 | tf_op jit(solution)/shard_map/ppermute | solution.py:220
